TPU v7x, 32 devices: a whole 2x2x4 slice. The times are simulated.
32 devices in a mesh: dp: 8 (over z, x), tensor: 4 (over y, core).
Axes of the slice: x: 2, y: 2, z: 4, core: 2. Of those that a mesh axis runs over, the one named last changes fastest.
Arguments:
- x_in: float32 [8192, 1024], P(('dp', 'tensor')), may hold values from -6 to 6
- cotangent: float32 [8192, 1024], P(('dp', 'tensor')), may hold values from -6 to 6
- lengths: int32 [8], P('dp'), may hold values from 512 to 1024, as said below
- norm_gains: float32 [5, 1024], replicated, may hold values from 0.5 to 1.5
- ffn_first: bfloat16 [2, 1024, 4096], P(None, None, 'tensor'), may hold values from -0.1875 to 0.1875
- attn_qkv: bfloat16 [3, 1024, 1024], P(None, None, 'tensor'), may hold values from -0.1875 to 0.1875
- attn_out: bfloat16 [1024, 1024], P(None, 'tensor'), may hold values from -0.75 to 0.75
- rel_table: float32 [73, 128], replicated, may hold values from -6 to 6
- conv_proj: bfloat16 [3, 1024, 1024], P(None, None, 'tensor'), may hold values from -0.1875 to 0.1875
- depthwise: float32 [5, 1024], P(None, 'tensor'), may hold values from -2.5 to 2.5
- bn_gain: float32 [1024], P('tensor'), may hold values from 0.25 to 1.75
- bn_bias: float32 [1024], P('tensor'), may hold values from -1 to 1
- running: float32 [2, 1024], P(None, 'tensor'), may hold values from 0.1 to 1
- ffn_second: bfloat16 [2, 1024, 4096], P(None, None, 'tensor'), may hold values from -0.1875 to 0.1875
Outputs:
- block_out: float32 [8192, 1024], P(('dp', 'tensor'))
- grad_input: float32 [8192, 1024], P(('dp', 'tensor'))
- grad_norm_gains: float32 [5, 1024], replicated
- grad_ffn_first: float32 [2, 1024, 4096], P(None, 'dp', 'tensor')
- grad_attn_qkv: float32 [3, 1024, 1024], P(None, 'dp', 'tensor')
- grad_attn_out: float32 [1024, 1024], P('dp', 'tensor')
- grad_rel_table: float32 [73, 128], replicated
- grad_conv_proj: float32 [3, 1024, 1024], P(None, 'dp', 'tensor')
- grad_depthwise: float32 [5, 1024], P(None, 'tensor')
- grad_bn_gain: float32 [1024], P('tensor')
- grad_bn_bias: float32 [1024], P('tensor')
- new_running: float32 [2, 1024], P(None, 'tensor')
- grad_ffn_second: float32 [2, 1024, 4096], P(None, 'dp', 'tensor')
Inputs may be any that keep to these rules, and one draw needn't show every extreme that they name: `lengths`: at least one utterance has exactly 1024 frames.
All inputs are finite; a program needn't handle non-finite values.
Results may differ from a plain program's by a relative error of at most 0.04.
Values may be sent and summed in bfloat16 or wider, within the bound.
No kernel may reach another device: no remote copies, remote signals or barrier semaphores. Data moves between devices by JAX's collectives and lax.ppermute only.
A program may use at most 192 MiB of HBM per device.

v0:
```python
import jax
import jax.numpy as jnp
from jax import lax
from jax.sharding import PartitionSpec as P

HEAD = 128
KERNEL = 5
LEFT = 64
RIGHT = 8
SLOT = 1024
UTT_DEV = 1
REL = 73


eps_norm = 1e-05
momentum = 0.5
highest = lax.Precision.HIGHEST


def layer_norm(residual, scaling):
    average = jnp.mean(residual, axis=1, keepdims=True)
    centred = residual - average
    variance = jnp.mean(centred * centred, axis=1, keepdims=True)
    inverse = lax.rsqrt(variance + eps_norm)
    normed = centred * inverse
    return (normed * scaling, normed, inverse)


def norm_back(upstream, normed, inverse, scaling):
    weighted = upstream * scaling
    first_mean = jnp.mean(weighted, axis=1, keepdims=True)
    second_mean = jnp.mean(weighted * normed, axis=1, keepdims=True)
    return (
        inverse * (weighted - first_mean - normed * second_mean),
        jnp.sum(upstream * normed, axis=0),
    )


def silu_slope(preact):
    logistic = jax.nn.sigmoid(preact)
    return logistic * (1.0 + preact * (1.0 - logistic))


def project(left_op, right_op):
    return jnp.dot(left_op, right_op, preferred_element_type=jnp.float32)


def project_back(left_op, right_op):
    return lax.dot_general(
        left_op, right_op, (((1,), (1,)), ((), ())), preferred_element_type=jnp.float32
    )


def outer_sum(left_op, right_op):
    return lax.dot_general(
        left_op, right_op, (((0,), (0,)), ((), ())), preferred_element_type=jnp.float32
    )


def share_rows(own_rows):
    return lax.all_gather(own_rows, "tensor", axis=0, tiled=True)


def reduce_rows(partial_value):
    return lax.psum_scatter(
        partial_value.astype(jnp.bfloat16), "tensor", scatter_dimension=0, tiled=True
    ).astype(jnp.float32)


def out_project(results, weight):
    return reduce_rows(project_back(results, weight))


def share_grads(own_rows):
    return lax.all_gather(own_rows, "tensor", axis=0, tiled=True)


def reduce_grads(partial_value):
    return lax.psum_scatter(
        partial_value.astype(jnp.bfloat16), "tensor", scatter_dimension=0, tiled=True
    ).astype(jnp.float32)


def block_input(own_rows):
    return lax.all_gather(own_rows, "tensor", axis=0, tiled=True)


def feed_forward(residual, scaling, weights):
    scaled, normed, inverse = layer_norm(residual, scaling)
    own_rows = scaled.astype(jnp.bfloat16)
    gathered = share_rows(own_rows)
    preact = project(gathered, weights[0])
    hidden = jax.nn.silu(preact).astype(jnp.bfloat16)
    change = reduce_rows(project_back(hidden, weights[1]))
    return (change, (normed, inverse, own_rows, gathered, preact, hidden))


def feed_back(upstream, scaling, weights, stored):
    normed, inverse, own_rows, gathered, preact, hidden = stored
    upper_grad = share_grads((0.5 * upstream).astype(jnp.bfloat16))
    grad_hidden = project(upper_grad, weights[1])
    grad_pre = (grad_hidden * silu_slope(preact)).astype(jnp.bfloat16)
    inputs_rows = block_input(own_rows)
    weight_grad = jnp.stack([outer_sum(inputs_rows, grad_pre), outer_sum(upper_grad, hidden)])
    grad_scaled = reduce_grads(project_back(grad_pre, weights[0]))
    grad_rows, grad_gain = norm_back(grad_scaled, normed, inverse, scaling)
    return (upstream + grad_rows, grad_gain, (weight_grad,))


def offset_table(count_rows, begin_row):
    width = SLOT + count_rows - 1
    column = jnp.clip(jnp.arange(width) - (count_rows - 1) - begin_row, -LEFT, RIGHT) + LEFT
    return (column[:, None] == jnp.arange(REL)[None, :]).astype(jnp.float32)


def skew_rows(spread):
    heads_dev, count_rows, width = spread.shape
    flat = spread.reshape(heads_dev, count_rows * width)
    flat = flat[:, count_rows - 1 : count_rows - 1 + count_rows * (width - 1)]
    return flat.reshape(heads_dev, count_rows, width - 1)[:, :, :SLOT]


def unskew_rows(band):
    heads_dev, count_rows, _ = band.shape
    width = SLOT + count_rows - 1
    padded = jnp.pad(band, ((0, 0), (0, 0), (0, width - 1 - SLOT)))
    flat = padded.reshape(heads_dev, count_rows * (width - 1))
    flat = jnp.pad(flat, ((0, 0), (count_rows - 1, 1)))
    return flat.reshape(heads_dev, count_rows, width)


def block_scores(query_blk, keys_all, rel_table, begin_row, length):
    count_rows = query_blk.shape[0]
    content = jnp.einsum("qhe,khe->hqk", query_blk, keys_all, preferred_element_type=jnp.float32)
    relative = jnp.einsum(
        "qhe,re->hqr", query_blk.astype(jnp.float32), rel_table, precision=highest
    )
    table = offset_table(count_rows, begin_row)
    spread = jnp.einsum("hqr,wr->hqw", relative, table, precision=highest)
    bias_term = skew_rows(spread)
    key_pos = jnp.arange(keys_all.shape[0])
    logits = (content + bias_term) * HEAD ** (-0.5)
    logits = jnp.where((key_pos < length)[None, None, :], logits, -1e30)
    return (logits, table)


def attend(queries, keys_all, values, length, rel_table):
    block_len = min(512, SLOT)
    outputs = []
    totals = []
    for begin_row in range(0, SLOT, block_len):
        logits, table = block_scores(
            queries[begin_row : begin_row + block_len], keys_all, rel_table, begin_row, length
        )
        row_peak = jnp.max(logits, axis=2, keepdims=True)
        exponent = jnp.exp(logits - row_peak)
        row_total = jnp.sum(exponent, axis=2, keepdims=True)
        soft_rows = (exponent / row_total).astype(jnp.bfloat16)
        outputs.append(
            jnp.einsum("hqk,khe->qhe", soft_rows, values, preferred_element_type=jnp.float32)
        )
        totals.append((row_peak + jnp.log(row_total))[:, :, 0])
    return (jnp.concatenate(outputs, axis=0), jnp.concatenate(totals, axis=1))


def attend_back(queries, keys_all, values, length, log_total, grad_out, rel_table):
    block_len = min(512, SLOT)
    factor = HEAD ** (-0.5)
    grad_queries = []
    grad_keys = jnp.zeros(keys_all.shape, jnp.float32)
    grad_values = jnp.zeros(values.shape, jnp.float32)
    grad_table = jnp.zeros(rel_table.shape, jnp.float32)
    for begin_row in range(0, SLOT, block_len):
        query_blk = queries[begin_row : begin_row + block_len]
        grad_blk = grad_out[begin_row : begin_row + block_len]
        logits, table = block_scores(query_blk, keys_all, rel_table, begin_row, length)
        soft_rows = jnp.exp(logits - log_total[:, begin_row : begin_row + block_len, None])
        grad_soft = jnp.einsum("qhe,khe->hqk", grad_blk, values, preferred_element_type=jnp.float32)
        grad_logit = (
            soft_rows * (grad_soft - jnp.sum(soft_rows * grad_soft, axis=2, keepdims=True))
        ).astype(jnp.bfloat16)
        grad_values = grad_values + jnp.einsum(
            "hqk,qhe->khe",
            soft_rows.astype(jnp.bfloat16),
            grad_blk,
            preferred_element_type=jnp.float32,
        )
        grad_keys = grad_keys + factor * jnp.einsum(
            "hqk,qhe->khe", grad_logit, query_blk, preferred_element_type=jnp.float32
        )
        grad_query = factor * jnp.einsum(
            "hqk,khe->qhe", grad_logit, keys_all, preferred_element_type=jnp.float32
        )
        scaled_grad = factor * grad_logit.astype(jnp.float32)
        grad_rel = jnp.einsum("hqw,wr->hqr", unskew_rows(scaled_grad), table, precision=highest)
        grad_query = grad_query + jnp.einsum("hqr,re->qhe", grad_rel, rel_table, precision=highest)
        grad_table = grad_table + jnp.einsum(
            "hqr,qhe->re", grad_rel, query_blk.astype(jnp.float32), precision=highest
        )
        grad_queries.append(grad_query)
    return (jnp.concatenate(grad_queries, axis=0), grad_keys, grad_values, grad_table)


def attention(residual, scaling, qkv_w, out_w, rel_table, lengths):
    scaled, normed, inverse = layer_norm(residual, scaling)
    own_rows = scaled.astype(jnp.bfloat16)
    gathered = share_rows(own_rows)
    shape_qkv = (UTT_DEV, SLOT, qkv_w.shape[2] // HEAD, HEAD)
    queries = project(gathered, qkv_w[0]).astype(jnp.bfloat16).reshape(shape_qkv)
    keys_all = project(gathered, qkv_w[1]).astype(jnp.bfloat16).reshape(shape_qkv)
    values = project(gathered, qkv_w[2]).astype(jnp.bfloat16).reshape(shape_qkv)
    mixed, log_total = lax.map(
        lambda packed: attend(packed[0], packed[1], packed[2], packed[3], rel_table),
        (queries, keys_all, values, lengths),
    )
    heads_out = mixed.reshape(gathered.shape[0], -1).astype(jnp.bfloat16)
    change = out_project(heads_out, out_w)
    return (
        change,
        (normed, inverse, own_rows, gathered, queries, keys_all, values, log_total, heads_out),
    )


def attention_back(upstream, scaling, qkv_w, out_w, rel_table, lengths, stored):
    normed, inverse, own_rows, gathered, queries, keys_all, values, log_total, heads_out = stored
    upper_grad = share_grads(upstream.astype(jnp.bfloat16))
    grad_heads = project(upper_grad, out_w).astype(jnp.bfloat16).reshape(queries.shape)
    out_grad = outer_sum(upper_grad, heads_out)
    grad_q, grad_k, grad_v, grad_tables = lax.map(
        lambda packed: attend_back(
            packed[0], packed[1], packed[2], packed[3], packed[4], packed[5], rel_table
        ),
        (queries, keys_all, values, lengths, log_total, grad_heads),
    )
    total_rows = gathered.shape[0]
    members = [
        member.reshape(total_rows, -1).astype(jnp.bfloat16) for member in (grad_q, grad_k, grad_v)
    ]
    inputs_rows = block_input(own_rows)
    qkv_grad = jnp.stack([outer_sum(inputs_rows, member) for member in members])
    partial_value = (
        project_back(members[0], qkv_w[0])
        + project_back(members[1], qkv_w[1])
        + project_back(members[2], qkv_w[2])
    )
    grad_scaled = reduce_grads(partial_value)
    grad_rows, grad_gain = norm_back(grad_scaled, normed, inverse, scaling)
    return (
        upstream + grad_rows,
        grad_gain,
        jnp.sum(grad_tables, axis=0),
        (qkv_grad, out_grad[None]),
    )


def depth_mix(kernel_w, framed):
    mixture = kernel_w[0] * framed[:, 0:SLOT]
    for tap_index in range(1, KERNEL):
        mixture = mixture + kernel_w[tap_index] * framed[:, tap_index : tap_index + SLOT]
    return mixture


def convolution(residual, scaling, conv_w, kernel_w, bn_gain, bn_bias, running, lengths, valid):
    scaled, normed, inverse = layer_norm(residual, scaling)
    own_rows = scaled.astype(jnp.bfloat16)
    gathered = share_rows(own_rows)
    linear = project(gathered, conv_w[0])
    gating = jax.nn.sigmoid(project(gathered, conv_w[1]))
    masked = linear * gating * valid[:, None]
    channels = masked.shape[1]
    margin = KERNEL // 2
    framed = jnp.pad(masked.reshape(UTT_DEV, SLOT, channels), ((0, 0), (margin, margin), (0, 0)))
    mixture = depth_mix(kernel_w, framed).reshape(-1, channels)
    sum_first, sum_second, frame_count = lax.psum(
        (
            jnp.sum(mixture * valid[:, None], axis=0),
            jnp.sum(mixture * mixture * valid[:, None], axis=0),
            jnp.sum(lengths).astype(jnp.float32),
        ),
        "dp",
    )
    batch_mean = sum_first / frame_count
    batch_var = sum_second / frame_count - batch_mean * batch_mean
    batch_inv = lax.rsqrt(batch_var + eps_norm)
    centred = (mixture - batch_mean) * batch_inv
    shifted = centred * bn_gain + bn_bias
    active = jax.nn.silu(shifted).astype(jnp.bfloat16)
    change = out_project(active, conv_w[2])
    updated = jnp.stack(
        [
            (1.0 - momentum) * running[0] + momentum * batch_mean,
            (1.0 - momentum) * running[1]
            + momentum * batch_var * frame_count / (frame_count - 1.0),
        ]
    )
    return (
        change,
        updated,
        (
            normed,
            inverse,
            own_rows,
            gathered,
            linear,
            gating,
            framed,
            centred,
            shifted,
            batch_inv,
            active,
            frame_count,
        ),
    )


def convolution_back(upstream, scaling, conv_w, kernel_w, bn_gain, valid, stored):
    (
        normed,
        inverse,
        own_rows,
        gathered,
        linear,
        gating,
        framed,
        centred,
        shifted,
        batch_inv,
        active,
        frame_count,
    ) = stored
    upper_grad = share_grads(upstream.astype(jnp.bfloat16))
    grad_active = project(upper_grad, conv_w[2])
    out_grad = outer_sum(upper_grad, active)
    grad_shift = grad_active * silu_slope(shifted) * valid[:, None]
    gain_grad, bias_grad = lax.psum(
        (jnp.sum(grad_shift * centred, axis=0), jnp.sum(grad_shift, axis=0)), "dp"
    )
    grad_mix = (
        valid[:, None]
        * bn_gain
        * batch_inv
        * (grad_shift - (bias_grad + centred * gain_grad) / frame_count)
    )
    channels = grad_mix.shape[1]
    margin = KERNEL // 2
    framed_grad = grad_mix.reshape(UTT_DEV, SLOT, channels)
    padded_grad = jnp.pad(framed_grad, ((0, 0), (margin, margin), (0, 0)))
    grad_glu = kernel_w[0] * padded_grad[:, 2 * margin : 2 * margin + SLOT]
    for tap_index in range(1, KERNEL):
        grad_glu = (
            grad_glu
            + kernel_w[tap_index]
            * padded_grad[:, 2 * margin - tap_index : 2 * margin - tap_index + SLOT]
        )
    kernel_grad = jnp.stack(
        [
            jnp.sum(framed_grad * framed[:, tap_index : tap_index + SLOT], axis=(0, 1))
            for tap_index in range(KERNEL)
        ]
    )
    kernel_grad = lax.psum(kernel_grad, "dp")
    grad_glu = grad_glu.reshape(-1, channels) * valid[:, None]
    grad_linear = (grad_glu * gating).astype(jnp.bfloat16)
    grad_gating = (grad_glu * linear * gating * (1.0 - gating)).astype(jnp.bfloat16)
    inputs_rows = block_input(own_rows)
    conv_grad = jnp.stack(
        [outer_sum(inputs_rows, grad_linear), outer_sum(inputs_rows, grad_gating), out_grad]
    )
    grad_scaled = reduce_grads(
        project_back(grad_linear, conv_w[0]) + project_back(grad_gating, conv_w[1])
    )
    grad_rows, grad_gain = norm_back(grad_scaled, normed, inverse, scaling)
    return (upstream + grad_rows, grad_gain, kernel_grad, gain_grad, bias_grad, (conv_grad,))


def per_device(
    x_in,
    cotangent,
    lengths,
    norm_gains,
    ffn_first,
    attn_qkv,
    attn_out,
    rel_table,
    conv_proj,
    depthwise,
    bn_gain,
    bn_bias,
    running,
    ffn_second,
):
    valid = (jnp.arange(SLOT)[None, :] < lengths[:, None]).astype(jnp.float32).reshape(-1)
    local_rows = x_in.shape[0]
    own_valid = lax.dynamic_slice_in_dim(valid, lax.axis_index("tensor") * local_rows, local_rows)[
        :, None
    ]
    change, stored_first = feed_forward(x_in, norm_gains[0], ffn_first)
    after_first = x_in + 0.5 * change
    change, stored_attn = attention(
        after_first, norm_gains[1], attn_qkv, attn_out, rel_table, lengths
    )
    after_attn = after_first + change
    change, updated, stored_conv = convolution(
        after_attn, norm_gains[2], conv_proj, depthwise, bn_gain, bn_bias, running, lengths, valid
    )
    after_conv = after_attn + change
    change, stored_last = feed_forward(after_conv, norm_gains[3], ffn_second)
    after_last = after_conv + 0.5 * change
    scaled, normed, inverse = layer_norm(after_last, norm_gains[4])
    output = scaled * own_valid
    upstream, gain_five = norm_back(cotangent * own_valid, normed, inverse, norm_gains[4])
    upstream, gain_four, grads_last = feed_back(upstream, norm_gains[3], ffn_second, stored_last)
    upstream, gain_three, kernel_grad, gain_grad, bias_grad, grads_conv = convolution_back(
        upstream, norm_gains[2], conv_proj, depthwise, bn_gain, valid, stored_conv
    )
    upstream, gain_two, table_grad, grads_attn = attention_back(
        upstream, norm_gains[1], attn_qkv, attn_out, rel_table, lengths, stored_attn
    )
    upstream, gain_one, grads_first = feed_back(upstream, norm_gains[0], ffn_first, stored_first)
    gains_grad, table_grad = lax.psum(
        (jnp.stack([gain_one, gain_two, gain_three, gain_four, gain_five]), table_grad),
        ("dp", "tensor"),
    )
    first_sum, qkv_sum, out_sum, conv_sum, last_sum = (
        lax.psum_scatter(
            grads_first[0].astype(jnp.bfloat16), "dp", scatter_dimension=1, tiled=True
        ).astype(jnp.float32),
        lax.psum_scatter(
            grads_attn[0].astype(jnp.bfloat16), "dp", scatter_dimension=1, tiled=True
        ).astype(jnp.float32),
        lax.psum_scatter(
            grads_attn[1].astype(jnp.bfloat16), "dp", scatter_dimension=1, tiled=True
        ).astype(jnp.float32),
        lax.psum_scatter(
            grads_conv[0].astype(jnp.bfloat16), "dp", scatter_dimension=1, tiled=True
        ).astype(jnp.float32),
        lax.psum_scatter(
            grads_last[0].astype(jnp.bfloat16), "dp", scatter_dimension=1, tiled=True
        ).astype(jnp.float32),
    )
    return (
        output,
        upstream,
        gains_grad,
        first_sum,
        qkv_sum,
        out_sum[0],
        table_grad,
        conv_sum,
        kernel_grad,
        gain_grad,
        bias_grad,
        updated,
        last_sum,
    )


def solution(mesh):
    placed = (
        P(("dp", "tensor"), None),
        P(("dp", "tensor"), None),
        P("dp"),
        P(),
        P(None, None, "tensor"),
        P(None, None, "tensor"),
        P(None, "tensor"),
        P(),
        P(None, None, "tensor"),
        P(None, "tensor"),
        P("tensor"),
        P("tensor"),
        P(None, "tensor"),
        P(None, None, "tensor"),
    )
    return jax.shard_map(
        per_device,
        mesh=mesh,
        in_specs=placed,
        out_specs=(
            P(("dp", "tensor"), None),
            P(("dp", "tensor"), None),
            P(),
            P(None, "dp", "tensor"),
            P(None, "dp", "tensor"),
            P("dp", "tensor"),
            P(),
            P(None, "dp", "tensor"),
            P(None, "tensor"),
            P("tensor"),
            P("tensor"),
            P(None, "tensor"),
            P(None, "dp", "tensor"),
        ),
        check_vma=False,
    )
```

profile of v0, /device:TPU:0, one launch (start us, length us, event | category | flops | bytes accessed | tf_op | source)
XLA Modules:
  0.0 1199.2 jit_solution(12126577997248438853)
XLA Ops:
  13.5 25.4 %all-gather.9.cloned.1.call-done = bf16[1024,1024]{1,0:T(8,128)(2,1)} async-done(((bf16[256,1024]{1,0:T(8,128)(2,1)}), bf16[1024,1024]{1,0:T(8,128)(2,1)}) %all-gather.9.cloned.1.call-update) | async-done | bytes 2097168 | tf_op jit(solution)/shard_map/all_gather | solution.py:61
  49.4 31.5 %reduce-scatter.14.cloned.1.call-done = bf16[256,1024]{1,0:T(8,128)(2,1)} async-done(((bf16[1024,1024]{1,0:T(8,128)(2,1)}), bf16[256,1024]{1,0:T(8,128)(2,1)}) %reduce-scatter.14.cloned.1.call-update) | async-done | bytes 524304 | tf_op jit(solution)/shard_map/reduce_scatter | solution.py:65
  84.3 22.0 %all-gather.11.cloned.1.call-done = bf16[1024,1024]{1,0:T(8,128)(2,1)} async-done(((bf16[256,1024]{1,0:T(8,128)(2,1)}), bf16[1024,1024]{1,0:T(8,128)(2,1)}) %all-gather.11.cloned.1.call-update) | async-done | bytes 2097168 | tf_op jit(solution)/shard_map/all_gather | solution.py:61
  213.9 31.5 %reduce-scatter.16.cloned.1.call-done = bf16[256,1024]{1,0:T(8,128)(2,1)} async-done(((bf16[1024,1024]{1,0:T(8,128)(2,1)}), bf16[256,1024]{1,0:T(8,128)(2,1)}) %reduce-scatter.16.cloned.1.call-update) | async-done | bytes 524304 | tf_op jit(solution)/shard_map/reduce_scatter | solution.py:65
  248.1 22.6 %all-gather.13.cloned.1.call-done = bf16[1024,1024]{1,0:T(8,128)(2,1)} async-done(((bf16[256,1024]{1,0:T(8,128)(2,1)}), bf16[1024,1024]{1,0:T(8,128)(2,1)}) %all-gather.13.cloned.1.call-update) | async-done | bytes 2097168 | tf_op jit(solution)/shard_map/all_gather | solution.py:61
  279.8 21.8 %all-reduce.8 = (f32[256]{0:T(256)S(1)}, f32[256]{0:T(256)S(1)}, f32[]{:T(128)}) all-reduce(f32[256]{0:T(256)S(1)} %get-tuple-element.89, f32[256]{0:T(256)S(1)} %get-tuple-element.88, f32[]{:T(128)S(6)} %convert_element_type.260), channel_id=1, replica_groups=mesh['dp'=8,'tensor'=4] {'dp'}, use_global_device_ids=true, to_apply=%region_16.17 | all-reduce | flops 513 | bytes 4104 | tf_op jit(solution)/shard_map/psum | solution.py:274
  309.0 27.9 %reduce-scatter.18.cloned.1.call-done = bf16[256,1024]{1,0:T(8,128)(2,1)} async-done(((bf16[1024,1024]{1,0:T(8,128)(2,1)}), bf16[256,1024]{1,0:T(8,128)(2,1)}) %reduce-scatter.18.cloned.1.call-update) | async-done | bytes 524304 | tf_op jit(solution)/shard_map/reduce_scatter | solution.py:65
  340.1 22.7 %all-gather.15.cloned.1.call-done = bf16[1024,1024]{1,0:T(8,128)(2,1)} async-done(((bf16[256,1024]{1,0:T(8,128)(2,1)}), bf16[1024,1024]{1,0:T(8,128)(2,1)}) %all-gather.15.cloned.1.call-update) | async-done | bytes 2097168 | tf_op jit(solution)/shard_map/all_gather | solution.py:61
  373.5 31.3 %reduce-scatter.20.cloned.1.call-done = bf16[256,1024]{1,0:T(8,128)(2,1)} async-done(((bf16[1024,1024]{1,0:T(8,128)(2,1)}), bf16[256,1024]{1,0:T(8,128)(2,1)}) %reduce-scatter.20.cloned.1.call-update) | async-done | bytes 524304 | tf_op jit(solution)/shard_map/reduce_scatter | solution.py:65
  409.9 22.7 %all-gather.17.cloned.1.call-done = bf16[1024,1024]{1,0:T(8,128)(2,1)} async-done(((bf16[256,1024]{1,0:T(8,128)(2,1)}), bf16[1024,1024]{1,0:T(8,128)(2,1)}) %all-gather.17.cloned.1.call-update) | async-done | bytes 2097168 | tf_op jit(solution)/shard_map/all_gather | solution.py:75
  444.4 31.5 %reduce-scatter.22.cloned.1.call-done = bf16[256,1024]{1,0:T(8,128)(2,1)} async-done(((bf16[1024,1024]{1,0:T(8,128)(2,1)}), bf16[256,1024]{1,0:T(8,128)(2,1)}) %reduce-scatter.22.cloned.1.call-update) | async-done | bytes 524304 | tf_op jit(solution)/shard_map/reduce_scatter | solution.py:79
  481.2 22.7 %all-gather.19.cloned.1.call-done = bf16[1024,1024]{1,0:T(8,128)(2,1)} async-done(((bf16[256,1024]{1,0:T(8,128)(2,1)}), bf16[1024,1024]{1,0:T(8,128)(2,1)}) %all-gather.19.cloned.1.call-update) | async-done | bytes 2097168 | tf_op jit(solution)/shard_map/all_gather | solution.py:75
  508.0 21.3 %all-reduce.7 = (f32[256]{0:T(256)S(1)}, f32[256]{0:T(256)S(1)}) all-reduce(f32[256]{0:T(256)S(1)} %get-tuple-element.91, f32[256]{0:T(256)S(1)} %get-tuple-element.90), channel_id=1, replica_groups=mesh['dp'=8,'tensor'=4] {'dp'}, use_global_device_ids=true, to_apply=%region_31.32 | all-reduce | flops 512 | bytes 4096 | tf_op jit(solution)/shard_map/psum | solution.py:335
  537.2 27.8 %reduce-scatter.24.cloned.1.call-done = bf16[256,1024]{1,0:T(8,128)(2,1)} async-done(((bf16[1024,1024]{1,0:T(8,128)(2,1)}), bf16[256,1024]{1,0:T(8,128)(2,1)}) %reduce-scatter.24.cloned.1.call-update) | async-done | bytes 524304 | tf_op jit(solution)/shard_map/reduce_scatter | solution.py:79
  569.6 22.7 %all-gather.21.cloned.1.call-done = bf16[1024,1024]{1,0:T(8,128)(2,1)} async-done(((bf16[256,1024]{1,0:T(8,128)(2,1)}), bf16[1024,1024]{1,0:T(8,128)(2,1)}) %all-gather.21.cloned.1.call-update) | async-done | bytes 2097168 | tf_op jit(solution)/shard_map/all_gather | solution.py:75
  711.4 31.5 %reduce-scatter.26.cloned.1.call-done = bf16[256,1024]{1,0:T(8,128)(2,1)} async-done(((bf16[1024,1024]{1,0:T(8,128)(2,1)}), bf16[256,1024]{1,0:T(8,128)(2,1)}) %reduce-scatter.26.cloned.1.call-update) | async-done | bytes 524304 | tf_op jit(solution)/shard_map/reduce_scatter | solution.py:79
  798.7 23.6 %psum.63 = f32[5,256]{1,0:T(8,128)} all-reduce(f32[5,256]{1,0:T(8,128)S(1)} %stack.123), channel_id=1, replica_groups=mesh['dp'=8,'tensor'=4] {'dp'}, use_global_device_ids=true, to_apply=%region_59.60 | all-reduce | flops 1280 | bytes 10240 | tf_op jit(solution)/shard_map/psum | solution.py:361
  822.3 40.4 %reduce-scatter.38.cloned.1.call-done = bf16[2,128,1024]{2,1,0:T(8,128)(2,1)} async-done(((bf16[2,1024,1024]{2,1,0:T(8,128)(2,1)}), bf16[2,128,1024]{2,1,0:T(8,128)(2,1)}) %reduce-scatter.38.cloned.1.call-update) | async-done | bytes 524304 | tf_op jit(solution)/shard_map/reduce_scatter | solution.py:437
  864.8 66.4 %reduce-scatter.36.cloned.1.call-done = bf16[3,128,256]{2,1,0:T(8,128)(2,1)} async-done(((bf16[3,1024,256]{2,1,0:T(8,128)(2,1)}), bf16[3,128,256]{2,1,0:T(8,128)(2,1)}) %reduce-scatter.36.cloned.1.call-update) | async-done | bytes 196624 | tf_op jit(solution)/shard_map/reduce_scatter | solution.py:434
  935.8 60.4 %reduce-scatter.34.cloned.1.call-done = bf16[1,128,256]{2,1,0:T(8,128)(2,1)} async-done(((bf16[1,1024,256]{2,1,0:T(8,128)(2,1)}), bf16[1,128,256]{2,1,0:T(8,128)(2,1)}) %reduce-scatter.34.cloned.1.call-update) | async-done | bytes 65552 | tf_op jit(solution)/shard_map/reduce_scatter | solution.py:431
  997.7 66.5 %reduce-scatter.32.cloned.1.call-done = bf16[3,128,256]{2,1,0:T(8,128)(2,1)} async-done(((bf16[3,1024,256]{2,1,0:T(8,128)(2,1)}), bf16[3,128,256]{2,1,0:T(8,128)(2,1)}) %reduce-scatter.32.cloned.1.call-update) | async-done | bytes 196624 | tf_op jit(solution)/shard_map/reduce_scatter | solution.py:428
  1066.0 31.2 %reduce-scatter.28.cloned.1.call-done = bf16[256,1024]{1,0:T(8,128)(2,1)} async-done(((bf16[1024,1024]{1,0:T(8,128)(2,1)}), bf16[256,1024]{1,0:T(8,128)(2,1)}) %reduce-scatter.28.cloned.1.call-update) | async-done | bytes 524304 | tf_op jit(solution)/shard_map/reduce_scatter | solution.py:79
  1098.7 43.3 %all-reduce.6 = (f32[5,1024]{1,0:T(8,128)}, f32[73,128]{1,0:T(8,128)}) all-reduce(f32[5,1024]{1,0:T(8,128)S(1)} %stack.106, f32[73,128]{1,0:T(8,128)S(1)} %fusion.91), channel_id=1, replica_groups=mesh['dp'=8,'tensor'=4] {'dp','tensor'}, use_global_device_ids=true, to_apply=%region_48.49 | all-reduce | flops 14464 | bytes 115712 | tf_op jit(solution)/shard_map/psum | solution.py:420
  1144.8 45.1 %reduce-scatter.30.cloned.1.call-done = bf16[2,128,1024]{2,1,0:T(8,128)(2,1)} async-done(((bf16[2,1024,1024]{2,1,0:T(8,128)(2,1)}), bf16[2,128,1024]{2,1,0:T(8,128)(2,1)}) %reduce-scatter.30.cloned.1.call-update) | async-done | bytes 524304 | tf_op jit(solution)/shard_map/reduce_scatter | solution.py:425
  (360 shorter events, 387.1 us)
Async XLA Ops:
  7.2 31.7 %all-gather.9.cloned.1.call-start = ((), (), s32[]{:S(2)}) async-start(), calls=%async_computation.13 | async-start | bytes 2621440 | tf_op jit(solution)/shard_map/all_gather | solution.py:61
  13.4 67.5 %reduce-scatter.14.cloned.1.call-start = ((), (), s32[]{:S(2)}) async-start(), calls=%async_computation.14 | async-start | bytes 2621440 | tf_op jit(solution)/shard_map/reduce_scatter | solution.py:65
  49.3 56.9 %all-gather.11.cloned.1.call-start = ((), (), s32[]{:S(2)}) async-start(), calls=%async_computation.15 | async-start | bytes 2621440 | tf_op jit(solution)/shard_map/all_gather | solution.py:61
  83.5 161.9 %reduce-scatter.16.cloned.1.call-start = ((), (), s32[]{:S(2)}) async-start(), calls=%async_computation.16 | async-start | bytes 2621440 | tf_op jit(solution)/shard_map/reduce_scatter | solution.py:65
  213.8 56.9 %all-gather.13.cloned.1.call-start = ((), (), s32[]{:S(2)}) async-start(), calls=%async_computation.17 | async-start | bytes 2621440 | tf_op jit(solution)/shard_map/all_gather | solution.py:61
  248.0 88.9 %reduce-scatter.18.cloned.1.call-start = ((), (), s32[]{:S(2)}) async-start(), calls=%async_computation.18 | async-start | bytes 2621440 | tf_op jit(solution)/shard_map/reduce_scatter | solution.py:65
  309.0 53.9 %all-gather.15.cloned.1.call-start = ((), (), s32[]{:S(2)}) async-start(), calls=%async_computation.19 | async-start | bytes 2621440 | tf_op jit(solution)/shard_map/all_gather | solution.py:61
  340.1 64.7 %reduce-scatter.20.cloned.1.call-start = ((), (), s32[]{:S(2)}) async-start(), calls=%async_computation.20 | async-start | bytes 2621440 | tf_op jit(solution)/shard_map/reduce_scatter | solution.py:65
  373.2 59.3 %all-gather.17.cloned.1.call-start = ((), (), s32[]{:S(2)}) async-start(), calls=%async_computation.21 | async-start | bytes 2621440 | tf_op jit(solution)/shard_map/all_gather | solution.py:75
  409.8 66.1 %reduce-scatter.22.cloned.1.call-start = ((), (), s32[]{:S(2)}) async-start(), calls=%async_computation.22 | async-start | bytes 2621440 | tf_op jit(solution)/shard_map/reduce_scatter | solution.py:79
  444.4 59.5 %all-gather.19.cloned.1.call-start = ((), (), s32[]{:S(2)}) async-start(), calls=%async_computation.23 | async-start | bytes 2621440 | tf_op jit(solution)/shard_map/all_gather | solution.py:75
  481.1 83.9 %reduce-scatter.24.cloned.1.call-start = ((), (), s32[]{:S(2)}) async-start(), calls=%async_computation.24 | async-start | bytes 2621440 | tf_op jit(solution)/shard_map/reduce_scatter | solution.py:79
  537.1 55.2 %all-gather.21.cloned.1.call-start = ((), (), s32[]{:S(2)}) async-start(), calls=%async_computation.25 | async-start | bytes 2621440 | tf_op jit(solution)/shard_map/all_gather | solution.py:75
  569.5 173.4 %reduce-scatter.26.cloned.1.call-start = ((), (), s32[]{:S(2)}) async-start(), calls=%async_computation.26 | async-start | bytes 2621440 | tf_op jit(solution)/shard_map/reduce_scatter | solution.py:79
  711.3 62.4 %all-gather.23.cloned.1.call-start = ((), (), s32[]{:S(2)}) async-start(), calls=%async_computation.27 | async-start | bytes 2621440 | tf_op jit(solution)/shard_map/all_gather | solution.py:75
  747.1 115.6 %reduce-scatter.38.cloned.1.call-start = ((), (), s32[]{:S(2)}) async-start(), calls=%async_computation.33 | async-start | bytes 4718592 | tf_op jit(solution)/shard_map/reduce_scatter | solution.py:437
  756.9 174.4 %reduce-scatter.36.cloned.1.call-start = ((), (), s32[]{:S(2)}) async-start(), calls=%async_computation.32 | async-start | bytes 1769472 | tf_op jit(solution)/shard_map/reduce_scatter | solution.py:434
  764.6 231.6 %reduce-scatter.34.cloned.1.call-start = ((), (), s32[]{:S(2)}) async-start(), calls=%async_computation.31 | async-start | bytes 589824 | tf_op jit(solution)/shard_map/reduce_scatter | solution.py:431
  767.9 296.3 %reduce-scatter.32.cloned.1.call-start = ((), (), s32[]{:S(2)}) async-start(), calls=%async_computation.30 | async-start | bytes 1769472 | tf_op jit(solution)/shard_map/reduce_scatter | solution.py:428
  773.7 323.4 %reduce-scatter.28.cloned.1.call-start = ((), (), s32[]{:S(2)}) async-start(), calls=%async_computation.28 | async-start | bytes 2621440 | tf_op jit(solution)/shard_map/reduce_scatter | solution.py:79
  785.6 404.4 %reduce-scatter.30.cloned.1.call-start = ((), (), s32[]{:S(2)}) async-start(), calls=%async_computation.29 | async-start | bytes 4718592 | tf_op jit(solution)/shard_map/reduce_scatter | solution.py:425
  795.6 301.5 %copy-start.8 = (f32[256,1024]{1,0:T(8,128)S(1)}, f32[256,1024]{1,0:T(8,128)}, u32[]{:S(2)}) copy-start(f32[256,1024]{1,0:T(8,128)} %param.14) | copy-start | bytes 3145732
  795.6 301.5 %copy-start.46 = (f32[1,1024]{1,0:T(1,128)S(1)}, f32[1,1024]{1,0:T(1,128)}, u32[]{:S(2)}) copy-start(f32[1,1024]{1,0:T(1,128)} %copy-done.45) | copy-start | bytes 12292
  795.6 303.0 %copy-start.55 = (f32[1024]{0:T(1024)S(1)}, f32[1024]{0:T(1024)}, u32[]{:S(2)}) copy-start(f32[1024]{0:T(1024)} %get-tuple-element.61) | copy-start | bytes 12292
  (80 other events, 2098.8 us)
Sparse Core Ops, SparseCore 0:
  13.5 25.2 all-gather.8
  49.5 31.4 reduce-scatter.13
  83.7 22.5 all-gather.10
  214.0 31.4 reduce-scatter.15
  248.1 22.5 all-gather.12
  309.1 27.7 reduce-scatter.17
  340.2 22.5 all-gather.14
  373.4 31.4 reduce-scatter.19
  409.9 22.5 all-gather.16
  444.5 31.4 reduce-scatter.21
  481.3 22.5 all-gather.18
  537.2 27.7 reduce-scatter.23
  569.7 22.5 all-gather.20
  711.5 31.4 reduce-scatter.25
  747.3 22.5 all-gather.22
  773.8 88.8 reduce-scatter.37
  866.0 65.2 reduce-scatter.35
  935.4 60.7 reduce-scatter.33
  999.7 64.5 reduce-scatter.31
  1066.8 30.2 reduce-scatter.27
  1100.8 89.1 reduce-scatter.29
where the time goes:
time: 1210 us; the launch traced here: 1200 us
  waiting for transfers between devices  684 us (57%)
  local copies, waits for them, and re-layouts  175 us (14%)
  matrix products  141 us (12%)
  blocking collectives  110 us (9%)
  other arithmetic  69.6 us (6%)
  between operations  17.8 us (1%)
    reduce_scatter x4, waiting for transfers between devices, reduce_rows(): lax.psum_scatter(partial_value.astype(jnp.bfloat16), 'tensor', scatter_di...  122 us
    reduce_scatter x4, waiting for transfers between devices, reduce_grads(): lax.psum_scatter(partial_value.astype(jnp.bfloat16), 'tensor', scatter_di...  122 us
    all_gather x4, waiting for transfers between devices, share_rows(): return lax.all_gather(own_rows, 'tensor', axis=0, tiled=True)  92.8 us
    all_gather x4, waiting for transfers between devices, share_grads(): return lax.all_gather(own_rows, 'tensor', axis=0, tiled=True)  68.1 us
    reduce_scatter x1, waiting for transfers between devices, per_device(): lax.psum_scatter(grads_attn[0].astype(jnp.bfloat16), 'dp', scatter_dimens...  66.5 us
    reduce_scatter x1, waiting for transfers between devices, per_device(): lax.psum_scatter(grads_conv[0].astype(jnp.bfloat16), 'dp', scatter_dimens...  66.4 us
    reduce_scatter x1, waiting for transfers between devices, per_device(): lax.psum_scatter(grads_attn[1].astype(jnp.bfloat16), 'dp', scatter_dimens...  60.4 us
    reduce_scatter x1, waiting for transfers between devices, per_device(): lax.psum_scatter(grads_first[0].astype(jnp.bfloat16), 'dp', scatter_dimen...  45.1 us
  transfers between devices with their start and end apart: 21, of which 20 were waited for; matrix products, arithmetic and copies ran while one was open for 5% of the time, Pallas kernels for 0%

commit v1 on v0

v1 whole, which is shorter than its diff:
```python
import functools

import jax
import jax.numpy as jnp
from jax import lax
from jax.experimental import pallas as pl
from jax.experimental.pallas import tpu as pltpu
from jax.sharding import PartitionSpec as P

HEAD = 128
KERNEL = 5
LEFT = 64
RIGHT = 8
SLOT = 1024
REL = 73
MARGIN = 16
SUB = 128
BLK = 256
WIN = 3 * SUB
WRAP = 512
LOG2E = 1.4426950408889634
VMEM_CAP = 48 * 1024 * 1024

eps_norm = 1e-05
momentum = 0.5
bf16 = jnp.bfloat16
f32 = jnp.float32


def nn(left_op, right_op):
    return lax.dot_general(
        left_op, right_op, (((1,), (0,)), ((), ())), preferred_element_type=f32
    )


def nt(left_op, right_op):
    return lax.dot_general(
        left_op, right_op, (((1,), (1,)), ((), ())), preferred_element_type=f32
    )


def tn(left_op, right_op):
    return lax.dot_general(
        left_op, right_op, (((0,), (0,)), ((), ())), preferred_element_type=f32
    )


def window_table(rel_table):
    u=jnp.arange(WRAP)
    dist=jnp.where(u<=WIN, jnp.clip(u-SUB,-LEFT,RIGHT), -LEFT)+LEFT
    ext=rel_table[dist]
    hi=ext.astype(jnp.bfloat16)
    lo=(ext-hi.astype(jnp.float32)).astype(jnp.bfloat16)
    return hi,lo

def order_in(dst, src, who, rows):
    for j in range(SLOT//rows):
        dst[j*rows:(j+1)*rows,:]=src[pl.ds(pl.multiple_of((j^who)*rows,rows),rows),:]

def attend_kernel(rows, who_ref, len_ref, q_ref, k_ref, v_ref, hi_ref, lo_ref, o_ref, p_ref, qs, ks, vs):
    who=who_ref[0]
    length=len_ref[0]
    order_in(qs,q_ref.at[0],who,rows); order_in(ks,k_ref.at[0],who,rows); order_in(vs,v_ref.at[0],who,rows)
    factor=HEAD**(-0.5)*LOG2E
    tail=lax.broadcasted_iota(jnp.int32,(SUB,SLOT//2),1)+SLOT//2<length
    for base in range(0,SLOT,BLK):
        q=qs[base:base+BLK,:]
        content=nt(q,ks[...])
        spread=nt(q,hi_ref[...])+nt(q,lo_ref[...])
        for off in range(0,BLK,SUB):
            i0=base+off
            e=spread[off:off+SUB]
            rolled=pltpu.roll(e,0,1,stride=1,stride_axis=0)
            lo_c=max(i0-SUB,0); hi_c=min(i0+2*SUB,SLOT)
            parts=[]
            if lo_c>0: parts.append(content[off:off+SUB,:lo_c]+e[:,0:1])
            parts.append(content[off:off+SUB,lo_c:hi_c]+rolled[:,lo_c-(i0-SUB):hi_c-(i0-SUB)])
            if hi_c<SLOT: parts.append(content[off:off+SUB,hi_c:]+e[:,WIN-1:WIN])
            logit=jnp.concatenate(parts,axis=1)*factor
            logit=jnp.concatenate([logit[:,:SLOT//2],jnp.where(tail,logit[:,SLOT//2:],-1e30)],axis=1)
            peak=jnp.max(logit,axis=1,keepdims=True)
            ex=jnp.exp2(logit-peak)
            tot=jnp.sum(ex,axis=1,keepdims=True)
            p_ref[0,i0:i0+SUB,:]=(ex*(1.0/tot)).astype(jnp.bfloat16)
        out=nn(p_ref[0,base:base+BLK,:],vs[...]).astype(jnp.bfloat16)
        for part in range(0,BLK,rows) if rows<BLK else (0,):
            n=min(rows,BLK)
            j=(base+part)//rows; inner=(base+part)%rows
            o_ref[pl.ds(pl.multiple_of((j^who)*rows+inner,n),n),:]=out[part:part+n]

def attend(qkv, who, length, rel_table, rows):
    heads=qkv.shape[2]//HEAD
    hi,lo=window_table(rel_table)
    spec=lambda m: pl.BlockSpec((1,SLOT,HEAD),lambda h,m=m:(m,0,h))
    smem=pl.BlockSpec(memory_space=pltpu.SMEM)
    tab=pl.BlockSpec((WRAP,HEAD),lambda h:(0,0))
    return pl.pallas_call(
        functools.partial(attend_kernel,rows),
        grid=(heads,),
        in_specs=[smem,smem,spec(0),spec(1),spec(2),tab,tab],
        out_specs=[pl.BlockSpec((SLOT,HEAD),lambda h:(0,h)),pl.BlockSpec((1,SLOT,SLOT),lambda h:(h,0,0))],
        out_shape=[jax.ShapeDtypeStruct((SLOT,heads*HEAD),jnp.bfloat16),jax.ShapeDtypeStruct((heads,SLOT,SLOT),jnp.bfloat16)],
        scratch_shapes=[pltpu.VMEM((SLOT,HEAD),jnp.bfloat16)]*3,
        compiler_params=pltpu.CompilerParams(vmem_limit_bytes=VMEM_CAP),
        cost_estimate=pl.CostEstimate(flops=heads*4*SLOT*SLOT*HEAD*2,bytes_accessed=heads*SLOT*SLOT*2,transcendentals=heads*SLOT*SLOT),
        name="attend",
    )(who,length,qkv,qkv,qkv,hi,lo)

def attend_back_kernel(rows, who_ref, q_ref, k_ref, v_ref, g_ref, p_ref, hi_ref, lo_ref, dq_ref, dk_ref, dv_ref, dt_ref, ds_ref, qs, ks, vs, gs, dkt, dvt):
    who=who_ref[0]
    for dst,src in ((qs,q_ref.at[0]),(ks,k_ref.at[0]),(vs,v_ref.at[0]),(gs,g_ref)):
        order_in(dst,src,who,rows)
    factor=HEAD**(-0.5)
    first=hi_ref[0:1,:].astype(jnp.float32)+lo_ref[0:1,:].astype(jnp.float32)
    final=hi_ref[WIN-1:WIN,:].astype(jnp.float32)+lo_ref[WIN-1:WIN,:].astype(jnp.float32)
    zero=jnp.zeros((SUB,SUB),jnp.float32)
    flip=(lax.broadcasted_iota(jnp.int32,(SUB,SUB),0)+lax.broadcasted_iota(jnp.int32,(SUB,SUB),1)==SUB-1).astype(jnp.bfloat16)
    table_acc=jnp.zeros((HEAD,WRAP),jnp.float32)
    left_acc=jnp.zeros((1,HEAD),jnp.float32)
    right_acc=jnp.zeros((1,HEAD),jnp.float32)
    for base in range(0,SLOT,BLK):
        q=qs[base:base+BLK,:]
        g=gs[base:base+BLK,:]
        pb=p_ref[0,base:base+BLK,:]
        p=pb.astype(jnp.float32)
        dp=nt(g,vs[...])
        delta=jnp.sum(p*dp,axis=1,keepdims=True)
        dsb=(p*(dp-delta)).astype(jnp.bfloat16)
        dv_part=tn(g,pb)
        dk_part=tn(q,dsb)
        if base==0:
            dvt[...]=dv_part; dkt[...]=dk_part
        else:
            dvt[...]+=dv_part; dkt[...]+=dk_part
        dq=nn(dsb,ks[...])
        ds=dsb.astype(jnp.float32)
        qf=q.astype(jnp.float32)
        extra=[]
        for off in range(0,BLK,SUB):
            i0=base+off
            d=ds[off:off+SUB]
            lo_c=max(i0-SUB,0); hi_c=min(i0+2*SUB,SLOT)
            turned=nn(flip,dsb[off:off+SUB,lo_c:hi_c])
            win=[zero]*((lo_c-(i0-SUB))//SUB)+[turned]+[zero]*((i0+2*SUB-hi_c)//SUB+1)
            moved=pltpu.roll(jnp.concatenate(win,axis=1),WRAP-SUB+1,1,stride=1,stride_axis=0)
            u=nn(flip,moved.astype(jnp.bfloat16)).astype(jnp.bfloat16)
            add=nn(u,hi_ref[...])+nn(u,lo_ref[...])
            table_acc=table_acc+tn(q[off:off+SUB],u)
            if lo_c>0:
                s=jnp.sum(d[:,:lo_c],axis=1,keepdims=True)
                add=add+s*first
                left_acc=left_acc+jnp.sum(s*qf[off:off+SUB],axis=0,keepdims=True)
            if hi_c<SLOT:
                s=jnp.sum(d[:,hi_c:],axis=1,keepdims=True)
                add=add+s*final
                right_acc=right_acc+jnp.sum(s*qf[off:off+SUB],axis=0,keepdims=True)
            extra.append(add)
        dq=((dq+jnp.concatenate(extra,axis=0))*factor).astype(jnp.bfloat16)
        for part in range(0,BLK,rows) if rows<BLK else (0,):
            n=min(rows,BLK)
            j=(base+part)//rows; inner=(base+part)%rows
            dq_ref[0,pl.ds(pl.multiple_of((j^who)*rows+inner,n),n),:]=dq[part:part+n]
    dt_ref[0]=table_acc*factor
    ds_ref[0]=jnp.concatenate([left_acc,right_acc,jnp.zeros((6,HEAD),jnp.float32)],axis=0)*factor
    for j in range(SLOT//rows):
        sl=pl.ds(pl.multiple_of((j^who)*rows,rows),rows)
        dk_ref[0,sl,:]=(jnp.transpose(dkt[:,j*rows:(j+1)*rows])*factor).astype(jnp.bfloat16)
        dv_ref[0,sl,:]=jnp.transpose(dvt[:,j*rows:(j+1)*rows]).astype(jnp.bfloat16)

def attend_back(qkv, grad, probs, who, rel_table, rows):
    heads=qkv.shape[2]//HEAD
    hi,lo=window_table(rel_table)
    spec=lambda m: pl.BlockSpec((1,SLOT,HEAD),lambda h,m=m:(m,0,h))
    smem=pl.BlockSpec(memory_space=pltpu.SMEM)
    tab=pl.BlockSpec((WRAP,HEAD),lambda h:(0,0))
    out=pl.BlockSpec((1,SLOT,HEAD),lambda h:(0,0,h))
    shape=jax.ShapeDtypeStruct((1,SLOT,heads*HEAD),jnp.bfloat16)
    dq,dk,dv,dt,ends=pl.pallas_call(
        functools.partial(attend_back_kernel,rows),
        grid=(heads,),
        in_specs=[smem,spec(0),spec(1),spec(2),pl.BlockSpec((SLOT,HEAD),lambda h:(0,h)),pl.BlockSpec((1,SLOT,SLOT),lambda h:(h,0,0)),tab,tab],
        out_specs=[out,out,out,pl.BlockSpec((1,HEAD,WRAP),lambda h:(h,0,0)),pl.BlockSpec((1,8,HEAD),lambda h:(h,0,0))],
        out_shape=[shape,shape,shape,jax.ShapeDtypeStruct((heads,HEAD,WRAP),jnp.float32),jax.ShapeDtypeStruct((heads,8,HEAD),jnp.float32)],
        scratch_shapes=[pltpu.VMEM((SLOT,HEAD),jnp.bfloat16)]*4+[pltpu.VMEM((HEAD,SLOT),jnp.float32)]*2,
        compiler_params=pltpu.CompilerParams(vmem_limit_bytes=VMEM_CAP),
        cost_estimate=pl.CostEstimate(flops=heads*6*SLOT*SLOT*HEAD*2,bytes_accessed=heads*SLOT*SLOT*2,transcendentals=0),
        name="attend_back",
    )(who,qkv,qkv,qkv,grad,probs,hi,lo)
    wide=jnp.sum(dt,axis=0).T
    ends=jnp.sum(ends,axis=0)
    near=SUB-LEFT; far=SUB+RIGHT
    left=jnp.sum(wide[:near+1],axis=0)+jnp.sum(wide[WIN+1:],axis=0)+ends[0]
    right=jnp.sum(wide[far:WIN+1],axis=0)+ends[1]
    return dq[0],dk[0],dv[0],jnp.concatenate([left[None],wide[near+1:far],right[None]],axis=0)


class Links:
    def __init__(self, dp, tensor):
        self.dp, self.tensor, self.ny = dp, tensor, tensor // 2
        masks = [1 << bit for bit in range(dp.bit_length() - 1)]
        if len(masks) > 2:
            masks[2] = 6
        self.masks = masks

    def core(self, value):
        return lax.ppermute(value, "tensor", [(i, i ^ 1) for i in range(self.tensor)])

    def chip(self, value, k):
        return lax.ppermute(value, "tensor", [(i, i ^ (2 * k)) for i in range(self.tensor)])

    def group(self, value, mask):
        return lax.ppermute(value, "dp", [(i, i ^ mask) for i in range(self.dp)])

    def sum_group(self, value):
        for mask in self.masks:
            value = value + self.group(value, mask)
        return value

    def sum_chips(self, pieces):
        stacked = jnp.stack(pieces)
        total = stacked
        for k in range(1, self.ny):
            other = self.chip(stacked, k)
            total = total + jnp.stack([other[r ^ k] for r in range(self.ny)])
        return [total[r] for r in range(self.ny)]

    def widen(self, own):
        return jnp.concatenate([own, self.core(own)], axis=0)

    def narrow(self, partial):
        rows = partial.shape[0] // 2
        return partial[:rows].astype(f32) + self.core(partial[rows:]).astype(f32)

    def gather_chips(self, own):
        return [own] + [self.chip(own, k) for k in range(1, self.ny)]

    def order(self):
        return list(range(1, self.ny)) + [0]

    def scatter_chips(self, parts):
        total = parts[0]
        for k in range(1, self.ny):
            total = total + self.chip(parts[k].astype(bf16), k).astype(f32)
        return total

    def spread_chips(self, parts):
        sent = [part.astype(bf16) for part in parts]
        totals = list(parts)
        for k in range(1, self.ny):
            for r in range(self.ny):
                totals[r] = totals[r] + self.chip(sent[r ^ k], k).astype(f32)
        return totals

    def halo(self, own_rows):
        count = own_rows.shape[0]
        y = lax.axis_index("tensor") // 2
        head, foot = own_rows[:MARGIN], own_rows[count - MARGIN :]
        if self.ny == 2:
            other = self.chip(jnp.where(y == 0, foot, head), 1)
            zero = jnp.zeros_like(other)
            return jnp.where(y == 0, zero, other), jnp.where(y == 0, other, zero)
        down = [(i, i + 2) for i in range(self.tensor - 2)]
        up = [(i + 2, i) for i in range(self.tensor - 2)]
        return lax.ppermute(foot, "tensor", down), lax.ppermute(head, "tensor", up)

    def in_order(self, own):
        c = lax.axis_index("tensor") % 2
        mate = self.core(own)
        rows = jnp.where(
            c == 0, jnp.concatenate([own, mate], axis=0), jnp.concatenate([mate, own], axis=0)
        )
        count = own.shape[0]
        y = lax.axis_index("tensor") // 2
        before, after = self.halo(rows)
        return jnp.concatenate([before, rows, after], axis=0)

    def out_order(self, partial):
        c = lax.axis_index("tensor") % 2
        rows = partial.shape[0] // 2
        own = lax.dynamic_slice_in_dim(partial, c * rows, rows)
        mate = lax.dynamic_slice_in_dim(partial, (1 - c) * rows, rows)
        return own.astype(f32) + self.core(mate).astype(f32)

    def reduce_grad(self, grad, turn):
        if self.dp == 1:
            return grad.astype(f32)
        count = len(self.masks)
        masks = [self.masks[(turn + i) % count] for i in range(count)]
        blocks = grad.reshape(self.dp, grad.shape[0] // self.dp, grad.shape[1])
        me = lax.axis_index("dp")

        def pick(offsets):
            return jnp.concatenate(
                [lax.dynamic_index_in_dim(blocks, me ^ off, 0, keepdims=True) for off in offsets]
            )

        offsets = [0]
        for mask in masks[:0:-1]:
            offsets = offsets + [off ^ mask for off in offsets]
        kept = pick(offsets).astype(f32)
        sent = pick([off ^ masks[0] for off in offsets])
        kept = kept + self.group(sent.astype(bf16), masks[0]).astype(f32)
        for mask in masks[1:]:
            half = kept.shape[0] // 2
            kept = kept[:half] + self.group(kept[half:].astype(bf16), mask).astype(f32)
        return kept[0]


def moments(rows):
    centred = rows - jnp.mean(rows, axis=1, keepdims=True)
    inverse = lax.rsqrt(jnp.mean(centred * centred, axis=1, keepdims=True) + eps_norm)
    return centred * inverse, inverse


def norm_back(upstream, rows, scaling):
    normed, inverse = moments(rows)
    weighted = upstream * scaling
    first_mean = jnp.mean(weighted, axis=1, keepdims=True)
    second_mean = jnp.mean(weighted * normed, axis=1, keepdims=True)
    return inverse * (weighted - first_mean - normed * second_mean)


def gain_sum(upstream, rows):
    return jnp.sum(upstream * moments(rows)[0], axis=0)


def normalized(rows, scaling):
    return (moments(rows)[0] * scaling).astype(bf16)


def silu_slope(preact):
    logistic = jax.nn.sigmoid(preact)
    return logistic * (1.0 + preact * (1.0 - logistic))


def feed_forward(links, rows, scaling, weights):
    parts, stored = {}, {}
    for k in range(links.ny):
        inputs = links.widen(normalized(rows[k], scaling))
        preact = nn(inputs, weights[0])
        hidden = jax.nn.silu(preact).astype(bf16)
        parts[k] = links.narrow(nt(hidden, weights[1]).astype(bf16))
        stored[k] = (inputs, preact.astype(bf16), hidden)
    return [parts[k] for k in range(links.ny)], stored


def feed_back(links, upstream, weights, stored):
    parts, seen = {}, {}
    for k in links.order():
        inputs, preact, hidden = stored[k]
        upper = links.widen((0.5 * upstream[k]).astype(bf16))
        grad_pre = (nn(upper, weights[1]) * silu_slope(preact.astype(f32))).astype(bf16)
        parts[k] = links.narrow(nt(grad_pre, weights[0]).astype(bf16))
        seen[k] = (inputs, grad_pre, upper, hidden)
    whole = [jnp.concatenate([seen[k][i] for k in range(links.ny)]) for i in range(4)]
    grads = (tn(whole[0], whole[1]).astype(bf16), tn(whole[2], whole[3]).astype(bf16))
    return [parts[k] for k in range(links.ny)], grads


def per_device(
    links,
    x_in,
    cotangent,
    lengths,
    norm_gains,
    ffn_first,
    attn_qkv,
    attn_out,
    rel_table,
    conv_proj,
    depthwise,
    bn_gain,
    bn_bias,
    running,
    ffn_second,
):
    ny = links.ny
    rows = x_in.shape[0]
    width = x_in.shape[1]
    channels = bn_gain.shape[0]
    who = lax.axis_index("tensor")
    y = who // 2
    length = lengths[0]

    me = lax.axis_index("dp")
    share = width // links.dp
    piece = lax.dynamic_slice_in_dim(conv_proj, me * share, share, axis=1)
    conv_w = [[conv_proj[m] for m in range(3)]]
    for k in range(1, ny):
        other = links.chip(piece, k).reshape(3 * share, channels)
        other = lax.all_gather(other, "dp", axis=0, tiled=True)
        other = other.reshape(links.dp, 3, share, channels)
        conv_w.append([other[:, m].reshape(width, channels) for m in range(3)])
    conv_w = [jnp.concatenate([conv_w[k][m] for k in range(ny)], axis=1) for m in range(3)]
    small = jnp.concatenate([depthwise, bn_gain[None], bn_bias[None], jnp.zeros((1, channels), f32)])
    small = jnp.concatenate(links.gather_chips(small), axis=1)
    taps, scale_bn, bias_bn = small[:KERNEL], small[KERNEL], small[KERNEL + 1]

    resid = [x_in] + [other.astype(f32) for other in links.gather_chips(x_in.astype(bf16))[1:]]
    parts, stored_first = feed_forward(links, resid, norm_gains[0], ffn_first)
    change = links.spread_chips(parts)
    first = [resid[k] + 0.5 * change[k] for k in range(ny)]

    attn_in = [links.widen(normalized(first[k], norm_gains[1])) for k in range(ny)]
    qkv = jnp.concatenate(
        [
            jnp.stack([nn(attn_in[k], attn_qkv[m]).astype(bf16) for m in range(3)])
            for k in range(ny)
        ],
        axis=1,
    )
    who_arr = who.reshape(1).astype(jnp.int32)
    heads_out, probs = attend(qkv, who_arr, lengths, rel_table, rows)
    parts = {}
    for k in links.order():
        piece_k = heads_out[2 * rows * k : 2 * rows * (k + 1)]
        parts[k] = links.narrow(nt(piece_k, attn_out).astype(bf16))
    after_attn = first[0] + links.scatter_chips(parts)

    count = 2 * rows
    lo, hi = MARGIN, MARGIN + count
    position = y * count - MARGIN + jnp.arange(count + 2 * MARGIN)
    valid = ((position >= 0) & (position < length)).astype(f32)[:, None]
    conv_in = links.in_order(normalized(after_attn, norm_gains[2]))
    linear = nn(conv_in, conv_w[0])
    gating = jax.nn.sigmoid(nn(conv_in, conv_w[1]))
    glu = linear * gating * valid

    def shifted_by(array, offset):
        wide = jnp.pad(array, ((2, 2), (0, 0)))
        return wide[2 + offset : 2 + offset + array.shape[0]]

    mixture = sum(taps[j] * shifted_by(glu, j - 2) for j in range(KERNEL))
    inside = valid[lo:hi] * mixture[lo:hi]
    tallies = jnp.concatenate(
        [
            jnp.sum(inside, axis=0)[None],
            jnp.sum(inside * mixture[lo:hi], axis=0)[None],
            jnp.broadcast_to(jnp.sum(valid[lo:hi]), (1, inside.shape[1])),
            jnp.zeros((5, inside.shape[1]), f32),
        ]
    )

    def sum_stats(array):
        cols = [array[:, k * channels : (k + 1) * channels] for k in range(ny)]
        return links.sum_group(jnp.concatenate(links.sum_chips(cols), axis=1))

    tallies = sum_stats(tallies)
    frame_count = tallies[2, 0]
    batch_mean = tallies[0] / frame_count
    batch_var = tallies[1] / frame_count - batch_mean * batch_mean
    batch_inv = lax.rsqrt(batch_var + eps_norm)
    updated = jnp.stack(
        [
            (1.0 - momentum) * running[0] + momentum * batch_mean[:channels],
            (1.0 - momentum) * running[1]
            + momentum * batch_var[:channels] * frame_count / (frame_count - 1.0),
        ]
    )
    centred = (mixture - batch_mean) * batch_inv
    shifted = centred * scale_bn + bias_bn
    active = jax.nn.silu(shifted[lo:hi]).astype(bf16)
    after_conv = after_attn + links.out_order(nt(active, conv_w[2]).astype(bf16))

    upstream_in = links.gather_chips(cotangent.astype(bf16))
    resid = [after_conv] + [o.astype(f32) for o in links.gather_chips(after_conv.astype(bf16))[1:]]
    parts, stored_last = feed_forward(links, resid, norm_gains[3], ffn_second)
    change = links.spread_chips(parts)
    last = [resid[k] + 0.5 * change[k] for k in range(ny)]
    c = who % 2
    own_valid = [
        ((((y ^ k) * 2 + c) * rows + jnp.arange(rows)) < length).astype(f32)[:, None]
        for k in range(ny)
    ]
    output = moments(last[0])[0] * norm_gains[4] * own_valid[0]
    upper = [cotangent] + [other.astype(f32) for other in upstream_in[1:]]
    upper = [upper[k] * own_valid[k] for k in range(ny)]
    gain_five = gain_sum(upper[0], last[0])
    grad = [norm_back(upper[k], last[k], norm_gains[4]) for k in range(ny)]

    parts, grads_last = feed_back(links, grad, ffn_second, stored_last)
    grad_scaled = links.scatter_chips(parts)
    gain_four = gain_sum(grad_scaled, after_conv)
    grad = grad[0] + norm_back(grad_scaled, after_conv, norm_gains[3])

    upper = links.in_order(grad.astype(bf16))
    grad_shift = nn(upper, conv_w[2]) * silu_slope(shifted) * valid
    inner = grad_shift[lo:hi]
    tallies = jnp.concatenate(
        [
            jnp.sum(inner * centred[lo:hi], axis=0)[None],
            jnp.sum(inner, axis=0)[None],
            jnp.zeros((6, inner.shape[1]), f32),
        ]
    )
    tallies = sum_stats(tallies)
    gain_grad, bias_grad = tallies[0], tallies[1]
    grad_mix = (
        valid
        * (scale_bn * batch_inv)
        * (grad_shift - (bias_grad + centred * gain_grad) / frame_count)
    )
    grad_glu = sum(taps[j] * shifted_by(grad_mix, 2 - j) for j in range(KERNEL))[lo:hi]
    grad_glu = grad_glu * valid[lo:hi]
    kernel_grad = jnp.stack(
        [
            jnp.sum(grad_mix[lo:hi] * glu[lo + j - 2 : hi + j - 2], axis=0)
            for j in range(KERNEL)
        ]
    )
    gates = gating[lo:hi]
    grad_linear = (grad_glu * gates).astype(bf16)
    grad_gating = (grad_glu * linear[lo:hi] * gates * (1.0 - gates)).astype(bf16)
    partial = nt(grad_linear, conv_w[0]) + nt(grad_gating, conv_w[1])
    grad_scaled = links.out_order(partial.astype(bf16))
    conv_grads = [
        tn(conv_in[lo:hi], grad_linear).astype(bf16),
        tn(conv_in[lo:hi], grad_gating).astype(bf16),
        tn(upper[lo:hi], active).astype(bf16),
    ]
    gain_three = gain_sum(grad_scaled, after_attn)
    grad = grad + norm_back(grad_scaled, after_attn, norm_gains[2])

    upper = links.gather_chips(grad.astype(bf16))
    grad = [grad] + [other.astype(f32) for other in upper[1:]]
    upper = jnp.concatenate([links.widen(upper[k]) for k in range(ny)])
    grad_heads = nn(upper, attn_out).astype(bf16)
    out_grad = tn(upper, heads_out).astype(bf16)
    grad_q, grad_k, grad_v, table_grad = attend_back(
        qkv, grad_heads, probs, who_arr, rel_table, rows
    )
    members = (grad_q, grad_k, grad_v)
    parts = {}
    for k in links.order():
        partial = sum(
            nt(members[m][2 * rows * k : 2 * rows * (k + 1)], attn_qkv[m]) for m in range(3)
        )
        parts[k] = links.narrow(partial.astype(bf16))
    inputs = jnp.concatenate(attn_in)
    qkv_grads = [tn(inputs, members[m]).astype(bf16) for m in range(3)]
    change = links.spread_chips([parts[k] for k in range(ny)])
    gain_two = gain_sum(change[0], first[0])
    grad = [grad[k] + norm_back(change[k], first[k], norm_gains[1]) for k in range(ny)]

    parts, grads_first = feed_back(links, grad, ffn_first, stored_first)
    grad_scaled = links.scatter_chips(parts)
    gain_one = gain_sum(grad_scaled, x_in)
    grad_input = grad[0] + norm_back(grad_scaled, x_in, norm_gains[0])

    first_sum = jnp.stack([links.reduce_grad(grads_first[m], m) for m in range(2)])
    last_sum = jnp.stack([links.reduce_grad(grads_last[m], m + 1) for m in range(2)])
    wide = jnp.concatenate(qkv_grads + [out_grad], axis=1)
    wide = links.reduce_grad(wide, 2)
    heads_cols = attn_qkv.shape[2]
    qkv_sum = jnp.stack([wide[:, m * heads_cols : (m + 1) * heads_cols] for m in range(3)])
    out_sum = wide[:, 3 * heads_cols :]
    conv_sum = links.reduce_grad(jnp.concatenate(conv_grads, axis=1), 1)
    conv_sum = conv_sum.reshape(share, 3, ny, channels)
    total = conv_sum[:, :, 0]
    for k in range(1, ny):
        total = total + links.chip(conv_sum[:, :, k].astype(bf16), k).astype(f32)
    conv_sum = jnp.swapaxes(total, 0, 1)

    kernel_grad = sum_stats(jnp.pad(kernel_grad, ((0, 3), (0, 0))))[:KERNEL, :channels]
    gains = jnp.stack([gain_one, gain_two, gain_three, gain_four, gain_five]).reshape(-1, HEAD)
    bundle = jnp.concatenate([gains, table_grad])
    bundle = jnp.pad(bundle, ((0, -bundle.shape[0] % 8), (0, 0)))
    bundle = bundle + links.core(bundle)
    for k in [1 << bit for bit in range(ny.bit_length() - 1)]:
        bundle = bundle + links.chip(bundle, k)
    bundle = links.sum_group(bundle)
    return (
        output,
        grad_input,
        bundle[: gains.shape[0]].reshape(5, width),
        first_sum,
        qkv_sum,
        out_sum,
        bundle[gains.shape[0] : gains.shape[0] + REL],
        conv_sum,
        kernel_grad,
        gain_grad[:channels],
        bias_grad[:channels],
        updated,
        last_sum,
    )


def solution(mesh):
    links = Links(mesh.shape["dp"], mesh.shape["tensor"])
    placed = (
        P(("dp", "tensor"), None),
        P(("dp", "tensor"), None),
        P("dp"),
        P(),
        P(None, None, "tensor"),
        P(None, None, "tensor"),
        P(None, "tensor"),
        P(),
        P(None, None, "tensor"),
        P(None, "tensor"),
        P("tensor"),
        P("tensor"),
        P(None, "tensor"),
        P(None, None, "tensor"),
    )
    return jax.shard_map(
        functools.partial(per_device, links),
        mesh=mesh,
        in_specs=placed,
        out_specs=(
            P(("dp", "tensor"), None),
            P(("dp", "tensor"), None),
            P(),
            P(None, "dp", "tensor"),
            P(None, "dp", "tensor"),
            P("dp", "tensor"),
            P(),
            P(None, "dp", "tensor"),
            P(None, "tensor"),
            P("tensor"),
            P("tensor"),
            P(None, "tensor"),
            P(None, "dp", "tensor"),
        ),
        check_vma=False,
    )
```

time: 1210 us -> 643 us (0.53)
  waiting for transfers between devices: 684 us -> 260 us
  local copies, waits for them, and re-layouts: 175 us -> 52.7 us
  starting transfers between devices: 1.52 us -> 117 us
  blocking collectives: 110 us -> 0 us
  matrix products: 141 us -> 82.7 us
  Pallas kernels: 0 us -> 25.5 us
    reduce_scatter x13 -> x0, waiting for transfers between devices: 523 us -> none  [the longest x4 122 us: reduce_rows(): lax.psum_scatter(partial_value.astype(jnp.bfloat16), 'tensor', scatter_di...]
    ppermute x0 -> x81, waiting for transfers between devices: none -> 241 us  [the longest x22 124 us: chip(): lax.ppermute(value, 'tensor', [(i, i ^ 2 * k) for i in range(self.tensor)])]
    all_gather x8 -> x1, waiting for transfers between devices: 161 us -> 18.9 us  [per_device(): other = lax.all_gather(other, 'dp', axis=0, tiled=True)]
    ppermute x0 -> x81, starting transfers between devices: none -> 116 us  [the longest x30 82.6 us: group(): return lax.ppermute(value, 'dp', [(i, i ^ mask) for i in range(self.dp)])]
    psum x4 -> x0, blocking collectives: 110 us -> none  [the longest x1 43.3 us: per_device(): lax.psum((jnp.stack([gain_one, gain_two, gain_three, gain_four, gain_five...]
    reshape x8 -> x4, local copies, waits for them, and re-layouts: 109 us -> 3.6 us  [the longest x1 2.85 us: reduce_grad(): blocks = grad.reshape(self.dp, grad.shape[0] // self.dp, grad.shape[1])]
    dot_general x55 -> x48, matrix products: 141 us -> 82.7 us  [the longest x18 31.9 us: nn(): lax.dot_general(left_op, right_op, (((1,), (0,)), ((), ())), preferred_el...]
    pad x4 -> x0, local copies, waits for them, and re-layouts: 27.5 us -> none  [the longest x2 20.8 us: unskew_rows(): flat = jnp.pad(flat, ((0, 0), (count_rows - 1, 1)))]
  transfers between devices with their start and end apart: 21 -> 82, of which waited for: 20 -> 34; matrix products, arithmetic and copies ran while one was open for 5% -> 27% of each run, Pallas kernels for 0% -> 2%
where the time goes in v1:
time: 643 us; the launch traced here: 633 us
  waiting for transfers between devices  260 us (40%)
  starting transfers between devices  117 us (18%)
  matrix products  82.7 us (13%)
  other arithmetic  76.5 us (12%)
  local copies, waits for them, and re-layouts  52.7 us (8%)
  Pallas kernels  25.5 us (4%)
  between operations  19.7 us (3%)
    ppermute x22, waiting for transfers between devices, chip(): lax.ppermute(value, 'tensor', [(i, i ^ 2 * k) for i in range(self.tensor)])  124 us
    ppermute x30, waiting for transfers between devices, group(): return lax.ppermute(value, 'dp', [(i, i ^ mask) for i in range(self.dp)])  115 us
    ppermute x30, starting transfers between devices, group(): return lax.ppermute(value, 'dp', [(i, i ^ mask) for i in range(self.dp)])  82.6 us
    dot_general x18, matrix products, nn(): lax.dot_general(left_op, right_op, (((1,), (0,)), ((), ())), preferred_el...  31.9 us
    ppermute x22, starting transfers between devices, chip(): lax.ppermute(value, 'tensor', [(i, i ^ 2 * k) for i in range(self.tensor)])  28.8 us
    dot_general x19, matrix products, nt(): lax.dot_general(left_op, right_op, (((1,), (1,)), ((), ())), preferred_el...  26.9 us
    dot_general x11, matrix products, tn(): lax.dot_general(left_op, right_op, (((0,), (0,)), ((), ())), preferred_el...  23.9 us
    all_gather x1, waiting for transfers between devices, per_device(): other = lax.all_gather(other, 'dp', axis=0, tiled=True)  18.9 us
  transfers between devices with their start and end apart: 82, of which 34 were waited for; matrix products, arithmetic and copies ran while one was open for 27% of the time, Pallas kernels for 2%

profile of v1, /device:TPU:0, one launch (start us, length us, event | category | flops | bytes accessed | tf_op | source)
XLA Modules:
  0.0 633.4 jit_solution(4009723748628739366)
XLA Ops:
  14.5 11.9 %collective-permute-done.2 = bf16[256,1024]{1,0:T(8,128)(2,1)S(1)} collective-permute-done((bf16[256,1024]{1,0:T(8,128)(2,1)S(1)}, bf16[256,1024]{1,0:T(8,128)(2,1)S(1)}, u32[]{:S(2)}, u32[]{:S(2)}) %collective-permute-start.2) | collective-permute-done | bytes 524320 | tf_op jit(solution)/shard_map/ppermute | solution.py:209
  37.5 12.6 %collective-permute-done.7 = bf16[256,1024]{1,0:T(8,128)(2,1)S(1)} collective-permute-done((bf16[256,1024]{1,0:T(8,128)(2,1)S(1)}, bf16[256,1024]{1,0:T(8,128)(2,1)S(1)}, u32[]{:S(2)}, u32[]{:S(2)}) %collective-permute-start.7) | collective-permute-done | bytes 524320 | tf_op jit(solution)/shard_map/ppermute | solution.py:209
  52.6 11.5 %collective-permute-done.5 = bf16[256,1024]{1,0:T(8,128)(2,1)S(1)} collective-permute-done((bf16[256,1024]{1,0:T(8,128)(2,1)S(1)}, bf16[256,1024]{1,0:T(8,128)(2,1)S(1)}, u32[]{:S(2)}, u32[]{:S(2)}) %collective-permute-start.5) | collective-permute-done | bytes 524320 | tf_op jit(solution)/shard_map/ppermute | solution.py:209
  74.6 10.3 %attend.1 = (bf16[1024,256]{1,0:T(8,128)(2,1)S(1)}, bf16[2,1024,1024]{2,1,0:T(8,128)(2,1)}) custom-call(s32[1]{0:T(128)} %bitcast.3.who_ref, s32[1]{0:T(128)} %copy.177.len_ref, bf16[3,1024,256]{2,1,0:T(8,128)(2,1)S(1)} %maximum_maximum_fusion.q_ref.k_ref.v_ref, bf16[3,1024,256]{2,1,0:T(8,128)(2,1)S(1)} %maximum_maximum_fusion.q_ref.k_ref.v_ref, ...), custom_call_target="tpu_custom_call" | custom-call | flops 2147483648 | bytes 4194304 | tf_op jit(solution)/shard_map/attend/pallas_call | solution.py:97
  89.5 5.4 collective-permute-done.15
  102.6 9.7 %collective-permute-done.11 = bf16[256,1024]{1,0:T(8,128)(2,1)} collective-permute-done((bf16[256,1024]{1,0:T(8,128)(2,1)S(1)}, bf16[256,1024]{1,0:T(8,128)(2,1)}, u32[]{:S(2)}, u32[]{:S(2)}) %collective-permute-start.11) | collective-permute-done | bytes 524320 | tf_op jit(solution)/shard_map/ppermute | solution.py:209
  121.6 18.9 %all-gather.2.cloned.1.call-done = bf16[3072,256]{1,0:T(8,128)(2,1)} async-done(((bf16[384,256]{1,0:T(8,128)(2,1)}), bf16[3072,256]{1,0:T(8,128)(2,1)}) %all-gather.2.cloned.1.call-update) | async-done | bytes 1572880 | tf_op jit(solution)/shard_map/all_gather | solution.py:391
  166.1 4.8 multiply_add_fusion
  178.9 12.5 %collective-permute-done.23 = bf16[256,1024]{1,0:T(8,128)(2,1)S(1)} collective-permute-done((bf16[256,1024]{1,0:T(8,128)(2,1)S(1)}, bf16[256,1024]{1,0:T(8,128)(2,1)S(1)}, u32[]{:S(2)}, u32[]{:S(2)}) %collective-permute-start.23) | collective-permute-done | bytes 524320 | tf_op jit(solution)/shard_map/ppermute | solution.py:209
  205.4 12.1 %collective-permute-done.29 = bf16[256,1024]{1,0:T(8,128)(2,1)} collective-permute-done((bf16[256,1024]{1,0:T(8,128)(2,1)}, bf16[256,1024]{1,0:T(8,128)(2,1)}, u32[]{:S(2)}, u32[]{:S(2)}) %collective-permute-start.29) | collective-permute-done | bytes 524320 | tf_op jit(solution)/shard_map/ppermute | solution.py:209
  221.1 18.4 %collective-permute-done.26 = bf16[256,1024]{1,0:T(8,128)(2,1)S(1)} collective-permute-done((bf16[256,1024]{1,0:T(8,128)(2,1)S(1)}, bf16[256,1024]{1,0:T(8,128)(2,1)S(1)}, u32[]{:S(2)}, u32[]{:S(2)}) %collective-permute-start.26) | collective-permute-done | bytes 524320 | tf_op jit(solution)/shard_map/ppermute | solution.py:209
  262.5 9.2 %collective-permute-done.33 = bf16[256,1024]{1,0:T(8,128)(2,1)S(1)} collective-permute-done((bf16[256,1024]{1,0:T(8,128)(2,1)S(1)}, bf16[256,1024]{1,0:T(8,128)(2,1)S(1)}, u32[]{:S(2)}, u32[]{:S(2)}) %collective-permute-start.33) | collective-permute-done | bytes 524320 | tf_op jit(solution)/shard_map/ppermute | solution.py:209
  282.7 5.0 collective-permute-done.75
  293.1 18.0 %collective-permute-done.78 = bf16[4,128,1024]{2,1,0:T(8,128)(2,1)S(1)} collective-permute-done((bf16[4,128,1024]{2,1,0:T(8,128)(2,1)S(1)}, bf16[4,128,1024]{2,1,0:T(8,128)(2,1)S(1)}, u32[]{:S(2)}, u32[]{:S(2)}) %collective-permute-start.78) | collective-permute-done | bytes 1048608 | tf_op jit(solution)/shard_map/ppermute | solution.py:212
  313.7 7.7 %collective-permute-done.76 = bf16[2,128,1024]{2,1,0:T(8,128)(2,1)S(1)} collective-permute-done((bf16[2,128,1024]{2,1,0:T(8,128)(2,1)S(1)}, bf16[2,128,1024]{2,1,0:T(8,128)(2,1)S(1)}, u32[]{:S(2)}, u32[]{:S(2)}) %collective-permute-start.76) | collective-permute-done | bytes 524320 | tf_op jit(solution)/shard_map/ppermute | solution.py:212
  323.9 28.0 %collective-permute-start.38 = (f32[8,512]{1,0:T(8,128)S(1)}, f32[8,512]{1,0:T(8,128)S(1)}, u32[]{:S(2)}, u32[]{:S(2)}) collective-permute-start(f32[8,512]{1,0:T(8,128)S(1)} %fusion.335), channel_id=1, source_target_pairs={{0,8},{4,12},{8,0},{12,4},{16,24},{20,28},{24,16},{28,20},{1,9},{5... | collective-permute-start | bytes 49160 | tf_op jit(solution)/shard_map/ppermute | solution.py:212
  374.9 6.5 %constant_dynamic-slice_fusion.23 = (bf16[1,128,1536]{1,0,2:T(2,128)(2,1)S(1)}, bf16[1,128,1536]{1,0,2:T(2,128)(2,1)S(1)}, bf16[1,128,1536]{1,0,2:T(2,128)(2,1)S...) fusion(bf16[8,128,1536]{1,0,2:T(8,128)(2,1)S(1)} %bitcast.273, ...), kind=kLoop, calls=%fused_computation.499 | loop fusion | bytes 6291488 | tf_op jit(solution)/shard_map/jit(dynamic_index_in_dim)/dynamic_slice | solution.py:294
  402.5 5.9 collective-permute-done.42
  408.4 17.5 %collective-permute-done.67 = bf16[4,128,1536]{1,2,0:T(8,128)(2,1)S(1)} collective-permute-done((bf16[4,128,1536]{1,2,0:T(8,128)(2,1)S(1)}, bf16[4,128,1536]{1,2,0:T(8,128)(2,1)S(1)}, u32[]{:S(2)}, u32[]{:S(2)}) %collective-permute-start.67) | collective-permute-done | bytes 1572896 | tf_op jit(solution)/shard_map/ppermute | solution.py:212
  429.9 15.2 %attend_back.1 = (bf16[1,1024,256]{2,1,0:T(8,128)(2,1)S(1)}, bf16[1,1024,256]{2,1,0:T(8,128)(2,1)S(1)}, bf16[1,1024,256]{2,1,0:T(8,128)(2,1)S(1)}, f32[2,128,512]{2,1,0:T(8,128)S(1)}, f32[2,8,128]{2,1,0:T(8,128)S(1)}) custom-call(s32[1]{0:T(128)} %bitcast.3.who_ref, bf16[3,1024,256]{2,1,0:T(8,128)(2,1)S(1)} %maximum_maximum_fusion.q_ref.k_ref.v_ref, ...), custom_call_target="tpu_custom_call" | custom-call | flops 3221225472 | bytes 4194304 | tf_op jit(solution)/shard_map/attend_back/pallas_call | solution.py:178
  484.2 18.1 %collective-permute-done.64 = bf16[4,128,1024]{2,1,0:T(8,128)(2,1)} collective-permute-done((bf16[4,128,1024]{2,1,0:T(8,128)(2,1)}, bf16[4,128,1024]{2,1,0:T(8,128)(2,1)}, u32[]{:S(2)}, u32[]{:S(2)}) %collective-permute-start.64) | collective-permute-done | bytes 1048608 | tf_op jit(solution)/shard_map/ppermute | solution.py:212
  521.2 20.1 %collective-permute-start.66 = (bf16[1,128,1024]{2,1,0:T(8,128)(2,1)S(1)}, bf16[1,128,1024]{2,1,0:T(8,128)(2,1)S(1)}, u32[]{:S(2)}, u32[]{:S(2)}) collective-permute-start(bf16[1,128,1024]{2,1,0:T(8,128)(2,1)S(1)} %slice.1163), channel_id=1, source_target_pairs={{0,8},{4,12},{8,0},{12,4},{16,24},{20,28},{24,16},{28,20},{1,9},{5... | collective-permute-start | bytes 786440 | tf_op jit(solution)/shard_map/ppermute | solution.py:212
  564.8 11.7 %collective-permute-done.52 = bf16[256,1024]{1,0:T(8,128)(2,1)S(1)} collective-permute-done((bf16[256,1024]{1,0:T(8,128)(2,1)S(1)}, bf16[256,1024]{1,0:T(8,128)(2,1)S(1)}, u32[]{:S(2)}, u32[]{:S(2)}) %collective-permute-start.52) | collective-permute-done | bytes 524320 | tf_op jit(solution)/shard_map/ppermute | solution.py:209
  595.0 15.1 %collective-permute-done.56 = f32[120,128]{0,1:T(8,128)S(1)} collective-permute-done((f32[120,128]{0,1:T(8,128)S(1)}, f32[120,128]{0,1:T(8,128)S(1)}, u32[]{:S(2)}, u32[]{:S(2)}) %collective-permute-start.56) | collective-permute-done | bytes 61472 | tf_op jit(solution)/shard_map/ppermute | solution.py:212
  (772 shorter events, 307.7 us)
Async XLA Ops:
  7.2 133.2 %all-gather.2.cloned.1.call-start = ((), (), s32[]{:S(2)}) async-start(), calls=%async_computation | async-start | bytes 1769472 | tf_op jit(solution)/shard_map/all_gather | solution.py:391
  119.8 23.1 %collective-permute-start.14 = (bf16[16,1024]{1,0:T(8,128)(2,1)S(1)}, bf16[16,1024]{1,0:T(8,128)(2,1)S(1)}, u32[]{:S(2)}, u32[]{:S(2)}) collective-permute-start(bf16[16,1024]{1,0:T(8,128)(2,1)S(1)} %slice_select_fusion.1), channel_id=1, source_target_pairs={{0,2},{1,3},{2,0},{3,1},{4,6},{5,7},{6,4},{7,5},{8,10},{9,11},{10,... | collective-permute-start | bytes 98312 | tf_op jit(solution)/shard_map/ppermute | solution.py:209
  204.8 35.2 %collective-permute-start.30 = (bf16[256,1024]{1,0:T(8,128)(2,1)}, bf16[256,1024]{1,0:T(8,128)(2,1)}, u32[]{:S(2)}, u32[]{:S(2)}) collective-permute-start(bf16[256,1024]{1,0:T(8,128)(2,1)} %convert_element_type.555), channel_id=1, source_target_pairs={{0,2},{1,3},{2,0},{3,1},{4,6},{5,7},{6,4},{7,5},{8,10},{9,11},{10,... | collective-permute-start | bytes 1572872 | tf_op jit(solution)/shard_map/ppermute | solution.py:209
  262.3 25.4 %collective-permute-start.75 = (bf16[4,128,1024]{2,1,0:T(8,128)(2,1)S(1)}, bf16[4,128,1024]{2,1,0:T(8,128)(2,1)S(1)}, u32[]{:S(2)}, u32[]{:S(2)}) collective-permute-start(bf16[4,128,1024]{2,1,0:T(8,128)(2,1)S(1)} %pad_maximum_fusion.14), channel_id=1, source_target_pairs={{0,8},{4,12},{8,0},{12,4},{16,24},{20,28},{24,16},{28,20},{1,9},{5... | collective-permute-start | bytes 3145736 | tf_op jit(solution)/shard_map/ppermute | solution.py:212
  278.4 32.6 %collective-permute-start.78 = (bf16[4,128,1024]{2,1,0:T(8,128)(2,1)S(1)}, bf16[4,128,1024]{2,1,0:T(8,128)(2,1)S(1)}, u32[]{:S(2)}, u32[]{:S(2)}) collective-permute-start(bf16[4,128,1024]{2,1,0:T(8,128)(2,1)S(1)} %pad_maximum_fusion.15), channel_id=1, source_target_pairs={{0,24},{4,28},{8,16},{12,20},{16,8},{20,12},{24,0},{28,4},{1,25},{... | collective-permute-start | bytes 3145736 | tf_op jit(solution)/shard_map/ppermute | solution.py:212
  288.1 33.3 %collective-permute-start.76 = (bf16[2,128,1024]{2,1,0:T(8,128)(2,1)S(1)}, bf16[2,128,1024]{2,1,0:T(8,128)(2,1)S(1)}, u32[]{:S(2)}, u32[]{:S(2)}) collective-permute-start(bf16[2,128,1024]{2,1,0:T(8,128)(2,1)S(1)} %slice.1156), channel_id=1, source_target_pairs={{0,24},{4,28},{8,16},{12,20},{16,8},{20,12},{24,0},{28,4},{1,25},{... | collective-permute-start | bytes 1572872 | tf_op jit(solution)/shard_map/ppermute | solution.py:212
  311.5 40.5 %collective-permute-start.79 = (bf16[2,128,1024]{2,1,0:T(8,128)(2,1)S(1)}, bf16[2,128,1024]{2,1,0:T(8,128)(2,1)S(1)}, u32[]{:S(2)}, u32[]{:S(2)}) collective-permute-start(bf16[2,128,1024]{2,1,0:T(8,128)(2,1)S(1)} %slice.1155), channel_id=1, source_target_pairs={{0,4},{4,0},{8,12},{12,8},{16,20},{20,16},{24,28},{28,24},{1,5},{5... | collective-permute-start | bytes 1572872 | tf_op jit(solution)/shard_map/ppermute | solution.py:212
  322.4 77.0 %collective-permute-start.77 = (bf16[1,128,1024]{2,1,0:T(8,128)(2,1)}, bf16[1,128,1024]{2,1,0:T(8,128)(2,1)}, u32[]{:S(2)}, u32[]{:S(2)}) collective-permute-start(bf16[1,128,1024]{2,1,0:T(8,128)(2,1)} %slice.1162), channel_id=1, source_target_pairs={{0,4},{4,0},{8,12},{12,8},{16,20},{20,16},{24,28},{28,24},{1,5},{5... | collective-permute-start | bytes 786440 | tf_op jit(solution)/shard_map/ppermute | solution.py:212
  323.9 29.8 %collective-permute-start.38 = (f32[8,512]{1,0:T(8,128)S(1)}, f32[8,512]{1,0:T(8,128)S(1)}, u32[]{:S(2)}, u32[]{:S(2)}) collective-permute-start(f32[8,512]{1,0:T(8,128)S(1)} %fusion.335), channel_id=1, source_target_pairs={{0,8},{4,12},{8,0},{12,4},{16,24},{20,28},{24,16},{28,20},{1,9},{5... | collective-permute-start | bytes 49160 | tf_op jit(solution)/shard_map/ppermute | solution.py:212
  352.9 47.4 %collective-permute-start.80 = (bf16[1,128,1024]{2,1,0:T(8,128)(2,1)}, bf16[1,128,1024]{2,1,0:T(8,128)(2,1)}, u32[]{:S(2)}, u32[]{:S(2)}) collective-permute-start(bf16[1,128,1024]{2,1,0:T(8,128)(2,1)} %slice.1161), channel_id=1, source_target_pairs={{0,8},{4,12},{8,0},{12,4},{16,24},{20,28},{24,16},{28,20},{1,9},{5... | collective-permute-start | bytes 786440 | tf_op jit(solution)/shard_map/ppermute | solution.py:212
  392.4 33.5 %collective-permute-start.67 = (bf16[4,128,1536]{1,2,0:T(8,128)(2,1)S(1)}, bf16[4,128,1536]{1,2,0:T(8,128)(2,1)S(1)}, u32[]{:S(2)}, u32[]{:S(2)}) collective-permute-start(bf16[4,128,1536]{1,2,0:T(8,128)(2,1)S(1)} %pad_maximum_fusion.3), channel_id=1, source_target_pairs={{0,8},{4,12},{8,0},{12,4},{16,24},{20,28},{24,16},{28,20},{1,9},{5... | collective-permute-start | bytes 4718600 | tf_op jit(solution)/shard_map/ppermute | solution.py:212
  402.5 26.6 %collective-permute-start.41 = (bf16[256,1024]{1,0:T(8,128)(2,1)S(1)}, bf16[256,1024]{1,0:T(8,128)(2,1)S(1)}, u32[]{:S(2)}, u32[]{:S(2)}) collective-permute-start(bf16[256,1024]{1,0:T(8,128)(2,1)S(1)} %get-tuple-element.126), channel_id=1, source_target_pairs={{0,1},{1,0},{2,3},{3,2},{4,5},{5,4},{6,7},{7,6},{8,9},{9,8},{10,11... | collective-permute-start | bytes 1572872 | tf_op jit(solution)/shard_map/ppermute | solution.py:206
  427.4 54.2 %collective-permute-start.68 = (bf16[2,128,1536]{1,2,0:T(8,128)(2,1)}, bf16[2,128,1536]{1,2,0:T(8,128)(2,1)}, u32[]{:S(2)}, u32[]{:S(2)}) collective-permute-start(bf16[2,128,1536]{1,2,0:T(8,128)(2,1)} %slice.1154), channel_id=1, source_target_pairs={{0,24},{4,28},{8,16},{12,20},{16,8},{20,12},{24,0},{28,4},{1,25},{... | collective-permute-start | bytes 2359304 | tf_op jit(solution)/shard_map/ppermute | solution.py:212
  475.0 27.3 %collective-permute-start.64 = (bf16[4,128,1024]{2,1,0:T(8,128)(2,1)}, bf16[4,128,1024]{2,1,0:T(8,128)(2,1)}, u32[]{:S(2)}, u32[]{:S(2)}) collective-permute-start(bf16[4,128,1024]{2,1,0:T(8,128)(2,1)} %pad_maximum_fusion.13), channel_id=1, source_target_pairs={{0,24},{4,28},{8,16},{12,20},{16,8},{20,12},{24,0},{28,4},{1,25},{... | collective-permute-start | bytes 3145736 | tf_op jit(solution)/shard_map/ppermute | solution.py:212
  479.2 27.9 %collective-permute-start.49 = (bf16[256,1024]{1,0:T(8,128)(2,1)S(1)}, bf16[256,1024]{1,0:T(8,128)(2,1)S(1)}, u32[]{:S(2)}, u32[]{:S(2)}) collective-permute-start(bf16[256,1024]{1,0:T(8,128)(2,1)S(1)} %fusion.243), channel_id=1, source_target_pairs={{0,2},{1,3},{2,0},{3,1},{4,6},{5,7},{6,4},{7,5},{8,10},{9,11},{10,... | collective-permute-start | bytes 1572872 | tf_op jit(solution)/shard_map/ppermute | solution.py:209
  480.1 27.1 %collective-permute-start.46 = (bf16[256,1024]{1,0:T(8,128)(2,1)S(1)}, bf16[256,1024]{1,0:T(8,128)(2,1)S(1)}, u32[]{:S(2)}, u32[]{:S(2)}) collective-permute-start(bf16[256,1024]{1,0:T(8,128)(2,1)S(1)} %fusion.244), channel_id=1, source_target_pairs={{0,2},{1,3},{2,0},{3,1},{4,6},{5,7},{6,4},{7,5},{8,10},{9,11},{10,... | collective-permute-start | bytes 1572872 | tf_op jit(solution)/shard_map/ppermute | solution.py:209
  483.4 26.0 %collective-permute-start.69 = (bf16[1,128,1536]{1,2,0:T(8,128)(2,1)S(1)}, bf16[1,128,1536]{1,2,0:T(8,128)(2,1)S(1)}, u32[]{:S(2)}, u32[]{:S(2)}) collective-permute-start(bf16[1,128,1536]{1,2,0:T(8,128)(2,1)S(1)} %slice.1160), channel_id=1, source_target_pairs={{0,4},{4,0},{8,12},{12,8},{16,20},{20,16},{24,28},{28,24},{1,5},{5... | collective-permute-start | bytes 1179656 | tf_op jit(solution)/shard_map/ppermute | solution.py:212
  514.1 32.1 %collective-permute-start.47 = (bf16[256,1024]{1,0:T(8,128)(2,1)}, bf16[256,1024]{1,0:T(8,128)(2,1)S(1)}, u32[]{:S(2)}, u32[]{:S(2)}) collective-permute-start(bf16[256,1024]{1,0:T(8,128)(2,1)} %get-tuple-element.124), channel_id=1, source_target_pairs={{0,1},{1,0},{2,3},{3,2},{4,5},{5,4},{6,7},{7,6},{8,9},{9,8},{10,11... | collective-permute-start | bytes 1572872 | tf_op jit(solution)/shard_map/ppermute | solution.py:206
  514.2 27.1 %collective-permute-start.50 = (bf16[256,1024]{1,0:T(8,128)(2,1)}, bf16[256,1024]{1,0:T(8,128)(2,1)S(1)}, u32[]{:S(2)}, u32[]{:S(2)}) collective-permute-start(bf16[256,1024]{1,0:T(8,128)(2,1)} %get-tuple-element.264), channel_id=1, source_target_pairs={{0,1},{1,0},{2,3},{3,2},{4,5},{5,4},{6,7},{7,6},{8,9},{9,8},{10,11... | collective-permute-start | bytes 1572872 | tf_op jit(solution)/shard_map/ppermute | solution.py:206
  521.2 42.1 %collective-permute-start.66 = (bf16[1,128,1024]{2,1,0:T(8,128)(2,1)S(1)}, bf16[1,128,1024]{2,1,0:T(8,128)(2,1)S(1)}, u32[]{:S(2)}, u32[]{:S(2)}) collective-permute-start(bf16[1,128,1024]{2,1,0:T(8,128)(2,1)S(1)} %slice.1163), channel_id=1, source_target_pairs={{0,8},{4,12},{8,0},{12,4},{16,24},{20,28},{24,16},{28,20},{1,9},{5... | collective-permute-start | bytes 786440 | tf_op jit(solution)/shard_map/ppermute | solution.py:212
  553.7 24.8 %collective-permute-start.58 = (bf16[4,128,1024]{2,1,0:T(8,128)(2,1)}, bf16[4,128,1024]{2,1,0:T(8,128)(2,1)}, u32[]{:S(2)}, u32[]{:S(2)}) collective-permute-start(bf16[4,128,1024]{2,1,0:T(8,128)(2,1)} %pad_maximum_fusion.10), channel_id=1, source_target_pairs={{0,4},{4,0},{8,12},{12,8},{16,20},{20,16},{24,28},{28,24},{1,5},{5... | collective-permute-start | bytes 3145736 | tf_op jit(solution)/shard_map/ppermute | solution.py:212
  560.5 26.3 %collective-permute-start.61 = (bf16[4,128,1024]{2,1,0:T(8,128)(2,1)}, bf16[4,128,1024]{2,1,0:T(8,128)(2,1)}, u32[]{:S(2)}, u32[]{:S(2)}) collective-permute-start(bf16[4,128,1024]{2,1,0:T(8,128)(2,1)} %pad_maximum_fusion.11), channel_id=1, source_target_pairs={{0,8},{4,12},{8,0},{12,4},{16,24},{20,28},{24,16},{28,20},{1,9},{5... | collective-permute-start | bytes 3145736 | tf_op jit(solution)/shard_map/ppermute | solution.py:212
  580.6 31.7 %collective-permute-start.59 = (bf16[2,128,1024]{2,1,0:T(8,128)(2,1)S(1)}, bf16[2,128,1024]{2,1,0:T(8,128)(2,1)S(1)}, u32[]{:S(2)}, u32[]{:S(2)}) collective-permute-start(bf16[2,128,1024]{2,1,0:T(8,128)(2,1)S(1)} %slice.1159), channel_id=1, source_target_pairs={{0,8},{4,12},{8,0},{12,4},{16,24},{20,28},{24,16},{28,20},{1,9},{5... | collective-permute-start | bytes 1572872 | tf_op jit(solution)/shard_map/ppermute | solution.py:212
  588.4 26.6 %collective-permute-start.62 = (bf16[2,128,1024]{2,1,0:T(8,128)(2,1)S(1)}, bf16[2,128,1024]{2,1,0:T(8,128)(2,1)S(1)}, u32[]{:S(2)}, u32[]{:S(2)}) collective-permute-start(bf16[2,128,1024]{2,1,0:T(8,128)(2,1)S(1)} %slice.1158), channel_id=1, source_target_pairs={{0,24},{4,28},{8,16},{12,20},{16,8},{20,12},{24,0},{28,4},{1,25},{... | collective-permute-start | bytes 1572872 | tf_op jit(solution)/shard_map/ppermute | solution.py:212
  (227 other events, 1905.4 us)
Sparse Core Ops, SparseCore 0:
  95.1 45.2 all-gather.1

commit v2 on v1

v2 whole, which is shorter than its diff:
```python
import functools

import jax
import jax.numpy as jnp
from jax import lax
from jax.experimental import pallas as pl
from jax.experimental.pallas import tpu as pltpu
from jax.sharding import PartitionSpec as P

HEAD = 128
KERNEL = 5
LEFT = 64
RIGHT = 8
SLOT = 1024
REL = 73
MARGIN = 16
SUB = 128
BLK = 256
WIN = 3 * SUB
WRAP = 512
LOG2E = 1.4426950408889634
VMEM_CAP = 32 * 1024 * 1024

eps_norm = 1e-05
momentum = 0.5
bf16 = jnp.bfloat16
f32 = jnp.float32


def nn(left_op, right_op):
    return lax.dot_general(
        left_op, right_op, (((1,), (0,)), ((), ())), preferred_element_type=f32
    )


def nt(left_op, right_op):
    return lax.dot_general(
        left_op, right_op, (((1,), (1,)), ((), ())), preferred_element_type=f32
    )


def tn(left_op, right_op):
    return lax.dot_general(
        left_op, right_op, (((0,), (0,)), ((), ())), preferred_element_type=f32
    )


def window_table(rel_table):
    near,far=SUB-LEFT,SUB+RIGHT
    width=rel_table.shape[1]
    ext=jnp.concatenate([
        jnp.broadcast_to(rel_table[:1],(near,width)),
        rel_table,
        jnp.broadcast_to(rel_table[REL-1:],(WIN-far,width)),
        jnp.broadcast_to(rel_table[:1],(WRAP-WIN-1,width)),
    ])
    hi=ext.astype(jnp.bfloat16)
    lo=(ext-hi.astype(jnp.float32)).astype(jnp.bfloat16)
    return hi,lo

def order_in(dst, src, who, rows):
    for j in range(SLOT//rows):
        dst[j*rows:(j+1)*rows,:]=src[pl.ds(pl.multiple_of((j^who)*rows,rows),rows),:]

def attend_kernel(rows, who_ref, len_ref, q_ref, k_ref, v_ref, hi_ref, lo_ref, o_ref, p_ref, qs, ks, vs):
    who=who_ref[0]
    length=len_ref[0]
    order_in(qs,q_ref.at[0],who,rows); order_in(ks,k_ref.at[0],who,rows); order_in(vs,v_ref.at[0],who,rows)
    factor=HEAD**(-0.5)*LOG2E
    tail=lax.broadcasted_iota(jnp.int32,(SUB,SLOT//2),1)+SLOT//2<length
    for base in range(0,SLOT,BLK):
        q=qs[base:base+BLK,:]
        content=nt(q,ks[...])
        spread=nt(q,hi_ref[...])+nt(q,lo_ref[...])
        for off in range(0,BLK,SUB):
            i0=base+off
            e=spread[off:off+SUB]
            rolled=pltpu.roll(e,0,1,stride=1,stride_axis=0)
            lo_c=max(i0-SUB,0); hi_c=min(i0+2*SUB,SLOT)
            parts=[]
            if lo_c>0: parts.append(content[off:off+SUB,:lo_c]+e[:,0:1])
            parts.append(content[off:off+SUB,lo_c:hi_c]+rolled[:,lo_c-(i0-SUB):hi_c-(i0-SUB)])
            if hi_c<SLOT: parts.append(content[off:off+SUB,hi_c:]+e[:,WIN-1:WIN])
            logit=jnp.concatenate(parts,axis=1)*factor
            logit=jnp.concatenate([logit[:,:SLOT//2],jnp.where(tail,logit[:,SLOT//2:],-1e30)],axis=1)
            peak=jnp.max(logit,axis=1,keepdims=True)
            ex=jnp.exp2(logit-peak)
            tot=jnp.sum(ex,axis=1,keepdims=True)
            p_ref[0,i0:i0+SUB,:]=(ex*(1.0/tot)).astype(jnp.bfloat16)
        out=nn(p_ref[0,base:base+BLK,:],vs[...]).astype(jnp.bfloat16)
        for part in range(0,BLK,rows) if rows<BLK else (0,):
            n=min(rows,BLK)
            j=(base+part)//rows; inner=(base+part)%rows
            o_ref[pl.ds(pl.multiple_of((j^who)*rows+inner,n),n),:]=out[part:part+n]

def attend(qkv, who, length, rel_table, rows):
    heads=qkv.shape[2]//HEAD
    hi,lo=window_table(rel_table)
    spec=lambda m: pl.BlockSpec((1,SLOT,HEAD),lambda h,m=m:(m,0,h))
    smem=pl.BlockSpec(memory_space=pltpu.SMEM)
    tab=pl.BlockSpec((WRAP,HEAD),lambda h:(0,0))
    return pl.pallas_call(
        functools.partial(attend_kernel,rows),
        grid=(heads,),
        in_specs=[smem,smem,spec(0),spec(1),spec(2),tab,tab],
        out_specs=[pl.BlockSpec((SLOT,HEAD),lambda h:(0,h)),pl.BlockSpec((1,SLOT,SLOT),lambda h:(h,0,0))],
        out_shape=[jax.ShapeDtypeStruct((SLOT,heads*HEAD),jnp.bfloat16),jax.ShapeDtypeStruct((heads,SLOT,SLOT),jnp.bfloat16)],
        scratch_shapes=[pltpu.VMEM((SLOT,HEAD),jnp.bfloat16)]*3,
        compiler_params=pltpu.CompilerParams(vmem_limit_bytes=VMEM_CAP),
        cost_estimate=pl.CostEstimate(flops=1<<20,bytes_accessed=1<<20,transcendentals=0),
        name="attend",
    )(who,length,qkv,qkv,qkv,hi,lo)

def attend_back_kernel(rows, who_ref, q_ref, k_ref, v_ref, g_ref, p_ref, hi_ref, lo_ref, d_ref, dt_ref, ds_ref, qs, ks, vs, gs, dkt, dvt):
    who=who_ref[0]
    for dst,src in ((qs,q_ref.at[0]),(ks,k_ref.at[0]),(vs,v_ref.at[0]),(gs,g_ref)):
        order_in(dst,src,who,rows)
    factor=HEAD**(-0.5)
    first=hi_ref[0:1,:].astype(jnp.float32)+lo_ref[0:1,:].astype(jnp.float32)
    final=hi_ref[WIN-1:WIN,:].astype(jnp.float32)+lo_ref[WIN-1:WIN,:].astype(jnp.float32)
    zero=jnp.zeros((SUB,SUB),jnp.float32)
    flip=(lax.broadcasted_iota(jnp.int32,(SUB,SUB),0)+lax.broadcasted_iota(jnp.int32,(SUB,SUB),1)==SUB-1).astype(jnp.bfloat16)
    table_acc=jnp.zeros((HEAD,WRAP),jnp.float32)
    left_acc=jnp.zeros((1,HEAD),jnp.float32)
    right_acc=jnp.zeros((1,HEAD),jnp.float32)
    for base in range(0,SLOT,BLK):
        q=qs[base:base+BLK,:]
        g=gs[base:base+BLK,:]
        pb=p_ref[0,base:base+BLK,:]
        p=pb.astype(jnp.float32)
        dp=nt(g,vs[...])
        delta=jnp.sum(p*dp,axis=1,keepdims=True)
        dsb=(p*(dp-delta)).astype(jnp.bfloat16)
        dv_part=tn(g,pb)
        dk_part=tn(q,dsb)
        if base==0:
            dvt[...]=dv_part; dkt[...]=dk_part
        else:
            dvt[...]+=dv_part; dkt[...]+=dk_part
        dq=nn(dsb,ks[...])
        ds=dsb.astype(jnp.float32)
        qf=q.astype(jnp.float32)
        extra=[]
        for off in range(0,BLK,SUB):
            i0=base+off
            d=ds[off:off+SUB]
            lo_c=max(i0-SUB,0); hi_c=min(i0+2*SUB,SLOT)
            turned=nn(flip,dsb[off:off+SUB,lo_c:hi_c])
            win=[zero]*((lo_c-(i0-SUB))//SUB)+[turned]+[zero]*((i0+2*SUB-hi_c)//SUB+1)
            moved=pltpu.roll(jnp.concatenate(win,axis=1),WRAP-SUB+1,1,stride=1,stride_axis=0)
            u=nn(flip,moved.astype(jnp.bfloat16)).astype(jnp.bfloat16)
            add=nn(u,hi_ref[...])+nn(u,lo_ref[...])
            table_acc=table_acc+tn(q[off:off+SUB],u)
            if lo_c>0:
                s=jnp.sum(d[:,:lo_c],axis=1,keepdims=True)
                add=add+s*first
                left_acc=left_acc+jnp.sum(s*qf[off:off+SUB],axis=0,keepdims=True)
            if hi_c<SLOT:
                s=jnp.sum(d[:,hi_c:],axis=1,keepdims=True)
                add=add+s*final
                right_acc=right_acc+jnp.sum(s*qf[off:off+SUB],axis=0,keepdims=True)
            extra.append(add)
        dq=((dq+jnp.concatenate(extra,axis=0))*factor).astype(jnp.bfloat16)
        for part in range(0,BLK,rows) if rows<BLK else (0,):
            n=min(rows,BLK)
            j=(base+part)//rows; inner=(base+part)%rows
            d_ref[0,pl.ds(pl.multiple_of((j^who)*rows+inner,n),n),:]=dq[part:part+n]
    dt_ref[0]=table_acc*factor
    ds_ref[0]=jnp.concatenate([left_acc,right_acc,jnp.zeros((6,HEAD),jnp.float32)],axis=0)*factor
    for j in range(SLOT//rows):
        sl=pl.ds(pl.multiple_of((j^who)*rows,rows),rows)
        d_ref[1,sl,:]=(jnp.transpose(dkt[:,j*rows:(j+1)*rows])*factor).astype(jnp.bfloat16)
        d_ref[2,sl,:]=jnp.transpose(dvt[:,j*rows:(j+1)*rows]).astype(jnp.bfloat16)

def attend_back(qkv, grad, probs, who, rel_table, rows):
    heads=qkv.shape[2]//HEAD
    hi,lo=window_table(rel_table)
    spec=lambda m: pl.BlockSpec((1,SLOT,HEAD),lambda h,m=m:(m,0,h))
    smem=pl.BlockSpec(memory_space=pltpu.SMEM)
    tab=pl.BlockSpec((WRAP,HEAD),lambda h:(0,0))
    out=pl.BlockSpec((3,SLOT,HEAD),lambda h:(0,0,h))
    shape=jax.ShapeDtypeStruct((3,SLOT,heads*HEAD),jnp.bfloat16)
    members,dt,ends=pl.pallas_call(
        functools.partial(attend_back_kernel,rows),
        grid=(heads,),
        in_specs=[smem,spec(0),spec(1),spec(2),pl.BlockSpec((SLOT,HEAD),lambda h:(0,h)),pl.BlockSpec((1,SLOT,SLOT),lambda h:(h,0,0)),tab,tab],
        out_specs=[out,pl.BlockSpec((1,HEAD,WRAP),lambda h:(h,0,0)),pl.BlockSpec((1,8,HEAD),lambda h:(h,0,0))],
        out_shape=[shape,jax.ShapeDtypeStruct((heads,HEAD,WRAP),jnp.float32),jax.ShapeDtypeStruct((heads,8,HEAD),jnp.float32)],
        scratch_shapes=[pltpu.VMEM((SLOT,HEAD),jnp.bfloat16)]*4+[pltpu.VMEM((HEAD,SLOT),jnp.float32)]*2,
        compiler_params=pltpu.CompilerParams(vmem_limit_bytes=VMEM_CAP),
        cost_estimate=pl.CostEstimate(flops=1<<20,bytes_accessed=1<<20,transcendentals=0),
        name="attend_back",
    )(who,qkv,qkv,qkv,grad,probs,hi,lo)
    wide=jnp.sum(dt,axis=0).T
    ends=jnp.sum(ends,axis=0)
    near=SUB-LEFT; far=SUB+RIGHT
    left=jnp.sum(wide[:near+1],axis=0)+jnp.sum(wide[WIN+1:],axis=0)+ends[0]
    right=jnp.sum(wide[far:WIN+1],axis=0)+ends[1]
    return members,jnp.concatenate([left[None],wide[near+1:far],right[None]],axis=0)


def run(kernel, outs, ins, after=(), name=None, grid=None, in_specs=None, out_specs=None, scratch=(), aliases=None):
    count = len(ins)
    waits = len(after)

    def body(*refs):
        kernel(*refs[:count], *refs[count + waits :])

    whole = pl.BlockSpec(memory_space=pltpu.VMEM)
    specs = list(in_specs) if in_specs is not None else [whole] * count
    specs = [whole if spec is None else spec for spec in specs]
    out_specs = list(out_specs) if out_specs is not None else [whole] * len(outs)
    extra = {} if grid is None else {"grid": grid}
    return pl.pallas_call(
        body,
        in_specs=specs + [pl.BlockSpec(memory_space=pl.ANY)] * waits,
        out_specs=out_specs,
        out_shape=[jax.ShapeDtypeStruct(shape, dtype) for shape, dtype in outs],
        scratch_shapes=list(scratch),
        input_output_aliases=aliases or {},
        compiler_params=pltpu.CompilerParams(vmem_limit_bytes=VMEM_CAP),
        cost_estimate=pl.CostEstimate(flops=1 << 20, bytes_accessed=1 << 20, transcendentals=0),
        name=name,
        **extra,
    )(*ins, *after)


SMEM_SPEC = pl.BlockSpec(memory_space=pltpu.SMEM)


def moments(rows):
    centred = rows - jnp.mean(rows, axis=1, keepdims=True)
    inverse = lax.rsqrt(jnp.mean(centred * centred, axis=1, keepdims=True) + eps_norm)
    return centred * inverse, inverse


def back(weighted, normed, inverse):
    first_mean = jnp.mean(weighted, axis=1, keepdims=True)
    second_mean = jnp.mean(weighted * normed, axis=1, keepdims=True)
    return inverse * (weighted - first_mean - normed * second_mean)


def wide(ref):
    return ref[...].astype(f32)


def add_up(parts, name, after=()):
    shape = parts[0].shape

    def kernel(*refs):
        total = wide(refs[0])
        for ref in refs[1:-1]:
            total = total + wide(ref)
        refs[-1][...] = total.astype(bf16)

    return run(kernel, [(shape, bf16)], parts, after, name)[0]


def norm_rows(resid, parts, factor, gain, name, after=(), keep=True, low=False, also=None):
    shape = resid.shape
    count = len(parts)
    ins = [resid, gain] + list(parts) + ([also] if also is not None else [])
    outs = [(shape, bf16)] + [(shape, f32)] * keep + [(shape, bf16)] * low
    outs = outs + ([(shape, bf16)] if also is not None else [])

    def kernel(resid_ref, gain_ref, *refs):
        rows = wide(resid_ref)
        if count:
            total = wide(refs[0])
            for ref in refs[1:count]:
                total = total + wide(ref)
            rows = rows + factor * total
        out = list(refs[count + (also is not None) :])
        out.pop(0)[...] = (moments(rows)[0] * gain_ref[...]).astype(bf16)
        if keep:
            out.pop(0)[...] = rows
        if low:
            out.pop(0)[...] = rows.astype(bf16)
        if also is not None:
            out.pop(0)[...] = refs[count][...].astype(bf16)

    return run(kernel, outs, ins, after, name)


def norm_last(resid, parts, gain, upper, begin, length, name, full, after=()):
    shape = resid.shape
    count = len(parts)
    outs = [(shape, bf16)]
    if full:
        outs = outs + [(shape, f32), (shape, f32), ((8, shape[1]), f32)]

    def kernel(begin_ref, length_ref, resid_ref, gain_ref, upper_ref, *refs):
        total = wide(refs[0])
        for ref in refs[1:count]:
            total = total + wide(ref)
        rows = wide(resid_ref) + 0.5 * total
        normed, inverse = moments(rows)
        place = lax.broadcasted_iota(jnp.int32, (shape[0], 1), 0) + begin_ref[0]
        valid = (place < length_ref[0]).astype(f32)
        seen = wide(upper_ref) * valid
        grad = back(seen * gain_ref[...], normed, inverse)
        refs[count][...] = (0.5 * grad).astype(bf16)
        if full:
            refs[count + 1][...] = grad
            refs[count + 2][...] = normed * gain_ref[...] * valid
            refs[count + 3][...] = jnp.broadcast_to(
                jnp.sum(seen * normed, axis=0, keepdims=True), (8, shape[1])
            )

    ins = [begin, length, resid, gain, upper] + list(parts)
    specs = [SMEM_SPEC, SMEM_SPEC] + [None] * (3 + count)
    return run(kernel, outs, ins, after, name, in_specs=specs)


def norm_grad(rows_in, parts, gain, grad, name, after=(), factor=None, keep=True, sums=True):
    shape = rows_in.shape
    count = len(parts)
    outs = [(shape, bf16)] * (factor is not None) + [(shape, f32)] * keep
    outs = outs + [((8, shape[1]), f32)] * sums

    def kernel(rows_ref, gain_ref, grad_ref, *refs):
        total = wide(refs[0])
        for ref in refs[1:count]:
            total = total + wide(ref)
        normed, inverse = moments(wide(rows_ref))
        result = wide(grad_ref) + back(total * gain_ref[...], normed, inverse)
        out = list(refs[count:])
        if factor is not None:
            out.pop(0)[...] = (factor * result).astype(bf16)
        if keep:
            out.pop(0)[...] = result
        if sums:
            out.pop(0)[...] = jnp.broadcast_to(
                jnp.sum(total * normed, axis=0, keepdims=True), (8, shape[1])
            )

    return run(kernel, outs, [rows_in, gain, grad] + list(parts), after, name)


def tile_of(total, most):
    return most if total % most == 0 else total


def feed(own, mate, weights, name, after=()):
    rows, width = own.shape
    hidden = weights.shape[2]
    tile = tile_of(hidden, 256)
    steps = hidden // tile

    def kernel(own_ref, mate_ref, in_ref, out_ref, p_own, p_mate, pre, hid, acc):
        step = pl.program_id(0)
        value = nn(jnp.concatenate([own_ref[...], mate_ref[...]], axis=0), in_ref[0])
        act = (value / (1.0 + jnp.exp(-value))).astype(bf16)
        pre[...] = value.astype(bf16)
        hid[...] = act
        part = nt(act, out_ref[0])

        @pl.when(step == 0)
        def _():
            acc[...] = part

        @pl.when(step > 0)
        def _():
            acc[...] += part

        @pl.when(step == steps - 1)
        def _():
            p_own[...] = acc[:rows].astype(bf16)
            p_mate[...] = acc[rows:].astype(bf16)

    fixed = pl.BlockSpec((rows, width), lambda i: (0, 0))
    cols = pl.BlockSpec((2 * rows, tile), lambda i: (0, i))
    weight = [pl.BlockSpec((1, width, tile), lambda i, m=m: (m, 0, i)) for m in range(2)]
    return run(
        kernel,
        [((rows, width), bf16)] * 2 + [((2 * rows, hidden), bf16)] * 2,
        [own, mate, weights, weights],
        after,
        name,
        grid=(steps,),
        in_specs=[fixed, fixed] + weight,
        out_specs=[fixed, fixed, cols, cols],
        scratch=[pltpu.VMEM((2 * rows, width), f32)],
    )


def feed_grad(own, mate, pre, weights, name, after=()):
    rows, width = own.shape
    hidden = weights.shape[2]
    tile = tile_of(hidden, 256)
    steps = hidden // tile

    def kernel(own_ref, mate_ref, pre_ref, in_ref, out_ref, p_own, p_mate, down, acc):
        step = pl.program_id(0)
        value = nn(jnp.concatenate([own_ref[...], mate_ref[...]], axis=0), out_ref[0])
        preact = wide(pre_ref)
        logistic = 1.0 / (1.0 + jnp.exp(-preact))
        slope = logistic * (1.0 + preact * (1.0 - logistic))
        grad = (value * slope).astype(bf16)
        down[...] = grad
        part = nt(grad, in_ref[0])

        @pl.when(step == 0)
        def _():
            acc[...] = part

        @pl.when(step > 0)
        def _():
            acc[...] += part

        @pl.when(step == steps - 1)
        def _():
            p_own[...] = acc[:rows].astype(bf16)
            p_mate[...] = acc[rows:].astype(bf16)

    fixed = pl.BlockSpec((rows, width), lambda i: (0, 0))
    cols = pl.BlockSpec((2 * rows, tile), lambda i: (0, i))
    weight = [pl.BlockSpec((1, width, tile), lambda i, m=m: (m, 0, i)) for m in range(2)]
    return run(
        kernel,
        [((rows, width), bf16)] * 2 + [((2 * rows, hidden), bf16)],
        [own, mate, pre, weights, weights],
        after,
        name,
        grid=(steps,),
        in_specs=[fixed, fixed, cols] + weight,
        out_specs=[fixed, fixed, cols],
        scratch=[pltpu.VMEM((2 * rows, width), f32)],
    )


def qkv_rows(own, mate, weights, k, total, held, name, after=()):
    rows, width = own.shape
    cols = weights.shape[2]

    def kernel(own_ref, mate_ref, w_ref, *refs):
        value = nn(jnp.concatenate([own_ref[...], mate_ref[...]], axis=0), w_ref[0])
        refs[-1][0] = value.astype(bf16)

    fixed = pl.BlockSpec((rows, width), lambda i: (0, 0))
    ins = [own, mate, weights] + ([held] if held is not None else [])
    specs = [fixed, fixed, pl.BlockSpec((1, width, cols), lambda i: (i, 0, 0))]
    specs = specs + [pl.BlockSpec(memory_space=pl.ANY)] * (held is not None)
    return run(
        kernel,
        [((3, total, cols), bf16)],
        ins,
        after,
        name,
        grid=(3,),
        in_specs=specs,
        out_specs=[pl.BlockSpec((1, 2 * rows, cols), lambda i: (i, k, 0))],
        aliases={3: 0} if held is not None else None,
    )[0]


def heads_rows(own, mate, weight, k, total, held, name, after=()):
    rows, width = own.shape
    cols = weight.shape[1]

    def kernel(own_ref, mate_ref, w_ref, *refs):
        value = nn(jnp.concatenate([own_ref[...], mate_ref[...]], axis=0), w_ref[...])
        refs[-1][...] = value.astype(bf16)

    fixed = pl.BlockSpec((rows, width), lambda i: (0, 0))
    ins = [own, mate, weight] + ([held] if held is not None else [])
    specs = [fixed, fixed, pl.BlockSpec((width, cols), lambda i: (0, 0))]
    specs = specs + [pl.BlockSpec(memory_space=pl.ANY)] * (held is not None)
    return run(
        kernel,
        [((total, cols), bf16)],
        ins,
        after,
        name,
        grid=(1,),
        in_specs=specs,
        out_specs=[pl.BlockSpec((2 * rows, cols), lambda i: (k, 0))],
        aliases={3: 0} if held is not None else None,
    )[0]


def out_rows(values, weight, k, rows, name, after=()):
    width, cols = weight.shape

    def kernel(value_ref, w_ref, p_own, p_mate):
        part = nt(value_ref[...], w_ref[...])
        p_own[...] = part[:rows].astype(bf16)
        p_mate[...] = part[rows:].astype(bf16)

    fixed = pl.BlockSpec((rows, width), lambda i: (0, 0))
    return run(
        kernel,
        [((rows, width), bf16)] * 2,
        [values, weight],
        after,
        name,
        grid=(1,),
        in_specs=[
            pl.BlockSpec((2 * rows, cols), lambda i: (k, 0)),
            pl.BlockSpec((width, cols), lambda i: (0, 0)),
        ],
        out_specs=[fixed, fixed],
    )


def members_rows(members, weights, k, rows, name, after=()):
    width, cols = weights.shape[1:]

    def kernel(value_ref, w_ref, p_own, p_mate):
        part = nt(value_ref[0], w_ref[0])
        for m in range(1, 3):
            part = part + nt(value_ref[m], w_ref[m])
        p_own[...] = part[:rows].astype(bf16)
        p_mate[...] = part[rows:].astype(bf16)

    fixed = pl.BlockSpec((rows, width), lambda i: (0, 0))
    return run(
        kernel,
        [((rows, width), bf16)] * 2,
        [members, weights],
        after,
        name,
        grid=(1,),
        in_specs=[
            pl.BlockSpec((3, 2 * rows, cols), lambda i: (0, k, 0)),
            pl.BlockSpec((3, width, cols), lambda i: (0, 0, 0)),
        ],
        out_specs=[fixed, fixed],
    )


def outer_halves(links, jobs, turn, name, after=()):
    offsets, masks = links.offsets(turn)
    width = jobs[0][0][0].shape[1]
    share = width // links.dp
    me = lax.axis_index("dp").reshape(1).astype(jnp.int32)
    if share % 128:
        whole = jnp.concatenate(
            [
                tn(
                    jnp.concatenate(left),
                    jnp.concatenate([r[0][r[1]] if isinstance(r, tuple) else r for r in right]),
                )
                for left, right in jobs
            ],
            axis=1,
        ).astype(bf16)
        blocks = whole.reshape(links.dp, share, whole.shape[1])

        def pick(which):
            return jnp.concatenate(
                [lax.dynamic_index_in_dim(blocks, me[0] ^ off, 0, keepdims=False) for off in which]
            )

        return pick([off ^ masks[0] for off in offsets]), pick(offsets)
    ins = [me]
    plan = []
    for left, right in jobs:
        picks = [item[1] if isinstance(item, tuple) else None for item in right]
        arrays = [item[0] if isinstance(item, tuple) else item for item in right]
        plan.append((len(left), picks, arrays[0].shape[-1]))
        ins = ins + list(left) + arrays
    total = sum(cols for _, _, cols in plan)
    half = len(offsets)

    def kernel(me_ref, *refs):
        who = me_ref[0]
        sent_ref, kept_ref = refs[-2], refs[-1]
        at, column = 0, 0
        for n_left, picks, cols in plan:
            left = refs[at : at + n_left]
            right = refs[at + n_left : at + n_left + len(picks)]
            at = at + n_left + len(picks)
            rights = [ref[...] if m is None else ref[m] for ref, m in zip(right, picks)]
            rights = rights[0] if len(picks) == 1 else jnp.concatenate(rights, axis=0)
            for flip, dest in ((masks[0], sent_ref), (0, kept_ref)):
                picked = []
                for off in offsets:
                    where = pl.ds(pl.multiple_of((who ^ off ^ flip) * share, 128), share)
                    parts = [ref[:, where] for ref in left]
                    picked.append(parts[0] if n_left == 1 else jnp.concatenate(parts, axis=0))
                picked = picked[0] if half == 1 else jnp.concatenate(picked, axis=1)
                dest[:, column : column + cols] = tn(picked, rights).astype(bf16)
            column = column + cols

    return run(
        kernel,
        [((half * share, total), bf16)] * 2,
        ins,
        after,
        name,
        in_specs=[SMEM_SPEC] + [None] * (len(ins) - 1),
    )


def halve(kept, came, name, after=()):
    count, cols = kept.shape
    half = count // 2

    def kernel(kept_ref, came_ref, sent_out, kept_out):
        total = wide(kept_ref) + wide(came_ref)
        kept_out[...] = total[:half].astype(bf16)
        sent_out[...] = total[half:].astype(bf16)

    return run(kernel, [((half, cols), bf16)] * 2, [kept, came], after, name)


def halves(ref_own, ref_mate, c):
    own, mate = ref_own[...], ref_mate[...]
    first = jnp.where(c == 0, own, mate)
    second = jnp.where(c == 0, mate, own)
    return first, second


def shift_rows(value, offset):
    if offset == 0:
        return value
    return pltpu.roll(value, (-offset) % value.shape[0], 0)


def place_mask(count, y, length):
    place = lax.broadcasted_iota(jnp.int32, (count + 2 * MARGIN, 1), 0) + (y * count - MARGIN)
    return ((place >= 0) & (place < length)).astype(f32)


def bordered(own_ref, mate_ref, before, after, who, ny):
    y, c = who // 2, who % 2
    first, second = halves(own_ref, mate_ref, c)
    above = wide(before[0])
    for ref in before[1:]:
        above = above + wide(ref)
    below = wide(after[0])
    for ref in after[1:]:
        below = below + wide(ref)
    above = jnp.where(y > 0, above, 0.0).astype(bf16)
    below = jnp.where(y < ny - 1, below, 0.0).astype(bf16)
    return jnp.concatenate([above, first, second, below], axis=0)


def conv_mix(ny, who, length, own, mate, before, after_rows, weights, taps, name, after=()):
    rows, width = own.shape
    cols = taps.shape[1]
    count = 2 * rows
    lo, hi = MARGIN, MARGIN + count
    n_before = len(before)

    def kernel(who_ref, len_ref, own_ref, mate_ref, w0, w1, taps_ref, *refs):
        rows_in = bordered(own_ref, mate_ref, refs[:n_before], refs[n_before:-4], who_ref[0], ny)
        lin_ref, gate_ref, mix_ref, tally_ref = refs[-4:]
        valid = place_mask(count, who_ref[0] // 2, len_ref[0])
        linear = nn(rows_in, w0[...])
        gating = 1.0 / (1.0 + jnp.exp(-nn(rows_in, w1[...])))
        lin_ref[...] = linear
        gate_ref[...] = gating
        glu = linear * gating * valid
        mixture = taps_ref[0:1, :] * shift_rows(glu, -2)
        for j in range(1, KERNEL):
            mixture = mixture + taps_ref[j : j + 1, :] * shift_rows(glu, j - 2)
        mix_ref[...] = mixture
        inside = (valid * mixture)[lo:hi]
        tally_ref[...] = jnp.concatenate(
            [
                jnp.sum(inside, axis=0, keepdims=True),
                jnp.sum(inside * mixture[lo:hi], axis=0, keepdims=True),
                jnp.broadcast_to(jnp.sum(valid[lo:hi], axis=0, keepdims=True), (1, cols)),
                jnp.zeros((5, cols), f32),
            ],
            axis=0,
        )

    ins = [who, length, own, mate, weights[0], weights[1], taps] + list(before) + list(after_rows)
    shape = (count + 2 * MARGIN, cols)
    return run(
        kernel,
        [(shape, f32)] * 3 + [((8, cols), f32)],
        ins,
        after,
        name,
        in_specs=[SMEM_SPEC, SMEM_SPEC] + [None] * (len(ins) - 2),
    )


def batch_terms(tally_ref):
    count = tally_ref[2:3, :]
    mean = tally_ref[0:1, :] / count
    var = tally_ref[1:2, :] / count - mean * mean
    return count, mean, var, lax.rsqrt(var + eps_norm)


def conv_out(who, mixture, tallies, affine, running, weight, rows, name, after=()):
    width, cols = weight.shape
    channels = running.shape[1]
    lo, mid, hi = MARGIN, MARGIN + rows, MARGIN + 2 * rows

    def kernel(who_ref, mix_ref, tally_ref, affine_ref, run_ref, w_ref, act_ref, p_own, p_mate, new_ref):
        c = who_ref[0] % 2
        count, mean, var, inverse = batch_terms(tally_ref)
        own = pl.ds(pl.multiple_of(lo + c * rows, 16), rows)
        mate = pl.ds(pl.multiple_of(lo + (1 - c) * rows, 16), rows)
        mixture = jnp.concatenate([mix_ref[own, :], mix_ref[mate, :]], axis=0)
        shifted = (mixture - mean) * inverse * affine_ref[0:1, :] + affine_ref[1:2, :]
        active = (shifted / (1.0 + jnp.exp(-shifted))).astype(bf16)
        act_ref[...] = active
        part = nt(active, w_ref[...])
        p_own[...] = part[:rows].astype(bf16)
        p_mate[...] = part[rows:].astype(bf16)
        grown = var * count / (count - 1.0)
        new_ref[...] = (1.0 - momentum) * run_ref[...] + momentum * jnp.concatenate(
            [mean[:, :channels], grown[:, :channels]], axis=0
        )

    return run(
        kernel,
        [((2 * rows, cols), bf16), ((rows, width), bf16), ((rows, width), bf16), (running.shape, f32)],
        [who, mixture, tallies, affine, running, weight],
        after,
        name,
        in_specs=[SMEM_SPEC] + [None] * 5,
    )


def conv_shift_grad(ny, who, length, own, mate, before, after_rows, mixture, tallies, affine, weight, name, after=()):
    rows, width = own.shape
    cols = weight.shape[1]
    count = 2 * rows
    lo, hi = MARGIN, MARGIN + count
    n_before = len(before)

    def kernel(who_ref, len_ref, own_ref, mate_ref, mix_ref, tally_ref, affine_ref, w_ref, *refs):
        rows_in = bordered(own_ref, mate_ref, refs[:n_before], refs[n_before:-2], who_ref[0], ny)
        dz_ref, out_ref = refs[-2:]
        valid = place_mask(count, who_ref[0] // 2, len_ref[0])
        _, mean, _, inverse = batch_terms(tally_ref)
        centred = (mix_ref[...] - mean) * inverse
        shifted = centred * affine_ref[0:1, :] + affine_ref[1:2, :]
        logistic = 1.0 / (1.0 + jnp.exp(-shifted))
        slope = logistic * (1.0 + shifted * (1.0 - logistic))
        grad = jnp.where(valid > 0.0, nn(rows_in, w_ref[...]) * slope, 0.0)
        dz_ref[...] = grad
        inner = grad[lo:hi]
        out_ref[...] = jnp.concatenate(
            [
                jnp.sum(inner * centred[lo:hi], axis=0, keepdims=True),
                jnp.sum(inner, axis=0, keepdims=True),
                jnp.zeros((6, cols), f32),
            ],
            axis=0,
        )

    ins = [who, length, own, mate, mixture, tallies, affine, weight] + list(before) + list(after_rows)
    return run(
        kernel,
        [(mixture.shape, f32), ((8, cols), f32)],
        ins,
        after,
        name,
        in_specs=[SMEM_SPEC, SMEM_SPEC] + [None] * (len(ins) - 2),
    )


def conv_in_grad(who, length, dz, mixture, tallies, sums, affine, taps, linear, gating, weights, rows, name, after=()):
    width, cols = weights[0].shape
    count = 2 * rows
    lo, mid, hi = MARGIN, MARGIN + rows, MARGIN + count

    def kernel(who_ref, len_ref, dz_ref, mix_ref, tally_ref, sum_ref, affine_ref, taps_ref, lin_ref, gate_ref, w0, w1, dl_ref, dg_ref, p_own, p_mate, tap_ref):
        c = who_ref[0] % 2
        valid = place_mask(count, who_ref[0] // 2, len_ref[0])
        total, mean, _, inverse = batch_terms(tally_ref)
        centred = (mix_ref[...] - mean) * inverse
        shrink = affine_ref[0:1, :] * inverse
        mixed = (sum_ref[1:2, :] + centred * sum_ref[0:1, :]) / total
        grad_mix = jnp.where(valid > 0.0, shrink * (dz_ref[...] - mixed), 0.0)
        grad_glu = taps_ref[0:1, :] * shift_rows(grad_mix, 2)
        for j in range(1, KERNEL):
            grad_glu = grad_glu + taps_ref[j : j + 1, :] * shift_rows(grad_mix, 2 - j)
        linear = lin_ref[...]
        gating = gate_ref[...]
        glu = linear * gating * valid
        inner = grad_mix[lo:hi]
        tap_ref[...] = jnp.concatenate(
            [
                jnp.sum(inner * shift_rows(glu, j - 2)[lo:hi], axis=0, keepdims=True)
                for j in range(KERNEL)
            ]
            + [jnp.zeros((8 - KERNEL, cols), f32)],
            axis=0,
        )
        held = grad_glu * valid * gating
        grad_linear = held.astype(bf16)
        grad_gate = (held * linear * (1.0 - gating)).astype(bf16)

        def turned(value):
            first, second = value[lo:mid], value[mid:hi]
            return jnp.concatenate(
                [jnp.where(c == 0, first, second), jnp.where(c == 0, second, first)], axis=0
            )

        grad_linear = turned(grad_linear)
        grad_gate = turned(grad_gate)
        dl_ref[...] = grad_linear
        dg_ref[...] = grad_gate
        part = nt(grad_linear, w0[...]) + nt(grad_gate, w1[...])
        p_own[...] = part[:rows].astype(bf16)
        p_mate[...] = part[rows:].astype(bf16)

    return run(
        kernel,
        [((count, cols), bf16)] * 2 + [((rows, width), bf16)] * 2 + [((8, cols), f32)],
        [who, length, dz, mixture, tallies, sums, affine, taps, linear, gating, weights[0], weights[1]],
        after,
        name,
        in_specs=[SMEM_SPEC, SMEM_SPEC] + [None] * 10,
    )


class Links:
    def __init__(self, dp, tensor):
        self.dp, self.tensor, self.ny = dp, tensor, tensor // 2
        masks = [1 << bit for bit in range(dp.bit_length() - 1)]
        if len(masks) > 2:
            masks[2] = 6
        self.masks = masks

    def core(self, value):
        return lax.ppermute(value, "tensor", [(i, i ^ 1) for i in range(self.tensor)])

    def chip(self, value, k):
        return lax.ppermute(value, "tensor", [(i, i ^ (2 * k)) for i in range(self.tensor)])

    def group(self, value, mask):
        return lax.ppermute(value, "dp", [(i, i ^ mask) for i in range(self.dp)])

    def sum_group(self, value):
        for mask in self.masks:
            value = value + self.group(value, mask)
        return value

    def sum_stats(self, value, channels):
        def cols(array, k):
            return array[:, k * channels : (k + 1) * channels]

        total = value
        for k in range(1, self.ny):
            other = self.chip(value, k)
            total = total + jnp.concatenate([cols(other, r ^ k) for r in range(self.ny)], axis=1)
        return self.sum_group(total)

    def offsets(self, turn):
        count = len(self.masks)
        masks = [self.masks[(turn + i) % count] for i in range(count)]
        offsets = [0]
        for mask in masks[:0:-1]:
            offsets = offsets + [off ^ mask for off in offsets]
        return offsets, masks

    def borders(self, own, mate):
        count = own.shape[0]
        who = lax.axis_index("tensor")
        y, c = who // 2, who % 2
        if self.ny == 2:
            edge = lax.dynamic_slice_in_dim(own, (1 - y) * (count - MARGIN), MARGIN)
            straight = lax.ppermute(edge, "tensor", [(1, 3), (2, 0)])
            across = lax.ppermute(edge, "tensor", [(1, 2), (2, 1)])
            return [straight, across], [straight, across]
        head = jnp.where(c == 0, own, mate)[:MARGIN]
        foot = jnp.where(c == 0, mate, own)[count - MARGIN :]
        down = [(i, i + 2) for i in range(self.tensor - 2)]
        up = [(i + 2, i) for i in range(self.tensor - 2)]
        return [lax.ppermute(foot, "tensor", down)], [lax.ppermute(head, "tensor", up)]


class Halving:
    def __init__(self, links, halves, turn, name):
        self.links, self.name = links, name
        self.masks = links.offsets(turn)[1]
        self.sent, self.kept = halves
        self.first = self.sent
        self.at = 0
        self.send()

    def send(self):
        self.came = self.links.group(self.sent, self.masks[self.at])
        self.at += 1

    def step(self, after=()):
        if self.at < len(self.masks):
            self.sent, self.kept = halve(self.kept, self.came, self.name + "_half", after)
            self.send()
        return self.kept

    def finish(self):
        while self.at < len(self.masks):
            self.step()
        return self.kept, self.came


def finish_pair(first, second, name, after=()):
    ins = list(first.finish() + second.finish())
    shape = ins[0].shape

    def kernel(a, b, c, d, out):
        out[0] = wide(a) + wide(b)
        out[1] = wide(c) + wide(d)

    return run(kernel, [((2,) + shape, f32)], ins, after, name)[0]


def finish_heads(pending, cols, name, after=()):
    ins = list(pending.finish())
    share = ins[0].shape[0]

    def kernel(a, b, three, one):
        total = wide(a) + wide(b)
        for m in range(3):
            three[m] = total[:, m * cols : (m + 1) * cols]
        one[...] = total[:, 3 * cols :]

    return run(kernel, [((3, share, cols), f32), ((share, cols), f32)], ins, after, name)


def finish_conv(links, pending, channels, name, after=()):
    ins = list(pending.finish())
    share = ins[0].shape[0]
    ny = links.ny

    def split(a, b, own, *others):
        total = wide(a) + wide(b)
        for m in range(3):
            for k in range(ny):
                at = (m * ny + k) * channels
                piece = total[:, at : at + channels]
                if k == 0:
                    own[m] = piece
                else:
                    others[k - 1][m] = piece.astype(bf16)

    shape = (3, share, channels)
    parts = run(split, [(shape, f32)] + [(shape, bf16)] * (ny - 1), ins, after, name)
    came = [links.chip(parts[k], k) for k in range(1, ny)]

    def close(*refs):
        total = refs[0][...]
        for ref in refs[1:-1]:
            total = total + wide(ref)
        refs[-1][...] = total

    return run(close, [(shape, f32)], [parts[0]] + came, (), name + "_close")[0]


def per_device(
    links,
    x_in,
    cotangent,
    lengths,
    norm_gains,
    ffn_first,
    attn_qkv,
    attn_out,
    rel_table,
    conv_proj,
    depthwise,
    bn_gain,
    bn_bias,
    running,
    ffn_second,
):
    ny = links.ny
    others = list(range(1, ny))
    rows, width = x_in.shape
    channels = bn_gain.shape[0]
    who = lax.axis_index("tensor").astype(jnp.int32)
    who_arr = who.reshape(1)
    y, c = who // 2, who % 2
    gain = [norm_gains[i : i + 1] for i in range(5)]
    begin = [(((y ^ k) * 2 + c) * rows).reshape(1) for k in range(ny)]

    me = lax.axis_index("dp")
    share = width // links.dp
    piece = lax.dynamic_slice_in_dim(conv_proj, me * share, share, axis=1)
    conv_w = [[conv_proj[m] for m in range(3)]]
    for k in others:
        blocks = links.chip(piece, k)[None]
        order = [0]
        for mask in links.masks:
            blocks = jnp.concatenate([blocks, links.group(blocks, mask)])
            order = order + [off ^ mask for off in order]
        where = {off: at for at, off in enumerate(order)}
        table = jnp.array([where[off] for off in range(links.dp)], jnp.int32)
        rows_of = [
            lax.dynamic_index_in_dim(blocks, table[me ^ b], 0, keepdims=False)
            for b in range(links.dp)
        ]
        whole = jnp.concatenate(rows_of, axis=1)
        conv_w.append([whole[m] for m in range(3)])
    conv_w = [jnp.concatenate([conv_w[k][m] for k in range(ny)], axis=1) for m in range(3)]
    small = jnp.concatenate([depthwise, bn_gain[None], bn_bias[None], jnp.zeros((1, channels), f32)])
    small = jnp.concatenate([small] + [links.chip(small, k) for k in others], axis=1)
    affine = small[KERNEL : KERNEL + 2]

    def send_sums(parts, name, after=()):
        return add_up([parts[0], links.core(parts[1])], name, after)

    normed, x_low = norm_rows(x_in, [], 0.0, gain[0], "ln_in", keep=False, low=True)
    x_rows = [x_in] + [links.chip(x_low, k) for k in others]
    na_first, kept_first, sums, came = {}, {}, {}, {}
    token = ()
    for k in range(ny):
        if k:
            (normed,) = norm_rows(x_rows[k], [], 0.0, gain[0], "ln_in", token, keep=False)
        na_first[k] = (normed, links.core(normed))
        p_own, p_mate, pre, hid = feed(*na_first[k], ffn_first, "ffn_one")
        kept_first[k] = (pre, hid)
        sums[k] = send_sums((p_own, p_mate), "ffn_one_sum")
        token = (sums[k],)

    def all_parts(sums, k):
        return [sums[k]] + [links.chip(sums[k ^ j], j) for j in others]

    token = ()
    na_attn, first, qkv, cot_low = {}, {}, None, None
    for k in others + [0]:
        also = cotangent if k == 0 else None
        made = norm_rows(
            x_rows[k], all_parts(sums, k), 0.5, gain[1], "ln_attn", token, also=also
        )
        na_attn[k] = (made[0], links.core(made[0]))
        first[k] = made[1]
        if k == 0:
            cot_low = made[2]
        qkv = qkv_rows(*na_attn[k], attn_qkv, k, SLOT, qkv, "qkv")
        token = (qkv,)
    cot_rows = [cotangent] + [links.chip(cot_low, k) for k in others]
    heads_out, probs = attend(qkv, who_arr, lengths, rel_table, rows)
    token = ()
    arrived = []
    for k in others:
        total = send_sums(out_rows(heads_out, attn_out, k, rows, "out_proj", token), "out_sum")
        arrived.append(links.chip(total, k))
        token = (total,)
    p_own, p_mate = out_rows(heads_out, attn_out, 0, rows, "out_proj", token)
    conv_own, after_attn = norm_rows(
        first[0], [p_own, links.core(p_mate)] + arrived, 1.0, gain[2], "ln_conv"
    )

    conv_mate = links.core(conv_own)
    before, after_rows = links.borders(conv_own, conv_mate)
    linear, gating, mixture, tallies = conv_mix(
        ny, who_arr, lengths, conv_own, conv_mate, before, after_rows, conv_w, small[:KERNEL], "conv_mix"
    )
    tallies = links.sum_stats(tallies, channels)
    active, p_own, p_mate, updated = conv_out(
        who_arr, mixture, tallies, affine, running, conv_w[2], rows, "conv_out"
    )
    normed, after_conv, low = norm_rows(
        after_attn, [p_own, links.core(p_mate)], 1.0, gain[3], "ln_ffn_two", low=True
    )

    x_rows = [after_conv] + [links.chip(low, k) for k in others]
    na_last, kept_last, sums = {}, {}, {}
    token = ()
    for k in range(ny):
        if k:
            (normed,) = norm_rows(x_rows[k], [], 0.0, gain[3], "ln_ffn_two", token, keep=False)
        na_last[k] = (normed, links.core(normed))
        p_own, p_mate, pre, hid = feed(*na_last[k], ffn_second, "ffn_two")
        kept_last[k] = (pre, hid)
        sums[k] = send_sums((p_own, p_mate), "ffn_two_sum")
        token = (sums[k],)

    token = ()
    upper, down, arrived = {}, {}, []
    for k in others + [0]:
        made = norm_last(
            x_rows[k],
            all_parts(sums, k),
            gain[4],
            cot_rows[k],
            begin[k],
            lengths,
            "ln_last",
            k == 0,
            token,
        )
        upper[k] = (made[0], links.core(made[0]))
        p_own, p_mate, down[k] = feed_grad(*upper[k], kept_last[k][0], ffn_second, "ffn_two_grad")
        if k:
            total = send_sums((p_own, p_mate), "ffn_two_grad_sum")
            arrived.append(links.chip(total, k))
            token = (total,)
        else:
            grad, output, gain_five = made[1:]
            parts = [p_own, links.core(p_mate)]

    def row_blocks(pairs):
        return [block for k in range(ny) for block in pairs[k]]

    wait_out = outer_halves(
        links, [(row_blocks(upper), [kept_last[k][1] for k in range(ny)])], 0, "ffn_two_out", (p_mate,)
    )
    wait_in = outer_halves(
        links, [(row_blocks(na_last), [down[k] for k in range(ny)])], 1, "ffn_two_in", (p_mate,)
    )
    low, grad, gain_four = norm_grad(
        after_conv, parts + arrived, gain[3], grad, "back_ffn_two", (wait_out[0], wait_in[0]), factor=1.0
    )

    up_own = low
    up_mate = links.core(low)
    before, after_rows = links.borders(up_own, up_mate)
    dz, sums = conv_shift_grad(
        ny, who_arr, lengths, up_own, up_mate, before, after_rows, mixture, tallies, affine, conv_w[2], "conv_dz"
    )
    bn_grads = links.sum_stats(sums, channels)
    grad_linear, grad_gate, p_own, p_mate, tap_grad = conv_in_grad(
        who_arr, lengths, dz, mixture, tallies, bn_grads, affine, small[:KERNEL], linear, gating, conv_w, rows, "conv_din"
    )
    low, grad, gain_three = norm_grad(
        after_attn, [p_own, links.core(p_mate)], gain[2], grad, "back_conv", factor=1.0
    )

    pend_two_out = Halving(links, wait_out, 0, "ffn_two_out")
    pend_two_in = Halving(links, wait_in, 1, "ffn_two_in")

    g_rows = [low] + [links.chip(low, k) for k in others]
    conv_halves = outer_halves(
        links,
        [
            ([conv_own, conv_mate], [grad_linear]),
            ([conv_own, conv_mate], [grad_gate]),
            ([up_own, up_mate], [active]),
        ],
        2,
        "conv_w",
        (low,),
    )
    pend_conv = Halving(links, conv_halves, 2, "conv_w")
    grad_heads = None
    upper_attn = {}
    for k in range(ny):
        upper_attn[k] = (g_rows[k], links.core(g_rows[k]))
        grad_heads = heads_rows(*upper_attn[k], attn_out, k, SLOT, grad_heads, "dheads")
    members, table_grad = attend_back(qkv, grad_heads, probs, who_arr, rel_table, rows)
    token = ()
    sums = {}
    for k in range(ny):
        sums[k] = send_sums(members_rows(members, attn_qkv, k, rows, "dqkv", token), "dqkv_sum")
        token = (sums[k],)
    heads_halves = outer_halves(
        links,
        [(row_blocks(na_attn), [(members, m)]) for m in range(3)]
        + [(row_blocks(upper_attn), [heads_out])],
        0,
        "attn_w",
        token,
    )
    pend_heads = Halving(links, heads_halves, 0, "attn_w")

    token = (heads_halves[0],)
    upper, down, arrived = {}, {}, []
    for k in others + [0]:
        made = norm_grad(
            first[k],
            all_parts(sums, k),
            gain[1],
            grad if k == 0 else g_rows[k],
            "back_attn",
            token,
            factor=0.5,
            keep=k == 0,
            sums=k == 0,
        )
        upper[k] = (made[0], links.core(made[0]))
        p_own, p_mate, down[k] = feed_grad(*upper[k], kept_first[k][0], ffn_first, "ffn_one_grad")
        if k:
            total = send_sums((p_own, p_mate), "ffn_one_grad_sum")
            arrived.append(links.chip(total, k))
            token = (total,)
        else:
            grad, gain_two = made[1:]
            parts = [p_own, links.core(p_mate)]
    halves_in = outer_halves(
        links, [(row_blocks(na_first), [down[k] for k in range(ny)])], 1, "ffn_one_in", (p_mate,)
    )
    pend_one_in = Halving(links, halves_in, 1, "ffn_one_in")
    halves_out = outer_halves(
        links,
        [(row_blocks(upper), [kept_first[k][1] for k in range(ny)])],
        2,
        "ffn_one_out",
        (halves_in[0],),
    )
    pend_one_out = Halving(links, halves_out, 2, "ffn_one_out")
    grad_input, gain_one = norm_grad(
        x_in, parts + arrived, gain[0], grad, "back_ffn_one", (halves_out[0],)
    )

    last_sum = finish_pair(pend_two_in, pend_two_out, "ffn_two_end")
    conv_sum = finish_conv(links, pend_conv, channels, "conv_end")
    qkv_sum, out_sum = finish_heads(pend_heads, attn_qkv.shape[2], "attn_end")
    first_sum = finish_pair(pend_one_in, pend_one_out, "ffn_one_end")

    kernel_grad = links.sum_stats(tap_grad, channels)[:KERNEL, :channels]
    gains = [gain_one, gain_two, gain_three, gain_four, gain_five]
    gains = jnp.stack([part[0] for part in gains]).reshape(-1, HEAD)
    bundle = jnp.concatenate([gains, table_grad])
    bundle = jnp.pad(bundle, ((0, -bundle.shape[0] % 8), (0, 0)))
    bundle = bundle + links.core(bundle)
    for k in [1 << bit for bit in range(ny.bit_length() - 1)]:
        bundle = bundle + links.chip(bundle, k)
    bundle = links.sum_group(bundle)
    return (
        output,
        grad_input,
        bundle[: gains.shape[0]].reshape(5, width),
        first_sum,
        qkv_sum,
        out_sum,
        bundle[gains.shape[0] : gains.shape[0] + REL],
        conv_sum,
        kernel_grad,
        bn_grads[0, :channels],
        bn_grads[1, :channels],
        updated,
        last_sum,
    )


def solution(mesh):
    links = Links(mesh.shape["dp"], mesh.shape["tensor"])
    placed = (
        P(("dp", "tensor"), None),
        P(("dp", "tensor"), None),
        P("dp"),
        P(),
        P(None, None, "tensor"),
        P(None, None, "tensor"),
        P(None, "tensor"),
        P(),
        P(None, None, "tensor"),
        P(None, "tensor"),
        P("tensor"),
        P("tensor"),
        P(None, "tensor"),
        P(None, None, "tensor"),
    )
    return jax.shard_map(
        functools.partial(per_device, links),
        mesh=mesh,
        in_specs=placed,
        out_specs=(
            P(("dp", "tensor"), None),
            P(("dp", "tensor"), None),
            P(),
            P(None, "dp", "tensor"),
            P(None, "dp", "tensor"),
            P("dp", "tensor"),
            P(),
            P(None, "dp", "tensor"),
            P(None, "tensor"),
            P("tensor"),
            P("tensor"),
            P(None, "tensor"),
            P(None, "dp", "tensor"),
        ),
        check_vma=False,
    )
```

time: 643 us -> 581 us (0.904)
  Pallas kernels: 25.5 us -> 148 us
  matrix products: 82.7 us -> 0 us
  other arithmetic: 76.5 us -> 5.99 us
  starting transfers between devices: 117 us -> 104 us
  local copies, waits for them, and re-layouts: 52.7 us -> 42.8 us
  waiting for transfers between devices: 260 us -> 252 us
    pallas_call x0 -> x66, Pallas kernels: none -> 124 us  [run(): pl.pallas_call(body, in_specs=specs + [pl.BlockSpec(memory_space=pl.ANY)]...]
    dot_general x48 -> x0, matrix products: 82.7 us -> none  [the longest x18 31.9 us: nn(): lax.dot_general(left_op, right_op, (((1,), (0,)), ((), ())), preferred_el...]
    reduce_sum x27 -> x0, other arithmetic: 22.7 us -> none  [the longest x5 8.23 us: gain_sum(): return jnp.sum(upstream * moments(rows)[0], axis=0)]
    unnamed x349 -> x300, local copies, waits for them, and re-layouts: 14.8 us -> 36.1 us
    add x24 -> x3, other arithmetic: 20.8 us -> 0.02 us  [sum_stats(): total + jnp.concatenate([cols(other, r ^ k) for r in range(self.ny)], axi...]
    ppermute x29, waiting for transfers between devices: 2.19 us -> 22.8 us  [core(): lax.ppermute(value, 'tensor', [(i, i ^ 1) for i in range(self.tensor)])]
    all_gather x1 -> x0, waiting for transfers between devices: 18.9 us -> none  [per_device(): other = lax.all_gather(other, 'dp', axis=0, tiled=True)]
    convert_element_type x21 -> x1, other arithmetic: 17.6 us -> 0.03 us  [window_table(): hi = ext.astype(jnp.bfloat16)]
  transfers between devices with their start and end apart: 82 -> 86, of which waited for: 34 -> 48; matrix products, arithmetic and copies ran while one was open for 27% -> 2% of each run, Pallas kernels for 2% -> 13%
where the time goes in v2:
time: 581 us; the launch traced here: 571 us
  waiting for transfers between devices  252 us (43%)
  Pallas kernels  148 us (25%)
  starting transfers between devices  104 us (18%)
  local copies, waits for them, and re-layouts  42.8 us (7%)
  between operations  18.8 us (3%)
  other arithmetic  5.99 us (1%)
    pallas_call x66, Pallas kernels, run(): pl.pallas_call(body, in_specs=specs + [pl.BlockSpec(memory_space=pl.ANY)]...  124 us
    ppermute x33, waiting for transfers between devices, group(): return lax.ppermute(value, 'dp', [(i, i ^ mask) for i in range(self.dp)])  110 us
    ppermute x20, waiting for transfers between devices, chip(): lax.ppermute(value, 'tensor', [(i, i ^ 2 * k) for i in range(self.tensor)])  109 us
    ppermute x33, starting transfers between devices, group(): return lax.ppermute(value, 'dp', [(i, i ^ mask) for i in range(self.dp)])  77.6 us
    unnamed x300, local copies, waits for them, and re-layouts  36.1 us
    ppermute x29, waiting for transfers between devices, core(): lax.ppermute(value, 'tensor', [(i, i ^ 1) for i in range(self.tensor)])  22.8 us
    ppermute x20, starting transfers between devices, chip(): lax.ppermute(value, 'tensor', [(i, i ^ 2 * k) for i in range(self.tensor)])  17.6 us
    pallas_call x1, Pallas kernels, attend_back(): pl.pallas_call(functools.partial(attend_back_kernel, rows), grid=(heads,)...  14.1 us
  transfers between devices with their start and end apart: 86, of which 48 were waited for; matrix products, arithmetic and copies ran while one was open for 2% of the time, Pallas kernels for 13%

profile of v2, /device:TPU:0, one launch (start us, length us, event | category | flops | bytes accessed | tf_op | source)
XLA Modules:
  0.0 571.1 jit_solution(17371198834645806098)
XLA Ops:
  7.4 6.6 %ffn_one.2 = (bf16[256,1024]{1,0:T(8,128)(2,1)S(1)}, bf16[256,1024]{1,0:T(8,128)(2,1)S(1)}, bf16[512,1024]{1,0:T(8,128)(2,1)S(1)}, bf16[512,1024]{1,0:T(8,128)(2,1)S(1)}) custom-call(bf16[256,1024]{1,0:T(8,128)(2,1)S(1)} %get-tuple-element.136.refs_0_.refs_1_, bf16[256,1024]{1,0:T(8,128)(2,1)S(1)} %collective-permute-done.refs_1_.refs_2_, ...), custom_call_target="tpu_custom_call" | custom-call | flops 1048576 | bytes 1048576 | tf_op jit(solution)/shard_map/ffn_one/pallas_call | solution.py:214
  17.4 12.3 %collective-permute-done.2.refs_0_ = bf16[256,1024]{1,0:T(8,128)(2,1)S(1)} collective-permute-done((bf16[256,1024]{1,0:T(8,128)(2,1)S(1)}, bf16[256,1024]{1,0:T(8,128)(2,1)S(1)}, u32[]{:S(2)}, u32[]{:S(2)}) %collective-permute-start.2) | collective-permute-done | bytes 524320 | tf_op jit(solution)/shard_map/ppermute | solution.py:829
  35.0 6.6 %ffn_one.3 = (bf16[256,1024]{1,0:T(8,128)(2,1)S(1)}, bf16[256,1024]{1,0:T(8,128)(2,1)S(1)}, bf16[512,1024]{1,0:T(8,128)(2,1)S(1)}, bf16[512,1024]{1,0:T(8,128)(2,1)S(1)}) custom-call(bf16[256,1024]{1,0:T(8,128)(2,1)S(1)} %ln_in.3.refs_0_.refs_3_, bf16[256,1024]{1,0:T(8,128)(2,1)S(1)} %collective-permute-done.3.refs_1_.refs_4_, ...), custom_call_target="tpu_custom_call" | custom-call | flops 1048576 | bytes 1048576 | tf_op jit(solution)/shard_map/ffn_one/pallas_call | solution.py:214
  96.3 9.1 %attend.1 = (bf16[1024,256]{1,0:T(8,128)(2,1)S(1)}, bf16[2,1024,1024]{2,1,0:T(8,128)(2,1)S(1)}) custom-call(s32[1]{0:T(128)} %bitcast.1.who_ref.refs_0_, s32[1]{0:T(128)S(6)} %copy.60.len_ref.refs_1_, bf16[3,1024,256]{2,1,0:T(8,128)(2,1)S(1)} %qkv.3.q_ref.k_ref.v_ref, bf16[3,1024,256]{2,1,0:T(8,128)(2,1)S(1)} %qkv.3.q_ref.k_ref.v_ref, ...), custom_call_target="tpu_custom_call" | custom-call | flops 1048576 | bytes 1048576 | tf_op jit(solution)/shard_map/attend/pallas_call | solution.py:102
  112.3 11.9 %collective-permute-done.11.refs_4_ = bf16[256,1024]{1,0:T(8,128)(2,1)S(1)} collective-permute-done((bf16[256,1024]{1,0:T(8,128)(2,1)S(1)}, bf16[256,1024]{1,0:T(8,128)(2,1)S(1)}, u32[]{:S(2)}, u32[]{:S(2)}) %collective-permute-start.11) | collective-permute-done | bytes 524320 | tf_op jit(solution)/shard_map/ppermute | solution.py:829
  158.1 6.8 %ffn_two.2 = (bf16[256,1024]{1,0:T(8,128)(2,1)S(1)}, bf16[256,1024]{1,0:T(8,128)(2,1)S(1)}, bf16[512,1024]{1,0:T(8,128)(2,1)S(1)}, bf16[512,1024]{1,0:T(8,128)(2,1)S(1)}) custom-call(bf16[256,1024]{1,0:T(8,128)(2,1)S(1)} %get-tuple-element.157.refs_0_.refs_1_, bf16[256,1024]{1,0:T(8,128)(2,1)S(1)} %collective-permute-done.25.refs_1_.refs_2_, ...), custom_call_target="tpu_custom_call" | custom-call | flops 1048576 | bytes 1048576 | tf_op jit(solution)/shard_map/ffn_two/pallas_call | solution.py:214
  167.8 11.5 %collective-permute-done.27.refs_0_.refs_2_ = bf16[256,1024]{1,0:T(8,128)(2,1)S(1)} collective-permute-done((bf16[256,1024]{1,0:T(8,128)(2,1)S(1)}, bf16[256,1024]{1,0:T(8,128)(2,1)S(1)}, u32[]{:S(2)}, u32[]{:S(2)}) %collective-permute-start.27) | collective-permute-done | bytes 524320 | tf_op jit(solution)/shard_map/ppermute | solution.py:829
  181.7 7.4 %ffn_two.3 = (bf16[256,1024]{1,0:T(8,128)(2,1)S(1)}, bf16[256,1024]{1,0:T(8,128)(2,1)}, bf16[512,1024]{1,0:T(8,128)(2,1)S(1)}, bf16[512,1024]{1,0:T(8,128)(2,1)S(1)}) custom-call(bf16[256,1024]{1,0:T(8,128)(2,1)S(1)} %ln_ffn_two.3.refs_0_.refs_3_, bf16[256,1024]{1,0:T(8,128)(2,1)S(1)} %collective-permute-done.28.refs_1_.refs_4_, ...), custom_call_target="tpu_custom_call" | custom-call | flops 1048576 | bytes 1048576 | tf_op jit(solution)/shard_map/ffn_two/pallas_call | solution.py:214
  197.3 9.8 %collective-permute-done.31.refs_4_ = bf16[256,1024]{1,0:T(8,128)(2,1)} collective-permute-done((bf16[256,1024]{1,0:T(8,128)(2,1)}, bf16[256,1024]{1,0:T(8,128)(2,1)}, u32[]{:S(2)}, u32[]{:S(2)}) %collective-permute-start.31) | collective-permute-done | bytes 524320 | tf_op jit(solution)/shard_map/ppermute | solution.py:829
  207.1 10.7 %collective-permute-done.32.refs_6_ = bf16[256,1024]{1,0:T(8,128)(2,1)} collective-permute-done((bf16[256,1024]{1,0:T(8,128)(2,1)}, bf16[256,1024]{1,0:T(8,128)(2,1)}, u32[]{:S(2)}, u32[]{:S(2)}) %collective-permute-start.32) | collective-permute-done | bytes 524320 | tf_op jit(solution)/shard_map/ppermute | solution.py:829
  224.4 7.4 %ffn_two_grad.2 = (bf16[256,1024]{1,0:T(8,128)(2,1)S(1)}, bf16[256,1024]{1,0:T(8,128)(2,1)}, bf16[512,1024]{1,0:T(8,128)(2,1)S(1)}) custom-call(bf16[256,1024]{1,0:T(8,128)(2,1)S(1)} %ln_last.2.refs_0_.refs_3_, bf16[256,1024]{1,0:T(8,128)(2,1)S(1)} %collective-permute-done.33.refs_1_.refs_4_, bf16[512,1024]{1,0:T(8,128)(2,1)S(1)} %copy-done.96, ...), custom_call_target="tpu_custom_call" | custom-call | flops 1048576 | bytes 1048576 | tf_op jit(solution)/shard_map/ffn_two_grad/pallas_call | solution.py:214
  238.2 10.0 %collective-permute-done.30.refs_6_ = bf16[256,1024]{1,0:T(8,128)(2,1)} collective-permute-done((bf16[256,1024]{1,0:T(8,128)(2,1)}, bf16[256,1024]{1,0:T(8,128)(2,1)}, u32[]{:S(2)}, u32[]{:S(2)}) %collective-permute-start.30) | collective-permute-done | bytes 524320 | tf_op jit(solution)/shard_map/ppermute | solution.py:829
  255.6 6.8 %ffn_two_grad.3 = (bf16[256,1024]{1,0:T(8,128)(2,1)S(1)}, bf16[256,1024]{1,0:T(8,128)(2,1)S(1)}, bf16[512,1024]{1,0:T(8,128)(2,1)S(1)}) custom-call(bf16[256,1024]{1,0:T(8,128)(2,1)S(1)} %get-tuple-element.169.refs_0_.refs_1_, bf16[256,1024]{1,0:T(8,128)(2,1)S(1)} %collective-permute-done.35.refs_1_.refs_2_, bf16[512,1024]{1,0:T(8,128)(2,1)S(1)} %copy-done.88, ...), custom_call_target="tpu_custom_call" | custom-call | flops 1048576 | bytes 1048576 | tf_op jit(solution)/shard_map/ffn_two_grad/pallas_call | solution.py:214
  302.4 13.7 %collective-permute-done.46.refs_0_.refs_18_.refs_2_ = bf16[256,1024]{1,0:T(8,128)(2,1)S(1)} collective-permute-done((bf16[256,1024]{1,0:T(8,128)(2,1)S(1)}, bf16[256,1024]{1,0:T(8,128)(2,1)S(1)}, u32[]{:S(2)}, u32[]{:S(2)}) %collective-permute-start.46) | collective-permute-done | bytes 524320 | tf_op jit(solution)/shard_map/ppermute | solution.py:829
  318.6 14.1 %attend_back.1 = (bf16[3,1024,256]{2,1,0:T(8,128)(2,1)S(1)}, f32[2,128,512]{2,1,0:T(8,128)S(1)}, f32[2,8,128]{2,1,0:T(8,128)S(1)}) custom-call(s32[1]{0:T(128)} %bitcast.1.who_ref.refs_0_, bf16[3,1024,256]{2,1,0:T(8,128)(2,1)S(1)} %qkv.3.q_ref.k_ref.v_ref, bf16[3,1024,256]{2,1,0:T(8,128)(2,1)S(1)} %qkv.3.q_ref.k_ref.v_ref, ...), custom_call_target="tpu_custom_call" | custom-call | flops 1048576 | bytes 1048576 | tf_op jit(solution)/shard_map/attend_back/pallas_call | solution.py:183
  354.0 6.8 %ffn_one_grad.2 = (bf16[256,1024]{1,0:T(8,128)(2,1)S(1)}, bf16[256,1024]{1,0:T(8,128)(2,1)S(1)}, bf16[512,1024]{1,0:T(8,128)(2,1)S(1)}) custom-call(bf16[256,1024]{1,0:T(8,128)(2,1)S(1)} %back_attn.2.refs_0_.refs_3_, bf16[256,1024]{1,0:T(8,128)(2,1)S(1)} %collective-permute-done.53.refs_1_.refs_4_, bf16[512,1024]{1,0:T(8,128)(2,1)S(1)} %copy-done.82, ...), custom_call_target="tpu_custom_call" | custom-call | flops 1048576 | bytes 1048576 | tf_op jit(solution)/shard_map/ffn_one_grad/pallas_call | solution.py:214
  368.9 7.3 %collective-permute-done.51.refs_4_ = bf16[256,1024]{1,0:T(8,128)(2,1)S(1)} collective-permute-done((bf16[256,1024]{1,0:T(8,128)(2,1)S(1)}, bf16[256,1024]{1,0:T(8,128)(2,1)S(1)}, u32[]{:S(2)}, u32[]{:S(2)}) %collective-permute-start.51) | collective-permute-done | bytes 524320 | tf_op jit(solution)/shard_map/ppermute | solution.py:829
  382.7 7.4 %ffn_one_grad.3 = (bf16[256,1024]{1,0:T(8,128)(2,1)S(1)}, bf16[256,1024]{1,0:T(8,128)(2,1)}, bf16[512,1024]{1,0:T(8,128)(2,1)S(1)}) custom-call(bf16[256,1024]{1,0:T(8,128)(2,1)S(1)} %get-tuple-element.201.refs_0_.refs_1_, bf16[256,1024]{1,0:T(8,128)(2,1)S(1)} %collective-permute-done.55.refs_1_.refs_2_, bf16[512,1024]{1,0:T(8,128)(2,1)S(1)} %copy-done.80, ...), custom_call_target="tpu_custom_call" | custom-call | flops 1048576 | bytes 1048576 | tf_op jit(solution)/shard_map/ffn_one_grad/pallas_call | solution.py:214
  392.0 11.3 %collective-permute-done.77 = f32[8,512]{1,0:T(8,128)S(1)} collective-permute-done((f32[8,512]{1,0:T(8,128)S(1)}, f32[8,512]{1,0:T(8,128)S(1)}, u32[]{:S(2)}, u32[]{:S(2)}) %collective-permute-start.77) | collective-permute-done | bytes 16416 | tf_op jit(solution)/shard_map/ppermute | solution.py:832
  415.4 21.0 %collective-permute-start.63 = (bf16[512,1024]{1,0:T(8,128)(2,1)}, bf16[512,1024]{1,0:T(8,128)(2,1)}, u32[]{:S(2)}, u32[]{:S(2)}) collective-permute-start(bf16[512,1024]{1,0:T(8,128)(2,1)} %get-tuple-element.209.refs_7_), channel_id=1, source_target_pairs={{0,8},{4,12},{8,0},{12,4},{16,24},{20,28},{24,16},{28,20},{1,9},{5... | collective-permute-start | bytes 3145736 | tf_op jit(solution)/shard_map/ppermute | solution.py:832
  448.4 32.6 %collective-permute-done.78 = f32[8,512]{1,0:T(8,128)S(1)} collective-permute-done((f32[8,512]{1,0:T(8,128)S(1)}, f32[8,512]{1,0:T(8,128)S(1)}, u32[]{:S(2)}, u32[]{:S(2)}) %collective-permute-start.78) | collective-permute-done | bytes 16416 | tf_op jit(solution)/shard_map/ppermute | solution.py:832
  499.3 11.3 %collective-permute-start.70 = (bf16[256,1024]{1,0:T(8,128)(2,1)S(1)}, bf16[256,1024]{1,0:T(8,128)(2,1)S(1)}, u32[]{:S(2)}, u32[]{:S(2)}) collective-permute-start(bf16[256,1024]{1,0:T(8,128)(2,1)S(1)} %get-tuple-element.231), channel_id=1, source_target_pairs={{0,8},{4,12},{8,0},{12,4},{16,24},{20,28},{24,16},{28,20},{1,9},{5... | collective-permute-start | bytes 1572872 | tf_op jit(solution)/shard_map/ppermute | solution.py:832
  516.9 8.8 %collective-permute-done.60 = f32[120,128]{0,1:T(8,128)S(1)} collective-permute-done((f32[120,128]{0,1:T(8,128)S(1)}, f32[120,128]{0,1:T(8,128)S(1)}, u32[]{:S(2)}, u32[]{:S(2)}) %collective-permute-start.60) | collective-permute-done | bytes 61472 | tf_op jit(solution)/shard_map/ppermute | solution.py:832
  538.9 13.3 %collective-permute-done.79 = f32[8,512]{1,0:T(8,128)S(1)} collective-permute-done((f32[8,512]{1,0:T(8,128)S(1)}, f32[8,512]{1,0:T(8,128)S(1)}, u32[]{:S(2)}, u32[]{:S(2)}) %collective-permute-start.79) | collective-permute-done | bytes 16416 | tf_op jit(solution)/shard_map/ppermute | solution.py:832
  (581 shorter events, 287.8 us)
Async XLA Ops:
  30.9 27.2 %collective-permute-start.6 = (bf16[256,1024]{1,0:T(8,128)(2,1)S(1)}, bf16[256,1024]{1,0:T(8,128)(2,1)S(1)}, u32[]{:S(2)}, u32[]{:S(2)}) collective-permute-start(bf16[256,1024]{1,0:T(8,128)(2,1)S(1)} %ffn_one_sum.2.refs_2_), channel_id=1, source_target_pairs={{0,2},{1,3},{2,0},{3,1},{4,6},{5,7},{6,4},{7,5},{8,10},{9,11},{10,... | collective-permute-start | bytes 1572872 | tf_op jit(solution)/shard_map/ppermute | solution.py:829
  61.1 47.1 %collective-permute-start.17 = (f32[8,256]{1,0:T(8,128)S(1)}, f32[8,256]{1,0:T(8,128)S(1)}, u32[]{:S(2)}, u32[]{:S(2)}) collective-permute-start(f32[8,256]{1,0:T(8,128)S(1)} %pad_maximum_fusion.8), channel_id=1, source_target_pairs={{0,2},{1,3},{2,0},{3,1},{4,6},{5,7},{6,4},{7,5},{8,10},{9,11},{10,... | collective-permute-start | bytes 24584 | tf_op jit(solution)/shard_map/ppermute | solution.py:829
  67.8 40.5 %collective-permute-start.16 = (bf16[4,3,128,256]{3,2,1,0:T(8,128)(2,1)}, bf16[4,3,128,256]{3,2,1,0:T(8,128)(2,1)}, u32[]{:S(2)}, u32[]{:S(2)}) collective-permute-start(bf16[4,3,128,256]{3,2,1,0:T(8,128)(2,1)} %pad_maximum_fusion.4), channel_id=1, source_target_pairs={{0,24},{4,28},{8,16},{12,20},{16,8},{20,12},{24,0},{28,4},{1,25},{... | collective-permute-start | bytes 2359304 | tf_op jit(solution)/shard_map/ppermute | solution.py:832
  75.5 18.2 %collective-permute-start.8 = (bf16[256,1024]{1,0:T(8,128)(2,1)}, bf16[256,1024]{1,0:T(8,128)(2,1)}, u32[]{:S(2)}, u32[]{:S(2)}) collective-permute-start(bf16[256,1024]{1,0:T(8,128)(2,1)} %get-tuple-element.144.refs_0_.refs_1_.refs_6_.refs_11_), channel_id=1, source_target_pairs={{0,1},{1,0},{2,3},{3,2},{4,5},{5,4},{6,7},{7,6},{8,9},{9,8},{10,11... | collective-permute-start | bytes 1572872 | tf_op jit(solution)/shard_map/ppermute | solution.py:826
  192.3 25.5 %collective-permute-start.32 = (bf16[256,1024]{1,0:T(8,128)(2,1)}, bf16[256,1024]{1,0:T(8,128)(2,1)}, u32[]{:S(2)}, u32[]{:S(2)}) collective-permute-start(bf16[256,1024]{1,0:T(8,128)(2,1)} %ffn_two_sum.2.refs_2_.refs_5_), channel_id=1, source_target_pairs={{0,2},{1,3},{2,0},{3,1},{4,6},{5,7},{6,4},{7,5},{8,10},{9,11},{10,... | collective-permute-start | bytes 1572872 | tf_op jit(solution)/shard_map/ppermute | solution.py:829
  366.3 47.6 %collective-permute-start.72 = (bf16[512,1536]{1,0:T(8,128)(2,1)}, bf16[512,1536]{1,0:T(8,128)(2,1)}, u32[]{:S(2)}, u32[]{:S(2)}) collective-permute-start(bf16[512,1536]{1,0:T(8,128)(2,1)} %get-tuple-element.240), channel_id=1, source_target_pairs={{0,24},{4,28},{8,16},{12,20},{16,8},{20,12},{24,0},{28,4},{1,25},{... | collective-permute-start | bytes 4718600 | tf_op jit(solution)/shard_map/ppermute | solution.py:832
  377.5 70.1 %collective-permute-start.80 = (bf16[512,1024]{1,0:T(8,128)(2,1)}, bf16[512,1024]{1,0:T(8,128)(2,1)}, u32[]{:S(2)}, u32[]{:S(2)}) collective-permute-start(bf16[512,1024]{1,0:T(8,128)(2,1)} %get-tuple-element.178.refs_7_), channel_id=1, source_target_pairs={{0,8},{4,12},{8,0},{12,4},{16,24},{20,28},{24,16},{28,20},{1,9},{5... | collective-permute-start | bytes 3145736 | tf_op jit(solution)/shard_map/ppermute | solution.py:832
  377.5 70.2 %collective-permute-start.83 = (bf16[512,1024]{1,0:T(8,128)(2,1)}, bf16[512,1024]{1,0:T(8,128)(2,1)}, u32[]{:S(2)}, u32[]{:S(2)}) collective-permute-start(bf16[512,1024]{1,0:T(8,128)(2,1)} %get-tuple-element.175.refs_6_), channel_id=1, source_target_pairs={{0,4},{4,0},{8,12},{12,8},{16,20},{20,16},{24,28},{28,24},{1,5},{5... | collective-permute-start | bytes 3145736 | tf_op jit(solution)/shard_map/ppermute | solution.py:832
  380.9 22.3 %collective-permute-start.77 = (f32[8,512]{1,0:T(8,128)S(1)}, f32[8,512]{1,0:T(8,128)S(1)}, u32[]{:S(2)}, u32[]{:S(2)}) collective-permute-start(f32[8,512]{1,0:T(8,128)S(1)} %maximum_add_fusion.2), channel_id=1, source_target_pairs={{0,4},{4,0},{8,12},{12,8},{16,20},{20,16},{24,28},{28,24},{1,5},{5... | collective-permute-start | bytes 49160 | tf_op jit(solution)/shard_map/ppermute | solution.py:832
  382.4 32.9 %collective-permute-start.57 = (bf16[256,1024]{1,0:T(8,128)(2,1)S(1)}, bf16[256,1024]{1,0:T(8,128)(2,1)}, u32[]{:S(2)}, u32[]{:S(2)}) collective-permute-start(bf16[256,1024]{1,0:T(8,128)(2,1)S(1)} %ffn_one_grad_sum.1.refs_5_), channel_id=1, source_target_pairs={{0,2},{1,3},{2,0},{3,1},{4,6},{5,7},{6,4},{7,5},{8,10},{9,11},{10,... | collective-permute-start | bytes 1572872 | tf_op jit(solution)/shard_map/ppermute | solution.py:829
  403.3 33.2 %collective-permute-start.56 = (bf16[256,1024]{1,0:T(8,128)(2,1)}, bf16[256,1024]{1,0:T(8,128)(2,1)}, u32[]{:S(2)}, u32[]{:S(2)}) collective-permute-start(bf16[256,1024]{1,0:T(8,128)(2,1)} %get-tuple-element.204.refs_7_), channel_id=1, source_target_pairs={{0,1},{1,0},{2,3},{3,2},{4,5},{5,4},{6,7},{7,6},{8,9},{9,8},{10,11... | collective-permute-start | bytes 1572872 | tf_op jit(solution)/shard_map/ppermute | solution.py:826
  413.9 72.2 %collective-permute-start.69 = (bf16[512,1024]{1,0:T(8,128)(2,1)}, bf16[512,1024]{1,0:T(8,128)(2,1)}, u32[]{:S(2)}, u32[]{:S(2)}) collective-permute-start(bf16[512,1024]{1,0:T(8,128)(2,1)} %get-tuple-element.196.refs_5_), channel_id=1, source_target_pairs={{0,4},{4,0},{8,12},{12,8},{16,20},{20,16},{24,28},{28,24},{1,5},{5... | collective-permute-start | bytes 3145736 | tf_op jit(solution)/shard_map/ppermute | solution.py:832
  415.4 95.2 %collective-permute-start.63 = (bf16[512,1024]{1,0:T(8,128)(2,1)}, bf16[512,1024]{1,0:T(8,128)(2,1)}, u32[]{:S(2)}, u32[]{:S(2)}) collective-permute-start(bf16[512,1024]{1,0:T(8,128)(2,1)} %get-tuple-element.209.refs_7_), channel_id=1, source_target_pairs={{0,8},{4,12},{8,0},{12,4},{16,24},{20,28},{24,16},{28,20},{1,9},{5... | collective-permute-start | bytes 3145736 | tf_op jit(solution)/shard_map/ppermute | solution.py:832
  436.4 52.9 %collective-permute-start.66 = (bf16[512,1024]{1,0:T(8,128)(2,1)}, bf16[512,1024]{1,0:T(8,128)(2,1)}, u32[]{:S(2)}, u32[]{:S(2)}) collective-permute-start(bf16[512,1024]{1,0:T(8,128)(2,1)} %get-tuple-element.210.refs_6_), channel_id=1, source_target_pairs={{0,24},{4,28},{8,16},{12,20},{16,8},{20,12},{24,0},{28,4},{1,25},{... | collective-permute-start | bytes 3145736 | tf_op jit(solution)/shard_map/ppermute | solution.py:832
  447.6 33.4 %collective-permute-start.78 = (f32[8,512]{1,0:T(8,128)S(1)}, f32[8,512]{1,0:T(8,128)S(1)}, u32[]{:S(2)}, u32[]{:S(2)}) collective-permute-start(f32[8,512]{1,0:T(8,128)S(1)} %add.180), channel_id=1, source_target_pairs={{0,8},{4,12},{8,0},{12,4},{16,24},{20,28},{24,16},{28,20},{1,9},{5... | collective-permute-start | bytes 49160 | tf_op jit(solution)/shard_map/ppermute | solution.py:832
  447.7 67.4 %collective-permute-start.73 = (bf16[256,1536]{1,0:T(8,128)(2,1)}, bf16[256,1536]{1,0:T(8,128)(2,1)S(1)}, u32[]{:S(2)}, u32[]{:S(2)}) collective-permute-start(bf16[256,1536]{1,0:T(8,128)(2,1)} %copy-done.125), channel_id=1, source_target_pairs={{0,4},{4,0},{8,12},{12,8},{16,20},{20,16},{24,28},{28,24},{1,5},{5... | collective-permute-start | bytes 2359304 | tf_op jit(solution)/shard_map/ppermute | solution.py:832
  486.1 26.5 %collective-permute-start.59 = (f32[120,128]{0,1:T(8,128)S(1)}, f32[120,128]{0,1:T(8,128)S(1)}, u32[]{:S(2)}, u32[]{:S(2)}) collective-permute-start(f32[120,128]{0,1:T(8,128)S(1)} %fusion.9), channel_id=1, source_target_pairs={{0,2},{1,3},{2,0},{3,1},{4,6},{5,7},{6,4},{7,5},{8,10},{9,11},{10,... | collective-permute-start | bytes 184328 | tf_op jit(solution)/shard_map/ppermute | solution.py:829
  489.4 36.5 %collective-permute-start.84 = (bf16[256,1024]{1,0:T(8,128)(2,1)S(1)}, bf16[256,1024]{1,0:T(8,128)(2,1)S(1)}, u32[]{:S(2)}, u32[]{:S(2)}) collective-permute-start(bf16[256,1024]{1,0:T(8,128)(2,1)S(1)} %get-tuple-element.256), channel_id=1, source_target_pairs={{0,8},{4,12},{8,0},{12,4},{16,24},{20,28},{24,16},{28,20},{1,9},{5... | collective-permute-start | bytes 1572872 | tf_op jit(solution)/shard_map/ppermute | solution.py:832
  499.3 28.7 %collective-permute-start.70 = (bf16[256,1024]{1,0:T(8,128)(2,1)S(1)}, bf16[256,1024]{1,0:T(8,128)(2,1)S(1)}, u32[]{:S(2)}, u32[]{:S(2)}) collective-permute-start(bf16[256,1024]{1,0:T(8,128)(2,1)S(1)} %get-tuple-element.231), channel_id=1, source_target_pairs={{0,8},{4,12},{8,0},{12,4},{16,24},{20,28},{24,16},{28,20},{1,9},{5... | collective-permute-start | bytes 1572872 | tf_op jit(solution)/shard_map/ppermute | solution.py:832
  512.6 24.5 %collective-permute-start.64 = (bf16[256,1024]{1,0:T(8,128)(2,1)S(1)}, bf16[256,1024]{1,0:T(8,128)(2,1)S(1)}, u32[]{:S(2)}, u32[]{:S(2)}) collective-permute-start(bf16[256,1024]{1,0:T(8,128)(2,1)S(1)} %get-tuple-element.221), channel_id=1, source_target_pairs={{0,24},{4,28},{8,16},{12,20},{16,8},{20,12},{24,0},{28,4},{1,25},{... | collective-permute-start | bytes 1572872 | tf_op jit(solution)/shard_map/ppermute | solution.py:832
  525.6 27.9 %collective-permute-start.74 = (bf16[128,1536]{1,0:T(8,128)(2,1)S(1)}, bf16[128,1536]{1,0:T(8,128)(2,1)S(1)}, u32[]{:S(2)}, u32[]{:S(2)}) collective-permute-start(bf16[128,1536]{1,0:T(8,128)(2,1)S(1)} %get-tuple-element.244), channel_id=1, source_target_pairs={{0,8},{4,12},{8,0},{12,4},{16,24},{20,28},{24,16},{28,20},{1,9},{5... | collective-permute-start | bytes 1179656 | tf_op jit(solution)/shard_map/ppermute | solution.py:832
  525.9 27.6 %collective-permute-start.61 = (f32[120,128]{0,1:T(8,128)S(1)}, f32[120,128]{0,1:T(8,128)S(1)}, u32[]{:S(2)}, u32[]{:S(2)}) collective-permute-start(f32[120,128]{0,1:T(8,128)S(1)} %add.176), channel_id=1, source_target_pairs={{0,8},{4,12},{8,0},{12,4},{16,24},{20,28},{24,16},{28,20},{1,9},{5... | collective-permute-start | bytes 184328 | tf_op jit(solution)/shard_map/ppermute | solution.py:832
  528.0 26.8 %collective-permute-start.82 = (bf16[128,1024]{1,0:T(8,128)(2,1)S(1)}, bf16[128,1024]{1,0:T(8,128)(2,1)S(1)}, u32[]{:S(2)}, u32[]{:S(2)}) collective-permute-start(bf16[128,1024]{1,0:T(8,128)(2,1)S(1)} %get-tuple-element.253), channel_id=1, source_target_pairs={{0,4},{4,0},{8,12},{12,8},{16,20},{20,16},{24,28},{28,24},{1,5},{5... | collective-permute-start | bytes 786440 | tf_op jit(solution)/shard_map/ppermute | solution.py:832
  528.6 28.0 %collective-permute-start.85 = (bf16[128,1024]{1,0:T(8,128)(2,1)S(1)}, bf16[128,1024]{1,0:T(8,128)(2,1)S(1)}, u32[]{:S(2)}, u32[]{:S(2)}) collective-permute-start(bf16[128,1024]{1,0:T(8,128)(2,1)S(1)} %get-tuple-element.258), channel_id=1, source_target_pairs={{0,24},{4,28},{8,16},{12,20},{16,8},{20,12},{24,0},{28,4},{1,25},{... | collective-permute-start | bytes 786440 | tf_op jit(solution)/shard_map/ppermute | solution.py:832
  (208 other events, 1740.2 us)

commit v3 on v2

--- a/solution.py
+++ b/solution.py
@@ -106,8 +106,8 @@
         out_specs=[pl.BlockSpec((SLOT,HEAD),lambda h:(0,h)),pl.BlockSpec((1,SLOT,SLOT),lambda h:(h,0,0))],
         out_shape=[jax.ShapeDtypeStruct((SLOT,heads*HEAD),jnp.bfloat16),jax.ShapeDtypeStruct((heads,SLOT,SLOT),jnp.bfloat16)],
         scratch_shapes=[pltpu.VMEM((SLOT,HEAD),jnp.bfloat16)]*3,
-        compiler_params=pltpu.CompilerParams(vmem_limit_bytes=VMEM_CAP),
-        cost_estimate=pl.CostEstimate(flops=1<<20,bytes_accessed=1<<20,transcendentals=0),
+        compiler_params=pltpu.CompilerParams(vmem_limit_bytes=28<<20),
+        cost_estimate=pl.CostEstimate(flops=int(heads*32*SLOT*SLOT*HEAD*WORK),bytes_accessed=1<<20,transcendentals=0),
         name="attend",
     )(who,length,qkv,qkv,qkv,hi,lo)
 
@@ -187,8 +187,8 @@
         out_specs=[out,pl.BlockSpec((1,HEAD,WRAP),lambda h:(h,0,0)),pl.BlockSpec((1,8,HEAD),lambda h:(h,0,0))],
         out_shape=[shape,jax.ShapeDtypeStruct((heads,HEAD,WRAP),jnp.float32),jax.ShapeDtypeStruct((heads,8,HEAD),jnp.float32)],
         scratch_shapes=[pltpu.VMEM((SLOT,HEAD),jnp.bfloat16)]*4+[pltpu.VMEM((HEAD,SLOT),jnp.float32)]*2,
-        compiler_params=pltpu.CompilerParams(vmem_limit_bytes=VMEM_CAP),
-        cost_estimate=pl.CostEstimate(flops=1<<20,bytes_accessed=1<<20,transcendentals=0),
+        compiler_params=pltpu.CompilerParams(vmem_limit_bytes=28<<20),
+        cost_estimate=pl.CostEstimate(flops=int(heads*50*SLOT*SLOT*HEAD*WORK),bytes_accessed=1<<20,transcendentals=0),
         name="attend_back",
     )(who,qkv,qkv,qkv,grad,probs,hi,lo)
     wide=jnp.sum(dt,axis=0).T
@@ -199,29 +199,70 @@
     return members,jnp.concatenate([left[None],wide[near+1:far],right[None]],axis=0)
 
 
-def run(kernel, outs, ins, after=(), name=None, grid=None, in_specs=None, out_specs=None, scratch=(), aliases=None):
-    count = len(ins)
+WORK = 3.0
+
+
+class Stack:
+    def __init__(self, refs):
+        self.refs = refs
+
+    def __getitem__(self, index):
+        return jnp.concatenate([ref[index] for ref in self.refs], axis=0)
+
+
+def run(
+    kernel,
+    outs,
+    ins,
+    after=(),
+    name=None,
+    grid=None,
+    in_specs=None,
+    out_specs=None,
+    scratch=(),
+    aliases=None,
+    room=24,
+    work=1 << 20,
+):
     waits = len(after)
+    sizes = [len(item) if isinstance(item, list) else 0 for item in ins]
 
     def body(*refs):
-        kernel(*refs[:count], *refs[count + waits :])
-
-    whole = pl.BlockSpec(memory_space=pltpu.VMEM)
-    specs = list(in_specs) if in_specs is not None else [whole] * count
-    specs = [whole if spec is None else spec for spec in specs]
-    out_specs = list(out_specs) if out_specs is not None else [whole] * len(outs)
-    extra = {} if grid is None else {"grid": grid}
+        args, at = [], 0
+        for size in sizes:
+            args.append(Stack(refs[at : at + size]) if size else refs[at])
+            at += max(size, 1)
+        kernel(*args, *refs[at + waits :])
+
+    def full(shape):
+        return pl.BlockSpec(tuple(shape), lambda i: (0,) * len(shape))
+
+    if grid is None:
+        grid = (1,)
+    given = list(in_specs) if in_specs is not None else [None] * len(ins)
+    specs, flat, start = [], [], []
+    for item, spec, size in zip(ins, given, sizes):
+        start.append(len(flat))
+        if spec is None:
+            spec = full((item[0] if size else item).shape)
+        elif size:
+            shape = spec.block_shape
+            spec = pl.BlockSpec((shape[0] // size,) + tuple(shape[1:]), spec.index_map)
+        specs += [spec] * max(size, 1)
+        flat += item if size else [item]
+    ins = flat
+    out_specs = list(out_specs) if out_specs is not None else [full(s) for s, _ in outs]
     return pl.pallas_call(
         body,
         in_specs=specs + [pl.BlockSpec(memory_space=pl.ANY)] * waits,
         out_specs=out_specs,
         out_shape=[jax.ShapeDtypeStruct(shape, dtype) for shape, dtype in outs],
         scratch_shapes=list(scratch),
-        input_output_aliases=aliases or {},
-        compiler_params=pltpu.CompilerParams(vmem_limit_bytes=VMEM_CAP),
-        cost_estimate=pl.CostEstimate(flops=1 << 20, bytes_accessed=1 << 20, transcendentals=0),
+        input_output_aliases={start[i]: o for i, o in (aliases or {}).items()},
+        compiler_params=pltpu.CompilerParams(vmem_limit_bytes=room << 20),
+        cost_estimate=pl.CostEstimate(flops=int(work * WORK), bytes_accessed=1 << 20, transcendentals=0),
         name=name,
-        **extra,
+        grid=grid,
     )(*ins, *after)
 
 
@@ -344,16 +385,22 @@
 def feed(own, mate, weights, name, after=()):
     rows, width = own.shape
     hidden = weights.shape[2]
-    tile = tile_of(hidden, 256)
+    tile = tile_of(hidden, 1024)
     steps = hidden // tile
 
-    def kernel(own_ref, mate_ref, in_ref, out_ref, p_own, p_mate, pre, hid, acc):
+    def kernel(own_ref, mate_ref, in_ref, out_ref, p_own, p_mate, pre, hid, seen, acc=None):
         step = pl.program_id(0)
-        value = nn(jnp.concatenate([own_ref[...], mate_ref[...]], axis=0), in_ref[0])
+        both = jnp.concatenate([own_ref[...], mate_ref[...]], axis=0)
+        seen[...] = both
+        value = nn(both, in_ref[0])
         act = (value / (1.0 + jnp.exp(-value))).astype(bf16)
         pre[...] = value.astype(bf16)
         hid[...] = act
         part = nt(act, out_ref[0])
+        if steps == 1:
+            p_own[...] = part[:rows].astype(bf16)
+            p_mate[...] = part[rows:].astype(bf16)
+            return
 
         @pl.when(step == 0)
         def _():
@@ -373,32 +420,40 @@
     weight = [pl.BlockSpec((1, width, tile), lambda i, m=m: (m, 0, i)) for m in range(2)]
     return run(
         kernel,
-        [((rows, width), bf16)] * 2 + [((2 * rows, hidden), bf16)] * 2,
+        [((rows, width), bf16)] * 2 + [((2 * rows, hidden), bf16)] * 2 + [((2 * rows, width), bf16)],
         [own, mate, weights, weights],
         after,
         name,
         grid=(steps,),
         in_specs=[fixed, fixed] + weight,
-        out_specs=[fixed, fixed, cols, cols],
-        scratch=[pltpu.VMEM((2 * rows, width), f32)],
+        out_specs=[fixed, fixed, cols, cols, pl.BlockSpec((2 * rows, width), lambda i: (0, 0))],
+        scratch=[pltpu.VMEM((2 * rows, width), f32)] if steps > 1 else (),
+        room=28,
+        work=8 * rows * width * hidden,
     )
 
 
 def feed_grad(own, mate, pre, weights, name, after=()):
     rows, width = own.shape
     hidden = weights.shape[2]
-    tile = tile_of(hidden, 256)
+    tile = tile_of(hidden, 1024)
     steps = hidden // tile
 
-    def kernel(own_ref, mate_ref, pre_ref, in_ref, out_ref, p_own, p_mate, down, acc):
+    def kernel(own_ref, mate_ref, pre_ref, in_ref, out_ref, p_own, p_mate, down, seen, acc=None):
         step = pl.program_id(0)
-        value = nn(jnp.concatenate([own_ref[...], mate_ref[...]], axis=0), out_ref[0])
+        both = jnp.concatenate([own_ref[...], mate_ref[...]], axis=0)
+        seen[...] = both
+        value = nn(both, out_ref[0])
         preact = wide(pre_ref)
         logistic = 1.0 / (1.0 + jnp.exp(-preact))
         slope = logistic * (1.0 + preact * (1.0 - logistic))
         grad = (value * slope).astype(bf16)
         down[...] = grad
         part = nt(grad, in_ref[0])
+        if steps == 1:
+            p_own[...] = part[:rows].astype(bf16)
+            p_mate[...] = part[rows:].astype(bf16)
+            return
 
         @pl.when(step == 0)
         def _():
@@ -418,14 +473,16 @@
     weight = [pl.BlockSpec((1, width, tile), lambda i, m=m: (m, 0, i)) for m in range(2)]
     return run(
         kernel,
-        [((rows, width), bf16)] * 2 + [((2 * rows, hidden), bf16)],
+        [((rows, width), bf16)] * 2 + [((2 * rows, hidden), bf16), ((2 * rows, width), bf16)],
         [own, mate, pre, weights, weights],
         after,
         name,
         grid=(steps,),
         in_specs=[fixed, fixed, cols] + weight,
-        out_specs=[fixed, fixed, cols],
-        scratch=[pltpu.VMEM((2 * rows, width), f32)],
+        out_specs=[fixed, fixed, cols, pl.BlockSpec((2 * rows, width), lambda i: (0, 0))],
+        scratch=[pltpu.VMEM((2 * rows, width), f32)] if steps > 1 else (),
+        room=28,
+        work=8 * rows * width * hidden,
     )
 
 
@@ -434,8 +491,9 @@
     cols = weights.shape[2]
 
     def kernel(own_ref, mate_ref, w_ref, *refs):
-        value = nn(jnp.concatenate([own_ref[...], mate_ref[...]], axis=0), w_ref[0])
-        refs[-1][0] = value.astype(bf16)
+        both = jnp.concatenate([own_ref[...], mate_ref[...]], axis=0)
+        refs[-1][...] = both
+        refs[-2][0] = nn(both, w_ref[0]).astype(bf16)
 
     fixed = pl.BlockSpec((rows, width), lambda i: (0, 0))
     ins = [own, mate, weights] + ([held] if held is not None else [])
@@ -443,15 +501,19 @@
     specs = specs + [pl.BlockSpec(memory_space=pl.ANY)] * (held is not None)
     return run(
         kernel,
-        [((3, total, cols), bf16)],
+        [((3, total, cols), bf16), ((2 * rows, width), bf16)],
         ins,
         after,
         name,
         grid=(3,),
         in_specs=specs,
-        out_specs=[pl.BlockSpec((1, 2 * rows, cols), lambda i: (i, k, 0))],
+        out_specs=[
+            pl.BlockSpec((1, 2 * rows, cols), lambda i: (i, k, 0)),
+            pl.BlockSpec((2 * rows, width), lambda i: (0, 0)),
+        ],
+        work=12 * rows * width * cols,
         aliases={3: 0} if held is not None else None,
-    )[0]
+    )
 
 
 def heads_rows(own, mate, weight, k, total, held, name, after=()):
@@ -459,8 +521,9 @@
     cols = weight.shape[1]
 
     def kernel(own_ref, mate_ref, w_ref, *refs):
-        value = nn(jnp.concatenate([own_ref[...], mate_ref[...]], axis=0), w_ref[...])
-        refs[-1][...] = value.astype(bf16)
+        both = jnp.concatenate([own_ref[...], mate_ref[...]], axis=0)
+        refs[-1][...] = both
+        refs[-2][...] = nn(both, w_ref[...]).astype(bf16)
 
     fixed = pl.BlockSpec((rows, width), lambda i: (0, 0))
     ins = [own, mate, weight] + ([held] if held is not None else [])
@@ -468,15 +531,19 @@
     specs = specs + [pl.BlockSpec(memory_space=pl.ANY)] * (held is not None)
     return run(
         kernel,
-        [((total, cols), bf16)],
+        [((total, cols), bf16), ((2 * rows, width), bf16)],
         ins,
         after,
         name,
         grid=(1,),
         in_specs=specs,
-        out_specs=[pl.BlockSpec((2 * rows, cols), lambda i: (k, 0))],
+        out_specs=[
+            pl.BlockSpec((2 * rows, cols), lambda i: (k, 0)),
+            pl.BlockSpec((2 * rows, width), lambda i: (0, 0)),
+        ],
+        work=4 * rows * width * cols,
         aliases={3: 0} if held is not None else None,
-    )[0]
+    )
 
 
 def out_rows(values, weight, k, rows, name, after=()):
@@ -500,6 +567,7 @@
             pl.BlockSpec((width, cols), lambda i: (0, 0)),
         ],
         out_specs=[fixed, fixed],
+        work=4 * rows * width * cols,
     )
 
 
@@ -526,7 +594,66 @@
             pl.BlockSpec((3, width, cols), lambda i: (0, 0, 0)),
         ],
         out_specs=[fixed, fixed],
-    )
+        work=12 * rows * width * cols,
+    )
+
+
+def part(array, m=None, begin=0, end=None):
+    value = array[...] if m is None else array[m]
+    return value if end is None else value[:, begin:end]
+
+
+def plain(item):
+    return item[0] if isinstance(item, tuple) else item
+
+
+def spot(item):
+    return item[1:] if isinstance(item, tuple) else ()
+
+
+def span(item):
+    return item[3] - item[2] if len(spot(item)) > 1 else plain(item).shape[-1]
+
+
+def lay_out(jobs):
+    plan, ins = [], []
+    for left, rights in jobs:
+        picks = [[spot(item) for item in right] for right in rights]
+        plan.append((len(left), picks, sum(span(right[0]) for right in rights)))
+        ins = ins + list(left) + [plain(item) for right in rights for item in right]
+    return plan, ins
+
+
+def sides(plan, refs):
+    at = 0
+    for n_left, picks, cols in plan:
+        left = refs[at : at + n_left]
+        at = at + n_left
+        columns = []
+        for places in picks:
+            values = []
+            for place in places:
+                values.append(part(refs[at], *place))
+                at = at + 1
+            columns.append(values[0] if len(values) == 1 else jnp.concatenate(values, axis=0))
+        yield left, columns[0] if len(columns) == 1 else jnp.concatenate(columns, axis=1), cols
+
+
+def outer(jobs, name, after=()):
+    plan, ins = lay_out(jobs)
+    total = sum(cols for _, _, cols in plan)
+    width = jobs[0][0][0].shape[1]
+
+    def kernel(*refs):
+        column = 0
+        for left, rights, cols in sides(plan, refs):
+            rows = [ref[...] for ref in left]
+            rows = rows[0] if len(rows) == 1 else jnp.concatenate(rows, axis=0)
+            refs[-1][:, column : column + cols] = tn(rows, rights).astype(bf16)
+            column = column + cols
+
+    work = sum(2 * width * cols * sum(r.shape[0] for r in left) for (left, _), (_, _, cols) in zip(jobs, plan))
+    return run(kernel, [((width, total), bf16)], ins, after, name, room=36, work=work)[0]
 
 
 def outer_halves(links, jobs, turn, name, after=()):
@@ -534,51 +661,23 @@
     width = jobs[0][0][0].shape[1]
     share = width // links.dp
     me = lax.axis_index("dp").reshape(1).astype(jnp.int32)
-    if share % 128:
-        whole = jnp.concatenate(
-            [
-                tn(
-                    jnp.concatenate(left),
-                    jnp.concatenate([r[0][r[1]] if isinstance(r, tuple) else r for r in right]),
-                )
-                for left, right in jobs
-            ],
-            axis=1,
-        ).astype(bf16)
-        blocks = whole.reshape(links.dp, share, whole.shape[1])
-
-        def pick(which):
-            return jnp.concatenate(
-                [lax.dynamic_index_in_dim(blocks, me[0] ^ off, 0, keepdims=False) for off in which]
-            )
-
-        return pick([off ^ masks[0] for off in offsets]), pick(offsets)
-    ins = [me]
-    plan = []
-    for left, right in jobs:
-        picks = [item[1] if isinstance(item, tuple) else None for item in right]
-        arrays = [item[0] if isinstance(item, tuple) else item for item in right]
-        plan.append((len(left), picks, arrays[0].shape[-1]))
-        ins = ins + list(left) + arrays
+
+    plan, ins = lay_out(jobs)
+    ins = [me] + ins
     total = sum(cols for _, _, cols in plan)
     half = len(offsets)
 
     def kernel(me_ref, *refs):
         who = me_ref[0]
         sent_ref, kept_ref = refs[-2], refs[-1]
-        at, column = 0, 0
-        for n_left, picks, cols in plan:
-            left = refs[at : at + n_left]
-            right = refs[at + n_left : at + n_left + len(picks)]
-            at = at + n_left + len(picks)
-            rights = [ref[...] if m is None else ref[m] for ref, m in zip(right, picks)]
-            rights = rights[0] if len(picks) == 1 else jnp.concatenate(rights, axis=0)
+        column = 0
+        for left, rights, cols in sides(plan, refs):
             for flip, dest in ((masks[0], sent_ref), (0, kept_ref)):
                 picked = []
                 for off in offsets:
                     where = pl.ds(pl.multiple_of((who ^ off ^ flip) * share, 128), share)
                     parts = [ref[:, where] for ref in left]
-                    picked.append(parts[0] if n_left == 1 else jnp.concatenate(parts, axis=0))
+                    picked.append(parts[0] if len(parts) == 1 else jnp.concatenate(parts, axis=0))
                 picked = picked[0] if half == 1 else jnp.concatenate(picked, axis=1)
                 dest[:, column : column + cols] = tn(picked, rights).astype(bf16)
             column = column + cols
@@ -590,19 +689,25 @@
         after,
         name,
         in_specs=[SMEM_SPEC] + [None] * (len(ins) - 1),
-    )
-
-
-def halve(kept, came, name, after=()):
-    count, cols = kept.shape
-    half = count // 2
-
-    def kernel(kept_ref, came_ref, sent_out, kept_out):
-        total = wide(kept_ref) + wide(came_ref)
-        kept_out[...] = total[:half].astype(bf16)
-        sent_out[...] = total[half:].astype(bf16)
-
-    return run(kernel, [((half, cols), bf16)] * 2, [kept, came], after, name)
+        room=24,
+        work=2 * SLOT * width * total,
+    )
+
+
+def halve_all(pairs, name, after=()):
+    shapes = [(kept.shape[0] // 2, kept.shape[1]) for kept, _ in pairs]
+    count = len(pairs)
+
+    def kernel(*refs):
+        for i in range(count):
+            total = wide(refs[2 * i]) + wide(refs[2 * i + 1])
+            half = shapes[i][0]
+            refs[2 * count + 2 * i][...] = total[half:].astype(bf16)
+            refs[2 * count + 2 * i + 1][...] = total[:half].astype(bf16)
+
+    outs = [(shape, bf16) for shape in shapes for _ in range(2)]
+    made = run(kernel, outs, [array for pair in pairs for array in pair], after, name)
+    return [(made[2 * i], made[2 * i + 1]) for i in range(count)]
 
 
 def halves(ref_own, ref_mate, c):
@@ -645,8 +750,9 @@
     n_before = len(before)
 
     def kernel(who_ref, len_ref, own_ref, mate_ref, w0, w1, taps_ref, *refs):
-        rows_in = bordered(own_ref, mate_ref, refs[:n_before], refs[n_before:-4], who_ref[0], ny)
-        lin_ref, gate_ref, mix_ref, tally_ref = refs[-4:]
+        rows_in = bordered(own_ref, mate_ref, refs[:n_before], refs[n_before:-5], who_ref[0], ny)
+        lin_ref, gate_ref, mix_ref, tally_ref, seen_ref = refs[-5:]
+        seen_ref[...] = jnp.concatenate([own_ref[...], mate_ref[...]], axis=0)
         valid = place_mask(count, who_ref[0] // 2, len_ref[0])
         linear = nn(rows_in, w0[...])
         gating = 1.0 / (1.0 + jnp.exp(-nn(rows_in, w1[...])))
@@ -672,11 +778,13 @@
     shape = (count + 2 * MARGIN, cols)
     return run(
         kernel,
-        [(shape, f32)] * 3 + [((8, cols), f32)],
+        [(shape, f32)] * 3 + [((8, cols), f32), ((count, width), bf16)],
         ins,
         after,
         name,
         in_specs=[SMEM_SPEC, SMEM_SPEC] + [None] * (len(ins) - 2),
+        room=28,
+        work=4 * count * width * cols,
     )
 
 
@@ -716,6 +824,8 @@
         after,
         name,
         in_specs=[SMEM_SPEC] + [None] * 5,
+        room=24,
+        work=4 * rows * width * cols,
     )
 
 
@@ -727,8 +837,9 @@
     n_before = len(before)
 
     def kernel(who_ref, len_ref, own_ref, mate_ref, mix_ref, tally_ref, affine_ref, w_ref, *refs):
-        rows_in = bordered(own_ref, mate_ref, refs[:n_before], refs[n_before:-2], who_ref[0], ny)
-        dz_ref, out_ref = refs[-2:]
+        rows_in = bordered(own_ref, mate_ref, refs[:n_before], refs[n_before:-3], who_ref[0], ny)
+        dz_ref, out_ref, seen_ref = refs[-3:]
+        seen_ref[...] = jnp.concatenate([own_ref[...], mate_ref[...]], axis=0)
         valid = place_mask(count, who_ref[0] // 2, len_ref[0])
         _, mean, _, inverse = batch_terms(tally_ref)
         centred = (mix_ref[...] - mean) * inverse
@@ -750,11 +861,13 @@
     ins = [who, length, own, mate, mixture, tallies, affine, weight] + list(before) + list(after_rows)
     return run(
         kernel,
-        [(mixture.shape, f32), ((8, cols), f32)],
+        [(mixture.shape, f32), ((8, cols), f32), ((count, width), bf16)],
         ins,
         after,
         name,
         in_specs=[SMEM_SPEC, SMEM_SPEC] + [None] * (len(ins) - 2),
+        room=28,
+        work=4 * count * width * cols,
     )
 
 
@@ -811,25 +924,32 @@
         after,
         name,
         in_specs=[SMEM_SPEC, SMEM_SPEC] + [None] * 10,
+        room=32,
+        work=4 * count * width * cols,
     )
 
 
 class Links:
     def __init__(self, dp, tensor):
         self.dp, self.tensor, self.ny = dp, tensor, tensor // 2
-        masks = [1 << bit for bit in range(dp.bit_length() - 1)]
-        if len(masks) > 2:
-            masks[2] = 6
-        self.masks = masks
+        self.masks = [1 << bit for bit in range(dp.bit_length() - 1)]
 
     def core(self, value):
         return lax.ppermute(value, "tensor", [(i, i ^ 1) for i in range(self.tensor)])
 
+    def mate(self, value):
+        pieces = 4 if value.shape[0] % 64 == 0 else 1
+        rows = value.shape[0] // pieces
+        return [self.core(value[i * rows : (i + 1) * rows]) for i in range(pieces)]
+
     def chip(self, value, k):
         return lax.ppermute(value, "tensor", [(i, i ^ (2 * k)) for i in range(self.tensor)])
 
     def group(self, value, mask):
         return lax.ppermute(value, "dp", [(i, i ^ mask) for i in range(self.dp)])
+
+    def scatter_grad(self, value):
+        return lax.psum_scatter(value, "dp", scatter_dimension=0, tiled=True)
 
     def sum_group(self, value):
         for mask in self.masks:
@@ -837,6 +957,9 @@
         return value
 
     def sum_stats(self, value, channels):
+        return self.sum_group(self.sum_columns(value, channels))
+
+    def sum_columns(self, value, channels):
         def cols(array, k):
             return array[:, k * channels : (k + 1) * channels]
 
@@ -844,11 +967,12 @@
         for k in range(1, self.ny):
             other = self.chip(value, k)
             total = total + jnp.concatenate([cols(other, r ^ k) for r in range(self.ny)], axis=1)
-        return self.sum_group(total)
+        return total
 
     def offsets(self, turn):
-        count = len(self.masks)
-        masks = [self.masks[(turn + i) % count] for i in range(count)]
+        masks = list(self.masks)
+        if turn:
+            masks[:2] = masks[1::-1]
         offsets = [0]
         for mask in masks[:0:-1]:
             offsets = offsets + [off ^ mask for off in offsets]
@@ -863,6 +987,7 @@
             straight = lax.ppermute(edge, "tensor", [(1, 3), (2, 0)])
             across = lax.ppermute(edge, "tensor", [(1, 2), (2, 1)])
             return [straight, across], [straight, across]
+        mate = jnp.concatenate(mate)
         head = jnp.where(c == 0, own, mate)[:MARGIN]
         foot = jnp.where(c == 0, mate, own)[count - MARGIN :]
         down = [(i, i + 2) for i in range(self.tensor - 2)]
@@ -870,82 +995,108 @@
         return [lax.ppermute(foot, "tensor", down)], [lax.ppermute(head, "tensor", up)]
 
 
-class Halving:
-    def __init__(self, links, halves, turn, name):
+class Pieces:
+    def __init__(self, links, pieces, name):
         self.links, self.name = links, name
-        self.masks = links.offsets(turn)[1]
-        self.sent, self.kept = halves
-        self.first = self.sent
+        self.count = len(pieces)
+        self.masks = [links.offsets(i % 2)[1] for i in range(self.count)]
+        self.kept = [kept for _, kept in pieces]
         self.at = 0
-        self.send()
-
-    def send(self):
-        self.came = self.links.group(self.sent, self.masks[self.at])
+        self.send([sent for sent, _ in pieces])
+
+    def send(self, sent):
+        self.came = [self.links.group(sent[i], self.masks[i][self.at]) for i in range(self.count)]
         self.at += 1
 
     def step(self, after=()):
-        if self.at < len(self.masks):
-            self.sent, self.kept = halve(self.kept, self.came, self.name + "_half", after)
-            self.send()
-        return self.kept
+        if self.at < len(self.links.masks):
+            made = halve_all(list(zip(self.kept, self.came)), self.name + "_half", after)
+            self.kept = [kept for _, kept in made]
+            self.send([sent for sent, _ in made])
+        return self.kept[0]
 
     def finish(self):
-        while self.at < len(self.masks):
+        while self.at < len(self.links.masks):
             self.step()
-        return self.kept, self.came
-
-
-def finish_pair(first, second, name, after=()):
-    ins = list(first.finish() + second.finish())
-    shape = ins[0].shape
-
-    def kernel(a, b, c, d, out):
-        out[0] = wide(a) + wide(b)
-        out[1] = wide(c) + wide(d)
-
-    return run(kernel, [((2,) + shape, f32)], ins, after, name)[0]
-
-
-def finish_heads(pending, cols, name, after=()):
-    ins = list(pending.finish())
+        return [array for pair in zip(self.kept, self.came) for array in pair]
+
+
+def finish_one(outs_of, ins_of, width_in, name):
+    ins = outs_of + ins_of
     share = ins[0].shape[0]
 
-    def kernel(a, b, three, one):
-        total = wide(a) + wide(b)
+    def kernel(*refs):
+        out = refs[-1]
+        parts = [wide(refs[2 * i]) + wide(refs[2 * i + 1]) for i in range(4)]
+        out[1] = jnp.concatenate(parts[:2], axis=1)
+        out[0] = jnp.concatenate(parts[2:], axis=1)
+
+    return run(kernel, [((2, share, width_in), f32)], ins, (), name)[0]
+
+
+def split_two(total, hidden, name, after=()):
+    share = total.shape[0]
+
+    def kernel(ref, out):
+        for m in range(2):
+            out[m] = wide(ref)[:, m * hidden : (m + 1) * hidden]
+
+    return run(kernel, [((2, share, hidden), f32)], [total], after, name)[0]
+
+
+def split_heads(total, begin, cols, name):
+    share = total.shape[0]
+
+    def kernel(ref, three, one):
+        value = wide(ref)[:, begin:]
         for m in range(3):
-            three[m] = total[:, m * cols : (m + 1) * cols]
-        one[...] = total[:, 3 * cols :]
-
-    return run(kernel, [((3, share, cols), f32), ((share, cols), f32)], ins, after, name)
-
-
-def finish_conv(links, pending, channels, name, after=()):
-    ins = list(pending.finish())
-    share = ins[0].shape[0]
+            three[m] = value[:, m * cols : (m + 1) * cols]
+        one[...] = value[:, 3 * cols :]
+
+    return run(kernel, [((3, share, cols), f32), ((share, cols), f32)], [total], (), name)
+
+
+def finish_conv(links, total, channels, name):
+    share = total.shape[0]
     ny = links.ny
 
-    def split(a, b, own, *others):
-        total = wide(a) + wide(b)
+    def split(ref, *others):
         for m in range(3):
-            for k in range(ny):
+            for k in range(1, ny):
                 at = (m * ny + k) * channels
-                piece = total[:, at : at + channels]
-                if k == 0:
-                    own[m] = piece
-                else:
-                    others[k - 1][m] = piece.astype(bf16)
+                others[k - 1][m] = ref[:, at : at + channels]
 
     shape = (3, share, channels)
-    parts = run(split, [(shape, f32)] + [(shape, bf16)] * (ny - 1), ins, after, name)
-    came = [links.chip(parts[k], k) for k in range(1, ny)]
+    parts = run(split, [(shape, bf16)] * (ny - 1), [total], (), name)
+    came = [links.chip(parts[k - 1], k) for k in range(1, ny)]
 
     def close(*refs):
-        total = refs[0][...]
-        for ref in refs[1:-1]:
-            total = total + wide(ref)
-        refs[-1][...] = total
-
-    return run(close, [(shape, f32)], [parts[0]] + came, (), name + "_close")[0]
+        for m in range(3):
+            piece = refs[0][:, m * ny * channels : (m * ny + 1) * channels].astype(f32)
+            for ref in refs[1:-1]:
+                piece = piece + ref[m].astype(f32)
+            refs[-1][m] = piece
+
+    return run(close, [(shape, f32)], [total] + came, (), name + "_close")[0]
+
+
+def arrange(conv_proj, gathered, dp, name):
+    _, width, channels = conv_proj.shape
+    share = width // dp
+    cols = channels * (1 + len(gathered))
+
+    def kernel(own_ref, *refs):
+        others, outs = refs[: len(gathered)], refs[len(gathered) :]
+        for m in range(3):
+            outs[m][:, :channels] = own_ref[m]
+            for k, ref in enumerate(others):
+                for b in range(dp):
+                    at = (b * 3 + m) * share
+                    outs[m][b * share : (b + 1) * share, (k + 1) * channels : (k + 2) * channels] = ref[
+                        at : at + share, :
+                    ]
+
+    return run(kernel, [((width, cols), bf16)] * 3, [conv_proj] + gathered, (), name)
 
 
 def per_device(
@@ -978,28 +1129,17 @@
     me = lax.axis_index("dp")
     share = width // links.dp
     piece = lax.dynamic_slice_in_dim(conv_proj, me * share, share, axis=1)
-    conv_w = [[conv_proj[m] for m in range(3)]]
+    gathered = []
     for k in others:
-        blocks = links.chip(piece, k)[None]
-        order = [0]
-        for mask in links.masks:
-            blocks = jnp.concatenate([blocks, links.group(blocks, mask)])
-            order = order + [off ^ mask for off in order]
-        where = {off: at for at, off in enumerate(order)}
-        table = jnp.array([where[off] for off in range(links.dp)], jnp.int32)
-        rows_of = [
-            lax.dynamic_index_in_dim(blocks, table[me ^ b], 0, keepdims=False)
-            for b in range(links.dp)
-        ]
-        whole = jnp.concatenate(rows_of, axis=1)
-        conv_w.append([whole[m] for m in range(3)])
-    conv_w = [jnp.concatenate([conv_w[k][m] for k in range(ny)], axis=1) for m in range(3)]
+        other = links.chip(piece, k).reshape(3 * share, channels)
+        gathered.append(lax.all_gather(other, "dp", axis=0, tiled=True))
+    conv_w = arrange(conv_proj, gathered, links.dp, "conv_weights")
     small = jnp.concatenate([depthwise, bn_gain[None], bn_bias[None], jnp.zeros((1, channels), f32)])
     small = jnp.concatenate([small] + [links.chip(small, k) for k in others], axis=1)
     affine = small[KERNEL : KERNEL + 2]
 
     def send_sums(parts, name, after=()):
-        return add_up([parts[0], links.core(parts[1])], name, after)
+        return add_up([parts[0], links.mate(parts[1])], name, after)
 
     normed, x_low = norm_rows(x_in, [], 0.0, gain[0], "ln_in", keep=False, low=True)
     x_rows = [x_in] + [links.chip(x_low, k) for k in others]
@@ -1008,8 +1148,8 @@
     for k in range(ny):
         if k:
             (normed,) = norm_rows(x_rows[k], [], 0.0, gain[0], "ln_in", token, keep=False)
-        na_first[k] = (normed, links.core(normed))
-        p_own, p_mate, pre, hid = feed(*na_first[k], ffn_first, "ffn_one")
+        na_first[k] = (normed, links.mate(normed))
+        p_own, p_mate, pre, hid, na_first[k] = feed(*na_first[k], ffn_first, "ffn_one")
         kept_first[k] = (pre, hid)
         sums[k] = send_sums((p_own, p_mate), "ffn_one_sum")
         token = (sums[k],)
@@ -1024,11 +1164,11 @@
         made = norm_rows(
             x_rows[k], all_parts(sums, k), 0.5, gain[1], "ln_attn", token, also=also
         )
-        na_attn[k] = (made[0], links.core(made[0]))
+        na_attn[k] = (made[0], links.mate(made[0]))
         first[k] = made[1]
         if k == 0:
             cot_low = made[2]
-        qkv = qkv_rows(*na_attn[k], attn_qkv, k, SLOT, qkv, "qkv")
+        qkv, na_attn[k] = qkv_rows(*na_attn[k], attn_qkv, k, SLOT, qkv, "qkv")
         token = (qkv,)
     cot_rows = [cotangent] + [links.chip(cot_low, k) for k in others]
     heads_out, probs = attend(qkv, who_arr, lengths, rel_table, rows)
@@ -1040,12 +1180,12 @@
         token = (total,)
     p_own, p_mate = out_rows(heads_out, attn_out, 0, rows, "out_proj", token)
     conv_own, after_attn = norm_rows(
-        first[0], [p_own, links.core(p_mate)] + arrived, 1.0, gain[2], "ln_conv"
-    )
-
-    conv_mate = links.core(conv_own)
+        first[0], [p_own, links.mate(p_mate)] + arrived, 1.0, gain[2], "ln_conv"
+    )
+
+    conv_mate = links.mate(conv_own)
     before, after_rows = links.borders(conv_own, conv_mate)
-    linear, gating, mixture, tallies = conv_mix(
+    linear, gating, mixture, tallies, conv_in = conv_mix(
         ny, who_arr, lengths, conv_own, conv_mate, before, after_rows, conv_w, small[:KERNEL], "conv_mix"
     )
     tallies = links.sum_stats(tallies, channels)
@@ -1053,7 +1193,7 @@
         who_arr, mixture, tallies, affine, running, conv_w[2], rows, "conv_out"
     )
     normed, after_conv, low = norm_rows(
-        after_attn, [p_own, links.core(p_mate)], 1.0, gain[3], "ln_ffn_two", low=True
+        after_attn, [p_own, links.mate(p_mate)], 1.0, gain[3], "ln_ffn_two", low=True
     )
 
     x_rows = [after_conv] + [links.chip(low, k) for k in others]
@@ -1062,8 +1202,8 @@
     for k in range(ny):
         if k:
             (normed,) = norm_rows(x_rows[k], [], 0.0, gain[3], "ln_ffn_two", token, keep=False)
-        na_last[k] = (normed, links.core(normed))
-        p_own, p_mate, pre, hid = feed(*na_last[k], ffn_second, "ffn_two")
+        na_last[k] = (normed, links.mate(normed))
+        p_own, p_mate, pre, hid, na_last[k] = feed(*na_last[k], ffn_second, "ffn_two")
         kept_last[k] = (pre, hid)
         sums[k] = send_sums((p_own, p_mate), "ffn_two_sum")
         token = (sums[k],)
@@ -1082,33 +1222,34 @@
             k == 0,
             token,
         )
-        upper[k] = (made[0], links.core(made[0]))
-        p_own, p_mate, down[k] = feed_grad(*upper[k], kept_last[k][0], ffn_second, "ffn_two_grad")
+        upper[k] = (made[0], links.mate(made[0]))
+        p_own, p_mate, down[k], upper[k] = feed_grad(
+            *upper[k], kept_last[k][0], ffn_second, "ffn_two_grad"
+        )
         if k:
             total = send_sums((p_own, p_mate), "ffn_two_grad_sum")
             arrived.append(links.chip(total, k))
             token = (total,)
         else:
             grad, output, gain_five = made[1:]
-            parts = [p_own, links.core(p_mate)]
-
-    def row_blocks(pairs):
-        return [block for k in range(ny) for block in pairs[k]]
-
-    wait_out = outer_halves(
-        links, [(row_blocks(upper), [kept_last[k][1] for k in range(ny)])], 0, "ffn_two_out", (p_mate,)
-    )
-    wait_in = outer_halves(
-        links, [(row_blocks(na_last), [down[k] for k in range(ny)])], 1, "ffn_two_in", (p_mate,)
+            parts = [p_own, links.mate(p_mate)]
+
+    def every(pieces):
+        return [pieces[k] for k in range(ny)]
+
+    hid_last = [kept_last[k][1] for k in range(ny)]
+    two_sum = outer(
+        [(every(na_last), [every(down)]), (every(upper), [hid_last])], "ffn_two_w", (p_mate,)
     )
     low, grad, gain_four = norm_grad(
-        after_conv, parts + arrived, gain[3], grad, "back_ffn_two", (wait_out[0], wait_in[0]), factor=1.0
-    )
+        after_conv, parts + arrived, gain[3], grad, "back_ffn_two", (two_sum,), factor=1.0
+    )
+    two_sum = links.scatter_grad(two_sum)
 
     up_own = low
-    up_mate = links.core(low)
+    up_mate = links.mate(low)
     before, after_rows = links.borders(up_own, up_mate)
-    dz, sums = conv_shift_grad(
+    dz, sums, conv_up = conv_shift_grad(
         ny, who_arr, lengths, up_own, up_mate, before, after_rows, mixture, tallies, affine, conv_w[2], "conv_dz"
     )
     bn_grads = links.sum_stats(sums, channels)
@@ -1116,47 +1257,38 @@
         who_arr, lengths, dz, mixture, tallies, bn_grads, affine, small[:KERNEL], linear, gating, conv_w, rows, "conv_din"
     )
     low, grad, gain_three = norm_grad(
-        after_attn, [p_own, links.core(p_mate)], gain[2], grad, "back_conv", factor=1.0
-    )
-
-    pend_two_out = Halving(links, wait_out, 0, "ffn_two_out")
-    pend_two_in = Halving(links, wait_in, 1, "ffn_two_in")
+        after_attn, [p_own, links.mate(p_mate)], gain[2], grad, "back_conv", factor=1.0
+    )
+
 
     g_rows = [low] + [links.chip(low, k) for k in others]
-    conv_halves = outer_halves(
-        links,
-        [
-            ([conv_own, conv_mate], [grad_linear]),
-            ([conv_own, conv_mate], [grad_gate]),
-            ([up_own, up_mate], [active]),
-        ],
-        2,
-        "conv_w",
-        (low,),
-    )
-    pend_conv = Halving(links, conv_halves, 2, "conv_w")
+    token = (low,)
     grad_heads = None
     upper_attn = {}
     for k in range(ny):
-        upper_attn[k] = (g_rows[k], links.core(g_rows[k]))
-        grad_heads = heads_rows(*upper_attn[k], attn_out, k, SLOT, grad_heads, "dheads")
+        grad_heads, upper_attn[k] = heads_rows(
+            g_rows[k], links.mate(g_rows[k]), attn_out, k, SLOT, grad_heads, "dheads", token
+        )
+        token = ()
     members, table_grad = attend_back(qkv, grad_heads, probs, who_arr, rel_table, rows)
     token = ()
     sums = {}
     for k in range(ny):
         sums[k] = send_sums(members_rows(members, attn_qkv, k, rows, "dqkv", token), "dqkv_sum")
         token = (sums[k],)
-    heads_halves = outer_halves(
-        links,
-        [(row_blocks(na_attn), [(members, m)]) for m in range(3)]
-        + [(row_blocks(upper_attn), [heads_out])],
-        0,
+    heads_sum = outer(
+        [
+            ([conv_in], [[grad_linear], [grad_gate]]),
+            ([conv_up], [[active]]),
+            (every(na_attn), [[(members, m)] for m in range(3)]),
+            (every(upper_attn), [[heads_out]]),
+        ],
         "attn_w",
         token,
     )
-    pend_heads = Halving(links, heads_halves, 0, "attn_w")
-
-    token = (heads_halves[0],)
+    token = (heads_sum,)
+    heads_sum = links.scatter_grad(heads_sum)
+
     upper, down, arrived = {}, {}, []
     for k in others + [0]:
         made = norm_grad(
@@ -1170,37 +1302,41 @@
             keep=k == 0,
             sums=k == 0,
         )
-        upper[k] = (made[0], links.core(made[0]))
-        p_own, p_mate, down[k] = feed_grad(*upper[k], kept_first[k][0], ffn_first, "ffn_one_grad")
+        upper[k] = (made[0], links.mate(made[0]))
+        p_own, p_mate, down[k], upper[k] = feed_grad(
+            *upper[k], kept_first[k][0], ffn_first, "ffn_one_grad"
+        )
         if k:
             total = send_sums((p_own, p_mate), "ffn_one_grad_sum")
             arrived.append(links.chip(total, k))
             token = (total,)
         else:
             grad, gain_two = made[1:]
-            parts = [p_own, links.core(p_mate)]
-    halves_in = outer_halves(
-        links, [(row_blocks(na_first), [down[k] for k in range(ny)])], 1, "ffn_one_in", (p_mate,)
-    )
-    pend_one_in = Halving(links, halves_in, 1, "ffn_one_in")
-    halves_out = outer_halves(
-        links,
-        [(row_blocks(upper), [kept_first[k][1] for k in range(ny)])],
-        2,
-        "ffn_one_out",
-        (halves_in[0],),
-    )
-    pend_one_out = Halving(links, halves_out, 2, "ffn_one_out")
+            parts = [p_own, links.mate(p_mate)]
+    hid_first = [kept_first[k][1] for k in range(ny)]
+    hidden = ffn_first.shape[2]
+    half = hidden // 2
+    one_down, one_up, one_in = every(down), every(upper), every(na_first)
+    token = (p_mate,)
+    pairs = []
+    if share % 128 == 0:
+        for left, right in ((one_up, hid_first), (one_in, one_down)):
+            pieces = []
+            for turn in range(2):
+                columns = [(r, None, turn * half, (turn + 1) * half) for r in right]
+                made = outer_halves(links, [(left, [columns])], turn, "ffn_one_w", token)
+                token = (made[0],)
+                pieces.append(made)
+            pairs.append(Pieces(links, pieces, "one"))
+    else:
+        first_sum = outer([(one_in, [one_down]), (one_up, [hid_first])], "ffn_one_w", token)
+        token = (first_sum,)
+        first_sum = links.scatter_grad(first_sum)
+    last_sum = split_two(two_sum, hidden, "two_end", token)
     grad_input, gain_one = norm_grad(
-        x_in, parts + arrived, gain[0], grad, "back_ffn_one", (halves_out[0],)
-    )
-
-    last_sum = finish_pair(pend_two_in, pend_two_out, "ffn_two_end")
-    conv_sum = finish_conv(links, pend_conv, channels, "conv_end")
-    qkv_sum, out_sum = finish_heads(pend_heads, attn_qkv.shape[2], "attn_end")
-    first_sum = finish_pair(pend_one_in, pend_one_out, "ffn_one_end")
-
-    kernel_grad = links.sum_stats(tap_grad, channels)[:KERNEL, :channels]
+        x_in, parts + arrived, gain[0], grad, "back_ffn_one", token + (last_sum,)
+    )
+
     gains = [gain_one, gain_two, gain_three, gain_four, gain_five]
     gains = jnp.stack([part[0] for part in gains]).reshape(-1, HEAD)
     bundle = jnp.concatenate([gains, table_grad])
@@ -1208,7 +1344,21 @@
     bundle = bundle + links.core(bundle)
     for k in [1 << bit for bit in range(ny.bit_length() - 1)]:
         bundle = bundle + links.chip(bundle, k)
-    bundle = links.sum_group(bundle)
+    taps_at = bundle.shape[0]
+    tap_sums = links.sum_columns(tap_grad, channels)[:, :channels]
+    bundle = jnp.concatenate([bundle, tap_sums.reshape(-1, HEAD)])
+    token = ()
+    for mask in links.masks:
+        bundle = bundle + links.group(bundle, mask)
+        for pair in pairs:
+            pair.step((bundle,))
+    kernel_grad = bundle[taps_at:].reshape(8, channels)[:KERNEL]
+    if pairs:
+        first_sum = finish_one(pairs[0].finish(), pairs[1].finish(), hidden, "one_end")
+    else:
+        first_sum = split_two(first_sum, hidden, "one_end")
+    qkv_sum, out_sum = split_heads(heads_sum, 3 * ny * channels, attn_qkv.shape[2], "heads_end")
+    conv_sum = finish_conv(links, heads_sum, channels, "conv_end")
     return (
         output,
         grad_input,

time: 581 us -> 493 us (0.85)
  waiting for transfers between devices: 252 us -> 177 us
  local copies, waits for them, and re-layouts: 42.8 us -> 92.6 us
  Pallas kernels: 148 us -> 99.7 us
  starting transfers between devices: 104 us -> 88.7 us
    ppermute x33 -> x21, starting transfers between devices: 77.6 us -> 28.6 us  [group(): return lax.ppermute(value, 'dp', [(i, i ^ mask) for i in range(self.dp)])]
    pallas_call x66 -> x59, Pallas kernels: 124 us -> 77.2 us  [run(): pl.pallas_call(body, in_specs=specs + [pl.BlockSpec(memory_space=pl.ANY)]...]
    unnamed x300 -> x330, local copies, waits for them, and re-layouts: 36.1 us -> 72.2 us
    ppermute x33 -> x21, waiting for transfers between devices: 110 us -> 77.6 us  [group(): return lax.ppermute(value, 'dp', [(i, i ^ mask) for i in range(self.dp)])]
    ppermute x20, waiting for transfers between devices: 109 us -> 77.7 us  [chip(): lax.ppermute(value, 'tensor', [(i, i ^ 2 * k) for i in range(self.tensor)])]
    ppermute x29 -> x113, starting transfers between devices: 4.42 us -> 31.2 us  [core(): lax.ppermute(value, 'tensor', [(i, i ^ 1) for i in range(self.tensor)])]
    ppermute x29 -> x113, waiting for transfers between devices: 22.8 us -> 12.6 us  [core(): lax.ppermute(value, 'tensor', [(i, i ^ 1) for i in range(self.tensor)])]
    slice x0 -> x30, local copies, waits for them, and re-layouts: none -> 9.67 us  [the longest x28 9.07 us: mate(): return [self.core(value[i * rows:(i + 1) * rows]) for i in range(pieces)]]
  transfers between devices with their start and end apart: 86 -> 161, of which waited for: 48 -> 68; matrix products, arithmetic and copies ran while one was open for 2% -> 6% of each run, Pallas kernels for 13% -> 18%
where the time goes in v3:
time: 493 us; the launch traced here: 484 us
  waiting for transfers between devices  177 us (36%)
  Pallas kernels  99.7 us (20%)
  local copies, waits for them, and re-layouts  92.6 us (19%)
  starting transfers between devices  88.7 us (18%)
  between operations  17.2 us (3%)
  other arithmetic  8.88 us (2%)
    ppermute x20, waiting for transfers between devices, chip(): lax.ppermute(value, 'tensor', [(i, i ^ 2 * k) for i in range(self.tensor)])  77.7 us
    ppermute x21, waiting for transfers between devices, group(): return lax.ppermute(value, 'dp', [(i, i ^ mask) for i in range(self.dp)])  77.6 us
    pallas_call x59, Pallas kernels, run(): pl.pallas_call(body, in_specs=specs + [pl.BlockSpec(memory_space=pl.ANY)]...  77.2 us
    unnamed x330, local copies, waits for them, and re-layouts  72.2 us
    ppermute x113, starting transfers between devices, core(): lax.ppermute(value, 'tensor', [(i, i ^ 1) for i in range(self.tensor)])  31.2 us
    ppermute x21, starting transfers between devices, group(): return lax.ppermute(value, 'dp', [(i, i ^ mask) for i in range(self.dp)])  28.6 us
    ppermute x20, starting transfers between devices, chip(): lax.ppermute(value, 'tensor', [(i, i ^ 2 * k) for i in range(self.tensor)])  24.2 us
    pallas_call x1, Pallas kernels, attend_back(): pl.pallas_call(functools.partial(attend_back_kernel, rows), grid=(heads,)...  13.8 us
  transfers between devices with their start and end apart: 161, of which 68 were waited for; matrix products, arithmetic and copies ran while one was open for 6% of the time, Pallas kernels for 18%

profile of v3, /device:TPU:0, one launch (start us, length us, event | category | flops | bytes accessed | tf_op | source)
XLA Modules:
  0.0 483.8 jit_solution(3656466591644832375)
XLA Ops:
  10.9 2.9 collective-permute-start.8
  20.8 5.2 %collective-permute-done.8.refs_0_ = bf16[256,1024]{1,0:T(8,128)(2,1)S(1)} collective-permute-done((bf16[256,1024]{1,0:T(8,128)(2,1)S(1)}, bf16[256,1024]{1,0:T(8,128)(2,1)S(1)}, u32[]{:S(2)}, u32[]{:S(2)}) %collective-permute-start.8) | collective-permute-done | bytes 524320 | tf_op jit(solution)/shard_map/ppermute | solution.py:946
  35.3 7.0 %collective-permute-done.18.refs_3_ = bf16[256,1024]{1,0:T(8,128)(2,1)S(1)} collective-permute-done((bf16[256,1024]{1,0:T(8,128)(2,1)S(1)}, bf16[256,1024]{1,0:T(8,128)(2,1)S(1)}, u32[]{:S(2)}, u32[]{:S(2)}) %collective-permute-start.18) | collective-permute-done | bytes 524320 | tf_op jit(solution)/shard_map/ppermute | solution.py:946
  69.8 8.6 %attend.1 = (bf16[1024,256]{1,0:T(8,128)(2,1)S(1)}, bf16[2,1024,1024]{2,1,0:T(8,128)(2,1)S(1)}) custom-call(s32[1]{0:T(128)} %bitcast.1.who_ref.refs_0_, s32[1]{0:T(128)S(6)} %copy.32.len_ref.refs_1_, bf16[3,1024,256]{2,1,0:T(8,128)(2,1)S(1)} %copy-done.21, bf16[3,1024,256]{2,1,0:T(8,128)(2,1)S(1)} %copy-done.21, bf16[3,1024,256]{2,1,0:T(8,128)(2,1)S(1)} %copy-done.21, ...), custom_call_target="tpu_custom_call" | custom-call | flops 25769803776 | bytes 1048576 | tf_op jit(solution)/shard_map/attend/pallas_call | solution.py:102
  89.3 8.3 %collective-permute-done.35.refs_7_ = bf16[256,1024]{1,0:T(8,128)(2,1)S(1)} collective-permute-done((bf16[256,1024]{1,0:T(8,128)(2,1)S(1)}, bf16[256,1024]{1,0:T(8,128)(2,1)S(1)}, u32[]{:S(2)}, u32[]{:S(2)}) %collective-permute-start.35) | collective-permute-done | bytes 524320 | tf_op jit(solution)/shard_map/ppermute | solution.py:946
  142.1 7.8 %collective-permute-done.60.refs_0_.refs_2_ = bf16[256,1024]{1,0:T(8,128)(2,1)S(1)} collective-permute-done((bf16[256,1024]{1,0:T(8,128)(2,1)S(1)}, bf16[256,1024]{1,0:T(8,128)(2,1)S(1)}, u32[]{:S(2)}, u32[]{:S(2)}) %collective-permute-start.60) | collective-permute-done | bytes 524320 | tf_op jit(solution)/shard_map/ppermute | solution.py:946
  166.5 10.4 %collective-permute-done.71.refs_6_ = bf16[256,1024]{1,0:T(8,128)(2,1)} collective-permute-done((bf16[256,1024]{1,0:T(8,128)(2,1)S(1)}, bf16[256,1024]{1,0:T(8,128)(2,1)}, u32[]{:S(2)}, u32[]{:S(2)}) %collective-permute-start.71) | collective-permute-done | bytes 524320 | tf_op jit(solution)/shard_map/ppermute | solution.py:946
  192.1 2.8 collective-permute-done.69.refs_6_
  195.0 2.9 ln_last.3
  205.2 4.5 ffn_two_w.1.refs_9_
  224.3 7.7 %collective-permute-done.93.refs_11_.refs_13_ = bf16[16,1024]{1,0:T(8,128)(2,1)S(1)} collective-permute-done((bf16[16,1024]{1,0:T(8,128)(2,1)S(1)}, bf16[16,1024]{1,0:T(8,128)(2,1)S(1)}, u32[]{:S(2)}, u32[]{:S(2)}) %collective-permute-start.93) | collective-permute-done | bytes 32800 | tf_op jit(solution)/shard_map/ppermute | solution.py:987
  235.9 3.7 collective-permute-done.95
  245.3 3.2 collective-permute-done.97
  250.6 3.8 collective-permute-done.98
  258.3 3.7 conv_din.1
  266.4 12.8 %collective-permute-done.103.refs_0_.refs_2_ = bf16[256,1024]{1,0:T(8,128)(2,1)S(1)} collective-permute-done((bf16[256,1024]{1,0:T(8,128)(2,1)S(1)}, bf16[256,1024]{1,0:T(8,128)(2,1)S(1)}, u32[]{:S(2)}, u32[]{:S(2)}) %collective-permute-start.103) | collective-permute-done | bytes 524320 | tf_op jit(solution)/shard_map/ppermute | solution.py:946
  282.4 13.8 %attend_back.1 = (bf16[3,1024,256]{2,1,0:T(8,128)(2,1)S(1)}, f32[2,128,512]{2,1,0:T(8,128)S(1)}, f32[2,8,128]{2,1,0:T(8,128)S(1)}) custom-call(s32[1]{0:T(128)} %bitcast.1.who_ref.refs_0_, bf16[3,1024,256]{2,1,0:T(8,128)(2,1)S(1)} %copy-done.22, bf16[3,1024,256]{2,1,0:T(8,128)(2,1)S(1)} %copy-done.22, bf16[3,1024,256]{2,1,0:T(8,128)(2,1)S(1)} %copy-done.22, ...), custom_call_target="tpu_custom_call" | custom-call | flops 40265318400 | bytes 1048576 | tf_op jit(solution)/shard_map/attend_back/pallas_call | solution.py:183
  303.1 4.0 attn_w.1.refs_5_
  309.9 13.7 %collective-permute-done.121.refs_4_ = bf16[256,1024]{1,0:T(8,128)(2,1)S(1)} collective-permute-done((bf16[256,1024]{1,0:T(8,128)(2,1)S(1)}, bf16[256,1024]{1,0:T(8,128)(2,1)S(1)}, u32[]{:S(2)}, u32[]{:S(2)}) %collective-permute-start.121) | collective-permute-done | bytes 524320 | tf_op jit(solution)/shard_map/ppermute | solution.py:946
  375.2 3.0 back_ffn_one.1
  390.7 29.3 %collective-permute-done.142 = f32[136,128]{1,0:T(8,128)S(1)} collective-permute-done((f32[136,128]{1,0:T(8,128)S(1)}, f32[136,128]{1,0:T(8,128)S(1)}, u32[]{:S(2)}, u32[]{:S(2)}) %collective-permute-start.142) | collective-permute-done | bytes 69664 | tf_op jit(solution)/shard_map/ppermute | solution.py:949
  428.7 17.0 %collective-permute-done.143 = f32[136,128]{1,0:T(8,128)S(1)} collective-permute-done((f32[136,128]{1,0:T(8,128)S(1)}, f32[136,128]{1,0:T(8,128)S(1)}, u32[]{:S(2)}, u32[]{:S(2)}) %collective-permute-start.143) | collective-permute-done | bytes 69664 | tf_op jit(solution)/shard_map/ppermute | solution.py:949
  454.3 9.5 %collective-permute-done.144 = f32[136,128]{1,0:T(8,128)S(1)} collective-permute-done((f32[136,128]{1,0:T(8,128)S(1)}, f32[136,128]{1,0:T(8,128)S(1)}, u32[]{:S(2)}, u32[]{:S(2)}) %collective-permute-start.144) | collective-permute-done | bytes 69664 | tf_op jit(solution)/shard_map/ppermute | solution.py:949
  469.4 2.8 collective-permute-done.155.refs_5_
  (775 shorter events, 278.0 us)
Async XLA Ops:
  7.2 99.7 %all-gather.2.cloned.1.call-start = ((), (), s32[]{:S(2)}) async-start(), calls=%async_computation.2 | async-start | bytes 1769472 | tf_op jit(solution)/shard_map/all_gather | solution.py:1135
  10.9 15.1 %collective-permute-start.8 = (bf16[256,1024]{1,0:T(8,128)(2,1)S(1)}, bf16[256,1024]{1,0:T(8,128)(2,1)S(1)}, u32[]{:S(2)}, u32[]{:S(2)}) collective-permute-start(bf16[256,1024]{1,0:T(8,128)(2,1)S(1)} %get-tuple-element.146), channel_id=1, source_target_pairs={{0,2},{1,3},{2,0},{3,1},{4,6},{5,7},{6,4},{7,5},{8,10},{9,11},{10,... | collective-permute-start | bytes 1572872 | tf_op jit(solution)/shard_map/ppermute | solution.py:946
  34.1 20.4 %collective-permute-start.17 = (bf16[256,1024]{1,0:T(8,128)(2,1)S(1)}, bf16[256,1024]{1,0:T(8,128)(2,1)S(1)}, u32[]{:S(2)}, u32[]{:S(2)}) collective-permute-start(bf16[256,1024]{1,0:T(8,128)(2,1)S(1)} %ffn_one_sum.3.refs_2_), channel_id=1, source_target_pairs={{0,2},{1,3},{2,0},{3,1},{4,6},{5,7},{6,4},{7,5},{8,10},{9,11},{10,... | collective-permute-start | bytes 1572872 | tf_op jit(solution)/shard_map/ppermute | solution.py:946
  61.8 309.7 %reduce-scatter.3.cloned.1.call-start = ((), (), s32[]{:S(2)}) async-start(), calls=%async_computation.3 | async-start | bytes 4718592 | tf_op jit(solution)/shard_map/reduce_scatter | solution.py:952
  88.1 17.1 %collective-permute-start.41 = (f32[8,256]{1,0:T(8,128)S(1)}, f32[8,256]{1,0:T(8,128)S(1)}, u32[]{:S(2)}, u32[]{:S(2)}) collective-permute-start(f32[8,256]{1,0:T(8,128)S(1)} %pad_maximum_fusion.4), channel_id=1, source_target_pairs={{0,2},{1,3},{2,0},{3,1},{4,6},{5,7},{6,4},{7,5},{8,10},{9,11},{10,... | collective-permute-start | bytes 24584 | tf_op jit(solution)/shard_map/ppermute | solution.py:946
  153.0 23.9 %collective-permute-start.71 = (bf16[256,1024]{1,0:T(8,128)(2,1)S(1)}, bf16[256,1024]{1,0:T(8,128)(2,1)}, u32[]{:S(2)}, u32[]{:S(2)}) collective-permute-start(bf16[256,1024]{1,0:T(8,128)(2,1)S(1)} %ffn_two_sum.2.refs_2_.refs_5_), channel_id=1, source_target_pairs={{0,2},{1,3},{2,0},{3,1},{4,6},{5,7},{6,4},{7,5},{8,10},{9,11},{10,... | collective-permute-start | bytes 1572872 | tf_op jit(solution)/shard_map/ppermute | solution.py:946
  224.1 229.1 %reduce-scatter.5.cloned.1.call-start = ((), (), s32[]{:S(2)}) async-start(), calls=%async_computation.4 | async-start | bytes 5898240 | tf_op jit(solution)/shard_map/reduce_scatter | solution.py:952
  332.6 16.5 %collective-permute-start.120 = (bf16[256,1024]{1,0:T(8,128)(2,1)S(1)}, bf16[256,1024]{1,0:T(8,128)(2,1)}, u32[]{:S(2)}, u32[]{:S(2)}) collective-permute-start(bf16[256,1024]{1,0:T(8,128)(2,1)S(1)} %dqkv_sum.3.refs_13_.refs_3_), channel_id=1, source_target_pairs={{0,2},{1,3},{2,0},{3,1},{4,6},{5,7},{6,4},{7,5},{8,10},{9,11},{10,... | collective-permute-start | bytes 1572872 | tf_op jit(solution)/shard_map/ppermute | solution.py:946
  355.0 18.9 %collective-permute-start.138 = (bf16[256,1024]{1,0:T(8,128)(2,1)S(1)}, bf16[256,1024]{1,0:T(8,128)(2,1)}, u32[]{:S(2)}, u32[]{:S(2)}) collective-permute-start(bf16[256,1024]{1,0:T(8,128)(2,1)S(1)} %ffn_one_grad_sum.1.refs_5_), channel_id=1, source_target_pairs={{0,2},{1,3},{2,0},{3,1},{4,6},{5,7},{6,4},{7,5},{8,10},{9,11},{10,... | collective-permute-start | bytes 1572872 | tf_op jit(solution)/shard_map/ppermute | solution.py:946
  380.0 40.1 %collective-permute-start.146 = (bf16[512,512]{1,0:T(8,128)(2,1)}, bf16[512,512]{1,0:T(8,128)(2,1)}, u32[]{:S(2)}, u32[]{:S(2)}) collective-permute-start(bf16[512,512]{1,0:T(8,128)(2,1)} %copy-done.91), channel_id=1, source_target_pairs={{0,8},{4,12},{8,0},{12,4},{16,24},{20,28},{24,16},{28,20},{1,9},{5... | collective-permute-start | bytes 1572872 | tf_op jit(solution)/shard_map/ppermute | solution.py:949
  381.0 39.1 %collective-permute-start.145 = (bf16[512,512]{1,0:T(8,128)(2,1)}, bf16[512,512]{1,0:T(8,128)(2,1)}, u32[]{:S(2)}, u32[]{:S(2)}) collective-permute-start(bf16[512,512]{1,0:T(8,128)(2,1)} %copy-done.90), channel_id=1, source_target_pairs={{0,4},{4,0},{8,12},{12,8},{16,20},{20,16},{24,28},{28,24},{1,5},{5... | collective-permute-start | bytes 1572872 | tf_op jit(solution)/shard_map/ppermute | solution.py:949
  382.5 43.8 %collective-permute-start.152 = (bf16[512,512]{1,0:T(8,128)(2,1)S(1)}, bf16[512,512]{1,0:T(8,128)(2,1)S(1)}, u32[]{:S(2)}, u32[]{:S(2)}) collective-permute-start(bf16[512,512]{1,0:T(8,128)(2,1)S(1)} %get-tuple-element.240.refs_1_.refs_9_), channel_id=1, source_target_pairs={{0,8},{4,12},{8,0},{12,4},{16,24},{20,28},{24,16},{28,20},{1,9},{5... | collective-permute-start | bytes 1572872 | tf_op jit(solution)/shard_map/ppermute | solution.py:949
  383.5 42.8 %collective-permute-start.151 = (bf16[512,512]{1,0:T(8,128)(2,1)}, bf16[512,512]{1,0:T(8,128)(2,1)S(1)}, u32[]{:S(2)}, u32[]{:S(2)}) collective-permute-start(bf16[512,512]{1,0:T(8,128)(2,1)} %copy-done.89), channel_id=1, source_target_pairs={{0,4},{4,0},{8,12},{12,8},{16,20},{20,16},{24,28},{28,24},{1,5},{5... | collective-permute-start | bytes 1572872 | tf_op jit(solution)/shard_map/ppermute | solution.py:949
  389.2 30.9 %collective-permute-start.142 = (f32[136,128]{1,0:T(8,128)S(1)}, f32[136,128]{1,0:T(8,128)S(1)}, u32[]{:S(2)}, u32[]{:S(2)}) collective-permute-start(f32[136,128]{1,0:T(8,128)S(1)} %pad_maximum_fusion.1), channel_id=1, source_target_pairs={{0,4},{4,0},{8,12},{12,8},{16,20},{20,16},{24,28},{28,24},{1,5},{5... | collective-permute-start | bytes 208904 | tf_op jit(solution)/shard_map/ppermute | solution.py:949
  423.6 23.3 %collective-permute-start.147 = (bf16[256,512]{1,0:T(8,128)(2,1)S(1)}, bf16[256,512]{1,0:T(8,128)(2,1)S(1)}, u32[]{:S(2)}, u32[]{:S(2)}) collective-permute-start(bf16[256,512]{1,0:T(8,128)(2,1)S(1)} %get-tuple-element.253), channel_id=1, source_target_pairs={{0,8},{4,12},{8,0},{12,4},{16,24},{20,28},{24,16},{28,20},{1,9},{5... | collective-permute-start | bytes 786440 | tf_op jit(solution)/shard_map/ppermute | solution.py:949
  423.7 23.2 %collective-permute-start.148 = (bf16[256,512]{1,0:T(8,128)(2,1)S(1)}, bf16[256,512]{1,0:T(8,128)(2,1)S(1)}, u32[]{:S(2)}, u32[]{:S(2)}) collective-permute-start(bf16[256,512]{1,0:T(8,128)(2,1)S(1)} %get-tuple-element.255), channel_id=1, source_target_pairs={{0,4},{4,0},{8,12},{12,8},{16,20},{20,16},{24,28},{28,24},{1,5},{5... | collective-permute-start | bytes 786440 | tf_op jit(solution)/shard_map/ppermute | solution.py:949
  426.6 23.5 %collective-permute-start.153 = (bf16[256,512]{1,0:T(8,128)(2,1)S(1)}, bf16[256,512]{1,0:T(8,128)(2,1)S(1)}, u32[]{:S(2)}, u32[]{:S(2)}) collective-permute-start(bf16[256,512]{1,0:T(8,128)(2,1)S(1)} %get-tuple-element.263), channel_id=1, source_target_pairs={{0,8},{4,12},{8,0},{12,4},{16,24},{20,28},{24,16},{28,20},{1,9},{5... | collective-permute-start | bytes 786440 | tf_op jit(solution)/shard_map/ppermute | solution.py:949
  428.6 21.5 %collective-permute-start.154 = (bf16[256,512]{1,0:T(8,128)(2,1)S(1)}, bf16[256,512]{1,0:T(8,128)(2,1)S(1)}, u32[]{:S(2)}, u32[]{:S(2)}) collective-permute-start(bf16[256,512]{1,0:T(8,128)(2,1)S(1)} %get-tuple-element.265), channel_id=1, source_target_pairs={{0,4},{4,0},{8,12},{12,8},{16,20},{20,16},{24,28},{28,24},{1,5},{5... | collective-permute-start | bytes 786440 | tf_op jit(solution)/shard_map/ppermute | solution.py:949
  428.6 17.2 %collective-permute-start.143 = (f32[136,128]{1,0:T(8,128)S(1)}, f32[136,128]{1,0:T(8,128)S(1)}, u32[]{:S(2)}, u32[]{:S(2)}) collective-permute-start(f32[136,128]{1,0:T(8,128)S(1)} %fusion.3.refs_4_), channel_id=1, source_target_pairs={{0,8},{4,12},{8,0},{12,4},{16,24},{20,28},{24,16},{28,20},{1,9},{5... | collective-permute-start | bytes 208904 | tf_op jit(solution)/shard_map/ppermute | solution.py:949
  445.8 18.0 %collective-permute-start.144 = (f32[136,128]{1,0:T(8,128)S(1)}, f32[136,128]{1,0:T(8,128)S(1)}, u32[]{:S(2)}, u32[]{:S(2)}) collective-permute-start(f32[136,128]{1,0:T(8,128)S(1)} %add.108.refs_4_), channel_id=1, source_target_pairs={{0,16},{4,20},{8,24},{12,28},{16,0},{20,4},{24,8},{28,12},{1,17},{... | collective-permute-start | bytes 208904 | tf_op jit(solution)/shard_map/ppermute | solution.py:949
  447.0 21.2 %collective-permute-start.149 = (bf16[128,512]{1,0:T(8,128)(2,1)S(1)}, bf16[128,512]{1,0:T(8,128)(2,1)S(1)}, u32[]{:S(2)}, u32[]{:S(2)}) collective-permute-start(bf16[128,512]{1,0:T(8,128)(2,1)S(1)} %get-tuple-element.257), channel_id=1, source_target_pairs={{0,16},{4,20},{8,24},{12,28},{16,0},{20,4},{24,8},{28,12},{1,17},{... | collective-permute-start | bytes 393224 | tf_op jit(solution)/shard_map/ppermute | solution.py:949
  449.0 20.4 %collective-permute-start.150 = (bf16[128,512]{1,0:T(8,128)(2,1)S(1)}, bf16[128,512]{1,0:T(8,128)(2,1)S(1)}, u32[]{:S(2)}, u32[]{:S(2)}) collective-permute-start(bf16[128,512]{1,0:T(8,128)(2,1)S(1)} %get-tuple-element.259), channel_id=1, source_target_pairs={{0,16},{4,20},{8,24},{12,28},{16,0},{20,4},{24,8},{28,12},{1,17},{... | collective-permute-start | bytes 393224 | tf_op jit(solution)/shard_map/ppermute | solution.py:949
  450.2 22.1 %collective-permute-start.155 = (bf16[128,512]{1,0:T(8,128)(2,1)S(1)}, bf16[128,512]{1,0:T(8,128)(2,1)S(1)}, u32[]{:S(2)}, u32[]{:S(2)}) collective-permute-start(bf16[128,512]{1,0:T(8,128)(2,1)S(1)} %get-tuple-element.267), channel_id=1, source_target_pairs={{0,16},{4,20},{8,24},{12,28},{16,0},{20,4},{24,8},{28,12},{1,17},{... | collective-permute-start | bytes 393224 | tf_op jit(solution)/shard_map/ppermute | solution.py:949
  452.1 22.1 %collective-permute-start.156 = (bf16[128,512]{1,0:T(8,128)(2,1)S(1)}, bf16[128,512]{1,0:T(8,128)(2,1)S(1)}, u32[]{:S(2)}, u32[]{:S(2)}) collective-permute-start(bf16[128,512]{1,0:T(8,128)(2,1)S(1)} %get-tuple-element.269), channel_id=1, source_target_pairs={{0,16},{4,20},{8,24},{12,28},{16,0},{20,4},{24,8},{28,12},{1,17},{... | collective-permute-start | bytes 393224 | tf_op jit(solution)/shard_map/ppermute | solution.py:949
  (302 other events, 1682.9 us)
Sparse Core Ops, SparseCore 0:
  61.9 44.8 all-gather.1
  224.2 94.6 reduce-scatter.2
  322.9 117.4 reduce-scatter.4

commit v4 on v3

--- a/solution.py
+++ b/solution.py
@@ -46,17 +46,22 @@
 
 
 def window_table(rel_table):
-    near,far=SUB-LEFT,SUB+RIGHT
     width=rel_table.shape[1]
-    ext=jnp.concatenate([
-        jnp.broadcast_to(rel_table[:1],(near,width)),
-        rel_table,
-        jnp.broadcast_to(rel_table[REL-1:],(WIN-far,width)),
-        jnp.broadcast_to(rel_table[:1],(WRAP-WIN-1,width)),
-    ])
-    hi=ext.astype(jnp.bfloat16)
-    lo=(ext-hi.astype(jnp.float32)).astype(jnp.bfloat16)
-    return hi,lo
+    def kernel(table_ref, hi_ref, lo_ref):
+        pick=spots(0)
+        table=table_ref[...]
+        hi=table.astype(jnp.bfloat16)
+        lo=(table-hi.astype(jnp.float32)).astype(jnp.bfloat16)
+        hi_ref[...]=nn(pick,hi).astype(jnp.bfloat16)
+        lo_ref[...]=nn(pick,lo).astype(jnp.bfloat16)
+    return run(kernel,[((WRAP,width),jnp.bfloat16)]*2,[rel_table],(),"window_table")
+
+def spots(axis):
+    shape=(WRAP,128) if axis==0 else (128,WRAP)
+    u=lax.broadcasted_iota(jnp.int32,shape,axis)
+    row=lax.broadcasted_iota(jnp.int32,shape,1-axis)
+    dist=jnp.where(u<=WIN,jnp.clip(u-SUB,-LEFT,RIGHT),-LEFT)+LEFT
+    return (dist==row).astype(jnp.bfloat16)
 
 def order_in(dst, src, who, rows):
     for j in range(SLOT//rows):
@@ -93,25 +98,23 @@
             j=(base+part)//rows; inner=(base+part)%rows
             o_ref[pl.ds(pl.multiple_of((j^who)*rows+inner,n),n),:]=out[part:part+n]
 
-def attend(qkv, who, length, rel_table, rows):
+def attend(qkv, who, length, table, rows):
     heads=qkv.shape[2]//HEAD
-    hi,lo=window_table(rel_table)
+    hi,lo=table
     spec=lambda m: pl.BlockSpec((1,SLOT,HEAD),lambda h,m=m:(m,0,h))
-    smem=pl.BlockSpec(memory_space=pltpu.SMEM)
     tab=pl.BlockSpec((WRAP,HEAD),lambda h:(0,0))
-    return pl.pallas_call(
+    return run(
         functools.partial(attend_kernel,rows),
-        grid=(heads,),
-        in_specs=[smem,smem,spec(0),spec(1),spec(2),tab,tab],
+        [((SLOT,heads*HEAD),jnp.bfloat16),((heads,SLOT,SLOT),jnp.bfloat16)],
+        [who,length,qkv,qkv,qkv,hi,lo],
+        (),"attend",grid=(heads,),
+        in_specs=[SMEM_SPEC,SMEM_SPEC,spec(0),spec(1),spec(2),tab,tab],
         out_specs=[pl.BlockSpec((SLOT,HEAD),lambda h:(0,h)),pl.BlockSpec((1,SLOT,SLOT),lambda h:(h,0,0))],
-        out_shape=[jax.ShapeDtypeStruct((SLOT,heads*HEAD),jnp.bfloat16),jax.ShapeDtypeStruct((heads,SLOT,SLOT),jnp.bfloat16)],
-        scratch_shapes=[pltpu.VMEM((SLOT,HEAD),jnp.bfloat16)]*3,
-        compiler_params=pltpu.CompilerParams(vmem_limit_bytes=28<<20),
-        cost_estimate=pl.CostEstimate(flops=int(heads*32*SLOT*SLOT*HEAD*WORK),bytes_accessed=1<<20,transcendentals=0),
-        name="attend",
-    )(who,length,qkv,qkv,qkv,hi,lo)
-
-def attend_back_kernel(rows, who_ref, q_ref, k_ref, v_ref, g_ref, p_ref, hi_ref, lo_ref, d_ref, dt_ref, ds_ref, qs, ks, vs, gs, dkt, dvt):
+        scratch=[pltpu.VMEM((SLOT,HEAD),jnp.bfloat16)]*3,
+        room=28,work=heads*32*SLOT*SLOT*HEAD,
+    )
+
+def attend_back_kernel(rows, heads, who_ref, q_ref, k_ref, v_ref, g_ref, p_ref, hi_ref, lo_ref, d_ref, dt_ref, qs, ks, vs, gs, dkt, dvt):
     who=who_ref[0]
     for dst,src in ((qs,q_ref.at[0]),(ks,k_ref.at[0]),(vs,v_ref.at[0]),(gs,g_ref)):
         order_in(dst,src,who,rows)
@@ -165,41 +168,43 @@
             n=min(rows,BLK)
             j=(base+part)//rows; inner=(base+part)%rows
             d_ref[0,pl.ds(pl.multiple_of((j^who)*rows+inner,n),n),:]=dq[part:part+n]
-    dt_ref[0]=table_acc*factor
-    ds_ref[0]=jnp.concatenate([left_acc,right_acc,jnp.zeros((6,HEAD),jnp.float32)],axis=0)*factor
+    spread=table_acc*factor
+    upper=spread.astype(jnp.bfloat16)
+    lower=(spread-upper.astype(jnp.float32)).astype(jnp.bfloat16)
+    pick=spots(1)
+    gathered=nt(pick,upper)+nt(pick,lower)
+    row=lax.broadcasted_iota(jnp.int32,(128,1),0)
+    gathered=gathered+jnp.where(row==0,left_acc*factor,0.0)+jnp.where(row==LEFT+RIGHT,right_acc*factor,0.0)
+    @pl.when(pl.program_id(0)==0)
+    def _():
+        dt_ref[...]=gathered
+    @pl.when(pl.program_id(0)>0)
+    def _():
+        dt_ref[...]+=gathered
     for j in range(SLOT//rows):
         sl=pl.ds(pl.multiple_of((j^who)*rows,rows),rows)
         d_ref[1,sl,:]=(jnp.transpose(dkt[:,j*rows:(j+1)*rows])*factor).astype(jnp.bfloat16)
         d_ref[2,sl,:]=jnp.transpose(dvt[:,j*rows:(j+1)*rows]).astype(jnp.bfloat16)
 
-def attend_back(qkv, grad, probs, who, rel_table, rows):
+def attend_back(qkv, grad, probs, who, table, rows):
     heads=qkv.shape[2]//HEAD
-    hi,lo=window_table(rel_table)
+    hi,lo=table
     spec=lambda m: pl.BlockSpec((1,SLOT,HEAD),lambda h,m=m:(m,0,h))
-    smem=pl.BlockSpec(memory_space=pltpu.SMEM)
     tab=pl.BlockSpec((WRAP,HEAD),lambda h:(0,0))
-    out=pl.BlockSpec((3,SLOT,HEAD),lambda h:(0,0,h))
-    shape=jax.ShapeDtypeStruct((3,SLOT,heads*HEAD),jnp.bfloat16)
-    members,dt,ends=pl.pallas_call(
-        functools.partial(attend_back_kernel,rows),
-        grid=(heads,),
-        in_specs=[smem,spec(0),spec(1),spec(2),pl.BlockSpec((SLOT,HEAD),lambda h:(0,h)),pl.BlockSpec((1,SLOT,SLOT),lambda h:(h,0,0)),tab,tab],
-        out_specs=[out,pl.BlockSpec((1,HEAD,WRAP),lambda h:(h,0,0)),pl.BlockSpec((1,8,HEAD),lambda h:(h,0,0))],
-        out_shape=[shape,jax.ShapeDtypeStruct((heads,HEAD,WRAP),jnp.float32),jax.ShapeDtypeStruct((heads,8,HEAD),jnp.float32)],
-        scratch_shapes=[pltpu.VMEM((SLOT,HEAD),jnp.bfloat16)]*4+[pltpu.VMEM((HEAD,SLOT),jnp.float32)]*2,
-        compiler_params=pltpu.CompilerParams(vmem_limit_bytes=28<<20),
-        cost_estimate=pl.CostEstimate(flops=int(heads*50*SLOT*SLOT*HEAD*WORK),bytes_accessed=1<<20,transcendentals=0),
-        name="attend_back",
-    )(who,qkv,qkv,qkv,grad,probs,hi,lo)
-    wide=jnp.sum(dt,axis=0).T
-    ends=jnp.sum(ends,axis=0)
-    near=SUB-LEFT; far=SUB+RIGHT
-    left=jnp.sum(wide[:near+1],axis=0)+jnp.sum(wide[WIN+1:],axis=0)+ends[0]
-    right=jnp.sum(wide[far:WIN+1],axis=0)+ends[1]
-    return members,jnp.concatenate([left[None],wide[near+1:far],right[None]],axis=0)
-
-
-WORK = 3.0
+    return run(
+        functools.partial(attend_back_kernel,rows,heads),
+        [((3,SLOT,heads*HEAD),jnp.bfloat16),((128,HEAD),jnp.float32)],
+        [who,qkv,qkv,qkv,grad,probs,hi,lo],
+        (),"attend_back",grid=(heads,),
+        in_specs=[SMEM_SPEC,spec(0),spec(1),spec(2),pl.BlockSpec((SLOT,HEAD),lambda h:(0,h)),pl.BlockSpec((1,SLOT,SLOT),lambda h:(h,0,0)),tab,tab],
+        out_specs=[pl.BlockSpec((3,SLOT,HEAD),lambda h:(0,0,h)),pl.BlockSpec((128,HEAD),lambda h:(0,0))],
+        scratch=[pltpu.VMEM((SLOT,HEAD),jnp.bfloat16)]*4+[pltpu.VMEM((HEAD,SLOT),jnp.float32)]*2,
+        room=28,work=heads*50*SLOT*SLOT*HEAD,
+    )
+
+
+MARKS = {}
+PIECES = 4
 
 
 class Stack:
@@ -223,8 +228,11 @@
     aliases=None,
     room=24,
     work=1 << 20,
+    mark=False,
 ):
+    after = [MARKS[id(item)][1] if id(item) in MARKS else item for item in after]
     waits = len(after)
+    outs = list(outs) + [((8, 128), f32)] * mark
     sizes = [len(item) if isinstance(item, list) else 0 for item in ins]
 
     def body(*refs):
@@ -232,7 +240,10 @@
         for size in sizes:
             args.append(Stack(refs[at : at + size]) if size else refs[at])
             at += max(size, 1)
-        kernel(*args, *refs[at + waits :])
+        last = at + waits + len(outs) - mark
+        kernel(*args, *refs[at + waits : last], *refs[last + mark :])
+        if mark:
+            refs[last][...] = jnp.zeros((8, 128), f32)
 
     def full(shape):
         return pl.BlockSpec(tuple(shape), lambda i: (0,) * len(shape))
@@ -251,8 +262,11 @@
         specs += [spec] * max(size, 1)
         flat += item if size else [item]
     ins = flat
-    out_specs = list(out_specs) if out_specs is not None else [full(s) for s, _ in outs]
-    return pl.pallas_call(
+    if out_specs is None:
+        out_specs = [full(shape) for shape, _ in outs]
+    else:
+        out_specs = list(out_specs) + [pl.BlockSpec((8, 128), lambda i: (0, 0))] * mark
+    made = pl.pallas_call(
         body,
         in_specs=specs + [pl.BlockSpec(memory_space=pl.ANY)] * waits,
         out_specs=out_specs,
@@ -260,10 +274,15 @@
         scratch_shapes=list(scratch),
         input_output_aliases={start[i]: o for i, o in (aliases or {}).items()},
         compiler_params=pltpu.CompilerParams(vmem_limit_bytes=room << 20),
-        cost_estimate=pl.CostEstimate(flops=int(work * WORK), bytes_accessed=1 << 20, transcendentals=0),
+        cost_estimate=pl.CostEstimate(flops=0, bytes_accessed=0, transcendentals=0),
         name=name,
         grid=grid,
     )(*ins, *after)
+    if not mark:
+        return list(made)
+    for array in made[:-1]:
+        MARKS[id(array)] = (array, made[-1])
+    return list(made[:-1])
 
 
 SMEM_SPEC = pl.BlockSpec(memory_space=pltpu.SMEM)
@@ -283,6 +302,20 @@
 
 def wide(ref):
     return ref[...].astype(f32)
+
+
+def cut(shape):
+    return [((shape[0] // PIECES,) + tuple(shape[1:]), bf16)] * PIECES
+
+
+def put(refs, value):
+    rows = value.shape[0] // len(refs)
+    for i, ref in enumerate(refs):
+        ref[...] = value[i * rows : (i + 1) * rows].astype(bf16)
+
+
+def take(items, count):
+    return [items.pop(0) for _ in range(count)]
 
 
 def add_up(parts, name, after=()):
@@ -297,85 +330,143 @@
     return run(kernel, [(shape, bf16)], parts, after, name)[0]
 
 
-def norm_rows(resid, parts, factor, gain, name, after=(), keep=True, low=False, also=None):
+def total_of(refs):
+    total = wide(refs[0])
+    for ref in refs[1:]:
+        total = total + wide(ref)
+    return total
+
+
+def gain_row(ref, index):
+    return ref[index : index + 1, :]
+
+
+def put_edge(ref, who, value):
+    value = value.astype(f32)
+    ref[...] = jnp.where(who // 2 == 0, value[-MARGIN:], value[:MARGIN]).astype(bf16)
+
+
+def norm_rows(
+    resid, parts, factor, gains, index, name, after=(), keep=True, low=False, also=None, edge=None
+):
     shape = resid.shape
     count = len(parts)
-    ins = [resid, gain] + list(parts) + ([also] if also is not None else [])
-    outs = [(shape, bf16)] + [(shape, f32)] * keep + [(shape, bf16)] * low
-    outs = outs + ([(shape, bf16)] if also is not None else [])
+    extra = ([also] if also is not None else []) + ([edge] if edge is not None else [])
+    ins = [resid, gains] + list(parts) + extra
+    outs = [(shape, bf16)] + cut(shape) + [(shape, f32)] * keep + [(shape, bf16)] * low
+    outs = outs + [(shape, bf16)] * (also is not None)
+    outs = outs + [((MARGIN, shape[1]), bf16)] * (edge is not None)
 
     def kernel(resid_ref, gain_ref, *refs):
+        refs = list(refs)
+        part_refs = take(refs, count)
+        also_ref = take(refs, also is not None)
+        edge_ref = take(refs, edge is not None)
         rows = wide(resid_ref)
         if count:
-            total = wide(refs[0])
-            for ref in refs[1:count]:
-                total = total + wide(ref)
-            rows = rows + factor * total
-        out = list(refs[count + (also is not None) :])
-        out.pop(0)[...] = (moments(rows)[0] * gain_ref[...]).astype(bf16)
+            rows = rows + factor * total_of(part_refs)
+        normed = (moments(rows)[0] * gain_row(gain_ref, index)).astype(bf16)
+        refs.pop(0)[...] = normed
+        put(take(refs, PIECES), normed)
         if keep:
-            out.pop(0)[...] = rows
+            refs.pop(0)[...] = rows
         if low:
-            out.pop(0)[...] = rows.astype(bf16)
-        if also is not None:
-            out.pop(0)[...] = refs[count][...].astype(bf16)
-
-    return run(kernel, outs, ins, after, name)
-
-
-def norm_last(resid, parts, gain, upper, begin, length, name, full, after=()):
+            refs.pop(0)[...] = rows.astype(bf16)
+        if also_ref:
+            refs.pop(0)[...] = also_ref[0][...].astype(bf16)
+        if edge_ref:
+            put_edge(refs.pop(0), edge_ref[0][0], normed)
+
+    specs = [None] * (2 + count + (also is not None)) + [SMEM_SPEC] * (edge is not None)
+    made = run(kernel, outs, ins, after, name, in_specs=specs)
+    return [(made[0], made[1 : 1 + PIECES])] + made[1 + PIECES :]
+
+
+def norm_last(resid, parts, gains, upper, who, k, length, name, full, after=()):
     shape = resid.shape
     count = len(parts)
-    outs = [(shape, bf16)]
+    outs = [(shape, bf16)] + cut(shape)
     if full:
         outs = outs + [(shape, f32), (shape, f32), ((8, shape[1]), f32)]
 
-    def kernel(begin_ref, length_ref, resid_ref, gain_ref, upper_ref, *refs):
-        total = wide(refs[0])
-        for ref in refs[1:count]:
-            total = total + wide(ref)
-        rows = wide(resid_ref) + 0.5 * total
+    def kernel(who_ref, length_ref, resid_ref, gain_ref, upper_ref, *refs):
+        refs = list(refs)
+        rows = wide(resid_ref) + 0.5 * total_of(take(refs, count))
+        gain = gain_row(gain_ref, 4)
         normed, inverse = moments(rows)
-        place = lax.broadcasted_iota(jnp.int32, (shape[0], 1), 0) + begin_ref[0]
+        begin = (who_ref[0] ^ (2 * k)) * shape[0]
+        place = lax.broadcasted_iota(jnp.int32, (shape[0], 1), 0) + begin
         valid = (place < length_ref[0]).astype(f32)
         seen = wide(upper_ref) * valid
-        grad = back(seen * gain_ref[...], normed, inverse)
-        refs[count][...] = (0.5 * grad).astype(bf16)
+        grad = back(seen * gain, normed, inverse)
+        rounded = (0.5 * grad).astype(bf16)
+        refs.pop(0)[...] = rounded
+        put(take(refs, PIECES), rounded)
         if full:
-            refs[count + 1][...] = grad
-            refs[count + 2][...] = normed * gain_ref[...] * valid
-            refs[count + 3][...] = jnp.broadcast_to(
+            refs.pop(0)[...] = grad
+            refs.pop(0)[...] = normed * gain * valid
+            refs.pop(0)[...] = jnp.broadcast_to(
                 jnp.sum(seen * normed, axis=0, keepdims=True), (8, shape[1])
             )
 
-    ins = [begin, length, resid, gain, upper] + list(parts)
+    ins = [who, length, resid, gains, upper] + list(parts)
     specs = [SMEM_SPEC, SMEM_SPEC] + [None] * (3 + count)
-    return run(kernel, outs, ins, after, name, in_specs=specs)
-
-
-def norm_grad(rows_in, parts, gain, grad, name, after=(), factor=None, keep=True, sums=True):
+    made = run(kernel, outs, ins, after, name, in_specs=specs)
+    return [(made[0], made[1 : 1 + PIECES])] + made[1 + PIECES :]
+
+
+def norm_grad(
+    rows_in, parts, gains, index, grad, name, after=(), factor=None, keep=True, sums=True, edge=None
+):
     shape = rows_in.shape
     count = len(parts)
-    outs = [(shape, bf16)] * (factor is not None) + [(shape, f32)] * keep
-    outs = outs + [((8, shape[1]), f32)] * sums
+    outs = ([(shape, bf16)] + cut(shape)) if factor is not None else []
+    outs = outs + [(shape, f32)] * keep + [((8, shape[1]), f32)] * sums
+    outs = outs + [((MARGIN, shape[1]), bf16)] * (edge is not None)
 
     def kernel(rows_ref, gain_ref, grad_ref, *refs):
-        total = wide(refs[0])
-        for ref in refs[1:count]:
-            total = total + wide(ref)
+        refs = list(refs)
+        total = total_of(take(refs, count))
+        edge_ref = take(refs, edge is not None)
         normed, inverse = moments(wide(rows_ref))
-        result = wide(grad_ref) + back(total * gain_ref[...], normed, inverse)
-        out = list(refs[count:])
+        result = wide(grad_ref) + back(total * gain_row(gain_ref, index), normed, inverse)
         if factor is not None:
-            out.pop(0)[...] = (factor * result).astype(bf16)
+            rounded = (factor * result).astype(bf16)
+            refs.pop(0)[...] = rounded
+            put(take(refs, PIECES), rounded)
         if keep:
-            out.pop(0)[...] = result
+            refs.pop(0)[...] = result
         if sums:
-            out.pop(0)[...] = jnp.broadcast_to(
+            refs.pop(0)[...] = jnp.broadcast_to(
                 jnp.sum(total * normed, axis=0, keepdims=True), (8, shape[1])
             )
-
-    return run(kernel, outs, [rows_in, gain, grad] + list(parts), after, name)
+        if edge_ref:
+            put_edge(refs.pop(0), edge_ref[0][0], rounded)
+
+    ins = [rows_in, gains, grad] + list(parts) + ([edge] if edge is not None else [])
+    specs = [None] * (3 + count) + [SMEM_SPEC] * (edge is not None)
+    made = run(kernel, outs, ins, after, name, in_specs=specs)
+    if factor is None:
+        return made
+    return [(made[0], made[1 : 1 + PIECES])] + made[1 + PIECES :]
+
+
+def add_stats(value, others, channels, name, after=()):
+    cols = value.shape[1]
+    ny = cols // channels if channels else 0
+
+    def kernel(*refs):
+        total = refs[0][...]
+        for k, ref in enumerate(refs[1:-1], 1):
+            if channels:
+                total = total + jnp.concatenate(
+                    [ref[:, (r ^ k) * channels : ((r ^ k) + 1) * channels] for r in range(ny)], axis=1
+                )
+            else:
+                total = total + ref[...]
+        refs[-1][...] = total
+
+    return run(kernel, [(value.shape, f32)], [value] + list(others), after, name)[0]
 
 
 def tile_of(total, most):
@@ -388,7 +479,9 @@
     tile = tile_of(hidden, 1024)
     steps = hidden // tile
 
-    def kernel(own_ref, mate_ref, in_ref, out_ref, p_own, p_mate, pre, hid, seen, acc=None):
+    def kernel(own_ref, mate_ref, in_ref, out_ref, p_own, *rest):
+        *p_mate, pre, hid, seen = rest[: PIECES + 3]
+        acc = rest[PIECES + 3] if steps > 1 else None
         step = pl.program_id(0)
         both = jnp.concatenate([own_ref[...], mate_ref[...]], axis=0)
         seen[...] = both
@@ -399,7 +492,7 @@
         part = nt(act, out_ref[0])
         if steps == 1:
             p_own[...] = part[:rows].astype(bf16)
-            p_mate[...] = part[rows:].astype(bf16)
+            put(p_mate, part[rows:])
             return
 
         @pl.when(step == 0)
@@ -413,20 +506,21 @@
         @pl.when(step == steps - 1)
         def _():
             p_own[...] = acc[:rows].astype(bf16)
-            p_mate[...] = acc[rows:].astype(bf16)
+            put(p_mate, acc[rows:])
 
     fixed = pl.BlockSpec((rows, width), lambda i: (0, 0))
+    quarter = [pl.BlockSpec((rows // PIECES, width), lambda i: (0, 0))] * PIECES
     cols = pl.BlockSpec((2 * rows, tile), lambda i: (0, i))
     weight = [pl.BlockSpec((1, width, tile), lambda i, m=m: (m, 0, i)) for m in range(2)]
     return run(
         kernel,
-        [((rows, width), bf16)] * 2 + [((2 * rows, hidden), bf16)] * 2 + [((2 * rows, width), bf16)],
+        [((rows, width), bf16)] + cut((rows, width)) + [((2 * rows, hidden), bf16)] * 2 + [((2 * rows, width), bf16)],
         [own, mate, weights, weights],
         after,
         name,
         grid=(steps,),
         in_specs=[fixed, fixed] + weight,
-        out_specs=[fixed, fixed, cols, cols, pl.BlockSpec((2 * rows, width), lambda i: (0, 0))],
+        out_specs=[fixed] + quarter + [cols, cols, pl.BlockSpec((2 * rows, width), lambda i: (0, 0))],
         scratch=[pltpu.VMEM((2 * rows, width), f32)] if steps > 1 else (),
         room=28,
         work=8 * rows * width * hidden,
@@ -439,7 +533,9 @@
     tile = tile_of(hidden, 1024)
     steps = hidden // tile
 
-    def kernel(own_ref, mate_ref, pre_ref, in_ref, out_ref, p_own, p_mate, down, seen, acc=None):
+    def kernel(own_ref, mate_ref, pre_ref, in_ref, out_ref, p_own, *rest):
+        *p_mate, down, seen = rest[: PIECES + 2]
+        acc = rest[PIECES + 2] if steps > 1 else None
         step = pl.program_id(0)
         both = jnp.concatenate([own_ref[...], mate_ref[...]], axis=0)
         seen[...] = both
@@ -452,7 +548,7 @@
         part = nt(grad, in_ref[0])
         if steps == 1:
             p_own[...] = part[:rows].astype(bf16)
-            p_mate[...] = part[rows:].astype(bf16)
+            put(p_mate, part[rows:])
             return
 
         @pl.when(step == 0)
@@ -466,20 +562,21 @@
         @pl.when(step == steps - 1)
         def _():
             p_own[...] = acc[:rows].astype(bf16)
-            p_mate[...] = acc[rows:].astype(bf16)
+            put(p_mate, acc[rows:])
 
     fixed = pl.BlockSpec((rows, width), lambda i: (0, 0))
+    quarter = [pl.BlockSpec((rows // PIECES, width), lambda i: (0, 0))] * PIECES
     cols = pl.BlockSpec((2 * rows, tile), lambda i: (0, i))
     weight = [pl.BlockSpec((1, width, tile), lambda i, m=m: (m, 0, i)) for m in range(2)]
     return run(
         kernel,
-        [((rows, width), bf16)] * 2 + [((2 * rows, hidden), bf16), ((2 * rows, width), bf16)],
+        [((rows, width), bf16)] + cut((rows, width)) + [((2 * rows, hidden), bf16), ((2 * rows, width), bf16)],
         [own, mate, pre, weights, weights],
         after,
         name,
         grid=(steps,),
         in_specs=[fixed, fixed, cols] + weight,
-        out_specs=[fixed, fixed, cols, pl.BlockSpec((2 * rows, width), lambda i: (0, 0))],
+        out_specs=[fixed] + quarter + [cols, pl.BlockSpec((2 * rows, width), lambda i: (0, 0))],
         scratch=[pltpu.VMEM((2 * rows, width), f32)] if steps > 1 else (),
         room=28,
         work=8 * rows * width * hidden,
@@ -496,6 +593,7 @@
         refs[-2][0] = nn(both, w_ref[0]).astype(bf16)
 
     fixed = pl.BlockSpec((rows, width), lambda i: (0, 0))
+    quarter = [pl.BlockSpec((rows // PIECES, width), lambda i: (0, 0))] * PIECES
     ins = [own, mate, weights] + ([held] if held is not None else [])
     specs = [fixed, fixed, pl.BlockSpec((1, width, cols), lambda i: (i, 0, 0))]
     specs = specs + [pl.BlockSpec(memory_space=pl.ANY)] * (held is not None)
@@ -526,6 +624,7 @@
         refs[-2][...] = nn(both, w_ref[...]).astype(bf16)
 
     fixed = pl.BlockSpec((rows, width), lambda i: (0, 0))
+    quarter = [pl.BlockSpec((rows // PIECES, width), lambda i: (0, 0))] * PIECES
     ins = [own, mate, weight] + ([held] if held is not None else [])
     specs = [fixed, fixed, pl.BlockSpec((width, cols), lambda i: (0, 0))]
     specs = specs + [pl.BlockSpec(memory_space=pl.ANY)] * (held is not None)
@@ -549,15 +648,16 @@
 def out_rows(values, weight, k, rows, name, after=()):
     width, cols = weight.shape
 
-    def kernel(value_ref, w_ref, p_own, p_mate):
+    def kernel(value_ref, w_ref, p_own, *p_mate):
         part = nt(value_ref[...], w_ref[...])
         p_own[...] = part[:rows].astype(bf16)
-        p_mate[...] = part[rows:].astype(bf16)
+        put(p_mate, part[rows:])
 
     fixed = pl.BlockSpec((rows, width), lambda i: (0, 0))
+    quarter = [pl.BlockSpec((rows // PIECES, width), lambda i: (0, 0))] * PIECES
     return run(
         kernel,
-        [((rows, width), bf16)] * 2,
+        [((rows, width), bf16)] + cut((rows, width)),
         [values, weight],
         after,
         name,
@@ -566,7 +666,7 @@
             pl.BlockSpec((2 * rows, cols), lambda i: (k, 0)),
             pl.BlockSpec((width, cols), lambda i: (0, 0)),
         ],
-        out_specs=[fixed, fixed],
+        out_specs=[fixed] + quarter,
         work=4 * rows * width * cols,
     )
 
@@ -574,17 +674,18 @@
 def members_rows(members, weights, k, rows, name, after=()):
     width, cols = weights.shape[1:]
 
-    def kernel(value_ref, w_ref, p_own, p_mate):
+    def kernel(value_ref, w_ref, p_own, *p_mate):
         part = nt(value_ref[0], w_ref[0])
         for m in range(1, 3):
             part = part + nt(value_ref[m], w_ref[m])
         p_own[...] = part[:rows].astype(bf16)
-        p_mate[...] = part[rows:].astype(bf16)
+        put(p_mate, part[rows:])
 
     fixed = pl.BlockSpec((rows, width), lambda i: (0, 0))
+    quarter = [pl.BlockSpec((rows // PIECES, width), lambda i: (0, 0))] * PIECES
     return run(
         kernel,
-        [((rows, width), bf16)] * 2,
+        [((rows, width), bf16)] + cut((rows, width)),
         [members, weights],
         after,
         name,
@@ -593,7 +694,7 @@
             pl.BlockSpec((3, 2 * rows, cols), lambda i: (0, k, 0)),
             pl.BlockSpec((3, width, cols), lambda i: (0, 0, 0)),
         ],
-        out_specs=[fixed, fixed],
+        out_specs=[fixed] + quarter,
         work=12 * rows * width * cols,
     )
 
@@ -639,10 +740,12 @@
         yield left, columns[0] if len(columns) == 1 else jnp.concatenate(columns, axis=1), cols
 
 
-def outer(jobs, name, after=()):
+def outer(jobs, name, after=(), sums=()):
     plan, ins = lay_out(jobs)
-    total = sum(cols for _, _, cols in plan)
+    total = sum(cols for _, _, cols in plan) + sum(parts[0].shape[1] for parts in sums)
     width = jobs[0][0][0].shape[1]
+    products = len(ins)
+    ins = ins + [array for parts in sums for array in parts]
 
     def kernel(*refs):
         column = 0
@@ -651,9 +754,15 @@
             rows = rows[0] if len(rows) == 1 else jnp.concatenate(rows, axis=0)
             refs[-1][:, column : column + cols] = tn(rows, rights).astype(bf16)
             column = column + cols
+        at = products
+        for parts in sums:
+            value = total_of(refs[at : at + len(parts)])
+            refs[-1][:, column : column + parts[0].shape[1]] = value.astype(bf16)
+            at = at + len(parts)
+            column = column + parts[0].shape[1]
 
     work = sum(2 * width * cols * sum(r.shape[0] for r in left) for (left, _), (_, _, cols) in zip(jobs, plan))
-    return run(kernel, [((width, total), bf16)], ins, after, name, room=36, work=work)[0]
+    return run(kernel, [((width, total), bf16)], ins, after, name, room=36, work=work, mark=True)[0]
 
 
 def outer_halves(links, jobs, turn, name, after=()):
@@ -691,6 +800,7 @@
         in_specs=[SMEM_SPEC] + [None] * (len(ins) - 1),
         room=24,
         work=2 * SLOT * width * total,
+        mark=True,
     )
 
 
@@ -706,7 +816,7 @@
             refs[2 * count + 2 * i + 1][...] = total[:half].astype(bf16)
 
     outs = [(shape, bf16) for shape in shapes for _ in range(2)]
-    made = run(kernel, outs, [array for pair in pairs for array in pair], after, name)
+    made = run(kernel, outs, [array for pair in pairs for array in pair], after, name, mark=True)
     return [(made[2 * i], made[2 * i + 1]) for i in range(count)]
 
 
@@ -800,18 +910,19 @@
     channels = running.shape[1]
     lo, mid, hi = MARGIN, MARGIN + rows, MARGIN + 2 * rows
 
-    def kernel(who_ref, mix_ref, tally_ref, affine_ref, run_ref, w_ref, act_ref, p_own, p_mate, new_ref):
+    def kernel(who_ref, mix_ref, tally_ref, affine_ref, run_ref, w_ref, act_ref, p_own, *rest):
+        *p_mate, new_ref = rest
         c = who_ref[0] % 2
         count, mean, var, inverse = batch_terms(tally_ref)
         own = pl.ds(pl.multiple_of(lo + c * rows, 16), rows)
         mate = pl.ds(pl.multiple_of(lo + (1 - c) * rows, 16), rows)
         mixture = jnp.concatenate([mix_ref[own, :], mix_ref[mate, :]], axis=0)
-        shifted = (mixture - mean) * inverse * affine_ref[0:1, :] + affine_ref[1:2, :]
+        shifted = (mixture - mean) * inverse * affine_ref[KERNEL : KERNEL + 1, :] + affine_ref[KERNEL + 1 : KERNEL + 2, :]
         active = (shifted / (1.0 + jnp.exp(-shifted))).astype(bf16)
         act_ref[...] = active
         part = nt(active, w_ref[...])
         p_own[...] = part[:rows].astype(bf16)
-        p_mate[...] = part[rows:].astype(bf16)
+        put(p_mate, part[rows:])
         grown = var * count / (count - 1.0)
         new_ref[...] = (1.0 - momentum) * run_ref[...] + momentum * jnp.concatenate(
             [mean[:, :channels], grown[:, :channels]], axis=0
@@ -819,7 +930,7 @@
 
     return run(
         kernel,
-        [((2 * rows, cols), bf16), ((rows, width), bf16), ((rows, width), bf16), (running.shape, f32)],
+        [((2 * rows, cols), bf16), ((rows, width), bf16)] + cut((rows, width)) + [(running.shape, f32)],
         [who, mixture, tallies, affine, running, weight],
         after,
         name,
@@ -843,7 +954,7 @@
         valid = place_mask(count, who_ref[0] // 2, len_ref[0])
         _, mean, _, inverse = batch_terms(tally_ref)
         centred = (mix_ref[...] - mean) * inverse
-        shifted = centred * affine_ref[0:1, :] + affine_ref[1:2, :]
+        shifted = centred * affine_ref[KERNEL : KERNEL + 1, :] + affine_ref[KERNEL + 1 : KERNEL + 2, :]
         logistic = 1.0 / (1.0 + jnp.exp(-shifted))
         slope = logistic * (1.0 + shifted * (1.0 - logistic))
         grad = jnp.where(valid > 0.0, nn(rows_in, w_ref[...]) * slope, 0.0)
@@ -876,12 +987,13 @@
     count = 2 * rows
     lo, mid, hi = MARGIN, MARGIN + rows, MARGIN + count
 
-    def kernel(who_ref, len_ref, dz_ref, mix_ref, tally_ref, sum_ref, affine_ref, taps_ref, lin_ref, gate_ref, w0, w1, dl_ref, dg_ref, p_own, p_mate, tap_ref):
+    def kernel(who_ref, len_ref, dz_ref, mix_ref, tally_ref, sum_ref, affine_ref, taps_ref, lin_ref, gate_ref, w0, w1, dl_ref, dg_ref, p_own, *rest):
+        *p_mate, tap_ref = rest
         c = who_ref[0] % 2
         valid = place_mask(count, who_ref[0] // 2, len_ref[0])
         total, mean, _, inverse = batch_terms(tally_ref)
         centred = (mix_ref[...] - mean) * inverse
-        shrink = affine_ref[0:1, :] * inverse
+        shrink = affine_ref[KERNEL : KERNEL + 1, :] * inverse
         mixed = (sum_ref[1:2, :] + centred * sum_ref[0:1, :]) / total
         grad_mix = jnp.where(valid > 0.0, shrink * (dz_ref[...] - mixed), 0.0)
         grad_glu = taps_ref[0:1, :] * shift_rows(grad_mix, 2)
@@ -915,11 +1027,11 @@
         dg_ref[...] = grad_gate
         part = nt(grad_linear, w0[...]) + nt(grad_gate, w1[...])
         p_own[...] = part[:rows].astype(bf16)
-        p_mate[...] = part[rows:].astype(bf16)
+        put(p_mate, part[rows:])
 
     return run(
         kernel,
-        [((count, cols), bf16)] * 2 + [((rows, width), bf16)] * 2 + [((8, cols), f32)],
+        [((count, cols), bf16)] * 2 + [((rows, width), bf16)] + cut((rows, width)) + [((8, cols), f32)],
         [who, length, dz, mixture, tallies, sums, affine, taps, linear, gating, weights[0], weights[1]],
         after,
         name,
@@ -937,10 +1049,8 @@
     def core(self, value):
         return lax.ppermute(value, "tensor", [(i, i ^ 1) for i in range(self.tensor)])
 
-    def mate(self, value):
-        pieces = 4 if value.shape[0] % 64 == 0 else 1
-        rows = value.shape[0] // pieces
-        return [self.core(value[i * rows : (i + 1) * rows]) for i in range(pieces)]
+    def mate(self, pieces):
+        return [self.core(piece) for piece in pieces]
 
     def chip(self, value, k):
         return lax.ppermute(value, "tensor", [(i, i ^ (2 * k)) for i in range(self.tensor)])
@@ -951,23 +1061,14 @@
     def scatter_grad(self, value):
         return lax.psum_scatter(value, "dp", scatter_dimension=0, tiled=True)
 
-    def sum_group(self, value):
+    def sum_group(self, value, name):
         for mask in self.masks:
-            value = value + self.group(value, mask)
+            value = add_stats(value, [self.group(value, mask)], 0, name)
         return value
 
-    def sum_stats(self, value, channels):
-        return self.sum_group(self.sum_columns(value, channels))
-
-    def sum_columns(self, value, channels):
-        def cols(array, k):
-            return array[:, k * channels : (k + 1) * channels]
-
-        total = value
-        for k in range(1, self.ny):
-            other = self.chip(value, k)
-            total = total + jnp.concatenate([cols(other, r ^ k) for r in range(self.ny)], axis=1)
-        return total
+    def sum_stats(self, value, channels, name, after=()):
+        others = [self.chip(value, k) for k in range(1, self.ny)]
+        return self.sum_group(add_stats(value, others, channels, name, after), name)
 
     def offsets(self, turn):
         masks = list(self.masks)
@@ -978,18 +1079,15 @@
             offsets = offsets + [off ^ mask for off in offsets]
         return offsets, masks
 
-    def borders(self, own, mate):
-        count = own.shape[0]
-        who = lax.axis_index("tensor")
-        y, c = who // 2, who % 2
+    def borders(self, own, mate, edge):
         if self.ny == 2:
-            edge = lax.dynamic_slice_in_dim(own, (1 - y) * (count - MARGIN), MARGIN)
             straight = lax.ppermute(edge, "tensor", [(1, 3), (2, 0)])
             across = lax.ppermute(edge, "tensor", [(1, 2), (2, 1)])
             return [straight, across], [straight, across]
+        c = lax.axis_index("tensor") % 2
         mate = jnp.concatenate(mate)
         head = jnp.where(c == 0, own, mate)[:MARGIN]
-        foot = jnp.where(c == 0, mate, own)[count - MARGIN :]
+        foot = jnp.where(c == 0, mate, own)[own.shape[0] - MARGIN :]
         down = [(i, i + 2) for i in range(self.tensor - 2)]
         up = [(i + 2, i) for i in range(self.tensor - 2)]
         return [lax.ppermute(foot, "tensor", down)], [lax.ppermute(head, "tensor", up)]
@@ -1041,46 +1139,102 @@
         for m in range(2):
             out[m] = wide(ref)[:, m * hidden : (m + 1) * hidden]
 
-    return run(kernel, [((2, share, hidden), f32)], [total], after, name)[0]
-
-
-def split_heads(total, begin, cols, name):
+    return run(kernel, [((2, share, hidden), f32)], [total], after, name, mark=True)[0]
+
+
+def split_heads(total, cols, channels, name):
     share = total.shape[0]
 
-    def kernel(ref, three, one):
-        value = wide(ref)[:, begin:]
+    def kernel(ref, three, one, conv):
+        value = wide(ref)
         for m in range(3):
             three[m] = value[:, m * cols : (m + 1) * cols]
-        one[...] = value[:, 3 * cols :]
-
-    return run(kernel, [((3, share, cols), f32), ((share, cols), f32)], [total], (), name)
-
-
-def finish_conv(links, total, channels, name):
-    share = total.shape[0]
-    ny = links.ny
-
-    def split(ref, *others):
+            at = 4 * cols + m * channels
+            conv[m] = value[:, at : at + channels]
+        one[...] = value[:, 3 * cols : 4 * cols]
+
+    outs = [((3, share, cols), f32), ((share, cols), f32), ((3, share, channels), f32)]
+    return run(kernel, outs, [total], (), name)
+
+
+def pack_small(depthwise, bn_gain, bn_bias, name):
+    channels = depthwise.shape[1]
+
+    def kernel(taps, gain, bias, out):
+        out[...] = jnp.concatenate(
+            [taps[...], gain[...], bias[...], jnp.zeros((1, channels), f32)], axis=0
+        )
+
+    rows = [depthwise, bn_gain[None], bn_bias[None]]
+    return run(kernel, [((8, channels), f32)], rows, (), name)[0]
+
+
+def side_by_side(arrays, name):
+    def kernel(*refs):
+        refs[-1][...] = jnp.concatenate([ref[...] for ref in refs[:-1]], axis=1)
+
+    shape = (arrays[0].shape[0], sum(array.shape[1] for array in arrays))
+    return run(kernel, [(shape, f32)], arrays, (), name)[0]
+
+
+def pack_sums(gains, table, name, after=()):
+    width = gains[0].shape[1]
+    each = width // 128
+
+    def kernel(*refs):
+        out = refs[-1]
+        for g in range(5):
+            for i in range(each):
+                out[g * each + i : g * each + i + 1, :] = refs[g][0:1, i * 128 : (i + 1) * 128]
+        out[5 * each :, :] = refs[5][...]
+
+    return run(kernel, [((5 * each + 128, 128), f32)], list(gains) + [table], after, name)[0]
+
+
+def with_taps(sums, taps, channels, name, after=()):
+    def kernel(sum_ref, tap_ref, out):
+        top = sums.shape[0]
+        out[:top, :] = sum_ref[...]
+        for i in range(channels // 128):
+            out[top + 8 * i : top + 8 * i + 8, :] = tap_ref[:, i * 128 : (i + 1) * 128]
+
+    rows = sums.shape[0] + 8 * (channels // 128)
+    return run(kernel, [((rows, 128), f32)], [sums, taps], after, name)[0]
+
+
+def unpack_sums(sums, bn_grads, width, channels, name):
+    each = width // 128
+    top = 5 * each + 128
+
+    def kernel(sum_ref, bn_ref, gains, table, kernel_grad, gain_grad, bias_grad):
+        for g in range(5):
+            for i in range(each):
+                gains[g : g + 1, i * 128 : (i + 1) * 128] = sum_ref[g * each + i : g * each + i + 1, :]
+        table[...] = sum_ref[5 * each : 5 * each + REL, :]
+        for i in range(channels // 128):
+            at = top + 8 * i
+            kernel_grad[:, i * 128 : (i + 1) * 128] = sum_ref[at : at + KERNEL, :]
+        gain_grad[...] = bn_ref[0:1, :channels]
+        bias_grad[...] = bn_ref[1:2, :channels]
+
+    outs = [((5, width), f32), ((REL, 128), f32), ((KERNEL, channels), f32)] + [((1, channels), f32)] * 2
+    return run(kernel, outs, [sums, bn_grads], (), name)
+
+
+def own_share(weights, me, share, name, after=()):
+    cols = weights.shape[2]
+
+    def kernel(me_ref, ref, out):
+        rows = pl.ds(pl.multiple_of(me_ref[0] * share, 16), share)
         for m in range(3):
-            for k in range(1, ny):
-                at = (m * ny + k) * channels
-                others[k - 1][m] = ref[:, at : at + channels]
-
-    shape = (3, share, channels)
-    parts = run(split, [(shape, bf16)] * (ny - 1), [total], (), name)
-    came = [links.chip(parts[k - 1], k) for k in range(1, ny)]
-
-    def close(*refs):
-        for m in range(3):
-            piece = refs[0][:, m * ny * channels : (m * ny + 1) * channels].astype(f32)
-            for ref in refs[1:-1]:
-                piece = piece + ref[m].astype(f32)
-            refs[-1][m] = piece
-
-    return run(close, [(shape, f32)], [total] + came, (), name + "_close")[0]
-
-
-def arrange(conv_proj, gathered, dp, name):
+            out[m * share : (m + 1) * share, :] = ref[m, rows, :]
+
+    return run(
+        kernel, [((3 * share, cols), bf16)], [me, weights], after, name, in_specs=[SMEM_SPEC, None]
+    )[0]
+
+
+def arrange(conv_proj, gathered, dp, name, after=()):
     _, width, channels = conv_proj.shape
     share = width // dp
     cols = channels * (1 + len(gathered))
@@ -1096,7 +1250,7 @@
                         at : at + share, :
                     ]
 
-    return run(kernel, [((width, cols), bf16)] * 3, [conv_proj] + gathered, (), name)
+    return run(kernel, [((width, cols), bf16)] * 3, [conv_proj] + gathered, after, name, mark=True)
 
 
 def per_device(
@@ -1116,96 +1270,105 @@
     running,
     ffn_second,
 ):
+    MARKS.clear()
     ny = links.ny
     others = list(range(1, ny))
     rows, width = x_in.shape
     channels = bn_gain.shape[0]
-    who = lax.axis_index("tensor").astype(jnp.int32)
-    who_arr = who.reshape(1)
-    y, c = who // 2, who % 2
-    gain = [norm_gains[i : i + 1] for i in range(5)]
-    begin = [(((y ^ k) * 2 + c) * rows).reshape(1) for k in range(ny)]
-
-    me = lax.axis_index("dp")
+    who = lax.axis_index("tensor").astype(jnp.int32).reshape(1)
+    gains = norm_gains
+    table = window_table(jnp.pad(rel_table, ((0, 128 - REL), (0, 0))))
+
+    me = lax.axis_index("dp").astype(jnp.int32).reshape(1)
     share = width // links.dp
-    piece = lax.dynamic_slice_in_dim(conv_proj, me * share, share, axis=1)
-    gathered = []
-    for k in others:
-        other = links.chip(piece, k).reshape(3 * share, channels)
-        gathered.append(lax.all_gather(other, "dp", axis=0, tiled=True))
-    conv_w = arrange(conv_proj, gathered, links.dp, "conv_weights")
-    small = jnp.concatenate([depthwise, bn_gain[None], bn_bias[None], jnp.zeros((1, channels), f32)])
-    small = jnp.concatenate([small] + [links.chip(small, k) for k in others], axis=1)
-    affine = small[KERNEL : KERNEL + 2]
+    halves_fit = share % 128 == 0
+    small = pack_small(depthwise, bn_gain, bn_bias, "conv_small")
+    small = side_by_side([small] + [links.chip(small, k) for k in others], "conv_small_all")
 
     def send_sums(parts, name, after=()):
         return add_up([parts[0], links.mate(parts[1])], name, after)
 
-    normed, x_low = norm_rows(x_in, [], 0.0, gain[0], "ln_in", keep=False, low=True)
+    def every(pieces):
+        return [pieces[k] for k in range(ny)]
+
+    def split(made):
+        return (made[0], made[1 : 1 + PIECES]), made[1 + PIECES :]
+
+    def all_parts(sums, k):
+        return [sums[k]] + [links.chip(sums[k ^ j], j) for j in others]
+
+    (normed, pieces), x_low = norm_rows(x_in, [], 0.0, gains, 0, "ln_in", keep=False, low=True)
     x_rows = [x_in] + [links.chip(x_low, k) for k in others]
-    na_first, kept_first, sums, came = {}, {}, {}, {}
+    na_first, pre_first, hid_first, sums = {}, {}, {}, {}
     token = ()
     for k in range(ny):
         if k:
-            (normed,) = norm_rows(x_rows[k], [], 0.0, gain[0], "ln_in", token, keep=False)
-        na_first[k] = (normed, links.mate(normed))
-        p_own, p_mate, pre, hid, na_first[k] = feed(*na_first[k], ffn_first, "ffn_one")
-        kept_first[k] = (pre, hid)
-        sums[k] = send_sums((p_own, p_mate), "ffn_one_sum")
+            ((normed, pieces),) = norm_rows(
+                x_rows[k], [], 0.0, gains, 0, "ln_in", token + (small,), keep=False
+            )
+        if k == 1:
+            piece = own_share(conv_proj, me, share, "conv_share", (normed,))
+            gathered = [
+                lax.all_gather(links.chip(piece, j), "dp", axis=0, tiled=True) for j in others
+            ]
+        parts, made = split(feed(normed, links.mate(pieces), ffn_first, "ffn_one"))
+        pre_first[k], hid_first[k], na_first[k] = made
+        sums[k] = send_sums(parts, "ffn_one_sum")
         token = (sums[k],)
-
-    def all_parts(sums, k):
-        return [sums[k]] + [links.chip(sums[k ^ j], j) for j in others]
 
     token = ()
     na_attn, first, qkv, cot_low = {}, {}, None, None
     for k in others + [0]:
         also = cotangent if k == 0 else None
         made = norm_rows(
-            x_rows[k], all_parts(sums, k), 0.5, gain[1], "ln_attn", token, also=also
+            x_rows[k], all_parts(sums, k), 0.5, gains, 1, "ln_attn", token, also=also
         )
-        na_attn[k] = (made[0], links.mate(made[0]))
-        first[k] = made[1]
+        (normed, pieces), first[k] = made[:2]
         if k == 0:
             cot_low = made[2]
-        qkv, na_attn[k] = qkv_rows(*na_attn[k], attn_qkv, k, SLOT, qkv, "qkv")
+        qkv, na_attn[k] = qkv_rows(normed, links.mate(pieces), attn_qkv, k, SLOT, qkv, "qkv")
         token = (qkv,)
     cot_rows = [cotangent] + [links.chip(cot_low, k) for k in others]
-    heads_out, probs = attend(qkv, who_arr, lengths, rel_table, rows)
-    token = ()
+    heads_out, probs = attend(qkv, who, lengths, table, rows)
+    token = tuple(cot_rows[1:])
     arrived = []
     for k in others:
-        total = send_sums(out_rows(heads_out, attn_out, k, rows, "out_proj", token), "out_sum")
+        parts, _ = split(out_rows(heads_out, attn_out, k, rows, "out_proj", token))
+        total = send_sums(parts, "out_sum")
         arrived.append(links.chip(total, k))
         token = (total,)
-    p_own, p_mate = out_rows(heads_out, attn_out, 0, rows, "out_proj", token)
-    conv_own, after_attn = norm_rows(
-        first[0], [p_own, links.mate(p_mate)] + arrived, 1.0, gain[2], "ln_conv"
-    )
-
-    conv_mate = links.mate(conv_own)
-    before, after_rows = links.borders(conv_own, conv_mate)
+    conv_w = arrange(conv_proj, gathered, links.dp, "conv_weights", token)
+    token = token + (conv_w[0],)
+    parts, _ = split(out_rows(heads_out, attn_out, 0, rows, "out_proj", token))
+    edge = who if ny == 2 else None
+    made = norm_rows(
+        first[0], [parts[0], links.mate(parts[1])] + arrived, 1.0, gains, 2, "ln_conv", edge=edge
+    )
+    (normed, pieces), after_attn = made[:2]
+
+    mate = links.mate(pieces)
+    before, after_rows = links.borders(normed, mate, made[-1])
     linear, gating, mixture, tallies, conv_in = conv_mix(
-        ny, who_arr, lengths, conv_own, conv_mate, before, after_rows, conv_w, small[:KERNEL], "conv_mix"
-    )
-    tallies = links.sum_stats(tallies, channels)
-    active, p_own, p_mate, updated = conv_out(
-        who_arr, mixture, tallies, affine, running, conv_w[2], rows, "conv_out"
-    )
-    normed, after_conv, low = norm_rows(
-        after_attn, [p_own, links.mate(p_mate)], 1.0, gain[3], "ln_ffn_two", low=True
+        ny, who, lengths, normed, mate, before, after_rows, conv_w, small, "conv_mix"
+    )
+    tallies = links.sum_stats(tallies, channels, "bn_sum")
+    active, *made = conv_out(who, mixture, tallies, small, running, conv_w[2], rows, "conv_out")
+    parts, (updated,) = split(made)
+    (normed, pieces), after_conv, low = norm_rows(
+        after_attn, [parts[0], links.mate(parts[1])], 1.0, gains, 3, "ln_ffn_two", low=True
     )
 
     x_rows = [after_conv] + [links.chip(low, k) for k in others]
-    na_last, kept_last, sums = {}, {}, {}
+    na_last, pre_last, hid_last, sums = {}, {}, {}, {}
     token = ()
     for k in range(ny):
         if k:
-            (normed,) = norm_rows(x_rows[k], [], 0.0, gain[3], "ln_ffn_two", token, keep=False)
-        na_last[k] = (normed, links.mate(normed))
-        p_own, p_mate, pre, hid, na_last[k] = feed(*na_last[k], ffn_second, "ffn_two")
-        kept_last[k] = (pre, hid)
-        sums[k] = send_sums((p_own, p_mate), "ffn_two_sum")
+            ((normed, pieces),) = norm_rows(
+                x_rows[k], [], 0.0, gains, 3, "ln_ffn_two", token, keep=False
+            )
+        parts, made = split(feed(normed, links.mate(pieces), ffn_second, "ffn_two"))
+        pre_last[k], hid_last[k], na_last[k] = made
+        sums[k] = send_sums(parts, "ffn_two_sum")
         token = (sums[k],)
 
     token = ()
@@ -1214,77 +1377,90 @@
         made = norm_last(
             x_rows[k],
             all_parts(sums, k),
-            gain[4],
+            gains,
             cot_rows[k],
-            begin[k],
+            who,
+            k,
             lengths,
             "ln_last",
             k == 0,
             token,
         )
-        upper[k] = (made[0], links.mate(made[0]))
-        p_own, p_mate, down[k], upper[k] = feed_grad(
-            *upper[k], kept_last[k][0], ffn_second, "ffn_two_grad"
+        normed, pieces = made[0]
+        if k == 0:
+            grad, output, gain_five = made[1:]
+        parts, made = split(
+            feed_grad(normed, links.mate(pieces), pre_last[k], ffn_second, "ffn_two_grad")
         )
+        down[k], upper[k] = made
         if k:
-            total = send_sums((p_own, p_mate), "ffn_two_grad_sum")
+            total = send_sums(parts, "ffn_two_grad_sum")
             arrived.append(links.chip(total, k))
             token = (total,)
-        else:
-            grad, output, gain_five = made[1:]
-            parts = [p_own, links.mate(p_mate)]
-
-    def every(pieces):
-        return [pieces[k] for k in range(ny)]
-
-    hid_last = [kept_last[k][1] for k in range(ny)]
+    made = norm_grad(
+        after_conv,
+        [parts[0], links.mate(parts[1])] + arrived,
+        gains,
+        3,
+        grad,
+        "back_ffn_two",
+        factor=1.0,
+        edge=edge,
+    )
+    (low, pieces), grad, gain_four = made[:3]
+
+    mate = links.mate(pieces)
+    before, after_rows = links.borders(low, mate, made[-1])
+    dz, sums, conv_up = conv_shift_grad(
+        ny, who, lengths, low, mate, before, after_rows, mixture, tallies, small, conv_w[2], "conv_dz"
+    )
     two_sum = outer(
-        [(every(na_last), [every(down)]), (every(upper), [hid_last])], "ffn_two_w", (p_mate,)
-    )
-    low, grad, gain_four = norm_grad(
-        after_conv, parts + arrived, gain[3], grad, "back_ffn_two", (two_sum,), factor=1.0
-    )
+        [(every(na_last), [every(down)]), (every(upper), [every(hid_last)])], "ffn_two_w", (sums,)
+    )
+    def by_chip(left, rights, name, after):
+        made = []
+        for k in range(ny):
+            spans = [[(right, None, k * channels, (k + 1) * channels)] for right in rights]
+            made.append(outer([([left], spans)], name, after))
+        return [made[0]] + [links.chip(made[k], k) for k in others]
+
+    out_grad = by_chip(conv_up, [active], "conv_out_w", (two_sum,))
+    bn_grads = links.sum_stats(sums, channels, "bn_grad_sum", (two_sum,))
     two_sum = links.scatter_grad(two_sum)
-
-    up_own = low
-    up_mate = links.mate(low)
-    before, after_rows = links.borders(up_own, up_mate)
-    dz, sums, conv_up = conv_shift_grad(
-        ny, who_arr, lengths, up_own, up_mate, before, after_rows, mixture, tallies, affine, conv_w[2], "conv_dz"
-    )
-    bn_grads = links.sum_stats(sums, channels)
-    grad_linear, grad_gate, p_own, p_mate, tap_grad = conv_in_grad(
-        who_arr, lengths, dz, mixture, tallies, bn_grads, affine, small[:KERNEL], linear, gating, conv_w, rows, "conv_din"
-    )
-    low, grad, gain_three = norm_grad(
-        after_attn, [p_own, links.mate(p_mate)], gain[2], grad, "back_conv", factor=1.0
-    )
-
+    grad_linear, grad_gate, *made = conv_in_grad(
+        who, lengths, dz, mixture, tallies, bn_grads, small, small, linear, gating, conv_w, rows, "conv_din"
+    )
+    parts, (tap_grad,) = split(made)
+    (low, pieces), grad, gain_three = norm_grad(
+        after_attn, [parts[0], links.mate(parts[1])], gains, 2, grad, "back_conv", factor=1.0
+    )
 
     g_rows = [low] + [links.chip(low, k) for k in others]
-    token = (low,)
+    in_grads = by_chip(conv_in, [grad_linear, grad_gate], "conv_in_w", (low,))
+    token = (in_grads[0],)
     grad_heads = None
     upper_attn = {}
     for k in range(ny):
+        mate = links.mate(pieces) if k == 0 else [links.core(g_rows[k])]
         grad_heads, upper_attn[k] = heads_rows(
-            g_rows[k], links.mate(g_rows[k]), attn_out, k, SLOT, grad_heads, "dheads", token
+            g_rows[k], mate, attn_out, k, SLOT, grad_heads, "dheads", token
         )
-        token = ()
-    members, table_grad = attend_back(qkv, grad_heads, probs, who_arr, rel_table, rows)
+        token = (grad_heads,)
+    members, table_grad = attend_back(qkv, grad_heads, probs, who, table, rows)
     token = ()
     sums = {}
     for k in range(ny):
-        sums[k] = send_sums(members_rows(members, attn_qkv, k, rows, "dqkv", token), "dqkv_sum")
+        parts, _ = split(members_rows(members, attn_qkv, k, rows, "dqkv", token))
+        sums[k] = send_sums(parts, "dqkv_sum")
         token = (sums[k],)
     heads_sum = outer(
         [
-            ([conv_in], [[grad_linear], [grad_gate]]),
-            ([conv_up], [[active]]),
             (every(na_attn), [[(members, m)] for m in range(3)]),
             (every(upper_attn), [[heads_out]]),
         ],
         "attn_w",
         token,
+        [in_grads, out_grad],
     )
     token = (heads_sum,)
     heads_sum = links.scatter_grad(heads_sum)
@@ -1294,7 +1470,8 @@
         made = norm_grad(
             first[k],
             all_parts(sums, k),
-            gain[1],
+            gains,
+            1,
             grad if k == 0 else g_rows[k],
             "back_attn",
             token,
@@ -1302,75 +1479,80 @@
             keep=k == 0,
             sums=k == 0,
         )
-        upper[k] = (made[0], links.mate(made[0]))
-        p_own, p_mate, down[k], upper[k] = feed_grad(
-            *upper[k], kept_first[k][0], ffn_first, "ffn_one_grad"
+        normed, pieces = made[0]
+        if k == 0:
+            grad, gain_two = made[1:]
+        parts, made = split(
+            feed_grad(normed, links.mate(pieces), pre_first[k], ffn_first, "ffn_one_grad")
         )
+        down[k], upper[k] = made
         if k:
-            total = send_sums((p_own, p_mate), "ffn_one_grad_sum")
+            total = send_sums(parts, "ffn_one_grad_sum")
             arrived.append(links.chip(total, k))
             token = (total,)
-        else:
-            grad, gain_two = made[1:]
-            parts = [p_own, links.mate(p_mate)]
-    hid_first = [kept_first[k][1] for k in range(ny)]
     hidden = ffn_first.shape[2]
     half = hidden // 2
-    one_down, one_up, one_in = every(down), every(upper), every(na_first)
-    token = (p_mate,)
+    token = (parts[0],)
     pairs = []
-    if share % 128 == 0:
-        for left, right in ((one_up, hid_first), (one_in, one_down)):
-            pieces = []
+    if halves_fit:
+        for left, right in ((every(upper), every(hid_first)), (every(na_first), every(down))):
+            halves = []
             for turn in range(2):
                 columns = [(r, None, turn * half, (turn + 1) * half) for r in right]
-                made = outer_halves(links, [(left, [columns])], turn, "ffn_one_w", token)
-                token = (made[0],)
-                pieces.append(made)
-            pairs.append(Pieces(links, pieces, "one"))
+                halves.append(outer_halves(links, [(left, [columns])], turn, "ffn_one_w", token))
+                token = (halves[-1][0],)
+            pairs.append(Pieces(links, halves, "one"))
     else:
-        first_sum = outer([(one_in, [one_down]), (one_up, [hid_first])], "ffn_one_w", token)
+        first_sum = outer(
+            [(every(na_first), [every(down)]), (every(upper), [every(hid_first)])], "ffn_one_w", token
+        )
         token = (first_sum,)
         first_sum = links.scatter_grad(first_sum)
+    for pair in pairs:
+        token = (pair.step(token),)
     last_sum = split_two(two_sum, hidden, "two_end", token)
     grad_input, gain_one = norm_grad(
-        x_in, parts + arrived, gain[0], grad, "back_ffn_one", token + (last_sum,)
-    )
-
-    gains = [gain_one, gain_two, gain_three, gain_four, gain_five]
-    gains = jnp.stack([part[0] for part in gains]).reshape(-1, HEAD)
-    bundle = jnp.concatenate([gains, table_grad])
-    bundle = jnp.pad(bundle, ((0, -bundle.shape[0] % 8), (0, 0)))
-    bundle = bundle + links.core(bundle)
+        x_in,
+        [parts[0], links.mate(parts[1])] + arrived,
+        gains,
+        0,
+        grad,
+        "back_ffn_one",
+        token + (last_sum,),
+    )
+
+    taps = add_stats(tap_grad, [links.chip(tap_grad, k) for k in others], channels, "taps_sum")
+    bundle = pack_sums([gain_one, gain_two, gain_three, gain_four, gain_five], table_grad, "pack")
+    bundle = add_stats(bundle, [links.core(bundle)], 0, "bundle_sum")
     for k in [1 << bit for bit in range(ny.bit_length() - 1)]:
-        bundle = bundle + links.chip(bundle, k)
-    taps_at = bundle.shape[0]
-    tap_sums = links.sum_columns(tap_grad, channels)[:, :channels]
-    bundle = jnp.concatenate([bundle, tap_sums.reshape(-1, HEAD)])
-    token = ()
+        bundle = add_stats(bundle, [links.chip(bundle, k)], 0, "bundle_sum")
+    token = (bundle,)
+    for _ in links.masks[2:]:
+        for pair in pairs:
+            token = (pair.step(token),)
+    bundle = with_taps(bundle, taps, channels, "pack_taps", token)
     for mask in links.masks:
-        bundle = bundle + links.group(bundle, mask)
-        for pair in pairs:
-            pair.step((bundle,))
-    kernel_grad = bundle[taps_at:].reshape(8, channels)[:KERNEL]
+        bundle = add_stats(bundle, [links.group(bundle, mask)], 0, "bundle_sum")
+    norm_sums, table_sums, kernel_grad, gain_grad, bias_grad = unpack_sums(
+        bundle, bn_grads, width, channels, "unpack"
+    )
     if pairs:
         first_sum = finish_one(pairs[0].finish(), pairs[1].finish(), hidden, "one_end")
     else:
         first_sum = split_two(first_sum, hidden, "one_end")
-    qkv_sum, out_sum = split_heads(heads_sum, 3 * ny * channels, attn_qkv.shape[2], "heads_end")
-    conv_sum = finish_conv(links, heads_sum, channels, "conv_end")
+    qkv_sum, out_sum, conv_sum = split_heads(heads_sum, attn_qkv.shape[2], channels, "heads_end")
     return (
         output,
         grad_input,
-        bundle[: gains.shape[0]].reshape(5, width),
+        norm_sums,
         first_sum,
         qkv_sum,
         out_sum,
-        bundle[gains.shape[0] : gains.shape[0] + REL],
+        table_sums,
         conv_sum,
         kernel_grad,
-        bn_grads[0, :channels],
-        bn_grads[1, :channels],
+        gain_grad.reshape(-1),
+        bias_grad.reshape(-1),
         updated,
         last_sum,
     )

time: 493 us -> 462 us (0.937)
  local copies, waits for them, and re-layouts: 92.6 us -> 64.3 us
  other arithmetic: 8.88 us -> 0 us
  Pallas kernels: 99.7 us -> 108 us
  waiting for transfers between devices: 177 us -> 182 us
    pallas_call x59 -> x84, Pallas kernels: 77.2 us -> 108 us  [run(): pl.pallas_call(body, in_specs=specs + [pl.BlockSpec(memory_space=pl.ANY)]...]
    pallas_call x2 -> x0, Pallas kernels: 22.4 us -> none  [the longest x1 13.8 us: attend_back(): pl.pallas_call(functools.partial(attend_back_kernel, rows), grid=(heads,)...]
    slice x43 -> x0, local copies, waits for them, and re-layouts: 17.3 us -> none  [the longest x28 9.07 us: mate(): return [self.core(value[i * rows:(i + 1) * rows]) for i in range(pieces)]]
    ppermute x21, waiting for transfers between devices: 77.6 us -> 64.6 us  [group(): return lax.ppermute(value, 'dp', [(i, i ^ mask) for i in range(self.dp)])]
    ppermute x113 -> x110, waiting for transfers between devices: 12.6 us -> 22.1 us  [core(): lax.ppermute(value, 'tensor', [(i, i ^ 1) for i in range(self.tensor)])]
    unnamed x330 -> x239, local copies, waits for them, and re-layouts: 72.2 us -> 64.3 us
    ppermute x20 -> x21, waiting for transfers between devices: 77.7 us -> 82.5 us  [chip(): lax.ppermute(value, 'tensor', [(i, i ^ 2 * k) for i in range(self.tensor)])]
    ppermute x113 -> x110, starting transfers between devices: 31.2 us -> 27.6 us  [core(): lax.ppermute(value, 'tensor', [(i, i ^ 1) for i in range(self.tensor)])]
  transfers between devices with their start and end apart: 161 -> 159, of which waited for: 68 -> 105; matrix products, arithmetic and copies ran while one was open for 6% -> 0% of each run, Pallas kernels for 18% -> 20%
where the time goes in v4:
time: 462 us; the launch traced here: 455 us
  waiting for transfers between devices  182 us (39%)
  Pallas kernels  108 us (23%)
  starting transfers between devices  84.2 us (18%)
  local copies, waits for them, and re-layouts  64.3 us (14%)
  between operations  16.2 us (4%)
    pallas_call x84, Pallas kernels, run(): pl.pallas_call(body, in_specs=specs + [pl.BlockSpec(memory_space=pl.ANY)]...  108 us
    ppermute x21, waiting for transfers between devices, chip(): lax.ppermute(value, 'tensor', [(i, i ^ 2 * k) for i in range(self.tensor)])  82.5 us
    ppermute x21, waiting for transfers between devices, group(): return lax.ppermute(value, 'dp', [(i, i ^ mask) for i in range(self.dp)])  64.6 us
    unnamed x239, local copies, waits for them, and re-layouts  64.3 us
    ppermute x21, starting transfers between devices, group(): return lax.ppermute(value, 'dp', [(i, i ^ mask) for i in range(self.dp)])  31.4 us
    ppermute x110, starting transfers between devices, core(): lax.ppermute(value, 'tensor', [(i, i ^ 1) for i in range(self.tensor)])  27.6 us
    ppermute x110, waiting for transfers between devices, core(): lax.ppermute(value, 'tensor', [(i, i ^ 1) for i in range(self.tensor)])  22.1 us
    ppermute x21, starting transfers between devices, chip(): lax.ppermute(value, 'tensor', [(i, i ^ 2 * k) for i in range(self.tensor)])  20.9 us
  transfers between devices with their start and end apart: 159, of which 105 were waited for; matrix products, arithmetic and copies ran while one was open for 0% of the time, Pallas kernels for 20%

profile of v4, /device:TPU:0, one launch (start us, length us, event | category | flops | bytes accessed | tf_op | source)
XLA Modules:
  0.0 454.7 jit_solution(1563432363779339884)
XLA Ops:
  18.4 3.1 ffn_one.2
  33.6 5.3 %collective-permute-done.33 = bf16[384,256]{1,0:T(8,128)(2,1)S(1)} collective-permute-done((bf16[384,256]{1,0:T(8,128)(2,1)S(1)}, bf16[384,256]{1,0:T(8,128)(2,1)S(1)}, u32[]{:S(2)}, u32[]{:S(2)}) %collective-permute-start.33) | collective-permute-done | bytes 196640 | tf_op jit(solution)/shard_map/ppermute | solution.py:1056
  62.6 3.5 collective-permute-done.18.refs_3_
  78.9 8.6 %attend.1 = (bf16[1024,256]{1,0:T(8,128)(2,1)S(1)}, bf16[2,1024,1024]{2,1,0:T(8,128)(2,1)S(1)}) custom-call(s32[1]{0:T(128)} %bitcast.refs_0_.refs_8_.refs_9_, s32[1]{0:T(128)S(6)} %copy.31.refs_1_, bf16[3,1024,256]{2,1,0:T(8,128)(2,1)S(1)} %get-tuple-element.303.refs_2_.refs_3_.refs_4_.refs_1_, ...), custom_call_target="tpu_custom_call" | custom-call | tf_op jit(solution)/shard_map/attend/pallas_call | solution.py:269
  99.3 8.4 %collective-permute-done.38.refs_7_ = bf16[256,1024]{1,0:T(8,128)(2,1)} collective-permute-done((bf16[256,1024]{1,0:T(8,128)(2,1)}, bf16[256,1024]{1,0:T(8,128)(2,1)}, u32[]{:S(2)}, u32[]{:S(2)}) %collective-permute-start.38) | collective-permute-done | bytes 524320 | tf_op jit(solution)/shard_map/ppermute | solution.py:1056
  112.5 6.5 %collective-permute-done.43.refs_10_.refs_12_ = bf16[16,1024]{1,0:T(8,128)(2,1)S(1)} collective-permute-done((bf16[16,1024]{1,0:T(8,128)(2,1)S(1)}, bf16[16,1024]{1,0:T(8,128)(2,1)S(1)}, u32[]{:S(2)}, u32[]{:S(2)}) %collective-permute-start.43) | collective-permute-done | bytes 32800 | tf_op jit(solution)/shard_map/ppermute | solution.py:1084
  123.5 3.7 collective-permute-done.45.refs_1_
  153.1 5.8 %collective-permute-done.61.refs_0_.refs_2_ = bf16[256,1024]{1,0:T(8,128)(2,1)S(1)} collective-permute-done((bf16[256,1024]{1,0:T(8,128)(2,1)S(1)}, bf16[256,1024]{1,0:T(8,128)(2,1)S(1)}, u32[]{:S(2)}, u32[]{:S(2)}) %collective-permute-start.61) | collective-permute-done | bytes 524320 | tf_op jit(solution)/shard_map/ppermute | solution.py:1056
  166.4 3.6 collective-permute-done.71.refs_6_
  188.1 5.2 %collective-permute-done.88.refs_8_ = bf16[256,1024]{1,0:T(8,128)(2,1)S(1)} collective-permute-done((bf16[256,1024]{1,0:T(8,128)(2,1)S(1)}, bf16[256,1024]{1,0:T(8,128)(2,1)S(1)}, u32[]{:S(2)}, u32[]{:S(2)}) %collective-permute-start.88) | collective-permute-done | bytes 524320 | tf_op jit(solution)/shard_map/ppermute | solution.py:1056
  198.9 6.7 %collective-permute-done.93.refs_11_.refs_13_ = bf16[16,1024]{1,0:T(8,128)(2,1)S(1)} collective-permute-done((bf16[16,1024]{1,0:T(8,128)(2,1)S(1)}, bf16[16,1024]{1,0:T(8,128)(2,1)S(1)}, u32[]{:S(2)}, u32[]{:S(2)}) %collective-permute-start.93) | collective-permute-done | bytes 32800 | tf_op jit(solution)/shard_map/ppermute | solution.py:1084
  208.9 4.5 ffn_two_w.1
  215.8 3.7 collective-permute-done.95.refs_1_
  230.1 4.2 collective-permute-done.98.refs_1_
  241.8 3.1 conv_din.1
  249.5 14.1 %collective-permute-done.103.refs_0_.refs_2_ = bf16[256,1024]{1,0:T(8,128)(2,1)S(1)} collective-permute-done((bf16[256,1024]{1,0:T(8,128)(2,1)S(1)}, bf16[256,1024]{1,0:T(8,128)(2,1)S(1)}, u32[]{:S(2)}, u32[]{:S(2)}) %collective-permute-start.103) | collective-permute-done | bytes 524320 | tf_op jit(solution)/shard_map/ppermute | solution.py:1056
  270.2 14.6 %attend_back.1 = (bf16[3,1024,256]{2,1,0:T(8,128)(2,1)S(1)}, f32[128,128]{1,0:T(8,128)S(1)}) custom-call(s32[1]{0:T(128)} %bitcast.refs_0_.refs_8_.refs_9_, bf16[3,1024,256]{2,1,0:T(8,128)(2,1)S(1)} %get-tuple-element.303.refs_2_.refs_3_.refs_4_.refs_1_, bf16[3,1024,256]{2,1,0:T(8,128)(2,1)S(1)} %get-tuple-element.303.refs_2_.refs_3_.refs_4_.refs_1_, ...), custom_call_target="tpu_custom_call" | custom-call | tf_op jit(solution)/shard_map/attend_back/pallas_call | solution.py:269
  294.9 6.8 %collective-permute-done.120.refs_11_ = bf16[1024,256]{1,0:T(8,128)(2,1)S(1)} collective-permute-done((bf16[1024,256]{1,0:T(8,128)(2,1)S(1)}, bf16[1024,256]{1,0:T(8,128)(2,1)S(1)}, u32[]{:S(2)}, u32[]{:S(2)}) %collective-permute-start.120) | collective-permute-done | bytes 524320 | tf_op jit(solution)/shard_map/ppermute | solution.py:1056
  308.9 12.8 %collective-permute-done.118.refs_4_ = bf16[256,1024]{1,0:T(8,128)(2,1)S(1)} collective-permute-done((bf16[256,1024]{1,0:T(8,128)(2,1)S(1)}, bf16[256,1024]{1,0:T(8,128)(2,1)S(1)}, u32[]{:S(2)}, u32[]{:S(2)}) %collective-permute-start.118) | collective-permute-done | bytes 524320 | tf_op jit(solution)/shard_map/ppermute | solution.py:1056
  349.6 9.1 %collective-permute-done.141.refs_3_ = bf16[512,512]{1,0:T(8,128)(2,1)S(1)} collective-permute-done((bf16[512,512]{1,0:T(8,128)(2,1)S(1)}, bf16[512,512]{1,0:T(8,128)(2,1)S(1)}, u32[]{:S(2)}, u32[]{:S(2)}) %collective-permute-start.141) | collective-permute-done | bytes 524320 | tf_op jit(solution)/shard_map/ppermute | solution.py:1059
  361.4 15.3 %collective-permute-done.138.refs_1_ = bf16[512,512]{1,0:T(8,128)(2,1)S(1)} collective-permute-done((bf16[512,512]{1,0:T(8,128)(2,1)S(1)}, bf16[512,512]{1,0:T(8,128)(2,1)S(1)}, u32[]{:S(2)}, u32[]{:S(2)}) %collective-permute-start.138) | collective-permute-done | bytes 524320 | tf_op jit(solution)/shard_map/ppermute | solution.py:1059
  404.7 3.2 collective-permute-done.143.refs_1_
  412.2 3.1 collective-permute-done.149.refs_1_
  424.8 10.8 %collective-permute-done.154.refs_5_ = bf16[128,512]{1,0:T(8,128)(2,1)S(1)} collective-permute-done((bf16[128,512]{1,0:T(8,128)(2,1)S(1)}, bf16[128,512]{1,0:T(8,128)(2,1)S(1)}, u32[]{:S(2)}, u32[]{:S(2)}) %collective-permute-start.154) | collective-permute-done | bytes 131104 | tf_op jit(solution)/shard_map/ppermute | solution.py:1059
  (621 shorter events, 272.8 us)
Async XLA Ops:
  7.2 86.4 %all-gather.2.cloned.1.call-start = ((), (), s32[]{:S(2)}) async-start(), calls=%async_computation.2 | async-start | bytes 1769472 | tf_op jit(solution)/shard_map/all_gather | solution.py:1312
  10.1 19.4 %collective-permute-start.8 = (bf16[256,1024]{1,0:T(8,128)(2,1)}, bf16[256,1024]{1,0:T(8,128)(2,1)}, u32[]{:S(2)}, u32[]{:S(2)}) collective-permute-start(bf16[256,1024]{1,0:T(8,128)(2,1)} %get-tuple-element.280), channel_id=1, source_target_pairs={{0,2},{1,3},{2,0},{3,1},{4,6},{5,7},{6,4},{7,5},{8,10},{9,11},{10,... | collective-permute-start | bytes 1572872 | tf_op jit(solution)/shard_map/ppermute | solution.py:1056
  39.6 346.4 %reduce-scatter.3.cloned.1.call-start = ((), (), s32[]{:S(2)}) async-start(), calls=%async_computation.3 | async-start | bytes 4718592 | tf_op jit(solution)/shard_map/reduce_scatter | solution.py:1062
  70.3 19.4 %collective-permute-start.28 = (bf16[256,1024]{1,0:T(8,128)(2,1)}, bf16[256,1024]{1,0:T(8,128)(2,1)}, u32[]{:S(2)}, u32[]{:S(2)}) collective-permute-start(bf16[256,1024]{1,0:T(8,128)(2,1)} %get-tuple-element.307), channel_id=1, source_target_pairs={{0,2},{1,3},{2,0},{3,1},{4,6},{5,7},{6,4},{7,5},{8,10},{9,11},{10,... | collective-permute-start | bytes 1572872 | tf_op jit(solution)/shard_map/ppermute | solution.py:1056
  151.2 18.8 %collective-permute-start.71 = (bf16[256,1024]{1,0:T(8,128)(2,1)S(1)}, bf16[256,1024]{1,0:T(8,128)(2,1)S(1)}, u32[]{:S(2)}, u32[]{:S(2)}) collective-permute-start(bf16[256,1024]{1,0:T(8,128)(2,1)S(1)} %ffn_two_sum.2.refs_2_.refs_5_), channel_id=1, source_target_pairs={{0,2},{1,3},{2,0},{3,1},{4,6},{5,7},{6,4},{7,5},{8,10},{9,11},{10,... | collective-permute-start | bytes 1572872 | tf_op jit(solution)/shard_map/ppermute | solution.py:1056
  215.5 230.3 %reduce-scatter.5.cloned.1.call-start = ((), (), s32[]{:S(2)}) async-start(), calls=%async_computation.4 | async-start | bytes 4128768 | tf_op jit(solution)/shard_map/reduce_scatter | solution.py:1062
  264.9 36.8 %collective-permute-start.119 = (bf16[1024,512]{1,0:T(8,128)(2,1)S(1)}, bf16[1024,512]{1,0:T(8,128)(2,1)S(1)}, u32[]{:S(2)}, u32[]{:S(2)}) collective-permute-start(bf16[1024,512]{1,0:T(8,128)(2,1)S(1)} %get-tuple-element.437), channel_id=1, source_target_pairs={{0,2},{1,3},{2,0},{3,1},{4,6},{5,7},{6,4},{7,5},{8,10},{9,11},{10,... | collective-permute-start | bytes 3145736 | tf_op jit(solution)/shard_map/ppermute | solution.py:1056
  308.1 24.3 %collective-permute-start.117 = (bf16[256,1024]{1,0:T(8,128)(2,1)S(1)}, bf16[256,1024]{1,0:T(8,128)(2,1)S(1)}, u32[]{:S(2)}, u32[]{:S(2)}) collective-permute-start(bf16[256,1024]{1,0:T(8,128)(2,1)S(1)} %dqkv_sum.3.refs_12_.refs_3_), channel_id=1, source_target_pairs={{0,2},{1,3},{2,0},{3,1},{4,6},{5,7},{6,4},{7,5},{8,10},{9,11},{10,... | collective-permute-start | bytes 1572872 | tf_op jit(solution)/shard_map/ppermute | solution.py:1056
  341.4 17.4 %collective-permute-start.141 = (bf16[512,512]{1,0:T(8,128)(2,1)S(1)}, bf16[512,512]{1,0:T(8,128)(2,1)S(1)}, u32[]{:S(2)}, u32[]{:S(2)}) collective-permute-start(bf16[512,512]{1,0:T(8,128)(2,1)S(1)} %get-tuple-element.484), channel_id=1, source_target_pairs={{0,8},{4,12},{8,0},{12,4},{16,24},{20,28},{24,16},{28,20},{1,9},{5... | collective-permute-start | bytes 1572872 | tf_op jit(solution)/shard_map/ppermute | solution.py:1059
  341.5 20.0 %collective-permute-start.140 = (bf16[512,512]{1,0:T(8,128)(2,1)S(1)}, bf16[512,512]{1,0:T(8,128)(2,1)S(1)}, u32[]{:S(2)}, u32[]{:S(2)}) collective-permute-start(bf16[512,512]{1,0:T(8,128)(2,1)S(1)} %get-tuple-element.482), channel_id=1, source_target_pairs={{0,4},{4,0},{8,12},{12,8},{16,20},{20,16},{24,28},{28,24},{1,5},{5... | collective-permute-start | bytes 1572872 | tf_op jit(solution)/shard_map/ppermute | solution.py:1059
  344.3 32.4 %collective-permute-start.138 = (bf16[512,512]{1,0:T(8,128)(2,1)S(1)}, bf16[512,512]{1,0:T(8,128)(2,1)S(1)}, u32[]{:S(2)}, u32[]{:S(2)}) collective-permute-start(bf16[512,512]{1,0:T(8,128)(2,1)S(1)} %get-tuple-element.477), channel_id=1, source_target_pairs={{0,4},{4,0},{8,12},{12,8},{16,20},{20,16},{24,28},{28,24},{1,5},{5... | collective-permute-start | bytes 1572872 | tf_op jit(solution)/shard_map/ppermute | solution.py:1059
  346.2 30.5 %collective-permute-start.139 = (bf16[512,512]{1,0:T(8,128)(2,1)S(1)}, bf16[512,512]{1,0:T(8,128)(2,1)S(1)}, u32[]{:S(2)}, u32[]{:S(2)}) collective-permute-start(bf16[512,512]{1,0:T(8,128)(2,1)S(1)} %get-tuple-element.480), channel_id=1, source_target_pairs={{0,8},{4,12},{8,0},{12,4},{16,24},{20,28},{24,16},{28,20},{1,9},{5... | collective-permute-start | bytes 1572872 | tf_op jit(solution)/shard_map/ppermute | solution.py:1059
  348.3 40.4 %collective-permute-start.137 = (bf16[256,1024]{1,0:T(8,128)(2,1)}, bf16[256,1024]{1,0:T(8,128)(2,1)}, u32[]{:S(2)}, u32[]{:S(2)}) collective-permute-start(bf16[256,1024]{1,0:T(8,128)(2,1)} %ffn_one_grad_sum.1.refs_5_), channel_id=1, source_target_pairs={{0,2},{1,3},{2,0},{3,1},{4,6},{5,7},{6,4},{7,5},{8,10},{9,11},{10,... | collective-permute-start | bytes 1572872 | tf_op jit(solution)/shard_map/ppermute | solution.py:1056
  358.7 21.9 %collective-permute-start.133 = (bf16[64,1024]{1,0:T(8,128)(2,1)S(1)}, bf16[64,1024]{1,0:T(8,128)(2,1)S(1)}, u32[]{:S(2)}, u32[]{:S(2)}) collective-permute-start(bf16[64,1024]{1,0:T(8,128)(2,1)S(1)} %get-tuple-element.462), channel_id=1, source_target_pairs={{0,1},{1,0},{2,3},{3,2},{4,5},{5,4},{6,7},{7,6},{8,9},{9,8},{10,11... | collective-permute-start | bytes 393224 | tf_op jit(solution)/shard_map/ppermute | solution.py:1050
  361.4 20.8 %collective-permute-start.134 = (bf16[64,1024]{1,0:T(8,128)(2,1)S(1)}, bf16[64,1024]{1,0:T(8,128)(2,1)S(1)}, u32[]{:S(2)}, u32[]{:S(2)}) collective-permute-start(bf16[64,1024]{1,0:T(8,128)(2,1)S(1)} %get-tuple-element.463), channel_id=1, source_target_pairs={{0,1},{1,0},{2,3},{3,2},{4,5},{5,4},{6,7},{7,6},{8,9},{9,8},{10,11... | collective-permute-start | bytes 393224 | tf_op jit(solution)/shard_map/ppermute | solution.py:1050
  380.6 27.3 %collective-permute-start.147 = (bf16[256,512]{1,0:T(8,128)(2,1)}, bf16[256,512]{1,0:T(8,128)(2,1)}, u32[]{:S(2)}, u32[]{:S(2)}) collective-permute-start(bf16[256,512]{1,0:T(8,128)(2,1)} %get-tuple-element.503), channel_id=1, source_target_pairs={{0,8},{4,12},{8,0},{12,4},{16,24},{20,28},{24,16},{28,20},{1,9},{5... | collective-permute-start | bytes 786440 | tf_op jit(solution)/shard_map/ppermute | solution.py:1059
  382.3 25.6 %collective-permute-start.148 = (bf16[256,512]{1,0:T(8,128)(2,1)}, bf16[256,512]{1,0:T(8,128)(2,1)}, u32[]{:S(2)}, u32[]{:S(2)}) collective-permute-start(bf16[256,512]{1,0:T(8,128)(2,1)} %get-tuple-element.505), channel_id=1, source_target_pairs={{0,4},{4,0},{8,12},{12,8},{16,20},{20,16},{24,28},{28,24},{1,5},{5... | collective-permute-start | bytes 786440 | tf_op jit(solution)/shard_map/ppermute | solution.py:1059
  384.4 25.1 %collective-permute-start.145 = (bf16[256,512]{1,0:T(8,128)(2,1)}, bf16[256,512]{1,0:T(8,128)(2,1)}, u32[]{:S(2)}, u32[]{:S(2)}) collective-permute-start(bf16[256,512]{1,0:T(8,128)(2,1)} %get-tuple-element.499), channel_id=1, source_target_pairs={{0,8},{4,12},{8,0},{12,4},{16,24},{20,28},{24,16},{28,20},{1,9},{5... | collective-permute-start | bytes 786440 | tf_op jit(solution)/shard_map/ppermute | solution.py:1059
  385.4 24.1 %collective-permute-start.146 = (bf16[256,512]{1,0:T(8,128)(2,1)}, bf16[256,512]{1,0:T(8,128)(2,1)}, u32[]{:S(2)}, u32[]{:S(2)}) collective-permute-start(bf16[256,512]{1,0:T(8,128)(2,1)} %get-tuple-element.501), channel_id=1, source_target_pairs={{0,4},{4,0},{8,12},{12,8},{16,20},{20,16},{24,28},{28,24},{1,5},{5... | collective-permute-start | bytes 786440 | tf_op jit(solution)/shard_map/ppermute | solution.py:1059
  416.7 18.8 %collective-permute-start.154 = (bf16[128,512]{1,0:T(8,128)(2,1)S(1)}, bf16[128,512]{1,0:T(8,128)(2,1)S(1)}, u32[]{:S(2)}, u32[]{:S(2)}) collective-permute-start(bf16[128,512]{1,0:T(8,128)(2,1)S(1)} %get-tuple-element.514), channel_id=1, source_target_pairs={{0,16},{4,20},{8,24},{12,28},{16,0},{20,4},{24,8},{28,12},{1,17},{... | collective-permute-start | bytes 393224 | tf_op jit(solution)/shard_map/ppermute | solution.py:1059
  418.8 19.5 %collective-permute-start.155 = (bf16[128,512]{1,0:T(8,128)(2,1)S(1)}, bf16[128,512]{1,0:T(8,128)(2,1)S(1)}, u32[]{:S(2)}, u32[]{:S(2)}) collective-permute-start(bf16[128,512]{1,0:T(8,128)(2,1)S(1)} %get-tuple-element.516), channel_id=1, source_target_pairs={{0,16},{4,20},{8,24},{12,28},{16,0},{20,4},{24,8},{28,12},{1,17},{... | collective-permute-start | bytes 393224 | tf_op jit(solution)/shard_map/ppermute | solution.py:1059
  419.6 21.5 %collective-permute-start.152 = (bf16[128,512]{1,0:T(8,128)(2,1)S(1)}, bf16[128,512]{1,0:T(8,128)(2,1)S(1)}, u32[]{:S(2)}, u32[]{:S(2)}) collective-permute-start(bf16[128,512]{1,0:T(8,128)(2,1)S(1)} %get-tuple-element.510), channel_id=1, source_target_pairs={{0,16},{4,20},{8,24},{12,28},{16,0},{20,4},{24,8},{28,12},{1,17},{... | collective-permute-start | bytes 393224 | tf_op jit(solution)/shard_map/ppermute | solution.py:1059
  421.8 22.2 %collective-permute-start.153 = (bf16[128,512]{1,0:T(8,128)(2,1)S(1)}, bf16[128,512]{1,0:T(8,128)(2,1)S(1)}, u32[]{:S(2)}, u32[]{:S(2)}) collective-permute-start(bf16[128,512]{1,0:T(8,128)(2,1)S(1)} %get-tuple-element.512), channel_id=1, source_target_pairs={{0,16},{4,20},{8,24},{12,28},{16,0},{20,4},{24,8},{28,12},{1,17},{... | collective-permute-start | bytes 393224 | tf_op jit(solution)/shard_map/ppermute | solution.py:1059
  422.6 22.5 %collective-permute-start.151 = (f32[184,128]{1,0:T(8,128)S(1)}, f32[184,128]{1,0:T(8,128)S(1)}, u32[]{:S(2)}, u32[]{:S(2)}) collective-permute-start(f32[184,128]{1,0:T(8,128)S(1)} %bundle_sum.8.refs_0_), channel_id=1, source_target_pairs={{0,16},{4,20},{8,24},{12,28},{16,0},{20,4},{24,8},{28,12},{1,17},{... | collective-permute-start | bytes 282632 | tf_op jit(solution)/shard_map/ppermute | solution.py:1059
  (254 other events, 1130.3 us)
Sparse Core Ops, SparseCore 0:
  39.7 45.6 all-gather.1
  215.6 89.1 reduce-scatter.2
  308.9 100.0 reduce-scatter.4

commit v5 on v4

--- a/solution.py
+++ b/solution.py
@@ -765,30 +765,44 @@
     return run(kernel, [((width, total), bf16)], ins, after, name, room=36, work=work, mark=True)[0]
 
 
-def outer_halves(links, jobs, turn, name, after=()):
+def outer_halves(links, jobs, turn, name, after=(), sums=()):
     offsets, masks = links.offsets(turn)
-    width = jobs[0][0][0].shape[1]
+    width = jobs[0][0][0].shape[1] if jobs else sums[0][0].shape[0]
     share = width // links.dp
     me = lax.axis_index("dp").reshape(1).astype(jnp.int32)
 
     plan, ins = lay_out(jobs)
-    ins = [me] + ins
-    total = sum(cols for _, _, cols in plan)
+    products = len(ins)
+    ins = [me] + ins + [array for parts in sums for array in parts]
+    total = sum(cols for _, _, cols in plan) + sum(parts[0].shape[1] for parts in sums)
     half = len(offsets)
 
     def kernel(me_ref, *refs):
         who = me_ref[0]
         sent_ref, kept_ref = refs[-2], refs[-1]
+        ways = ((masks[0], sent_ref), (0, kept_ref))
         column = 0
+
+        def block(off):
+            return pl.ds(pl.multiple_of((who ^ off) * share, 128), share)
+
         for left, rights, cols in sides(plan, refs):
-            for flip, dest in ((masks[0], sent_ref), (0, kept_ref)):
+            for flip, dest in ways:
                 picked = []
                 for off in offsets:
-                    where = pl.ds(pl.multiple_of((who ^ off ^ flip) * share, 128), share)
-                    parts = [ref[:, where] for ref in left]
+                    parts = [ref[:, block(off ^ flip)] for ref in left]
                     picked.append(parts[0] if len(parts) == 1 else jnp.concatenate(parts, axis=0))
                 picked = picked[0] if half == 1 else jnp.concatenate(picked, axis=1)
                 dest[:, column : column + cols] = tn(picked, rights).astype(bf16)
+            column = column + cols
+        at = products
+        for parts in sums:
+            cols = parts[0].shape[1]
+            for flip, dest in ways:
+                for i, off in enumerate(offsets):
+                    value = total_of([ref.at[block(off ^ flip), :] for ref in refs[at : at + len(parts)]])
+                    dest[i * share : (i + 1) * share, column : column + cols] = value.astype(bf16)
+            at = at + len(parts)
             column = column + cols
 
     return run(
@@ -1094,10 +1108,10 @@
 
 
 class Pieces:
-    def __init__(self, links, pieces, name):
+    def __init__(self, links, pieces, turns, name):
         self.links, self.name = links, name
         self.count = len(pieces)
-        self.masks = [links.offsets(i % 2)[1] for i in range(self.count)]
+        self.masks = [links.offsets(turn)[1] for turn in turns]
         self.kept = [kept for _, kept in pieces]
         self.at = 0
         self.send([sent for sent, _ in pieces])
@@ -1142,19 +1156,22 @@
     return run(kernel, [((2, share, hidden), f32)], [total], after, name, mark=True)[0]
 
 
-def split_heads(total, cols, channels, name):
-    share = total.shape[0]
-
-    def kernel(ref, three, one, conv):
-        value = wide(ref)
+def split_heads(ins, cols, channels, name, after=()):
+    share = ins[0].shape[0]
+
+    def kernel(*refs):
+        three, one, conv = refs[-3:]
+        if len(ins) == 1:
+            value, rest = wide(refs[0]), wide(refs[0])[:, 4 * cols :]
+        else:
+            value, rest = wide(refs[0]) + wide(refs[1]), wide(refs[2]) + wide(refs[3])
         for m in range(3):
             three[m] = value[:, m * cols : (m + 1) * cols]
-            at = 4 * cols + m * channels
-            conv[m] = value[:, at : at + channels]
+            conv[m] = rest[:, m * channels : (m + 1) * channels]
         one[...] = value[:, 3 * cols : 4 * cols]
 
     outs = [((3, share, cols), f32), ((share, cols), f32), ((3, share, channels), f32)]
-    return run(kernel, outs, [total], (), name)
+    return run(kernel, outs, list(ins), after, name, mark=True)
 
 
 def pack_small(depthwise, bn_gain, bn_bias, name):
@@ -1297,6 +1314,10 @@
     def all_parts(sums, k):
         return [sums[k]] + [links.chip(sums[k ^ j], j) for j in others]
 
+    piece = own_share(conv_proj, me, share, "conv_share")
+    came = [links.chip(piece, k) for k in others]
+    gathered = [lax.all_gather(other, "dp", axis=0, tiled=True) for other in came]
+
     (normed, pieces), x_low = norm_rows(x_in, [], 0.0, gains, 0, "ln_in", keep=False, low=True)
     x_rows = [x_in] + [links.chip(x_low, k) for k in others]
     na_first, pre_first, hid_first, sums = {}, {}, {}, {}
@@ -1306,12 +1327,9 @@
             ((normed, pieces),) = norm_rows(
                 x_rows[k], [], 0.0, gains, 0, "ln_in", token + (small,), keep=False
             )
-        if k == 1:
-            piece = own_share(conv_proj, me, share, "conv_share", (normed,))
-            gathered = [
-                lax.all_gather(links.chip(piece, j), "dp", axis=0, tiled=True) for j in others
-            ]
-        parts, made = split(feed(normed, links.mate(pieces), ffn_first, "ffn_one"))
+        parts, made = split(
+            feed(normed, links.mate(pieces), ffn_first, "ffn_one", tuple(came) if k == 0 else ())
+        )
         pre_first[k], hid_first[k], na_first[k] = made
         sums[k] = send_sums(parts, "ffn_one_sum")
         token = (sums[k],)
@@ -1424,11 +1442,26 @@
             made.append(outer([([left], spans)], name, after))
         return [made[0]] + [links.chip(made[k], k) for k in others]
 
-    out_grad = by_chip(conv_up, [active], "conv_out_w", (two_sum,))
-    bn_grads = links.sum_stats(sums, channels, "bn_grad_sum", (two_sum,))
+    came = [links.chip(sums, k) for k in others]
+    bn_grads = add_stats(sums, came, channels, "bn_grad_sum", (two_sum,))
+    out_grad = by_chip(conv_up, [active], "conv_out_w", (bn_grads,))
+    bn_grads = links.sum_group(bn_grads, "bn_grad_sum")
     two_sum = links.scatter_grad(two_sum)
     grad_linear, grad_gate, *made = conv_in_grad(
-        who, lengths, dz, mixture, tallies, bn_grads, small, small, linear, gating, conv_w, rows, "conv_din"
+        who,
+        lengths,
+        dz,
+        mixture,
+        tallies,
+        bn_grads,
+        small,
+        small,
+        linear,
+        gating,
+        conv_w,
+        rows,
+        "conv_din",
+        tuple(out_grad[1:]),
     )
     parts, (tap_grad,) = split(made)
     (low, pieces), grad, gain_three = norm_grad(
@@ -1453,17 +1486,20 @@
         parts, _ = split(members_rows(members, attn_qkv, k, rows, "dqkv", token))
         sums[k] = send_sums(parts, "dqkv_sum")
         token = (sums[k],)
-    heads_sum = outer(
-        [
-            (every(na_attn), [[(members, m)] for m in range(3)]),
-            (every(upper_attn), [[heads_out]]),
-        ],
-        "attn_w",
-        token,
-        [in_grads, out_grad],
-    )
-    token = (heads_sum,)
-    heads_sum = links.scatter_grad(heads_sum)
+    heads_jobs = [
+        (every(na_attn), [[(members, m)] for m in range(3)]),
+        (every(upper_attn), [[heads_out]]),
+    ]
+    conv_grads = [in_grads, out_grad]
+    if halves_fit:
+        made = outer_halves(links, heads_jobs, 0, "attn_w", token)
+        halves = [made, outer_halves(links, [], 1, "conv_w", (made[0],), conv_grads)]
+        heads_sum = Pieces(links, halves, (0, 1), "heads")
+        token = (halves[1][0],)
+    else:
+        heads_sum = outer(heads_jobs, "attn_w", token, conv_grads)
+        token = (heads_sum,)
+        heads_sum = links.scatter_grad(heads_sum)
 
     upper, down, arrived = {}, {}, []
     for k in others + [0]:
@@ -1490,35 +1526,40 @@
             total = send_sums(parts, "ffn_one_grad_sum")
             arrived.append(links.chip(total, k))
             token = (total,)
+            if halves_fit and k == others[-1]:
+                token = (heads_sum.step(token),)
     hidden = ffn_first.shape[2]
     half = hidden // 2
     token = (parts[0],)
     pairs = []
     if halves_fit:
-        for left, right in ((every(upper), every(hid_first)), (every(na_first), every(down))):
+        sides_of = ((every(upper), every(hid_first), (0, 0)), (every(na_first), every(down), (1, 0)))
+        for left, right, turns in sides_of:
             halves = []
-            for turn in range(2):
-                columns = [(r, None, turn * half, (turn + 1) * half) for r in right]
+            for i, turn in enumerate(turns):
+                columns = [(r, None, i * half, (i + 1) * half) for r in right]
                 halves.append(outer_halves(links, [(left, [columns])], turn, "ffn_one_w", token))
                 token = (halves[-1][0],)
-            pairs.append(Pieces(links, halves, "one"))
+            pairs.append(Pieces(links, halves, turns, "one"))
     else:
         first_sum = outer(
             [(every(na_first), [every(down)]), (every(upper), [every(hid_first)])], "ffn_one_w", token
         )
         token = (first_sum,)
         first_sum = links.scatter_grad(first_sum)
+    if halves_fit:
+        token = (heads_sum.step(token),)
     for pair in pairs:
         token = (pair.step(token),)
-    last_sum = split_two(two_sum, hidden, "two_end", token)
+    heads_parts = heads_sum.finish() if halves_fit else [heads_sum]
+    qkv_sum, out_sum, conv_sum = split_heads(
+        heads_parts, attn_qkv.shape[2], channels, "heads_end", token
+    )
+    token = (out_sum,)
+    for pair in pairs[:1]:
+        token = (pair.step(token),)
     grad_input, gain_one = norm_grad(
-        x_in,
-        [parts[0], links.mate(parts[1])] + arrived,
-        gains,
-        0,
-        grad,
-        "back_ffn_one",
-        token + (last_sum,),
+        x_in, [parts[0], links.mate(parts[1])] + arrived, gains, 0, grad, "back_ffn_one", token
     )
 
     taps = add_stats(tap_grad, [links.chip(tap_grad, k) for k in others], channels, "taps_sum")
@@ -1527,10 +1568,10 @@
     for k in [1 << bit for bit in range(ny.bit_length() - 1)]:
         bundle = add_stats(bundle, [links.chip(bundle, k)], 0, "bundle_sum")
     token = (bundle,)
-    for _ in links.masks[2:]:
-        for pair in pairs:
-            token = (pair.step(token),)
+    for pair in pairs[1:]:
+        token = (pair.step(token),)
     bundle = with_taps(bundle, taps, channels, "pack_taps", token)
+    last_sum = split_two(two_sum, hidden, "two_end", token)
     for mask in links.masks:
         bundle = add_stats(bundle, [links.group(bundle, mask)], 0, "bundle_sum")
     norm_sums, table_sums, kernel_grad, gain_grad, bias_grad = unpack_sums(
@@ -1540,7 +1581,6 @@
         first_sum = finish_one(pairs[0].finish(), pairs[1].finish(), hidden, "one_end")
     else:
         first_sum = split_two(first_sum, hidden, "one_end")
-    qkv_sum, out_sum, conv_sum = split_heads(heads_sum, attn_qkv.shape[2], channels, "heads_end")
     return (
         output,
         grad_input,

time: 462 us -> 436 us (0.944)
  local copies, waits for them, and re-layouts: 64.3 us -> 34.8 us
  Pallas kernels: 108 us -> 97.7 us
  waiting for transfers between devices: 182 us -> 189 us
  starting transfers between devices: 84.2 us -> 91.1 us
    unnamed x239 -> x161, local copies, waits for them, and re-layouts: 64.3 us -> 34.8 us
    ppermute x21 -> x27, waiting for transfers between devices: 64.6 us -> 76.5 us  [group(): return lax.ppermute(value, 'dp', [(i, i ^ mask) for i in range(self.dp)])]
    pallas_call x84 -> x87, Pallas kernels: 108 us -> 97.7 us  [run(): pl.pallas_call(body, in_specs=specs + [pl.BlockSpec(memory_space=pl.ANY)]...]
    ppermute x21, waiting for transfers between devices: 82.5 us -> 75.2 us  [chip(): lax.ppermute(value, 'tensor', [(i, i ^ 2 * k) for i in range(self.tensor)])]
    ppermute x21 -> x27, starting transfers between devices: 31.4 us -> 38.4 us  [group(): return lax.ppermute(value, 'dp', [(i, i ^ mask) for i in range(self.dp)])]
  transfers between devices with their start and end apart: 159 -> 164, of which waited for: 105 -> 108; matrix products, arithmetic and copies ran while one was open for 0% -> 0% of each run, Pallas kernels for 20% -> 20%
where the time goes in v5:
time: 436 us; the launch traced here: 429 us
  waiting for transfers between devices  189 us (43%)
  Pallas kernels  97.7 us (22%)
  starting transfers between devices  91.1 us (21%)
  local copies, waits for them, and re-layouts  34.8 us (8%)
  between operations  16.2 us (4%)
    pallas_call x87, Pallas kernels, run(): pl.pallas_call(body, in_specs=specs + [pl.BlockSpec(memory_space=pl.ANY)]...  97.7 us
    ppermute x27, waiting for transfers between devices, group(): return lax.ppermute(value, 'dp', [(i, i ^ mask) for i in range(self.dp)])  76.5 us
    ppermute x21, waiting for transfers between devices, chip(): lax.ppermute(value, 'tensor', [(i, i ^ 2 * k) for i in range(self.tensor)])  75.2 us
    ppermute x27, starting transfers between devices, group(): return lax.ppermute(value, 'dp', [(i, i ^ mask) for i in range(self.dp)])  38.4 us
    unnamed x161, local copies, waits for them, and re-layouts  34.8 us
    ppermute x110, starting transfers between devices, core(): lax.ppermute(value, 'tensor', [(i, i ^ 1) for i in range(self.tensor)])  27.5 us
    ppermute x110, waiting for transfers between devices, core(): lax.ppermute(value, 'tensor', [(i, i ^ 1) for i in range(self.tensor)])  24.5 us
    ppermute x21, starting transfers between devices, chip(): lax.ppermute(value, 'tensor', [(i, i ^ 2 * k) for i in range(self.tensor)])  20.8 us
  transfers between devices with their start and end apart: 164, of which 108 were waited for; matrix products, arithmetic and copies ran while one was open for 0% of the time, Pallas kernels for 20%

profile of v5, /device:TPU:0, one launch (start us, length us, event | category | flops | bytes accessed | tf_op | source)
XLA Modules:
  0.0 429.4 jit_solution(12778584546875897207)
XLA Ops:
  11.8 4.9 %collective-permute-done.4.refs_7_ = bf16[384,256]{1,0:T(8,128)(2,1)S(1)} collective-permute-done((bf16[384,256]{1,0:T(8,128)(2,1)S(1)}, bf16[384,256]{1,0:T(8,128)(2,1)S(1)}, u32[]{:S(2)}, u32[]{:S(2)}) %collective-permute-start.4) | collective-permute-done | bytes 196640 | tf_op jit(solution)/shard_map/ppermute | solution.py:1070
  41.5 7.4 %collective-permute-done.20.refs_3_ = bf16[256,1024]{1,0:T(8,128)(2,1)S(1)} collective-permute-done((bf16[256,1024]{1,0:T(8,128)(2,1)S(1)}, bf16[256,1024]{1,0:T(8,128)(2,1)S(1)}, u32[]{:S(2)}, u32[]{:S(2)}) %collective-permute-start.20) | collective-permute-done | bytes 524320 | tf_op jit(solution)/shard_map/ppermute | solution.py:1070
  54.0 5.3 %collective-permute-done.19.refs_3_ = bf16[256,1024]{1,0:T(8,128)(2,1)S(1)} collective-permute-done((bf16[256,1024]{1,0:T(8,128)(2,1)S(1)}, bf16[256,1024]{1,0:T(8,128)(2,1)S(1)}, u32[]{:S(2)}, u32[]{:S(2)}) %collective-permute-start.19) | collective-permute-done | bytes 524320 | tf_op jit(solution)/shard_map/ppermute | solution.py:1070
  70.8 8.6 %attend.1 = (bf16[1024,256]{1,0:T(8,128)(2,1)S(1)}, bf16[2,1024,1024]{2,1,0:T(8,128)(2,1)S(1)}) custom-call(s32[1]{0:T(128)} %bitcast.refs_0_.refs_8_.refs_9_, s32[1]{0:T(128)S(6)} %copy.31.refs_1_, bf16[3,1024,256]{2,1,0:T(8,128)(2,1)S(1)} %get-tuple-element.317.refs_2_.refs_3_.refs_4_.refs_1_, ...), custom_call_target="tpu_custom_call" | custom-call | tf_op jit(solution)/shard_map/attend/pallas_call | solution.py:269
  91.4 8.1 %collective-permute-done.38.refs_7_ = bf16[256,1024]{1,0:T(8,128)(2,1)} collective-permute-done((bf16[256,1024]{1,0:T(8,128)(2,1)}, bf16[256,1024]{1,0:T(8,128)(2,1)}, u32[]{:S(2)}, u32[]{:S(2)}) %collective-permute-start.38) | collective-permute-done | bytes 524320 | tf_op jit(solution)/shard_map/ppermute | solution.py:1070
  104.3 6.8 %collective-permute-done.43.refs_10_.refs_12_ = bf16[16,1024]{1,0:T(8,128)(2,1)S(1)} collective-permute-done((bf16[16,1024]{1,0:T(8,128)(2,1)S(1)}, bf16[16,1024]{1,0:T(8,128)(2,1)S(1)}, u32[]{:S(2)}, u32[]{:S(2)}) %collective-permute-start.43) | collective-permute-done | bytes 32800 | tf_op jit(solution)/shard_map/ppermute | solution.py:1098
  114.6 3.7 collective-permute-done.45.refs_1_
  143.4 5.8 %collective-permute-done.61.refs_0_.refs_2_ = bf16[256,1024]{1,0:T(8,128)(2,1)S(1)} collective-permute-done((bf16[256,1024]{1,0:T(8,128)(2,1)S(1)}, bf16[256,1024]{1,0:T(8,128)(2,1)S(1)}, u32[]{:S(2)}, u32[]{:S(2)}) %collective-permute-start.61) | collective-permute-done | bytes 524320 | tf_op jit(solution)/shard_map/ppermute | solution.py:1070
  156.6 3.7 collective-permute-done.71.refs_6_
  178.4 5.3 %collective-permute-done.88.refs_8_ = bf16[256,1024]{1,0:T(8,128)(2,1)S(1)} collective-permute-done((bf16[256,1024]{1,0:T(8,128)(2,1)S(1)}, bf16[256,1024]{1,0:T(8,128)(2,1)S(1)}, u32[]{:S(2)}, u32[]{:S(2)}) %collective-permute-start.88) | collective-permute-done | bytes 524320 | tf_op jit(solution)/shard_map/ppermute | solution.py:1070
  188.8 6.5 %collective-permute-done.93.refs_11_.refs_13_ = bf16[16,1024]{1,0:T(8,128)(2,1)S(1)} collective-permute-done((bf16[16,1024]{1,0:T(8,128)(2,1)S(1)}, bf16[16,1024]{1,0:T(8,128)(2,1)S(1)}, u32[]{:S(2)}, u32[]{:S(2)}) %collective-permute-start.93) | collective-permute-done | bytes 32800 | tf_op jit(solution)/shard_map/ppermute | solution.py:1098
  198.6 4.5 %ffn_two_w.1 = (bf16[1024,2048]{1,0:T(8,128)(2,1)S(1)}, f32[8,128]{1,0:T(8,128)S(1)}) custom-call(bf16[512,1024]{1,0:T(8,128)(2,1)S(1)} %get-tuple-element.405.refs_0_, bf16[512,1024]{1,0:T(8,128)(2,1)S(1)} %get-tuple-element.406.refs_1_, bf16[512,1024]{1,0:T(8,128)(2,1)S(1)} %get-tuple-element.407.refs_2_, ...), custom_call_target="tpu_custom_call" | custom-call | tf_op jit(solution)/shard_map/ffn_two_w/pallas_call | solution.py:269
  205.9 3.7 collective-permute-done.95.refs_1_
  224.3 3.5 collective-permute-done.98.refs_1_
  240.2 3.1 collective-permute-start.104
  243.3 12.4 %collective-permute-done.104.refs_0_.refs_2_ = bf16[256,1024]{1,0:T(8,128)(2,1)S(1)} collective-permute-done((bf16[256,1024]{1,0:T(8,128)(2,1)S(1)}, bf16[256,1024]{1,0:T(8,128)(2,1)S(1)}, u32[]{:S(2)}, u32[]{:S(2)}) %collective-permute-start.104) | collective-permute-done | bytes 524320 | tf_op jit(solution)/shard_map/ppermute | solution.py:1070
  263.6 14.8 %attend_back.1 = (bf16[3,1024,256]{2,1,0:T(8,128)(2,1)S(1)}, f32[128,128]{1,0:T(8,128)S(1)}) custom-call(s32[1]{0:T(128)} %bitcast.refs_0_.refs_8_.refs_9_, bf16[3,1024,256]{2,1,0:T(8,128)(2,1)S(1)} %get-tuple-element.317.refs_2_.refs_3_.refs_4_.refs_1_, bf16[3,1024,256]{2,1,0:T(8,128)(2,1)S(1)} %get-tuple-element.317.refs_2_.refs_3_.refs_4_.refs_1_, ...), custom_call_target="tpu_custom_call" | custom-call | tf_op jit(solution)/shard_map/attend_back/pallas_call | solution.py:269
  290.9 7.4 %collective-permute-done.122.refs_4_ = bf16[256,1024]{1,0:T(8,128)(2,1)S(1)} collective-permute-done((bf16[256,1024]{1,0:T(8,128)(2,1)S(1)}, bf16[256,1024]{1,0:T(8,128)(2,1)S(1)}, u32[]{:S(2)}, u32[]{:S(2)}) %collective-permute-start.122) | collective-permute-done | bytes 524320 | tf_op jit(solution)/shard_map/ppermute | solution.py:1070
  332.4 6.0 %collective-permute-done.140.refs_1_ = bf16[512,512]{1,0:T(8,128)(2,1)S(1)} collective-permute-done((bf16[512,512]{1,0:T(8,128)(2,1)S(1)}, bf16[512,512]{1,0:T(8,128)(2,1)S(1)}, u32[]{:S(2)}, u32[]{:S(2)}) %collective-permute-start.140) | collective-permute-done | bytes 524320 | tf_op jit(solution)/shard_map/ppermute | solution.py:1073
  338.6 11.0 %collective-permute-done.141.refs_3_ = bf16[512,512]{1,0:T(8,128)(2,1)S(1)} collective-permute-done((bf16[512,512]{1,0:T(8,128)(2,1)S(1)}, bf16[512,512]{1,0:T(8,128)(2,1)S(1)}, u32[]{:S(2)}, u32[]{:S(2)}) %collective-permute-start.141) | collective-permute-done | bytes 524320 | tf_op jit(solution)/shard_map/ppermute | solution.py:1073
  354.8 5.6 %collective-permute-done.149.refs_3_ = bf16[512,512]{1,0:T(8,128)(2,1)S(1)} collective-permute-done((bf16[512,512]{1,0:T(8,128)(2,1)S(1)}, bf16[512,512]{1,0:T(8,128)(2,1)S(1)}, u32[]{:S(2)}, u32[]{:S(2)}) %collective-permute-start.149) | collective-permute-done | bytes 524320 | tf_op jit(solution)/shard_map/ppermute | solution.py:1073
  362.9 9.3 %collective-permute-done.147.refs_3_ = bf16[128,768]{1,0:T(8,128)(2,1)S(1)} collective-permute-done((bf16[128,768]{1,0:T(8,128)(2,1)S(1)}, bf16[128,768]{1,0:T(8,128)(2,1)S(1)}, u32[]{:S(2)}, u32[]{:S(2)}) %collective-permute-start.147) | collective-permute-done | bytes 196640 | tf_op jit(solution)/shard_map/ppermute | solution.py:1073
  387.2 4.0 collective-permute-done.155.refs_1_
  399.3 11.6 %collective-permute-done.158.refs_1_ = bf16[128,512]{1,0:T(8,128)(2,1)S(1)} collective-permute-done((bf16[128,512]{1,0:T(8,128)(2,1)S(1)}, bf16[128,512]{1,0:T(8,128)(2,1)S(1)}, u32[]{:S(2)}, u32[]{:S(2)}) %collective-permute-start.158) | collective-permute-done | bytes 131104 | tf_op jit(solution)/shard_map/ppermute | solution.py:1073
  (555 shorter events, 250.0 us)
Async XLA Ops:
  7.2 78.5 %all-gather.2.cloned.1.call-start = ((), (), s32[]{:S(2)}) async-start(), calls=%async_computation.1 | async-start | bytes 1769472 | tf_op jit(solution)/shard_map/all_gather | solution.py:1319
  17.4 402.9 %reduce-scatter.2.cloned.1.call-start = ((), (), s32[]{:S(2)}) async-start(), calls=%async_computation.2 | async-start | bytes 4718592 | tf_op jit(solution)/shard_map/reduce_scatter | solution.py:1076
  40.3 19.0 %collective-permute-start.19 = (bf16[256,1024]{1,0:T(8,128)(2,1)S(1)}, bf16[256,1024]{1,0:T(8,128)(2,1)S(1)}, u32[]{:S(2)}, u32[]{:S(2)}) collective-permute-start(bf16[256,1024]{1,0:T(8,128)(2,1)S(1)} %ffn_one_sum.3.refs_2_), channel_id=1, source_target_pairs={{0,2},{1,3},{2,0},{3,1},{4,6},{5,7},{6,4},{7,5},{8,10},{9,11},{10,... | collective-permute-start | bytes 1572872 | tf_op jit(solution)/shard_map/ppermute | solution.py:1070
  62.5 19.0 %collective-permute-start.29 = (bf16[256,1024]{1,0:T(8,128)(2,1)}, bf16[256,1024]{1,0:T(8,128)(2,1)}, u32[]{:S(2)}, u32[]{:S(2)}) collective-permute-start(bf16[256,1024]{1,0:T(8,128)(2,1)} %get-tuple-element.321), channel_id=1, source_target_pairs={{0,2},{1,3},{2,0},{3,1},{4,6},{5,7},{6,4},{7,5},{8,10},{9,11},{10,... | collective-permute-start | bytes 1572872 | tf_op jit(solution)/shard_map/ppermute | solution.py:1070
  141.4 18.9 %collective-permute-start.71 = (bf16[256,1024]{1,0:T(8,128)(2,1)S(1)}, bf16[256,1024]{1,0:T(8,128)(2,1)S(1)}, u32[]{:S(2)}, u32[]{:S(2)}) collective-permute-start(bf16[256,1024]{1,0:T(8,128)(2,1)S(1)} %ffn_two_sum.2.refs_2_.refs_5_), channel_id=1, source_target_pairs={{0,2},{1,3},{2,0},{3,1},{4,6},{5,7},{6,4},{7,5},{8,10},{9,11},{10,... | collective-permute-start | bytes 1572872 | tf_op jit(solution)/shard_map/ppermute | solution.py:1070
  240.2 15.5 %collective-permute-start.104 = (bf16[256,1024]{1,0:T(8,128)(2,1)S(1)}, bf16[256,1024]{1,0:T(8,128)(2,1)S(1)}, u32[]{:S(2)}, u32[]{:S(2)}) collective-permute-start(bf16[256,1024]{1,0:T(8,128)(2,1)S(1)} %get-tuple-element.425.refs_3_.refs_0_), channel_id=1, source_target_pairs={{0,2},{1,3},{2,0},{3,1},{4,6},{5,7},{6,4},{7,5},{8,10},{9,11},{10,... | collective-permute-start | bytes 1572872 | tf_op jit(solution)/shard_map/ppermute | solution.py:1070
  257.0 32.1 %collective-permute-start.120 = (bf16[1024,512]{1,0:T(8,128)(2,1)S(1)}, bf16[1024,512]{1,0:T(8,128)(2,1)S(1)}, u32[]{:S(2)}, u32[]{:S(2)}) collective-permute-start(bf16[1024,512]{1,0:T(8,128)(2,1)S(1)} %get-tuple-element.455), channel_id=1, source_target_pairs={{0,2},{1,3},{2,0},{3,1},{4,6},{5,7},{6,4},{7,5},{8,10},{9,11},{10,... | collective-permute-start | bytes 3145736 | tf_op jit(solution)/shard_map/ppermute | solution.py:1070
  287.6 25.4 %collective-permute-start.119 = (bf16[512,1024]{1,0:T(8,128)(2,1)S(1)}, bf16[512,1024]{1,0:T(8,128)(2,1)S(1)}, u32[]{:S(2)}, u32[]{:S(2)}) collective-permute-start(bf16[512,1024]{1,0:T(8,128)(2,1)S(1)} %get-tuple-element.453), channel_id=1, source_target_pairs={{0,4},{4,0},{8,12},{12,8},{16,20},{20,16},{24,28},{28,24},{1,5},{5... | collective-permute-start | bytes 3145736 | tf_op jit(solution)/shard_map/ppermute | solution.py:1073
  289.5 21.1 %collective-permute-start.121 = (bf16[512,768]{1,0:T(8,128)(2,1)S(1)}, bf16[512,768]{1,0:T(8,128)(2,1)S(1)}, u32[]{:S(2)}, u32[]{:S(2)}) collective-permute-start(bf16[512,768]{1,0:T(8,128)(2,1)S(1)} %get-tuple-element.459), channel_id=1, source_target_pairs={{0,8},{4,12},{8,0},{12,4},{16,24},{20,28},{24,16},{28,20},{1,9},{5... | collective-permute-start | bytes 2359304 | tf_op jit(solution)/shard_map/ppermute | solution.py:1073
  322.8 15.6 %collective-permute-start.140 = (bf16[512,512]{1,0:T(8,128)(2,1)S(1)}, bf16[512,512]{1,0:T(8,128)(2,1)S(1)}, u32[]{:S(2)}, u32[]{:S(2)}) collective-permute-start(bf16[512,512]{1,0:T(8,128)(2,1)S(1)} %get-tuple-element.491), channel_id=1, source_target_pairs={{0,4},{4,0},{8,12},{12,8},{16,20},{20,16},{24,28},{28,24},{1,5},{5... | collective-permute-start | bytes 1572872 | tf_op jit(solution)/shard_map/ppermute | solution.py:1073
  324.7 24.9 %collective-permute-start.141 = (bf16[512,512]{1,0:T(8,128)(2,1)S(1)}, bf16[512,512]{1,0:T(8,128)(2,1)S(1)}, u32[]{:S(2)}, u32[]{:S(2)}) collective-permute-start(bf16[512,512]{1,0:T(8,128)(2,1)S(1)} %get-tuple-element.494), channel_id=1, source_target_pairs={{0,4},{4,0},{8,12},{12,8},{16,20},{20,16},{24,28},{28,24},{1,5},{5... | collective-permute-start | bytes 1572872 | tf_op jit(solution)/shard_map/ppermute | solution.py:1073
  326.2 26.5 %collective-permute-start.139 = (bf16[256,1024]{1,0:T(8,128)(2,1)S(1)}, bf16[256,1024]{1,0:T(8,128)(2,1)S(1)}, u32[]{:S(2)}, u32[]{:S(2)}) collective-permute-start(bf16[256,1024]{1,0:T(8,128)(2,1)S(1)} %ffn_one_grad_sum.1.refs_4_), channel_id=1, source_target_pairs={{0,2},{1,3},{2,0},{3,1},{4,6},{5,7},{6,4},{7,5},{8,10},{9,11},{10,... | collective-permute-start | bytes 1572872 | tf_op jit(solution)/shard_map/ppermute | solution.py:1070
  329.9 30.4 %collective-permute-start.149 = (bf16[512,512]{1,0:T(8,128)(2,1)S(1)}, bf16[512,512]{1,0:T(8,128)(2,1)S(1)}, u32[]{:S(2)}, u32[]{:S(2)}) collective-permute-start(bf16[512,512]{1,0:T(8,128)(2,1)S(1)} %get-tuple-element.518), channel_id=1, source_target_pairs={{0,4},{4,0},{8,12},{12,8},{16,20},{20,16},{24,28},{28,24},{1,5},{5... | collective-permute-start | bytes 1572872 | tf_op jit(solution)/shard_map/ppermute | solution.py:1073
  330.5 32.4 %collective-permute-start.148 = (bf16[512,512]{1,0:T(8,128)(2,1)S(1)}, bf16[512,512]{1,0:T(8,128)(2,1)S(1)}, u32[]{:S(2)}, u32[]{:S(2)}) collective-permute-start(bf16[512,512]{1,0:T(8,128)(2,1)S(1)} %get-tuple-element.516), channel_id=1, source_target_pairs={{0,8},{4,12},{8,0},{12,4},{16,24},{20,28},{24,16},{28,20},{1,9},{5... | collective-permute-start | bytes 1572872 | tf_op jit(solution)/shard_map/ppermute | solution.py:1073
  338.4 15.4 %collective-permute-start.135 = (bf16[64,1024]{1,0:T(8,128)(2,1)S(1)}, bf16[64,1024]{1,0:T(8,128)(2,1)S(1)}, u32[]{:S(2)}, u32[]{:S(2)}) collective-permute-start(bf16[64,1024]{1,0:T(8,128)(2,1)S(1)} %get-tuple-element.482), channel_id=1, source_target_pairs={{0,1},{1,0},{2,3},{3,2},{4,5},{5,4},{6,7},{7,6},{8,9},{9,8},{10,11... | collective-permute-start | bytes 393224 | tf_op jit(solution)/shard_map/ppermute | solution.py:1064
  349.6 22.7 %collective-permute-start.146 = (bf16[128,1024]{1,0:T(8,128)(2,1)S(1)}, bf16[128,1024]{1,0:T(8,128)(2,1)S(1)}, u32[]{:S(2)}, u32[]{:S(2)}) collective-permute-start(bf16[128,1024]{1,0:T(8,128)(2,1)S(1)} %get-tuple-element.512), channel_id=1, source_target_pairs={{0,16},{4,20},{8,24},{12,28},{16,0},{20,4},{24,8},{28,12},{1,17},{... | collective-permute-start | bytes 786440 | tf_op jit(solution)/shard_map/ppermute | solution.py:1073
  352.7 20.3 %collective-permute-start.144 = (bf16[256,512]{1,0:T(8,128)(2,1)S(1)}, bf16[256,512]{1,0:T(8,128)(2,1)S(1)}, u32[]{:S(2)}, u32[]{:S(2)}) collective-permute-start(bf16[256,512]{1,0:T(8,128)(2,1)S(1)} %get-tuple-element.508), channel_id=1, source_target_pairs={{0,8},{4,12},{8,0},{12,4},{16,24},{20,28},{24,16},{28,20},{1,9},{5... | collective-permute-start | bytes 786440 | tf_op jit(solution)/shard_map/ppermute | solution.py:1073
  353.8 20.2 %collective-permute-start.145 = (bf16[256,512]{1,0:T(8,128)(2,1)S(1)}, bf16[256,512]{1,0:T(8,128)(2,1)S(1)}, u32[]{:S(2)}, u32[]{:S(2)}) collective-permute-start(bf16[256,512]{1,0:T(8,128)(2,1)S(1)} %get-tuple-element.510), channel_id=1, source_target_pairs={{0,8},{4,12},{8,0},{12,4},{16,24},{20,28},{24,16},{28,20},{1,9},{5... | collective-permute-start | bytes 786440 | tf_op jit(solution)/shard_map/ppermute | solution.py:1073
  362.9 15.1 %collective-permute-start.136 = (bf16[64,1024]{1,0:T(8,128)(2,1)S(1)}, bf16[64,1024]{1,0:T(8,128)(2,1)S(1)}, u32[]{:S(2)}, u32[]{:S(2)}) collective-permute-start(bf16[64,1024]{1,0:T(8,128)(2,1)S(1)} %get-tuple-element.483), channel_id=1, source_target_pairs={{0,1},{1,0},{2,3},{3,2},{4,5},{5,4},{6,7},{7,6},{8,9},{9,8},{10,11... | collective-permute-start | bytes 393224 | tf_op jit(solution)/shard_map/ppermute | solution.py:1064
  391.3 19.7 %collective-permute-start.158 = (bf16[128,512]{1,0:T(8,128)(2,1)S(1)}, bf16[128,512]{1,0:T(8,128)(2,1)S(1)}, u32[]{:S(2)}, u32[]{:S(2)}) collective-permute-start(bf16[128,512]{1,0:T(8,128)(2,1)S(1)} %get-tuple-element.538), channel_id=1, source_target_pairs={{0,16},{4,20},{8,24},{12,28},{16,0},{20,4},{24,8},{28,12},{1,17},{... | collective-permute-start | bytes 393224 | tf_op jit(solution)/shard_map/ppermute | solution.py:1073
  393.4 20.3 %collective-permute-start.159 = (bf16[128,512]{1,0:T(8,128)(2,1)S(1)}, bf16[128,512]{1,0:T(8,128)(2,1)S(1)}, u32[]{:S(2)}, u32[]{:S(2)}) collective-permute-start(bf16[128,512]{1,0:T(8,128)(2,1)S(1)} %get-tuple-element.540), channel_id=1, source_target_pairs={{0,16},{4,20},{8,24},{12,28},{16,0},{20,4},{24,8},{28,12},{1,17},{... | collective-permute-start | bytes 393224 | tf_op jit(solution)/shard_map/ppermute | solution.py:1073
  394.2 22.3 %collective-permute-start.160 = (bf16[128,512]{1,0:T(8,128)(2,1)S(1)}, bf16[128,512]{1,0:T(8,128)(2,1)S(1)}, u32[]{:S(2)}, u32[]{:S(2)}) collective-permute-start(bf16[128,512]{1,0:T(8,128)(2,1)S(1)} %get-tuple-element.542), channel_id=1, source_target_pairs={{0,16},{4,20},{8,24},{12,28},{16,0},{20,4},{24,8},{28,12},{1,17},{... | collective-permute-start | bytes 393224 | tf_op jit(solution)/shard_map/ppermute | solution.py:1073
  396.3 22.2 %collective-permute-start.161 = (bf16[128,512]{1,0:T(8,128)(2,1)S(1)}, bf16[128,512]{1,0:T(8,128)(2,1)S(1)}, u32[]{:S(2)}, u32[]{:S(2)}) collective-permute-start(bf16[128,512]{1,0:T(8,128)(2,1)S(1)} %get-tuple-element.544), channel_id=1, source_target_pairs={{0,16},{4,20},{8,24},{12,28},{16,0},{20,4},{24,8},{28,12},{1,17},{... | collective-permute-start | bytes 393224 | tf_op jit(solution)/shard_map/ppermute | solution.py:1073
  397.2 22.4 %collective-permute-start.157 = (f32[184,128]{1,0:T(8,128)S(1)}, f32[184,128]{1,0:T(8,128)S(1)}, u32[]{:S(2)}, u32[]{:S(2)}) collective-permute-start(f32[184,128]{1,0:T(8,128)S(1)} %bundle_sum.8.refs_0_), channel_id=1, source_target_pairs={{0,16},{4,20},{8,24},{12,28},{16,0},{20,4},{24,8},{28,12},{1,17},{... | collective-permute-start | bytes 282632 | tf_op jit(solution)/shard_map/ppermute | solution.py:1073
  (220 other events, 1164.6 us)
Sparse Core Ops, SparseCore 0:
  17.5 45.6 all-gather.1
  205.9 89.3 reduce-scatter.1

commit v6 on v5

--- a/solution.py
+++ b/solution.py
@@ -469,6 +469,16 @@
     return run(kernel, [(value.shape, f32)], [value] + list(others), after, name)[0]
 
 
+def add_four(value, others, channels, name, after=()):
+    def kernel(a, b, c, d, out):
+        rest = c[...] + d[...]
+        if channels:
+            rest = jnp.concatenate([rest[:, channels:], rest[:, :channels]], axis=1)
+        out[...] = (a[...] + b[...]) + rest
+
+    return run(kernel, [(value.shape, f32)], [value] + others, after, name)[0]
+
+
 def tile_of(total, most):
     return most if total % most == 0 else total
 
@@ -1075,14 +1085,35 @@
     def scatter_grad(self, value):
         return lax.psum_scatter(value, "dp", scatter_dimension=0, tiled=True)
 
+    def two_rounds(self):
+        return self.ny == 2 and len(self.masks) == 3
+
+    def first_sums(self, value, channels, name, after=()):
+        if not self.two_rounds():
+            others = [self.chip(value, k) for k in range(1, self.ny)]
+            return add_stats(value, others, channels, name, after)
+        size = self.dp * self.tensor
+        far = [(i, i ^ (self.masks[0] * self.tensor + 2)) for i in range(size)]
+        others = [
+            self.group(value, self.masks[0]),
+            self.chip(value, 1),
+            lax.ppermute(value, ("dp", "tensor"), far),
+        ]
+        return add_four(value, others, channels, name, after)
+
+    def last_sums(self, value, name):
+        if not self.two_rounds():
+            return self.sum_group(value, name)
+        one, two = self.masks[1:]
+        return add_four(value, [self.group(value, mask) for mask in (one, two, one ^ two)], 0, name)
+
     def sum_group(self, value, name):
         for mask in self.masks:
             value = add_stats(value, [self.group(value, mask)], 0, name)
         return value
 
-    def sum_stats(self, value, channels, name, after=()):
-        others = [self.chip(value, k) for k in range(1, self.ny)]
-        return self.sum_group(add_stats(value, others, channels, name, after), name)
+    def sum_stats(self, value, channels, name):
+        return self.last_sums(self.first_sums(value, channels, name), name)
 
     def offsets(self, turn):
         masks = list(self.masks)
@@ -1442,10 +1473,9 @@
             made.append(outer([([left], spans)], name, after))
         return [made[0]] + [links.chip(made[k], k) for k in others]
 
-    came = [links.chip(sums, k) for k in others]
-    bn_grads = add_stats(sums, came, channels, "bn_grad_sum", (two_sum,))
+    bn_grads = links.first_sums(sums, channels, "bn_grad_sum", (two_sum,))
     out_grad = by_chip(conv_up, [active], "conv_out_w", (bn_grads,))
-    bn_grads = links.sum_group(bn_grads, "bn_grad_sum")
+    bn_grads = links.last_sums(bn_grads, "bn_grad_sum")
     two_sum = links.scatter_grad(two_sum)
     grad_linear, grad_gate, *made = conv_in_grad(
         who,

time: 436 us -> 433 us (level)
  waiting for transfers between devices: 189 us -> 182 us
  starting transfers between devices: 91.1 us -> 95.8 us
    ppermute x27 -> x29, waiting for transfers between devices: 76.5 us -> 70.1 us  [group(): return lax.ppermute(value, 'dp', [(i, i ^ mask) for i in range(self.dp)])]
    ppermute x27 -> x29, starting transfers between devices: 38.4 us -> 39.1 us  [group(): return lax.ppermute(value, 'dp', [(i, i ^ mask) for i in range(self.dp)])]
    pallas_call x87 -> x83, Pallas kernels: 97.7 us -> 97.7 us  [run(): pl.pallas_call(body, in_specs=specs + [pl.BlockSpec(memory_space=pl.ANY)]...]
  transfers between devices with their start and end apart: 164 -> 168, of which waited for: 108 -> 110; matrix products, arithmetic and copies ran while one was open for 0% -> 0% of each run, Pallas kernels for 20% -> 20%
where the time goes in v6:
time: 433 us; the launch traced here: 426 us
  waiting for transfers between devices  182 us (42%)
  Pallas kernels  97.7 us (23%)
  starting transfers between devices  95.8 us (22%)
  local copies, waits for them, and re-layouts  34.8 us (8%)
  between operations  16.2 us (4%)
    pallas_call x83, Pallas kernels, run(): pl.pallas_call(body, in_specs=specs + [pl.BlockSpec(memory_space=pl.ANY)]...  97.7 us
    ppermute x21, waiting for transfers between devices, chip(): lax.ppermute(value, 'tensor', [(i, i ^ 2 * k) for i in range(self.tensor)])  71.5 us
    ppermute x29, waiting for transfers between devices, group(): return lax.ppermute(value, 'dp', [(i, i ^ mask) for i in range(self.dp)])  70.1 us
    ppermute x29, starting transfers between devices, group(): return lax.ppermute(value, 'dp', [(i, i ^ mask) for i in range(self.dp)])  39.1 us
    unnamed x161, local copies, waits for them, and re-layouts  34.8 us
    ppermute x110, starting transfers between devices, core(): lax.ppermute(value, 'tensor', [(i, i ^ 1) for i in range(self.tensor)])  27.6 us
    ppermute x110, waiting for transfers between devices, core(): lax.ppermute(value, 'tensor', [(i, i ^ 1) for i in range(self.tensor)])  24.1 us
    ppermute x21, starting transfers between devices, chip(): lax.ppermute(value, 'tensor', [(i, i ^ 2 * k) for i in range(self.tensor)])  24.1 us
  transfers between devices with their start and end apart: 168, of which 110 were waited for; matrix products, arithmetic and copies ran while one was open for 0% of the time, Pallas kernels for 20%

profile of v6, /device:TPU:0, one launch (start us, length us, event | category | flops | bytes accessed | tf_op | source)
XLA Modules:
  0.0 426.0 jit_solution(7763594460528783764)
XLA Ops:
  11.8 4.9 %collective-permute-done.4.refs_7_ = bf16[384,256]{1,0:T(8,128)(2,1)S(1)} collective-permute-done((bf16[384,256]{1,0:T(8,128)(2,1)S(1)}, bf16[384,256]{1,0:T(8,128)(2,1)S(1)}, u32[]{:S(2)}, u32[]{:S(2)}) %collective-permute-start.4) | collective-permute-done | bytes 196640 | tf_op jit(solution)/shard_map/ppermute | solution.py:1080
  41.5 7.4 %collective-permute-done.20.refs_3_ = bf16[256,1024]{1,0:T(8,128)(2,1)S(1)} collective-permute-done((bf16[256,1024]{1,0:T(8,128)(2,1)S(1)}, bf16[256,1024]{1,0:T(8,128)(2,1)S(1)}, u32[]{:S(2)}, u32[]{:S(2)}) %collective-permute-start.20) | collective-permute-done | bytes 524320 | tf_op jit(solution)/shard_map/ppermute | solution.py:1080
  54.0 5.3 %collective-permute-done.19.refs_3_ = bf16[256,1024]{1,0:T(8,128)(2,1)S(1)} collective-permute-done((bf16[256,1024]{1,0:T(8,128)(2,1)S(1)}, bf16[256,1024]{1,0:T(8,128)(2,1)S(1)}, u32[]{:S(2)}, u32[]{:S(2)}) %collective-permute-start.19) | collective-permute-done | bytes 524320 | tf_op jit(solution)/shard_map/ppermute | solution.py:1080
  70.7 8.6 %attend.1 = (bf16[1024,256]{1,0:T(8,128)(2,1)S(1)}, bf16[2,1024,1024]{2,1,0:T(8,128)(2,1)S(1)}) custom-call(s32[1]{0:T(128)} %bitcast.refs_0_.refs_8_.refs_9_, s32[1]{0:T(128)S(6)} %copy.31.refs_1_, bf16[3,1024,256]{2,1,0:T(8,128)(2,1)S(1)} %get-tuple-element.317.refs_2_.refs_3_.refs_4_.refs_1_, ...), custom_call_target="tpu_custom_call" | custom-call | tf_op jit(solution)/shard_map/attend/pallas_call | solution.py:269
  91.3 8.0 %collective-permute-done.38.refs_7_ = bf16[256,1024]{1,0:T(8,128)(2,1)} collective-permute-done((bf16[256,1024]{1,0:T(8,128)(2,1)}, bf16[256,1024]{1,0:T(8,128)(2,1)}, u32[]{:S(2)}, u32[]{:S(2)}) %collective-permute-start.38) | collective-permute-done | bytes 524320 | tf_op jit(solution)/shard_map/ppermute | solution.py:1080
  104.3 6.8 %collective-permute-done.43.refs_10_.refs_12_ = bf16[16,1024]{1,0:T(8,128)(2,1)S(1)} collective-permute-done((bf16[16,1024]{1,0:T(8,128)(2,1)S(1)}, bf16[16,1024]{1,0:T(8,128)(2,1)S(1)}, u32[]{:S(2)}, u32[]{:S(2)}) %collective-permute-start.43) | collective-permute-done | bytes 32800 | tf_op jit(solution)/shard_map/ppermute | solution.py:1129
  121.2 3.6 collective-permute-start.50
  142.4 5.8 %collective-permute-done.63.refs_0_.refs_2_ = bf16[256,1024]{1,0:T(8,128)(2,1)S(1)} collective-permute-done((bf16[256,1024]{1,0:T(8,128)(2,1)S(1)}, bf16[256,1024]{1,0:T(8,128)(2,1)S(1)}, u32[]{:S(2)}, u32[]{:S(2)}) %collective-permute-start.63) | collective-permute-done | bytes 524320 | tf_op jit(solution)/shard_map/ppermute | solution.py:1080
  155.6 3.7 collective-permute-done.73.refs_6_
  177.4 5.2 %collective-permute-done.90.refs_8_ = bf16[256,1024]{1,0:T(8,128)(2,1)S(1)} collective-permute-done((bf16[256,1024]{1,0:T(8,128)(2,1)S(1)}, bf16[256,1024]{1,0:T(8,128)(2,1)S(1)}, u32[]{:S(2)}, u32[]{:S(2)}) %collective-permute-start.90) | collective-permute-done | bytes 524320 | tf_op jit(solution)/shard_map/ppermute | solution.py:1080
  187.7 6.5 %collective-permute-done.95.refs_11_.refs_13_ = bf16[16,1024]{1,0:T(8,128)(2,1)S(1)} collective-permute-done((bf16[16,1024]{1,0:T(8,128)(2,1)S(1)}, bf16[16,1024]{1,0:T(8,128)(2,1)S(1)}, u32[]{:S(2)}, u32[]{:S(2)}) %collective-permute-start.95) | collective-permute-done | bytes 32800 | tf_op jit(solution)/shard_map/ppermute | solution.py:1129
  197.5 4.5 %ffn_two_w.1 = (bf16[1024,2048]{1,0:T(8,128)(2,1)S(1)}, f32[8,128]{1,0:T(8,128)S(1)}) custom-call(bf16[512,1024]{1,0:T(8,128)(2,1)S(1)} %get-tuple-element.405.refs_0_, bf16[512,1024]{1,0:T(8,128)(2,1)S(1)} %get-tuple-element.406.refs_1_, bf16[512,1024]{1,0:T(8,128)(2,1)S(1)} %get-tuple-element.407.refs_2_, ...), custom_call_target="tpu_custom_call" | custom-call | tf_op jit(solution)/shard_map/ffn_two_w/pallas_call | solution.py:269
  222.3 3.6 collective-permute-done.103.refs_12_.refs_4_
  240.1 12.4 %collective-permute-done.108.refs_0_.refs_2_ = bf16[256,1024]{1,0:T(8,128)(2,1)S(1)} collective-permute-done((bf16[256,1024]{1,0:T(8,128)(2,1)S(1)}, bf16[256,1024]{1,0:T(8,128)(2,1)S(1)}, u32[]{:S(2)}, u32[]{:S(2)}) %collective-permute-start.108) | collective-permute-done | bytes 524320 | tf_op jit(solution)/shard_map/ppermute | solution.py:1080
  260.3 14.8 %attend_back.1 = (bf16[3,1024,256]{2,1,0:T(8,128)(2,1)S(1)}, f32[128,128]{1,0:T(8,128)S(1)}) custom-call(s32[1]{0:T(128)} %bitcast.refs_0_.refs_8_.refs_9_, bf16[3,1024,256]{2,1,0:T(8,128)(2,1)S(1)} %get-tuple-element.317.refs_2_.refs_3_.refs_4_.refs_1_, bf16[3,1024,256]{2,1,0:T(8,128)(2,1)S(1)} %get-tuple-element.317.refs_2_.refs_3_.refs_4_.refs_1_, ...), custom_call_target="tpu_custom_call" | custom-call | tf_op jit(solution)/shard_map/attend_back/pallas_call | solution.py:269
  287.3 7.7 %collective-permute-done.126.refs_4_ = bf16[256,1024]{1,0:T(8,128)(2,1)S(1)} collective-permute-done((bf16[256,1024]{1,0:T(8,128)(2,1)S(1)}, bf16[256,1024]{1,0:T(8,128)(2,1)S(1)}, u32[]{:S(2)}, u32[]{:S(2)}) %collective-permute-start.126) | collective-permute-done | bytes 524320 | tf_op jit(solution)/shard_map/ppermute | solution.py:1080
  304.5 3.1 collective-permute-done.125.refs_3_
  329.1 6.0 %collective-permute-done.144.refs_1_ = bf16[512,512]{1,0:T(8,128)(2,1)S(1)} collective-permute-done((bf16[512,512]{1,0:T(8,128)(2,1)S(1)}, bf16[512,512]{1,0:T(8,128)(2,1)S(1)}, u32[]{:S(2)}, u32[]{:S(2)}) %collective-permute-start.144) | collective-permute-done | bytes 524320 | tf_op jit(solution)/shard_map/ppermute | solution.py:1083
  335.3 11.0 %collective-permute-done.145.refs_3_ = bf16[512,512]{1,0:T(8,128)(2,1)S(1)} collective-permute-done((bf16[512,512]{1,0:T(8,128)(2,1)S(1)}, bf16[512,512]{1,0:T(8,128)(2,1)S(1)}, u32[]{:S(2)}, u32[]{:S(2)}) %collective-permute-start.145) | collective-permute-done | bytes 524320 | tf_op jit(solution)/shard_map/ppermute | solution.py:1083
  350.8 6.3 %collective-permute-done.153.refs_3_ = bf16[512,512]{1,0:T(8,128)(2,1)S(1)} collective-permute-done((bf16[512,512]{1,0:T(8,128)(2,1)S(1)}, bf16[512,512]{1,0:T(8,128)(2,1)S(1)}, u32[]{:S(2)}, u32[]{:S(2)}) %collective-permute-start.153) | collective-permute-done | bytes 524320 | tf_op jit(solution)/shard_map/ppermute | solution.py:1083
  359.3 9.6 %collective-permute-done.151.refs_3_ = bf16[128,768]{1,0:T(8,128)(2,1)S(1)} collective-permute-done((bf16[128,768]{1,0:T(8,128)(2,1)S(1)}, bf16[128,768]{1,0:T(8,128)(2,1)S(1)}, u32[]{:S(2)}, u32[]{:S(2)}) %collective-permute-start.151) | collective-permute-done | bytes 196640 | tf_op jit(solution)/shard_map/ppermute | solution.py:1083
  383.0 3.3 collective-permute-done.159.refs_1_
  387.6 3.3 collective-permute-start.162
  396.8 10.0 %collective-permute-done.162.refs_1_ = bf16[128,512]{1,0:T(8,128)(2,1)S(1)} collective-permute-done((bf16[128,512]{1,0:T(8,128)(2,1)S(1)}, bf16[128,512]{1,0:T(8,128)(2,1)S(1)}, u32[]{:S(2)}, u32[]{:S(2)}) %collective-permute-start.162) | collective-permute-done | bytes 131104 | tf_op jit(solution)/shard_map/ppermute | solution.py:1083
  (559 shorter events, 248.2 us)
Async XLA Ops:
  7.2 78.4 %all-gather.2.cloned.1.call-start = ((), (), s32[]{:S(2)}) async-start(), calls=%async_computation.1 | async-start | bytes 1769472 | tf_op jit(solution)/shard_map/all_gather | solution.py:1350
  17.4 399.5 %reduce-scatter.2.cloned.1.call-start = ((), (), s32[]{:S(2)}) async-start(), calls=%async_computation.2 | async-start | bytes 4718592 | tf_op jit(solution)/shard_map/reduce_scatter | solution.py:1086
  17.8 14.8 %collective-permute-start.9 = (bf16[256,1024]{1,0:T(8,128)(2,1)S(1)}, bf16[256,1024]{1,0:T(8,128)(2,1)S(1)}, u32[]{:S(2)}, u32[]{:S(2)}) collective-permute-start(bf16[256,1024]{1,0:T(8,128)(2,1)S(1)} %get-tuple-element.294), channel_id=1, source_target_pairs={{0,2},{1,3},{2,0},{3,1},{4,6},{5,7},{6,4},{7,5},{8,10},{9,11},{10,... | collective-permute-start | bytes 1572872 | tf_op jit(solution)/shard_map/ppermute | solution.py:1080
  34.1 14.8 %collective-permute-start.20 = (bf16[256,1024]{1,0:T(8,128)(2,1)S(1)}, bf16[256,1024]{1,0:T(8,128)(2,1)S(1)}, u32[]{:S(2)}, u32[]{:S(2)}) collective-permute-start(bf16[256,1024]{1,0:T(8,128)(2,1)S(1)} %ffn_one_sum.2.refs_2_), channel_id=1, source_target_pairs={{0,2},{1,3},{2,0},{3,1},{4,6},{5,7},{6,4},{7,5},{8,10},{9,11},{10,... | collective-permute-start | bytes 1572872 | tf_op jit(solution)/shard_map/ppermute | solution.py:1080
  40.3 19.0 %collective-permute-start.19 = (bf16[256,1024]{1,0:T(8,128)(2,1)S(1)}, bf16[256,1024]{1,0:T(8,128)(2,1)S(1)}, u32[]{:S(2)}, u32[]{:S(2)}) collective-permute-start(bf16[256,1024]{1,0:T(8,128)(2,1)S(1)} %ffn_one_sum.3.refs_2_), channel_id=1, source_target_pairs={{0,2},{1,3},{2,0},{3,1},{4,6},{5,7},{6,4},{7,5},{8,10},{9,11},{10,... | collective-permute-start | bytes 1572872 | tf_op jit(solution)/shard_map/ppermute | solution.py:1080
  62.5 18.9 %collective-permute-start.29 = (bf16[256,1024]{1,0:T(8,128)(2,1)}, bf16[256,1024]{1,0:T(8,128)(2,1)}, u32[]{:S(2)}, u32[]{:S(2)}) collective-permute-start(bf16[256,1024]{1,0:T(8,128)(2,1)} %get-tuple-element.321), channel_id=1, source_target_pairs={{0,2},{1,3},{2,0},{3,1},{4,6},{5,7},{6,4},{7,5},{8,10},{9,11},{10,... | collective-permute-start | bytes 1572872 | tf_op jit(solution)/shard_map/ppermute | solution.py:1080
  133.3 14.8 %collective-permute-start.63 = (bf16[256,1024]{1,0:T(8,128)(2,1)S(1)}, bf16[256,1024]{1,0:T(8,128)(2,1)S(1)}, u32[]{:S(2)}, u32[]{:S(2)}) collective-permute-start(bf16[256,1024]{1,0:T(8,128)(2,1)S(1)} %get-tuple-element.361), channel_id=1, source_target_pairs={{0,2},{1,3},{2,0},{3,1},{4,6},{5,7},{6,4},{7,5},{8,10},{9,11},{10,... | collective-permute-start | bytes 1572872 | tf_op jit(solution)/shard_map/ppermute | solution.py:1080
  140.4 18.9 %collective-permute-start.73 = (bf16[256,1024]{1,0:T(8,128)(2,1)S(1)}, bf16[256,1024]{1,0:T(8,128)(2,1)S(1)}, u32[]{:S(2)}, u32[]{:S(2)}) collective-permute-start(bf16[256,1024]{1,0:T(8,128)(2,1)S(1)} %ffn_two_sum.2.refs_2_.refs_5_), channel_id=1, source_target_pairs={{0,2},{1,3},{2,0},{3,1},{4,6},{5,7},{6,4},{7,5},{8,10},{9,11},{10,... | collective-permute-start | bytes 1572872 | tf_op jit(solution)/shard_map/ppermute | solution.py:1080
  253.8 33.1 %collective-permute-start.124 = (bf16[1024,512]{1,0:T(8,128)(2,1)S(1)}, bf16[1024,512]{1,0:T(8,128)(2,1)S(1)}, u32[]{:S(2)}, u32[]{:S(2)}) collective-permute-start(bf16[1024,512]{1,0:T(8,128)(2,1)S(1)} %get-tuple-element.455), channel_id=1, source_target_pairs={{0,2},{1,3},{2,0},{3,1},{4,6},{5,7},{6,4},{7,5},{8,10},{9,11},{10,... | collective-permute-start | bytes 3145736 | tf_op jit(solution)/shard_map/ppermute | solution.py:1080
  284.3 25.4 %collective-permute-start.123 = (bf16[512,1024]{1,0:T(8,128)(2,1)S(1)}, bf16[512,1024]{1,0:T(8,128)(2,1)S(1)}, u32[]{:S(2)}, u32[]{:S(2)}) collective-permute-start(bf16[512,1024]{1,0:T(8,128)(2,1)S(1)} %get-tuple-element.453), channel_id=1, source_target_pairs={{0,4},{4,0},{8,12},{12,8},{16,20},{20,16},{24,28},{28,24},{1,5},{5... | collective-permute-start | bytes 3145736 | tf_op jit(solution)/shard_map/ppermute | solution.py:1083
  287.3 20.3 %collective-permute-start.125 = (bf16[512,768]{1,0:T(8,128)(2,1)S(1)}, bf16[512,768]{1,0:T(8,128)(2,1)S(1)}, u32[]{:S(2)}, u32[]{:S(2)}) collective-permute-start(bf16[512,768]{1,0:T(8,128)(2,1)S(1)} %get-tuple-element.459), channel_id=1, source_target_pairs={{0,8},{4,12},{8,0},{12,4},{16,24},{20,28},{24,16},{28,20},{1,9},{5... | collective-permute-start | bytes 2359304 | tf_op jit(solution)/shard_map/ppermute | solution.py:1083
  319.2 15.9 %collective-permute-start.144 = (bf16[512,512]{1,0:T(8,128)(2,1)S(1)}, bf16[512,512]{1,0:T(8,128)(2,1)S(1)}, u32[]{:S(2)}, u32[]{:S(2)}) collective-permute-start(bf16[512,512]{1,0:T(8,128)(2,1)S(1)} %get-tuple-element.491), channel_id=1, source_target_pairs={{0,4},{4,0},{8,12},{12,8},{16,20},{20,16},{24,28},{28,24},{1,5},{5... | collective-permute-start | bytes 1572872 | tf_op jit(solution)/shard_map/ppermute | solution.py:1083
  321.3 25.0 %collective-permute-start.145 = (bf16[512,512]{1,0:T(8,128)(2,1)S(1)}, bf16[512,512]{1,0:T(8,128)(2,1)S(1)}, u32[]{:S(2)}, u32[]{:S(2)}) collective-permute-start(bf16[512,512]{1,0:T(8,128)(2,1)S(1)} %get-tuple-element.494), channel_id=1, source_target_pairs={{0,4},{4,0},{8,12},{12,8},{16,20},{20,16},{24,28},{28,24},{1,5},{5... | collective-permute-start | bytes 1572872 | tf_op jit(solution)/shard_map/ppermute | solution.py:1083
  322.6 26.1 %collective-permute-start.143 = (bf16[256,1024]{1,0:T(8,128)(2,1)S(1)}, bf16[256,1024]{1,0:T(8,128)(2,1)S(1)}, u32[]{:S(2)}, u32[]{:S(2)}) collective-permute-start(bf16[256,1024]{1,0:T(8,128)(2,1)S(1)} %ffn_one_grad_sum.1.refs_4_), channel_id=1, source_target_pairs={{0,2},{1,3},{2,0},{3,1},{4,6},{5,7},{6,4},{7,5},{8,10},{9,11},{10,... | collective-permute-start | bytes 1572872 | tf_op jit(solution)/shard_map/ppermute | solution.py:1080
  326.3 30.7 %collective-permute-start.153 = (bf16[512,512]{1,0:T(8,128)(2,1)S(1)}, bf16[512,512]{1,0:T(8,128)(2,1)S(1)}, u32[]{:S(2)}, u32[]{:S(2)}) collective-permute-start(bf16[512,512]{1,0:T(8,128)(2,1)S(1)} %get-tuple-element.518), channel_id=1, source_target_pairs={{0,4},{4,0},{8,12},{12,8},{16,20},{20,16},{24,28},{28,24},{1,5},{5... | collective-permute-start | bytes 1572872 | tf_op jit(solution)/shard_map/ppermute | solution.py:1083
  327.3 31.9 %collective-permute-start.152 = (bf16[512,512]{1,0:T(8,128)(2,1)S(1)}, bf16[512,512]{1,0:T(8,128)(2,1)S(1)}, u32[]{:S(2)}, u32[]{:S(2)}) collective-permute-start(bf16[512,512]{1,0:T(8,128)(2,1)S(1)} %get-tuple-element.516), channel_id=1, source_target_pairs={{0,8},{4,12},{8,0},{12,4},{16,24},{20,28},{24,16},{28,20},{1,9},{5... | collective-permute-start | bytes 1572872 | tf_op jit(solution)/shard_map/ppermute | solution.py:1083
  346.3 22.6 %collective-permute-start.150 = (bf16[128,1024]{1,0:T(8,128)(2,1)S(1)}, bf16[128,1024]{1,0:T(8,128)(2,1)S(1)}, u32[]{:S(2)}, u32[]{:S(2)}) collective-permute-start(bf16[128,1024]{1,0:T(8,128)(2,1)S(1)} %get-tuple-element.512), channel_id=1, source_target_pairs={{0,16},{4,20},{8,24},{12,28},{16,0},{20,4},{24,8},{28,12},{1,17},{... | collective-permute-start | bytes 786440 | tf_op jit(solution)/shard_map/ppermute | solution.py:1083
  348.7 20.9 %collective-permute-start.148 = (bf16[256,512]{1,0:T(8,128)(2,1)S(1)}, bf16[256,512]{1,0:T(8,128)(2,1)S(1)}, u32[]{:S(2)}, u32[]{:S(2)}) collective-permute-start(bf16[256,512]{1,0:T(8,128)(2,1)S(1)} %get-tuple-element.508), channel_id=1, source_target_pairs={{0,8},{4,12},{8,0},{12,4},{16,24},{20,28},{24,16},{28,20},{1,9},{5... | collective-permute-start | bytes 786440 | tf_op jit(solution)/shard_map/ppermute | solution.py:1083
  349.8 21.5 %collective-permute-start.149 = (bf16[256,512]{1,0:T(8,128)(2,1)S(1)}, bf16[256,512]{1,0:T(8,128)(2,1)S(1)}, u32[]{:S(2)}, u32[]{:S(2)}) collective-permute-start(bf16[256,512]{1,0:T(8,128)(2,1)S(1)} %get-tuple-element.510), channel_id=1, source_target_pairs={{0,8},{4,12},{8,0},{12,4},{16,24},{20,28},{24,16},{28,20},{1,9},{5... | collective-permute-start | bytes 786440 | tf_op jit(solution)/shard_map/ppermute | solution.py:1083
  387.6 19.2 %collective-permute-start.162 = (bf16[128,512]{1,0:T(8,128)(2,1)S(1)}, bf16[128,512]{1,0:T(8,128)(2,1)S(1)}, u32[]{:S(2)}, u32[]{:S(2)}) collective-permute-start(bf16[128,512]{1,0:T(8,128)(2,1)S(1)} %get-tuple-element.538), channel_id=1, source_target_pairs={{0,16},{4,20},{8,24},{12,28},{16,0},{20,4},{24,8},{28,12},{1,17},{... | collective-permute-start | bytes 393224 | tf_op jit(solution)/shard_map/ppermute | solution.py:1083
  390.9 18.7 %collective-permute-start.163 = (bf16[128,512]{1,0:T(8,128)(2,1)S(1)}, bf16[128,512]{1,0:T(8,128)(2,1)S(1)}, u32[]{:S(2)}, u32[]{:S(2)}) collective-permute-start(bf16[128,512]{1,0:T(8,128)(2,1)S(1)} %get-tuple-element.540), channel_id=1, source_target_pairs={{0,16},{4,20},{8,24},{12,28},{16,0},{20,4},{24,8},{28,12},{1,17},{... | collective-permute-start | bytes 393224 | tf_op jit(solution)/shard_map/ppermute | solution.py:1083
  390.9 21.5 %collective-permute-start.164 = (bf16[128,512]{1,0:T(8,128)(2,1)S(1)}, bf16[128,512]{1,0:T(8,128)(2,1)S(1)}, u32[]{:S(2)}, u32[]{:S(2)}) collective-permute-start(bf16[128,512]{1,0:T(8,128)(2,1)S(1)} %get-tuple-element.542), channel_id=1, source_target_pairs={{0,16},{4,20},{8,24},{12,28},{16,0},{20,4},{24,8},{28,12},{1,17},{... | collective-permute-start | bytes 393224 | tf_op jit(solution)/shard_map/ppermute | solution.py:1083
  393.8 21.3 %collective-permute-start.165 = (bf16[128,512]{1,0:T(8,128)(2,1)S(1)}, bf16[128,512]{1,0:T(8,128)(2,1)S(1)}, u32[]{:S(2)}, u32[]{:S(2)}) collective-permute-start(bf16[128,512]{1,0:T(8,128)(2,1)S(1)} %get-tuple-element.544), channel_id=1, source_target_pairs={{0,16},{4,20},{8,24},{12,28},{16,0},{20,4},{24,8},{28,12},{1,17},{... | collective-permute-start | bytes 393224 | tf_op jit(solution)/shard_map/ppermute | solution.py:1083
  393.9 22.3 %collective-permute-start.161 = (f32[184,128]{1,0:T(8,128)S(1)}, f32[184,128]{1,0:T(8,128)S(1)}, u32[]{:S(2)}, u32[]{:S(2)}) collective-permute-start(f32[184,128]{1,0:T(8,128)S(1)} %bundle_sum.8.refs_0_), channel_id=1, source_target_pairs={{0,16},{4,20},{8,24},{12,28},{16,0},{20,4},{24,8},{28,12},{1,17},{... | collective-permute-start | bytes 282632 | tf_op jit(solution)/shard_map/ppermute | solution.py:1083
  (224 other events, 1167.0 us)
Sparse Core Ops, SparseCore 0:
  17.5 45.6 all-gather.1
  204.9 87.1 reduce-scatter.1
